TPU v7x, 128 devices: a whole 4x4x4 slice. The times are simulated.
128 devices in a mesh: shard: 8 (over z, y_lo), ctx: 16 (over y_hi, x, core).
Axes of the slice: x: 4, y: 4 (y_hi: 2, y_lo: 2; y = y_hi * 2 + y_lo), z: 4, core: 2. Of those that a mesh axis runs over, the one named last changes fastest.
Arguments:
- states: bfloat16 [8, 2048, 768], P('shard', 'ctx'), may hold values from -6 to 6
- cotangent: bfloat16 [8, 2048, 768], P('shard', 'ctx'), may hold values from -6 to 6
- pair_order: int32 [16], replicated, may hold values from 0 to 15, each once
- norm1_gain: bfloat16 [2, 768], P(None, 'shard'), may hold values from 0.5 to 1.5
- norm1_bias: bfloat16 [2, 768], P(None, 'shard'), may hold values from -2 to 2
- qkv_weight: bfloat16 [2, 768, 2304], P(None, 'shard'), may hold values from -0.21875 to 0.21875
- query_bias: bfloat16 [2, 768], P(None, 'shard'), may hold values from -2 to 2
- value_bias: bfloat16 [2, 768], P(None, 'shard'), may hold values from -0.29882812 to 0.29882812
- out_weight: bfloat16 [2, 768, 768], P(None, 'shard'), may hold values from -1.75 to 1.75
- out_bias: bfloat16 [2, 768], P(None, 'shard'), may hold values from -2 to 2
- norm2_gain: bfloat16 [2, 768], P(None, 'shard'), may hold values from 0.5 to 1.5
- norm2_bias: bfloat16 [2, 768], P(None, 'shard'), may hold values from -2 to 2
- up_weight: bfloat16 [2, 768, 3072], P(None, 'shard'), may hold values from -0.21875 to 0.21875
- up_bias: bfloat16 [2, 3072], P(None, 'shard'), may hold values from -2 to 2
- down_weight: bfloat16 [2, 3072, 768], P(None, 'shard'), may hold values from -0.109375 to 0.109375
- down_bias: bfloat16 [2, 768], P(None, 'shard'), may hold values from -2 to 2
Outputs:
- states_out: bfloat16 [8, 2048, 768], P('shard', 'ctx')
- states_grad: bfloat16 [8, 2048, 768], P('shard', 'ctx')
- norm1_gain_grad: float32 [2, 768], P(None, 'shard')
- norm1_bias_grad: float32 [2, 768], P(None, 'shard')
- qkv_weight_grad: float32 [2, 768, 2304], P(None, 'shard')
- query_bias_grad: float32 [2, 768], P(None, 'shard')
- value_bias_grad: float32 [2, 768], P(None, 'shard')
- out_weight_grad: float32 [2, 768, 768], P(None, 'shard')
- out_bias_grad: float32 [2, 768], P(None, 'shard')
- norm2_gain_grad: float32 [2, 768], P(None, 'shard')
- norm2_bias_grad: float32 [2, 768], P(None, 'shard')
- up_weight_grad: float32 [2, 768, 3072], P(None, 'shard')
- up_bias_grad: float32 [2, 3072], P(None, 'shard')
- down_weight_grad: float32 [2, 3072, 768], P(None, 'shard')
- down_bias_grad: float32 [2, 768], P(None, 'shard')
Inputs may be any that keep to these rules, and one draw needn't show every extreme that they name: `pair_order`: each number appears once.
All inputs are finite; a program needn't handle non-finite values.
Results may differ from a plain program's by a relative error of at most 0.02.
Values may be sent and summed in bfloat16 or wider, within the bound.
No kernel may reach another device: no remote copies, remote signals or barrier semaphores. Data moves between devices by JAX's collectives and lax.ppermute only.
A program may use at most 192 MiB of HBM per device.

v0:
```python
import math

import jax
import jax.numpy as jnp
from jax import lax
from jax.sharding import PartitionSpec as P

H = 12
HD = 64


EPSILON = 1e-05
NEGATIVE = -1e30


def layer_norm(states, gain, shift):
    average = jnp.mean(states, axis=-1, keepdims=True)
    centered = states - average
    spread = jnp.mean(centered * centered, axis=-1, keepdims=True)
    return centered * lax.rsqrt(spread + EPSILON) * gain + shift


def attention_probs(queries, keys_all, visible):
    scale = 1.0 / math.sqrt(HD)
    scores = (
        jnp.einsum("sqhd,skhd->shqk", queries, keys_all, preferred_element_type=jnp.float32) * scale
    )
    scores = jnp.where(visible[None, None], scores, NEGATIVE)
    highest = jnp.max(scores, axis=-1, keepdims=True)
    weights = jnp.exp(scores - highest)
    total = jnp.sum(weights, axis=-1, keepdims=True)
    log_total = (highest + jnp.log(total))[..., 0]
    return (weights / total, log_total)


def forward_layer(flowing, params, visible, seq_dev, tok_dev):
    (
        gain_one,
        bias_one,
        qkv_full,
        query_shift,
        value_shift,
        out_full,
        out_shift,
        gain_two,
        bias_two,
        up_full,
        up_shift,
        down_full,
        down_shift,
    ) = params
    width = flowing.shape[1]
    normed = layer_norm(flowing, gain_one.astype(jnp.float32), bias_one.astype(jnp.float32)).astype(
        jnp.bfloat16
    )
    projected = jnp.dot(normed, qkv_full, preferred_element_type=jnp.float32)
    queries = (projected[:, :width] + query_shift.astype(jnp.float32)).astype(jnp.bfloat16)
    keys_local = projected[:, width : 2 * width].astype(jnp.bfloat16)
    values_local = (projected[:, 2 * width :] + value_shift.astype(jnp.float32)).astype(
        jnp.bfloat16
    )
    keys_all, values_all = (
        lax.all_gather(keys_local.reshape(seq_dev, tok_dev, width), "ctx", axis=1, tiled=True),
        lax.all_gather(values_local.reshape(seq_dev, tok_dev, width), "ctx", axis=1, tiled=True),
    )
    query_heads = queries.reshape(seq_dev, tok_dev, H, HD)
    probs, unused = attention_probs(query_heads, keys_all.reshape(seq_dev, -1, H, HD), visible)
    mixed = (
        jnp.einsum(
            "shqk,skhd->sqhd",
            probs.astype(jnp.bfloat16),
            values_all.reshape(seq_dev, -1, H, HD),
            preferred_element_type=jnp.float32,
        )
        .reshape(-1, width)
        .astype(jnp.bfloat16)
    )
    middle = (
        flowing
        + jnp.dot(mixed, out_full, preferred_element_type=jnp.float32)
        + out_shift.astype(jnp.float32)
    )
    second = layer_norm(middle, gain_two.astype(jnp.float32), bias_two.astype(jnp.float32)).astype(
        jnp.bfloat16
    )
    hidden = jnp.dot(second, up_full, preferred_element_type=jnp.float32) + up_shift.astype(
        jnp.float32
    )
    activated = jax.nn.gelu(hidden, approximate=True).astype(jnp.bfloat16)
    output = (
        middle
        + jnp.dot(activated, down_full, preferred_element_type=jnp.float32)
        + down_shift.astype(jnp.float32)
    )
    saved = (
        flowing,
        normed,
        queries,
        keys_all,
        values_all,
        mixed,
        middle,
        second,
        hidden,
        activated,
    )
    return (output, saved)


def backward_layer(grad_out, saved, params, visible, seq_dev, tok_dev):
    (
        gain_one,
        bias_one,
        qkv_full,
        query_shift,
        value_shift,
        out_full,
        out_shift,
        gain_two,
        bias_two,
        up_full,
        up_shift,
        down_full,
        down_shift,
    ) = params
    flowing, normed, queries, keys_all, values_all, mixed, middle, second, hidden, activated = saved
    width = flowing.shape[1]
    scale = 1.0 / math.sqrt(HD)
    down_in = grad_out.astype(jnp.bfloat16)
    down_shift_grad = jnp.sum(down_in.astype(jnp.float32), axis=0)
    down_full_grad = jnp.dot(activated.T, down_in, preferred_element_type=jnp.float32)
    activated_grad = jnp.dot(down_in, down_full.T, preferred_element_type=jnp.float32)
    unused, gelu_back = jax.vjp(lambda inner: jax.nn.gelu(inner, approximate=True), hidden)
    hidden_grad = gelu_back(activated_grad)[0].astype(jnp.bfloat16)
    up_shift_grad = jnp.sum(hidden_grad.astype(jnp.float32), axis=0)
    up_full_grad = jnp.dot(second.T, hidden_grad, preferred_element_type=jnp.float32)
    second_grad = jnp.dot(hidden_grad, up_full.T, preferred_element_type=jnp.float32)
    unused, norm_back = jax.vjp(
        layer_norm, middle, gain_two.astype(jnp.float32), bias_two.astype(jnp.float32)
    )
    middle_part, gain_two_grad, bias_two_grad = norm_back(second_grad)
    middle_grad = grad_out + middle_part
    attended_in = middle_grad.astype(jnp.bfloat16)
    out_shift_grad = jnp.sum(attended_in.astype(jnp.float32), axis=0)
    out_full_grad = jnp.dot(mixed.T, attended_in, preferred_element_type=jnp.float32)
    mixed_grad = jnp.dot(attended_in, out_full.T, preferred_element_type=jnp.float32).astype(
        jnp.bfloat16
    )
    query_heads = queries.reshape(seq_dev, tok_dev, H, HD)
    key_heads = keys_all.reshape(seq_dev, -1, H, HD)
    value_heads = values_all.reshape(seq_dev, -1, H, HD)
    mixed_heads = mixed_grad.reshape(seq_dev, tok_dev, H, HD)
    probs, log_total = attention_probs(query_heads, key_heads, visible)
    probs_grad = jnp.einsum(
        "sqhd,skhd->shqk", mixed_heads, value_heads, preferred_element_type=jnp.float32
    )
    inner_sum = jnp.sum(probs * probs_grad, axis=-1, keepdims=True)
    scores_grad = (probs * (probs_grad - inner_sum)).astype(jnp.bfloat16)
    queries_grad = (
        scale
        * jnp.einsum("shqk,skhd->sqhd", scores_grad, key_heads, preferred_element_type=jnp.float32)
    ).astype(jnp.bfloat16)
    values_part = jnp.einsum(
        "shqk,sqhd->skhd",
        probs.astype(jnp.bfloat16),
        mixed_heads,
        preferred_element_type=jnp.float32,
    )
    keys_part = scale * jnp.einsum(
        "shqk,sqhd->skhd", scores_grad, query_heads, preferred_element_type=jnp.float32
    )
    keys_summed, values_summed = (
        lax.psum_scatter(
            keys_part.reshape(seq_dev, -1, width).astype(jnp.bfloat16),
            "ctx",
            scatter_dimension=1,
            tiled=True,
        ).astype(jnp.float32),
        lax.psum_scatter(
            values_part.reshape(seq_dev, -1, width).astype(jnp.bfloat16),
            "ctx",
            scatter_dimension=1,
            tiled=True,
        ).astype(jnp.float32),
    )
    keys_grad = keys_summed.reshape(-1, width).astype(jnp.bfloat16)
    values_grad = values_summed.reshape(-1, width).astype(jnp.bfloat16)
    queries_grad = queries_grad.reshape(-1, width)
    project_grad = jnp.concatenate([queries_grad, keys_grad, values_grad], axis=1)
    query_shift_grad = jnp.sum(queries_grad.astype(jnp.float32), axis=0)
    value_shift_grad = jnp.sum(values_grad.astype(jnp.float32), axis=0)
    qkv_full_grad = jnp.dot(normed.T, project_grad, preferred_element_type=jnp.float32)
    normed_grad = jnp.dot(project_grad, qkv_full.T, preferred_element_type=jnp.float32)
    unused, first_back = jax.vjp(
        layer_norm, flowing, gain_one.astype(jnp.float32), bias_one.astype(jnp.float32)
    )
    flowing_part, gain_one_grad, bias_one_grad = first_back(normed_grad)
    grads = (
        gain_one_grad,
        bias_one_grad,
        qkv_full_grad,
        query_shift_grad,
        value_shift_grad,
        out_full_grad,
        out_shift_grad,
        gain_two_grad,
        bias_two_grad,
        up_full_grad,
        up_shift_grad,
        down_full_grad,
        down_shift_grad,
    )
    return (middle_grad + flowing_part, grads)


def reduce_grads(grads):
    pieces = (
        lax.psum_scatter(
            grads[0].astype(jnp.bfloat16), "shard", scatter_dimension=0, tiled=True
        ).astype(jnp.float32),
        lax.psum_scatter(
            grads[1].astype(jnp.bfloat16), "shard", scatter_dimension=0, tiled=True
        ).astype(jnp.float32),
        lax.psum_scatter(
            grads[2].astype(jnp.bfloat16), "shard", scatter_dimension=0, tiled=True
        ).astype(jnp.float32),
        lax.psum_scatter(
            grads[3].astype(jnp.bfloat16), "shard", scatter_dimension=0, tiled=True
        ).astype(jnp.float32),
        lax.psum_scatter(
            grads[4].astype(jnp.bfloat16), "shard", scatter_dimension=0, tiled=True
        ).astype(jnp.float32),
        lax.psum_scatter(
            grads[5].astype(jnp.bfloat16), "shard", scatter_dimension=0, tiled=True
        ).astype(jnp.float32),
        lax.psum_scatter(
            grads[6].astype(jnp.bfloat16), "shard", scatter_dimension=0, tiled=True
        ).astype(jnp.float32),
        lax.psum_scatter(
            grads[7].astype(jnp.bfloat16), "shard", scatter_dimension=0, tiled=True
        ).astype(jnp.float32),
        lax.psum_scatter(
            grads[8].astype(jnp.bfloat16), "shard", scatter_dimension=0, tiled=True
        ).astype(jnp.float32),
        lax.psum_scatter(
            grads[9].astype(jnp.bfloat16), "shard", scatter_dimension=0, tiled=True
        ).astype(jnp.float32),
        lax.psum_scatter(
            grads[10].astype(jnp.bfloat16), "shard", scatter_dimension=0, tiled=True
        ).astype(jnp.float32),
        lax.psum_scatter(
            grads[11].astype(jnp.bfloat16), "shard", scatter_dimension=0, tiled=True
        ).astype(jnp.float32),
        lax.psum_scatter(
            grads[12].astype(jnp.bfloat16), "shard", scatter_dimension=0, tiled=True
        ).astype(jnp.float32),
    )
    return (
        lax.psum(pieces[0].astype(jnp.bfloat16), "ctx").astype(jnp.float32),
        lax.psum(pieces[1].astype(jnp.bfloat16), "ctx").astype(jnp.float32),
        lax.psum(pieces[2].astype(jnp.bfloat16), "ctx").astype(jnp.float32),
        lax.psum(pieces[3].astype(jnp.bfloat16), "ctx").astype(jnp.float32),
        lax.psum(pieces[4].astype(jnp.bfloat16), "ctx").astype(jnp.float32),
        lax.psum(pieces[5].astype(jnp.bfloat16), "ctx").astype(jnp.float32),
        lax.psum(pieces[6].astype(jnp.bfloat16), "ctx").astype(jnp.float32),
        lax.psum(pieces[7].astype(jnp.bfloat16), "ctx").astype(jnp.float32),
        lax.psum(pieces[8].astype(jnp.bfloat16), "ctx").astype(jnp.float32),
        lax.psum(pieces[9].astype(jnp.bfloat16), "ctx").astype(jnp.float32),
        lax.psum(pieces[10].astype(jnp.bfloat16), "ctx").astype(jnp.float32),
        lax.psum(pieces[11].astype(jnp.bfloat16), "ctx").astype(jnp.float32),
        lax.psum(pieces[12].astype(jnp.bfloat16), "ctx").astype(jnp.float32),
    )


def shards(
    states,
    cotangent,
    pair_order,
    norm1_gain,
    norm1_bias,
    qkv_weight,
    query_bias,
    value_bias,
    out_weight,
    out_bias,
    norm2_gain,
    norm2_bias,
    up_weight,
    up_bias,
    down_weight,
    down_bias,
):
    seq_dev, tok_dev, width = states.shape
    ctx_count = lax.axis_size("ctx")
    half_block = tok_dev // 2
    within = jnp.arange(tok_dev, dtype=jnp.int32)

    def place(pair):
        blocks = jnp.where(within < half_block, pair, 2 * ctx_count - 1 - pair)
        return blocks * half_block + within % half_block

    key_spots = jax.vmap(place)(pair_order).reshape(-1)
    query_spots = place(pair_order[lax.axis_index("ctx")])
    visible = query_spots[:, None] >= key_spots[None, :]
    layers_count = norm1_gain.shape[0]
    flowing = states.reshape(-1, width).astype(jnp.float32)
    kept_params = []
    saved_all = []
    for layer_index in range(layers_count):
        full = (
            lax.all_gather(norm1_gain[layer_index], "shard", axis=0, tiled=True),
            lax.all_gather(norm1_bias[layer_index], "shard", axis=0, tiled=True),
            lax.all_gather(qkv_weight[layer_index], "shard", axis=0, tiled=True),
            lax.all_gather(query_bias[layer_index], "shard", axis=0, tiled=True),
            lax.all_gather(value_bias[layer_index], "shard", axis=0, tiled=True),
            lax.all_gather(out_weight[layer_index], "shard", axis=0, tiled=True),
            lax.all_gather(out_bias[layer_index], "shard", axis=0, tiled=True),
            lax.all_gather(norm2_gain[layer_index], "shard", axis=0, tiled=True),
            lax.all_gather(norm2_bias[layer_index], "shard", axis=0, tiled=True),
            lax.all_gather(up_weight[layer_index], "shard", axis=0, tiled=True),
            lax.all_gather(up_bias[layer_index], "shard", axis=0, tiled=True),
            lax.all_gather(down_weight[layer_index], "shard", axis=0, tiled=True),
            lax.all_gather(down_bias[layer_index], "shard", axis=0, tiled=True),
        )
        kept_params.append(full)
        flowing, saved = forward_layer(flowing, full, visible, seq_dev, tok_dev)
        saved_all.append(saved)
    result = flowing.astype(jnp.bfloat16).reshape(states.shape)
    grad_flow = cotangent.reshape(-1, width).astype(jnp.float32)
    collected = [None] * layers_count
    for layer_index in range(layers_count - 1, -1, -1):
        full = (
            lax.all_gather(norm1_gain[layer_index], "shard", axis=0, tiled=True),
            lax.all_gather(norm1_bias[layer_index], "shard", axis=0, tiled=True),
            lax.all_gather(qkv_weight[layer_index], "shard", axis=0, tiled=True),
            lax.all_gather(query_bias[layer_index], "shard", axis=0, tiled=True),
            lax.all_gather(value_bias[layer_index], "shard", axis=0, tiled=True),
            lax.all_gather(out_weight[layer_index], "shard", axis=0, tiled=True),
            lax.all_gather(out_bias[layer_index], "shard", axis=0, tiled=True),
            lax.all_gather(norm2_gain[layer_index], "shard", axis=0, tiled=True),
            lax.all_gather(norm2_bias[layer_index], "shard", axis=0, tiled=True),
            lax.all_gather(up_weight[layer_index], "shard", axis=0, tiled=True),
            lax.all_gather(up_bias[layer_index], "shard", axis=0, tiled=True),
            lax.all_gather(down_weight[layer_index], "shard", axis=0, tiled=True),
            lax.all_gather(down_bias[layer_index], "shard", axis=0, tiled=True),
        )
        grad_flow, grads = backward_layer(
            grad_flow, saved_all[layer_index], full, visible, seq_dev, tok_dev
        )
        collected[layer_index] = reduce_grads(grads)
    stacked = tuple(
        (
            jnp.stack([collected[layer_index][member_index] for layer_index in range(layers_count)])
            for member_index in range(13)
        )
    )
    return (result, grad_flow.astype(jnp.bfloat16).reshape(states.shape)) + stacked


def solution(mesh):
    placed = (
        P("shard", "ctx", None),
        P("shard", "ctx", None),
        P(),
        P(None, "shard"),
        P(None, "shard"),
        P(None, "shard", None),
        P(None, "shard"),
        P(None, "shard"),
        P(None, "shard", None),
        P(None, "shard"),
        P(None, "shard"),
        P(None, "shard"),
        P(None, "shard", None),
        P(None, "shard"),
        P(None, "shard", None),
        P(None, "shard"),
    )
    return jax.shard_map(
        shards,
        mesh=mesh,
        in_specs=placed,
        out_specs=(
            P("shard", "ctx", None),
            P("shard", "ctx", None),
            P(None, "shard"),
            P(None, "shard"),
            P(None, "shard", None),
            P(None, "shard"),
            P(None, "shard"),
            P(None, "shard", None),
            P(None, "shard"),
            P(None, "shard"),
            P(None, "shard"),
            P(None, "shard", None),
            P(None, "shard"),
            P(None, "shard", None),
            P(None, "shard"),
        ),
        check_vma=False,
    )
```

profile of v0, /device:TPU:1, one launch (start us, length us, event | category | flops | bytes accessed | tf_op | source)
XLA Modules:
  0.0 2134.0 jit_solution(1110647845852133789)
XLA Ops:
  32.9 34.1 %all-reduce.37 = (bf16[768]{0:T(1024)(128)(2,1)S(1)}, bf16[768]{0:T(1024)(128)(2,1)S(1)}, bf16[768]{0:T(1024)(128)(2,1)}, bf16[768]{0:T(1024)(128)(2,1)}, bf16[7...) all-reduce(bf16[768]{0:T(1024)(128)(2,1)} %dynamic-update-slice.1, ...), channel_id=3, replica_groups=mesh['shard'=8,'ctx'=16] {'shard'}, use_global_device_ids=true, to_apply=%add.1 | all-reduce | flops 11520 | bytes 46080
  69.3 24.1 %all-gather.43.cloned.1.call-done = bf16[1,768,2304]{2,1,0:T(8,128)(2,1)} async-done(((bf16[1,96,2304]{2,1,0:T(8,128)(2,1)}), bf16[1,768,2304]{2,1,0:T(8,128)(2,1)}) %all-gather.43.cloned.1.call-update) | async-done | bytes 3538960 | tf_op jit(solution)/shard_map/all_gather | solution.py:313
  104.2 19.9 all-gather.12
  127.3 22.3 %all-gather.47.cloned.1.call-done = bf16[2048,768]{1,0:T(8,128)(2,1)} async-done(((bf16[128,768]{1,0:T(8,128)(2,1)}), bf16[2048,768]{1,0:T(8,128)(2,1)}) %all-gather.47.cloned.1.call-update) | async-done | bytes 3145744 | tf_op jit(solution)/shard_map/all_gather | solution.py:63
  152.8 50.9 %all-gather.45.cloned.1.call-done = bf16[2048,768]{1,0:T(8,128)(2,1)} async-done(((bf16[128,768]{1,0:T(8,128)(2,1)}), bf16[2048,768]{1,0:T(8,128)(2,1)}) %all-gather.45.cloned.1.call-update) | async-done | bytes 3145744 | tf_op jit(solution)/shard_map/all_gather | solution.py:64
  203.7 4.7 copy.55
  208.5 8.1 fusion.162
  216.6 8.0 fusion.95
  224.6 15.2 all-gather.49.cloned.1.call-done
  241.7 104.6 %all-gather.51.cloned.1.call-done = bf16[1,768,3072]{2,1,0:T(8,128)(2,1)} async-done(((bf16[1,96,3072]{2,1,0:T(8,128)(2,1)}), bf16[1,768,3072]{2,1,0:T(8,128)(2,1)}) %all-gather.51.cloned.1.call-update) | async-done | bytes 4718608 | tf_op jit(solution)/shard_map/all_gather | solution.py:320
  349.6 99.4 %all-gather.53.cloned.1.call-done = bf16[1,3072,768]{2,1,0:T(8,128)(2,1)} async-done(((bf16[1,384,768]{2,1,0:T(8,128)(2,1)}), bf16[1,3072,768]{2,1,0:T(8,128)(2,1)}) %all-gather.53.cloned.1.call-update) | async-done | bytes 4718608 | tf_op jit(solution)/shard_map/all_gather | solution.py:322
  449.0 3.5 fusion.164
  453.2 76.3 %all-gather.55.cloned.1.call-done = bf16[1,768,2304]{2,1,0:T(8,128)(2,1)} async-done(((bf16[1,96,2304]{2,1,0:T(8,128)(2,1)}), bf16[1,768,2304]{2,1,0:T(8,128)(2,1)}) %all-gather.55.cloned.1.call-update) | async-done | bytes 3538960 | tf_op jit(solution)/shard_map/all_gather | solution.py:313
  535.8 19.3 all-gather.27
  555.3 30.3 %all-gather.59.cloned.1.call-done = bf16[2048,768]{1,0:T(8,128)(2,1)} async-done(((bf16[128,768]{1,0:T(8,128)(2,1)}), bf16[2048,768]{1,0:T(8,128)(2,1)}) %all-gather.59.cloned.1.call-update) | async-done | bytes 3145744 | tf_op jit(solution)/shard_map/all_gather | solution.py:63
  585.6 4.7 copy.60
  590.3 49.4 %all-gather.57.cloned.1.call-done = bf16[2048,768]{1,0:T(8,128)(2,1)} async-done(((bf16[128,768]{1,0:T(8,128)(2,1)}), bf16[2048,768]{1,0:T(8,128)(2,1)}) %all-gather.57.cloned.1.call-update) | async-done | bytes 3145744 | tf_op jit(solution)/shard_map/all_gather | solution.py:64
  639.7 5.2 copy.58
  644.9 10.7 fusion.165
  655.6 8.0 fusion.98
  663.6 12.1 all-gather.61.cloned.1.call-done
  677.7 104.9 %all-gather.63.cloned.1.call-done = bf16[1,768,3072]{2,1,0:T(8,128)(2,1)} async-done(((bf16[1,96,3072]{2,1,0:T(8,128)(2,1)}), bf16[1,768,3072]{2,1,0:T(8,128)(2,1)}) %all-gather.63.cloned.1.call-update) | async-done | bytes 4718608 | tf_op jit(solution)/shard_map/all_gather | solution.py:320
  785.8 99.4 %all-gather.65.cloned.1.call-done = bf16[1,3072,768]{2,1,0:T(8,128)(2,1)} async-done(((bf16[1,384,768]{2,1,0:T(8,128)(2,1)}), bf16[1,3072,768]{2,1,0:T(8,128)(2,1)}) %all-gather.65.cloned.1.call-update) | async-done | bytes 4718608 | tf_op jit(solution)/shard_map/all_gather | solution.py:322
  885.2 5.0 fusion.167
  895.0 12.5 multiply_reduce_fusion.1
  907.6 5.9 multiply_convert_fusion.1
  917.2 15.8 copy.63
  933.0 5.0 copy.84
  939.0 7.3 convolution_convert_fusion.7
  946.3 15.8 copy.65
  962.1 5.0 copy.83
  967.2 7.3 bitcast_reduce_fusion
  974.4 38.1 %reduce-scatter.37.cloned.1.call-done = bf16[128,768]{1,0:T(8,128)(2,1)} async-done(((bf16[2048,768]{1,0:T(8,128)(2,1)}), bf16[128,768]{1,0:T(8,128)(2,1)}) %reduce-scatter.37.cloned.1.call-update) | async-done | bytes 196624
  1014.6 75.9 %reduce-scatter.39.cloned.1.call-done = bf16[128,768]{1,0:T(8,128)(2,1)} async-done(((bf16[2048,768]{1,0:T(8,128)(2,1)}), bf16[128,768]{1,0:T(8,128)(2,1)}) %reduce-scatter.39.cloned.1.call-update) | async-done | bytes 196624
  1093.6 4.4 multiply_reduce_fusion.4
  1099.0 5.1 fusion.168
  1109.5 12.5 multiply_reduce_fusion
  1122.1 5.9 multiply_convert_fusion
  1131.5 15.7 copy.67
  1147.2 5.0 copy.82
  1153.1 7.4 convolution_convert_fusion.6
  1160.5 15.8 copy.69
  1176.3 5.1 copy.81
  1187.3 4.8 convolution_convert_fusion.2
  1193.1 3.8 convolution_convert_fusion
  1202.1 3.6 convolution_convert_fusion.3
  1207.1 3.8 convolution_convert_fusion.1
  1212.8 5.9 bitcast_reduce_fusion.1
  1218.7 7.8 reduce-scatter.41.cloned.1.call-done
  1228.1 76.4 %reduce-scatter.43.cloned.1.call-done = bf16[128,768]{1,0:T(8,128)(2,1)} async-done(((bf16[2048,768]{1,0:T(8,128)(2,1)}), bf16[128,768]{1,0:T(8,128)(2,1)}) %reduce-scatter.43.cloned.1.call-update) | async-done | bytes 196624
  1307.0 4.0 convolution_convert_fusion.5
  1315.4 28.6 %reduce-scatter.27.cloned.1.call-done = bf16[96,768]{1,0:T(8,128)(2,1)} async-done(((bf16[768,768]{1,0:T(8,128)(2,1)}), bf16[96,768]{1,0:T(8,128)(2,1)}) %reduce-scatter.27.cloned.1.call-update) | async-done | bytes 147472 | tf_op jit(solution)/shard_map/reduce_scatter | solution.py:233
  1344.1 42.9 %reduce-scatter.25.cloned.1.call-done = bf16[96,768]{1,0:T(8,128)(2,1)} async-done(((bf16[768,768]{1,0:T(8,128)(2,1)}), bf16[96,768]{1,0:T(8,128)(2,1)}) %reduce-scatter.25.cloned.1.call-update) | async-done | bytes 147472 | tf_op jit(solution)/shard_map/reduce_scatter | solution.py:233
  1386.9 107.4 %reduce-scatter.31.cloned.1.call-done = bf16[96,3072]{1,0:T(8,128)(2,1)} async-done(((bf16[768,3072]{1,0:T(8,128)(2,1)}), bf16[96,3072]{1,0:T(8,128)(2,1)}) %reduce-scatter.31.cloned.1.call-update) | async-done | bytes 589840 | tf_op jit(solution)/shard_map/reduce_scatter | solution.py:245
  1494.4 103.4 %reduce-scatter.35.cloned.1.call-done = bf16[384,768]{1,0:T(8,128)(2,1)} async-done(((bf16[3072,768]{1,0:T(8,128)(2,1)}), bf16[384,768]{1,0:T(8,128)(2,1)}) %reduce-scatter.35.cloned.1.call-update) | async-done | bytes 589840 | tf_op jit(solution)/shard_map/reduce_scatter | solution.py:251
  1597.8 81.8 %reduce-scatter.23.cloned.1.call-done = bf16[96,2304]{1,0:T(8,128)(2,1)} async-done(((bf16[768,2304]{1,0:T(8,128)(2,1)}), bf16[96,2304]{1,0:T(8,128)(2,1)}) %reduce-scatter.23.cloned.1.call-update) | async-done | bytes 442384 | tf_op jit(solution)/shard_map/reduce_scatter | solution.py:224
  1679.6 103.3 %reduce-scatter.29.cloned.1.call-done = bf16[96,3072]{1,0:T(8,128)(2,1)} async-done(((bf16[768,3072]{1,0:T(8,128)(2,1)}), bf16[96,3072]{1,0:T(8,128)(2,1)}) %reduce-scatter.29.cloned.1.call-update) | async-done | bytes 589840 | tf_op jit(solution)/shard_map/reduce_scatter | solution.py:245
  1782.9 103.7 %reduce-scatter.33.cloned.1.call-done = bf16[384,768]{1,0:T(8,128)(2,1)} async-done(((bf16[3072,768]{1,0:T(8,128)(2,1)}), bf16[384,768]{1,0:T(8,128)(2,1)}) %reduce-scatter.33.cloned.1.call-update) | async-done | bytes 589840 | tf_op jit(solution)/shard_map/reduce_scatter | solution.py:251
  1886.7 81.8 %reduce-scatter.21.cloned.1.call-done = bf16[96,2304]{1,0:T(8,128)(2,1)} async-done(((bf16[768,2304]{1,0:T(8,128)(2,1)}), bf16[96,2304]{1,0:T(8,128)(2,1)}) %reduce-scatter.21.cloned.1.call-update) | async-done | bytes 442384 | tf_op jit(solution)/shard_map/reduce_scatter | solution.py:224
  1968.5 4.3 fusion.146
  1973.2 27.2 %all-reduce.36 = (bf16[768]{0:T(1024)(128)(2,1)S(1)}, bf16[768]{0:T(1024)(128)(2,1)S(1)}, bf16[768]{0:T(1024)(128)(2,1)S(1)}, bf16[768]{0:T(1024)(128)(2,1)S(1)}...) all-reduce(bf16[768]{0:T(1024)(128)(2,1)} %copy-done.84, ...), channel_id=31, replica_groups=mesh['shard'=8,'ctx'=16] {'shard'}, use_global_device_ids=true, to_apply=%add.15 | all-reduce | flops 19200 | bytes 76800
  2001.1 67.0 %all-reduce.34 = (bf16[1,96]{1,0:T(2,128)(2,1)S(1)}, bf16[1,96]{1,0:T(2,128)(2,1)S(1)}, bf16[1,96]{1,0:T(2,128)(2,1)S(1)}, bf16[1,96]{1,0:T(2,128)(2,1)S(1)}, bf...) all-reduce(bf16[1,96]{1,0:T(2,128)(2,1)S(1)} %get-tuple-element.176, ...), channel_id=1, replica_groups=mesh['shard'=8,'ctx'=16] {'ctx'}, use_global_device_ids=true, to_apply=%region_31.32 | all-reduce | flops 2304 | bytes 9216 | tf_op jit(solution)/shard_map/psum | solution.py:259
  2074.9 4.1 fusion.101
  2079.0 41.2 %all-reduce.40.cloned.1.call-done = (bf16[1,96,2304]{2,1,0:T(8,128)(2,1)}, bf16[1,96,2304]{2,1,0:T(8,128)(2,1)}, bf16[1,96,768]{2,1,0:T(8,128)(2,1)}, bf16[1,96,...) async-done(((bf16[1,96,2304]{2,1,0:T(8,128)(2,1)}, ...) | async-done | bytes 3538960 | tf_op jit(solution)/shard_map/psum | solution.py:261
  (437 shorter events, 123.1 us)
Async XLA Ops:
  7.2 86.2 %all-gather.43.cloned.1.call-start = ((), (), s32[]{:S(2)}) async-start(), calls=%async_computation.20 | async-start | bytes 3981312 | tf_op jit(solution)/shard_map/all_gather | solution.py:313
  9.4 140.2 %all-gather.47.cloned.1.call-start = ((), (), s32[]{:S(2)}) async-start(), calls=%async_computation.22 | async-start | bytes 3342336 | tf_op jit(solution)/shard_map/all_gather | solution.py:63
  67.0 26.3 %copy-start.45 = (f32[768]{0:T(1024)}, f32[768]{0:T(1024)S(1)}, u32[]{:S(2)}) copy-start(f32[768]{0:T(1024)S(1)} %convert_element_type.545) | copy-start | bytes 9220
  67.0 26.3 %copy-start.53 = (f32[768]{0:T(1024)}, f32[768]{0:T(1024)S(1)}, u32[]{:S(2)}) copy-start(f32[768]{0:T(1024)S(1)} %convert_element_type.546) | copy-start | bytes 9220
  68.1 25.3 %copy-start.62 = (f32[128]{0:T(128)}, f32[128]{0:T(128)S(1)}, u32[]{:S(2)}) copy-start(f32[128]{0:T(128)S(1)} %broadcast_multiply_fusion.3) | copy-start | bytes 1540
  69.2 24.2 %copy-start.96 = (f32[128]{0:T(128)}, f32[128]{0:T(128)S(1)}, u32[]{:S(2)}) copy-start(f32[128]{0:T(128)S(1)} %fusion.118) | copy-start | bytes 1540
  69.2 24.1 %copy-start.73 = (f32[128]{0:T(128)}, f32[128]{0:T(128)S(1)}, u32[]{:S(2)}) copy-start(f32[128]{0:T(128)S(1)} %fusion.129) | copy-start | bytes 1540
  69.3 31.8 %copy-start.27 = (bf16[2,96,3072]{2,1,0:T(8,128)(2,1)S(1)}, bf16[2,96,3072]{2,1,0:T(8,128)(2,1)}, u32[]{:S(2)}) copy-start(bf16[2,96,3072]{2,1,0:T(8,128)(2,1)} %param.28) | copy-start | bytes 3538948
  96.9 106.8 %all-gather.45.cloned.1.call-start = ((), (), s32[]{:S(2)}) async-start(), calls=%async_computation.21 | async-start | bytes 3342336 | tf_op jit(solution)/shard_map/all_gather | solution.py:64
  99.1 140.6 %all-gather.49.cloned.1.call-start = ((), (), s32[]{:S(2)}) async-start(), calls=%async_computation.23 | async-start | bytes 1327104 | tf_op jit(solution)/shard_map/all_gather | solution.py:316
  101.0 23.2 %copy-start.102 = (s32[16]{0:T(128)S(1)}, s32[16]{0:T(128)}, u32[]{:S(2)}) copy-start(s32[16]{0:T(128)} %param.18) | copy-start | bytes 196
  101.0 26.2 %copy-start.32 = (bf16[128,768]{1,0:T(8,128)(2,1)S(1)}, bf16[128,768]{1,0:T(8,128)(2,1)}, u32[]{:S(2)}) copy-start(bf16[128,768]{1,0:T(8,128)(2,1)} %get-tuple-element.110) | copy-start | bytes 589828
  101.0 245.3 %all-gather.51.cloned.1.call-start = ((), (), s32[]{:S(2)}) async-start(), calls=%async_computation.24 | async-start | bytes 5308416 | tf_op jit(solution)/shard_map/all_gather | solution.py:320
  102.2 346.8 %all-gather.53.cloned.1.call-start = ((), (), s32[]{:S(2)}) async-start(), calls=%async_computation.25 | async-start | bytes 5308416 | tf_op jit(solution)/shard_map/all_gather | solution.py:322
  103.4 426.2 %all-gather.55.cloned.1.call-start = ((), (), s32[]{:S(2)}) async-start(), calls=%async_computation.26 | async-start | bytes 3981312 | tf_op jit(solution)/shard_map/all_gather | solution.py:313
  104.1 481.5 %all-gather.59.cloned.1.call-start = ((), (), s32[]{:S(2)}) async-start(), calls=%async_computation.28 | async-start | bytes 3342336 | tf_op jit(solution)/shard_map/all_gather | solution.py:63
  104.2 242.1 %copy-start.49 = (f32[768]{0:T(1024)}, f32[768]{0:T(1024)S(1)}, u32[]{:S(2)}) copy-start(f32[768]{0:T(1024)S(1)} %convert_element_type.551) | copy-start | bytes 9220
  124.2 405.3 %copy-start.55 = (f32[768]{0:T(1024)}, f32[768]{0:T(1024)S(1)}, u32[]{:S(2)}) copy-start(f32[768]{0:T(1024)S(1)} %convert_element_type.554) | copy-start | bytes 9220
  127.3 81.1 %copy-start.33 = (bf16[128,768]{0,1:T(8,128)(2,1)}, bf16[128,768]{0,1:T(8,128)(2,1)S(1)}, u32[]{:S(2)}) copy-start(bf16[128,768]{0,1:T(8,128)(2,1)S(1)} %copy.56) | copy-start | bytes 589828
  152.8 55.7 %copy-start.3 = (bf16[2048,768]{0,1:T(8,128)(2,1)}, bf16[2048,768]{0,1:T(8,128)(2,1)S(1)}, u32[]{:S(2)}) copy-start(bf16[2048,768]{0,1:T(8,128)(2,1)S(1)} %copy.57) | copy-start | bytes 9437188
  224.6 124.9 %copy-start.30 = (bf16[12,64,128]{2,1,0:T(8,128)(2,1)}, bf16[12,64,128]{2,1,0:T(8,128)(2,1)S(1)}, u32[]{:S(2)}) copy-start(bf16[12,64,128]{2,1,0:T(8,128)(2,1)S(1)} %fusion.95) | copy-start | bytes 589828
  241.5 108.0 %copy-start.57 = (f32[128]{0:T(128)}, f32[128]{0:T(128)S(1)}, u32[]{:S(2)}) copy-start(f32[128]{0:T(128)S(1)} %broadcast_multiply_fusion.2) | copy-start | bytes 1540
  241.7 107.8 %copy-start.98 = (f32[128]{0:T(128)}, f32[128]{0:T(128)S(1)}, u32[]{:S(2)}) copy-start(f32[128]{0:T(128)S(1)} %multiply_reduce_fusion.10) | copy-start | bytes 1540
  241.7 107.8 %copy-start.65 = (f32[128]{0:T(128)}, f32[128]{0:T(128)S(1)}, u32[]{:S(2)}) copy-start(f32[128]{0:T(128)S(1)} %fusion.130) | copy-start | bytes 1540
  349.6 102.9 %copy-start.7 = (f32[128,3072]{1,0:T(8,128)}, f32[128,3072]{1,0:T(8,128)S(1)}, u32[]{:S(2)}) copy-start(f32[128,3072]{1,0:T(8,128)S(1)} %fusion.26) | copy-start | bytes 4718596
  452.5 80.5 %copy-start.90 = (bf16[768]{0:T(1024)(128)(2,1)S(1)}, bf16[768]{0:T(1024)(128)(2,1)}, u32[]{:S(2)}) copy-start(bf16[768]{0:T(1024)(128)(2,1)} %get-tuple-element.83) | copy-start | bytes 4612
  452.5 80.5 %copy-start.89 = (bf16[768]{0:T(1024)(128)(2,1)S(1)}, bf16[768]{0:T(1024)(128)(2,1)}, u32[]{:S(2)}) copy-start(bf16[768]{0:T(1024)(128)(2,1)} %get-tuple-element.84) | copy-start | bytes 4612
  452.5 80.5 %copy-start.68 = (f32[128]{0:T(128)}, f32[128]{0:T(128)S(1)}, u32[]{:S(2)}) copy-start(f32[128]{0:T(128)S(1)} %broadcast_multiply_fusion.1) | copy-start | bytes 1540
  453.2 80.5 %copy-start.80 = (f32[128]{0:T(128)}, f32[128]{0:T(128)S(1)}, u32[]{:S(2)}) copy-start(f32[128]{0:T(128)S(1)} %fusion.131) | copy-start | bytes 1540
  453.2 82.5 %copy-start.88 = (bf16[768]{0:T(1024)(128)(2,1)S(1)}, bf16[768]{0:T(1024)(128)(2,1)}, u32[]{:S(2)}) copy-start(bf16[768]{0:T(1024)(128)(2,1)} %get-tuple-element.85) | copy-start | bytes 4612
  453.2 82.6 %copy-start.87 = (bf16[768]{0:T(1024)(128)(2,1)S(1)}, bf16[768]{0:T(1024)(128)(2,1)}, u32[]{:S(2)}) copy-start(bf16[768]{0:T(1024)(128)(2,1)} %get-tuple-element.86) | copy-start | bytes 4612
  532.9 106.8 %all-gather.57.cloned.1.call-start = ((), (), s32[]{:S(2)}) async-start(), calls=%async_computation.27 | async-start | bytes 3342336 | tf_op jit(solution)/shard_map/all_gather | solution.py:64
  533.8 141.9 %all-gather.61.cloned.1.call-start = ((), (), s32[]{:S(2)}) async-start(), calls=%async_computation.29 | async-start | bytes 1327104 | tf_op jit(solution)/shard_map/all_gather | solution.py:316
  534.4 248.2 %all-gather.63.cloned.1.call-start = ((), (), s32[]{:S(2)}) async-start(), calls=%async_computation.30 | async-start | bytes 5308416 | tf_op jit(solution)/shard_map/all_gather | solution.py:320
  535.1 350.1 %all-gather.65.cloned.1.call-start = ((), (), s32[]{:S(2)}) async-start(), calls=%async_computation.31 | async-start | bytes 5308416 | tf_op jit(solution)/shard_map/all_gather | solution.py:322
  535.7 476.8 %reduce-scatter.37.cloned.1.call-start = ((), (), s32[]{:S(2)}) async-start(), calls=%async_computation.32 | async-start | bytes 3342336
  555.3 89.6 %copy-start.35 = (bf16[128,768]{0,1:T(8,128)(2,1)}, bf16[128,768]{0,1:T(8,128)(2,1)S(1)}, u32[]{:S(2)}) copy-start(bf16[128,768]{0,1:T(8,128)(2,1)S(1)} %copy.59) | copy-start | bytes 589828
  590.3 54.6 %copy-start.44 = (pred[128,2048]{1,0:T(8,128)(4,1)S(1)}, pred[128,2048]{1,0:T(8,128)(4,1)}, u32[]{:S(2)}) copy-start(pred[128,2048]{1,0:T(8,128)(4,1)} %broadcast_compare_fusion) | copy-start | bytes 786436
  663.6 118.9 %copy-start.31 = (bf16[12,64,128]{2,1,0:T(8,128)(2,1)}, bf16[12,64,128]{2,1,0:T(8,128)(2,1)S(1)}, u32[]{:S(2)}) copy-start(bf16[12,64,128]{2,1,0:T(8,128)(2,1)S(1)} %fusion.98) | copy-start | bytes 589828
  677.5 215.2 %copy-start.60 = (f32[128]{0:T(128)}, f32[128]{0:T(128)S(1)}, u32[]{:S(2)}) copy-start(f32[128]{0:T(128)S(1)} %broadcast_multiply_fusion) | copy-start | bytes 1540
  677.7 215.0 %copy-start.71 = (f32[128]{0:T(128)}, f32[128]{0:T(128)S(1)}, u32[]{:S(2)}) copy-start(f32[128]{0:T(128)S(1)} %fusion.132) | copy-start | bytes 1540
  782.5 102.7 %copy-start.21 = (bf16[1,128,768]{2,1,0:T(8,128)(2,1)S(1)}, bf16[1,128,768]{2,1,0:T(8,128)(2,1)}, u32[]{:S(2)}) copy-start(bf16[1,128,768]{2,1,0:T(8,128)(2,1)} %param.17) | copy-start | bytes 589828
  785.8 406.4 %copy-start.5 = (f32[128,3072]{1,0:T(8,128)}, f32[128,3072]{1,0:T(8,128)S(1)}, u32[]{:S(2)}) copy-start(f32[128,3072]{1,0:T(8,128)S(1)} %fusion.29) | copy-start | bytes 4718596
  938.1 152.5 %reduce-scatter.39.cloned.1.call-start = ((), (), s32[]{:S(2)}) async-start(), calls=%async_computation.33 | async-start | bytes 3342336
  967.1 259.4 %reduce-scatter.41.cloned.1.call-start = ((), (), s32[]{:S(2)}) async-start(), calls=%async_computation.34 | async-start | bytes 3342336
  1099.0 106.8 %copy-start.12 = (f32[128,768]{1,0:T(8,128)}, f32[128,768]{1,0:T(8,128)S(1)}, u32[]{:S(2)}) copy-start(f32[128,768]{1,0:T(8,128)S(1)} %get-tuple-element.89) | copy-start | bytes 1179652
  1152.2 152.3 %reduce-scatter.43.cloned.1.call-start = ((), (), s32[]{:S(2)}) async-start(), calls=%async_computation.35 | async-start | bytes 3342336
  1181.4 162.7 %reduce-scatter.27.cloned.1.call-start = ((), (), s32[]{:S(2)}) async-start(), calls=%async_computation.15 | async-start | bytes 1327104 | tf_op jit(solution)/shard_map/reduce_scatter | solution.py:233
  1184.7 202.2 %reduce-scatter.25.cloned.1.call-start = ((), (), s32[]{:S(2)}) async-start(), calls=%async_computation.14 | async-start | bytes 1327104 | tf_op jit(solution)/shard_map/reduce_scatter | solution.py:233
  1187.2 307.1 %reduce-scatter.31.cloned.1.call-start = ((), (), s32[]{:S(2)}) async-start(), calls=%async_computation.17 | async-start | bytes 5308416 | tf_op jit(solution)/shard_map/reduce_scatter | solution.py:245
  1192.2 405.6 %reduce-scatter.35.cloned.1.call-start = ((), (), s32[]{:S(2)}) async-start(), calls=%async_computation.19 | async-start | bytes 5308416 | tf_op jit(solution)/shard_map/reduce_scatter | solution.py:251
  1196.9 482.7 %reduce-scatter.23.cloned.1.call-start = ((), (), s32[]{:S(2)}) async-start(), calls=%async_computation.13 | async-start | bytes 3981312 | tf_op jit(solution)/shard_map/reduce_scatter | solution.py:224
  1201.0 581.9 %reduce-scatter.29.cloned.1.call-start = ((), (), s32[]{:S(2)}) async-start(), calls=%async_computation.16 | async-start | bytes 5308416 | tf_op jit(solution)/shard_map/reduce_scatter | solution.py:245
  1205.7 680.9 %reduce-scatter.33.cloned.1.call-start = ((), (), s32[]{:S(2)}) async-start(), calls=%async_computation.18 | async-start | bytes 5308416 | tf_op jit(solution)/shard_map/reduce_scatter | solution.py:251
  1210.9 96.0 %copy-start.46 = (f32[768]{0:T(1024)S(1)}, f32[768]{0:T(1024)}, u32[]{:S(2)}) copy-start(f32[768]{0:T(1024)} %copy-done.45) | copy-start | bytes 9220
  1210.9 96.0 %copy-start.54 = (f32[768]{0:T(1024)S(1)}, f32[768]{0:T(1024)}, u32[]{:S(2)}) copy-start(f32[768]{0:T(1024)} %copy-done.53) | copy-start | bytes 9220
  1211.0 96.0 %copy-start.63 = (f32[128]{0:T(128)S(1)}, f32[128]{0:T(128)}, u32[]{:S(2)}) copy-start(f32[128]{0:T(128)} %copy-done.62) | copy-start | bytes 1540
  1211.0 757.5 %reduce-scatter.21.cloned.1.call-start = ((), (), s32[]{:S(2)}) async-start(), calls=%async_computation.12 | async-start | bytes 3981312 | tf_op jit(solution)/shard_map/reduce_scatter | solution.py:224
  1311.0 657.5 %copy-start.11 = (bf16[1,128,768]{2,1,0:T(8,128)(2,1)S(1)}, bf16[1,128,768]{2,1,0:T(8,128)(2,1)}, u32[]{:S(2)}) copy-start(bf16[1,128,768]{2,1,0:T(8,128)(2,1)} %param.16) | copy-start | bytes 589828
  1311.0 809.2 %all-reduce.40.cloned.1.call-start = ((), (), s32[]{:S(2)}) async-start(), calls=%async_computation.36 | async-start | bytes 7077888 | tf_op jit(solution)/shard_map/psum | solution.py:261
  1314.1 654.4 %copy-start.84 = (bf16[768]{0:T(1024)(128)(2,1)}, bf16[768]{0:T(1024)(128)(2,1)S(1)}, u32[]{:S(2)}) copy-start(bf16[768]{0:T(1024)(128)(2,1)S(1)} %dynamic-update-slice.15) | copy-start | bytes 4612
  1968.5 104.8 %copy-start.13 = (f32[128,768]{1,0:T(8,128)S(1)}, f32[128,768]{1,0:T(8,128)}, u32[]{:S(2)}) copy-start(f32[128,768]{1,0:T(8,128)} %copy-done.12) | copy-start | bytes 1179652
  1968.5 104.8 %copy-start.17 = (f32[128,768]{1,0:T(8,128)S(1)}, f32[128,768]{1,0:T(8,128)}, u32[]{:S(2)}) copy-start(f32[128,768]{1,0:T(8,128)} %copy-done.16) | copy-start | bytes 1179652
  1968.5 106.4 %copy-start.6 = (f32[128,3072]{1,0:T(8,128)S(1)}, f32[128,3072]{1,0:T(8,128)}, u32[]{:S(2)}) copy-start(f32[128,3072]{1,0:T(8,128)} %copy-done.5) | copy-start | bytes 4718596
  (73 other events, 382.5 us)
Sparse Core Ops, SparseCore 0:
  10.2 83.0 all-gather.42
  97.1 52.5 all-gather.46
  152.6 51.0 all-gather.44
  205.2 34.5 all-gather.48
  241.8 104.4 all-gather.50
  348.4 100.5 all-gather.52
  450.6 78.8 all-gather.54
  533.1 52.4 all-gather.58
  588.6 51.0 all-gather.56
  641.2 34.4 all-gather.60
  678.0 104.5 all-gather.62
  784.6 100.5 all-gather.64
  938.2 74.2 reduce-scatter.36
  1016.4 74.1 reduce-scatter.38
  1152.3 74.1 reduce-scatter.40
  1230.4 74.0 reduce-scatter.42
  1307.3 36.7 reduce-scatter.26
  1346.3 40.5 reduce-scatter.24
  1389.4 104.9 reduce-scatter.30
  1496.6 101.1 reduce-scatter.34
  1600.2 79.3 reduce-scatter.22
  1682.1 100.7 reduce-scatter.28
  1785.5 101.1 reduce-scatter.32
  1889.1 79.3 reduce-scatter.20
  1971.6 148.6 all-reduce.39
where the time goes:
time: 2140 us; the launch traced here: 2130 us
  waiting for transfers between devices  1580 us (74%)
  matrix products  169 us (8%)
  blocking collectives  168 us (8%)
  local copies, waits for them, and re-layouts  153 us (7%)
  other arithmetic  40.3 us (2%)
    reduce_scatter x2, waiting for transfers between devices, reduce_grads(): lax.psum_scatter(grads[9].astype(jnp.bfloat16), 'shard', scatter_dimensio...  211 us
    all_gather x2, waiting for transfers between devices, shards(): lax.all_gather(up_weight[layer_index], 'shard', axis=0, tiled=True)  209 us
    reduce_scatter x2, waiting for transfers between devices, reduce_grads(): lax.psum_scatter(grads[11].astype(jnp.bfloat16), 'shard', scatter_dimensi...  207 us
    unnamed x29, waiting for transfers between devices  201 us
    all_gather x2, waiting for transfers between devices, shards(): lax.all_gather(down_weight[layer_index], 'shard', axis=0, tiled=True)  199 us
    reduce_scatter x2, waiting for transfers between devices, reduce_grads(): lax.psum_scatter(grads[2].astype(jnp.bfloat16), 'shard', scatter_dimensio...  164 us
    unnamed x281, local copies, waits for them, and re-layouts  123 us
    all_gather x2, waiting for transfers between devices, shards(): lax.all_gather(qkv_weight[layer_index], 'shard', axis=0, tiled=True)  100 us
  transfers between devices with their start and end apart: 25, of which 25 were waited for; matrix products, arithmetic and copies ran while one was open for 10% of the time, Pallas kernels for 0%

commit v1 on v0

v1 whole, which is shorter than its diff:
```python
import math

import jax
import jax.numpy as jnp
from jax import lax
from jax.experimental import pallas as pl
from jax.experimental.pallas import tpu as pltpu
from jax.sharding import PartitionSpec as P

H = 12
HD = 64
D = 768
FF = 3072
LAYERS = 2
S = 8
C = 16
TOK = 128
LEN = TOK * C
BLK = TOK // 2
ROWS = 256
EPSILON = 1e-05
NEGATIVE = -1e30
F32 = jnp.float32
BF16 = jnp.bfloat16

CHIP_GROUPS = [[2 * q + core for q in range(8)] for core in range(2)]
X_GROUPS = [[8 * y + 2 * x + core for x in range(4)] for y in range(2) for core in range(2)]
SWAP = [(i, i ^ 1) for i in range(C)]


def layer_norm(states, gain, shift):
    average = jnp.mean(states, axis=-1, keepdims=True)
    centered = states - average
    spread = jnp.mean(centered * centered, axis=-1, keepdims=True)
    return centered * lax.rsqrt(spread + EPSILON) * gain + shift


def exchange(parts, axis, groups=None):
    return lax.all_to_all(parts, axis, 0, 0, tiled=True, axis_index_groups=groups)


def spread_to(part, count, axis, groups=None):
    return exchange(jnp.broadcast_to(part[None], (count,) + part.shape), axis, groups)


def swap_core(part):
    return lax.ppermute(part, "ctx", SWAP)


def gather_ctx(part):
    own = spread_to(part, 8, "ctx", CHIP_GROUPS)
    return own, swap_core(own)


def gather_x(part):
    own = spread_to(part, 4, "ctx", X_GROUPS)
    return jnp.concatenate([own, swap_core(own)], axis=0)


def scatter_x(partial):
    theirs = swap_core(partial[4:].astype(BF16))
    mine = partial[:4] + theirs.astype(F32)
    parts = exchange(mine.astype(BF16), "ctx", X_GROUPS)
    return jnp.sum(parts.astype(F32), axis=0)


def dot(left, right, dims=((1,), (0,))):
    return lax.dot_general(left, right, (dims, ((), ())), preferred_element_type=F32)


def rows_of(block):
    return pl.ds(pl.multiple_of(block * BLK, BLK), BLK)


def attend_kernel(arrive_pos, ctx_pos, normed_ref, weight_ref, shift_ref, mixed_ref, q_ref, k_ref, v_ref, out_ref):
    for step in range(LEN // ROWS):
        piece = dot(normed_ref[step * ROWS : (step + 1) * ROWS, :], weight_ref[...]) + shift_ref[...]
        for part in range(ROWS // BLK):
            rows = rows_of(arrive_pos[step * (ROWS // BLK) + part])
            block = piece[part * BLK : (part + 1) * BLK, :]
            q_ref[rows, :] = (block[:, :HD].astype(BF16).astype(F32) * 0.125).astype(BF16)
            k_ref[rows, :] = block[:, HD : 2 * HD].astype(BF16)
            v_ref[rows, :] = block[:, 2 * HD :].astype(BF16)
    keep = lax.broadcasted_iota(jnp.int32, (ROWS, ROWS), 0) >= lax.broadcasted_iota(
        jnp.int32, (ROWS, ROWS), 1
    )
    for step in range(LEN // ROWS):
        start = step * ROWS
        queries = q_ref[start : start + ROWS, :]
        near = dot(queries, k_ref[start : start + ROWS, :], ((1,), (1,)))
        near = jnp.where(keep, near, NEGATIVE)
        highest = jnp.max(near, axis=1, keepdims=True)
        if step:
            far = dot(queries, k_ref[:start, :], ((1,), (1,)))
            highest = jnp.maximum(highest, jnp.max(far, axis=1, keepdims=True))
        weights = jnp.exp(near - highest)
        total = jnp.sum(weights, axis=1, keepdims=True)
        mixed = dot(weights.astype(BF16), v_ref[start : start + ROWS, :])
        if step:
            weights = jnp.exp(far - highest)
            total = total + jnp.sum(weights, axis=1, keepdims=True)
            mixed = mixed + dot(weights.astype(BF16), v_ref[:start, :])
        out_ref[start : start + ROWS, :] = (mixed / total).astype(BF16)
    for block in range(LEN // BLK):
        mixed_ref[block * BLK : (block + 1) * BLK, :] = out_ref[rows_of(ctx_pos[block]), :]


def attend_back_kernel(
    arrive_pos, ctx_pos, q_ref, k_ref, v_ref, grad_ref, to_ctx_ref, to_arrive_ref, do_ref, dk_ref, dv_ref, all_ref
):
    for block in range(LEN // BLK):
        do_ref[rows_of(ctx_pos[block]), :] = grad_ref[block * BLK : (block + 1) * BLK, :]
    keep = lax.broadcasted_iota(jnp.int32, (ROWS, ROWS), 0) <= lax.broadcasted_iota(
        jnp.int32, (ROWS, ROWS), 1
    )
    for step in range(LEN // ROWS - 1, -1, -1):
        start = step * ROWS
        end = start + ROWS
        queries = q_ref[start:end, :]
        grads = do_ref[start:end, :]
        near_keys, near_values = k_ref[start:end, :], v_ref[start:end, :]
        near = jnp.where(keep, dot(near_keys, queries, ((1,), (1,))), NEGATIVE)
        highest = jnp.max(near, axis=0, keepdims=True)
        if step:
            far_keys, far_values = k_ref[:start, :], v_ref[:start, :]
            far = dot(far_keys, queries, ((1,), (1,)))
            highest = jnp.maximum(highest, jnp.max(far, axis=0, keepdims=True))
        near = jnp.exp(near - highest)
        total = jnp.sum(near, axis=0, keepdims=True)
        if step:
            far = jnp.exp(far - highest)
            total = total + jnp.sum(far, axis=0, keepdims=True)
        inverse = 1.0 / total
        near = near * inverse
        near_grad = dot(near_values, grads, ((1,), (1,)))
        inner = jnp.sum(near * near_grad, axis=0, keepdims=True)
        if step:
            far = far * inverse
            far_grad = dot(far_values, grads, ((1,), (1,)))
            inner = inner + jnp.sum(far * far_grad, axis=0, keepdims=True)
        near_scores = (near * (near_grad - inner)).astype(BF16)
        near_dk = dot(near_scores, queries)
        near_dv = dot(near.astype(BF16), grads)
        query_grad = dot(near_scores, near_keys, ((0,), (0,)))
        if step == LEN // ROWS - 1:
            dk_ref[start:end, :] = near_dk
            dv_ref[start:end, :] = near_dv
        else:
            dk_ref[start:end, :] += near_dk
            dv_ref[start:end, :] += near_dv
        if step:
            far_scores = (far * (far_grad - inner)).astype(BF16)
            far_dk = dot(far_scores, queries)
            far_dv = dot(far.astype(BF16), grads)
            query_grad = query_grad + dot(far_scores, far_keys, ((0,), (0,)))
            if step == LEN // ROWS - 1:
                dk_ref[:start, :] = far_dk
                dv_ref[:start, :] = far_dv
            else:
                dk_ref[:start, :] += far_dk
                dv_ref[:start, :] += far_dv
        all_ref[start:end, :] = jnp.concatenate(
            [query_grad * 0.125, dk_ref[start:end, :], dv_ref[start:end, :]], axis=1
        ).astype(BF16)
    for block in range(LEN // BLK):
        to_ctx_ref[block * BLK : (block + 1) * BLK, :] = all_ref[rows_of(ctx_pos[block]), :]
        to_arrive_ref[block * BLK : (block + 1) * BLK, :] = all_ref[rows_of(arrive_pos[block]), :]


SMEM = pl.BlockSpec(memory_space=pltpu.SMEM)
VMEM = pl.BlockSpec(memory_space=pltpu.VMEM)
VMEM_BYTES = 48 * 2**20


def attend(arrive_pos, ctx_pos, normed, weight, shift):
    head = jax.ShapeDtypeStruct((LEN, HD), BF16)
    return pl.pallas_call(
        attend_kernel,
        out_shape=(head, head, head, head),
        in_specs=[SMEM, SMEM, VMEM, VMEM, VMEM],
        out_specs=(VMEM, VMEM, VMEM, VMEM),
        scratch_shapes=[pltpu.VMEM((LEN, HD), BF16)],
        compiler_params=pltpu.CompilerParams(vmem_limit_bytes=VMEM_BYTES),
        cost_estimate=pl.CostEstimate(flops=2 * 10**9, bytes_accessed=5 * 10**6, transcendentals=2 * 10**6),
    )(arrive_pos, ctx_pos, normed, weight, shift)


def attend_back(arrive_pos, ctx_pos, queries, keys, values, grads):
    wide = jax.ShapeDtypeStruct((LEN, 3 * HD), BF16)
    return pl.pallas_call(
        attend_back_kernel,
        out_shape=(wide, wide),
        in_specs=[SMEM, SMEM, VMEM, VMEM, VMEM, VMEM],
        out_specs=(VMEM, VMEM),
        scratch_shapes=[
            pltpu.VMEM((LEN, HD), BF16),
            pltpu.VMEM((LEN, HD), F32),
            pltpu.VMEM((LEN, HD), F32),
            pltpu.VMEM((LEN, 3 * HD), BF16),
        ],
        compiler_params=pltpu.CompilerParams(vmem_limit_bytes=VMEM_BYTES),
        cost_estimate=pl.CostEstimate(flops=4 * 10**9, bytes_accessed=5 * 10**6, transcendentals=2 * 10**6),
    )(arrive_pos, ctx_pos, queries, keys, values, grads)


def join_cores(core, own, other, axis):
    return jnp.where(
        core == 0, jnp.concatenate([own, other], axis=axis), jnp.concatenate([other, own], axis=axis)
    )


def gather_halves(core, weight):
    layers, rows, columns = weight.shape
    half = columns // 2
    piece = lax.dynamic_slice_in_dim(weight, core * half, half, axis=2)
    own = lax.all_gather(piece, "shard", axis=0)
    other = swap_core(own)
    return [
        join_cores(core, own[:, layer], other[:, layer], 2).reshape(S * rows, columns) for layer in range(layers)
    ]


def forward_layer(flowing, params, small, places):
    arrive_pos, ctx_pos = places
    head_weight, out_full, up_part, down_part = params
    head_shift, vectors, up_shift = small
    gain_one, bias_one, unused, unused, out_shift, gain_two, bias_two, down_shift = vectors
    normed = layer_norm(flowing, gain_one, bias_one).astype(BF16)
    own, other = gather_ctx(normed)
    normed_all = jnp.concatenate([own, other], axis=0).reshape(LEN, D)
    mixed_head, queries, keys, values = attend(arrive_pos, ctx_pos, normed_all, head_weight, head_shift)
    mixed = exchange(mixed_head.reshape(C, TOK, HD), "ctx")[:H]
    mixed = mixed.transpose(1, 0, 2).reshape(TOK, D)
    middle = flowing + dot(mixed, out_full) + out_shift
    second = layer_norm(middle, gain_two, bias_two).astype(BF16)
    second_all = gather_x(second).reshape(8 * TOK, D)
    hidden = dot(second_all, up_part) + up_shift
    activated = jax.nn.gelu(hidden, approximate=True).astype(BF16)
    partial = dot(activated, down_part).reshape(8, TOK, D)
    output = middle + scatter_x(partial) + down_shift
    saved = (flowing, normed_all, queries, keys, values, mixed, middle, second_all, hidden, activated)
    return output, saved


def backward_layer(grad_out, saved, params, small, places):
    arrive_pos, ctx_pos = places
    qkv_full, out_full, up_part, down_part = params
    unused, vectors, unused = small
    gain_one, bias_one, unused, unused, unused, gain_two, bias_two, unused = vectors
    flowing, normed_all, queries, keys, values, mixed, middle, second_all, hidden, activated = saved
    down_in = grad_out.astype(BF16)
    down_shift_grad = jnp.sum(down_in.astype(F32), axis=0)
    down_all = gather_x(down_in).reshape(8 * TOK, D)
    activated_grad = dot(down_all, down_part, ((1,), (1,)))
    unused, gelu_back = jax.vjp(lambda inner: jax.nn.gelu(inner, approximate=True), hidden)
    hidden_grad = gelu_back(activated_grad)[0].astype(BF16)
    second_grad = scatter_x(dot(hidden_grad, up_part, ((1,), (1,))).reshape(8, TOK, D))
    down_grad = dot(activated, down_all, ((0,), (0,)))
    up_grad = dot(second_all, hidden_grad, ((0,), (0,)))
    up_shift_grad = jnp.sum(hidden_grad.astype(F32), axis=0)
    unused, norm_back = jax.vjp(layer_norm, middle, gain_two, bias_two)
    middle_part, gain_two_grad, bias_two_grad = norm_back(second_grad)
    middle_grad = grad_out + middle_part
    attended_in = middle_grad.astype(BF16)
    out_shift_grad = jnp.sum(attended_in.astype(F32), axis=0)
    mixed_grad = dot(attended_in, out_full, ((1,), (1,))).astype(BF16)
    mixed_grad = mixed_grad.reshape(TOK, H, HD).transpose(1, 0, 2)
    mixed_grad = jnp.concatenate([mixed_grad, jnp.zeros((C - H, TOK, HD), BF16)], axis=0)
    mixed_grad = exchange(mixed_grad, "ctx").reshape(LEN, HD)
    out_grad = dot(mixed, attended_in, ((0,), (0,))).astype(BF16)
    out_grad = lax.psum_scatter(out_grad, "shard", scatter_dimension=0, tiled=True)
    to_ctx, to_arrive = attend_back(arrive_pos, ctx_pos, queries, keys, values, mixed_grad)
    project_grad = exchange(to_ctx.reshape(C, TOK, 3 * HD), "ctx")[:H]
    project_grad = project_grad.reshape(H, TOK, 3, HD).transpose(1, 2, 0, 3).reshape(TOK, 3 * D)
    query_shift_grad = jnp.sum(project_grad[:, :D].astype(F32), axis=0)
    value_shift_grad = jnp.sum(project_grad[:, 2 * D :].astype(F32), axis=0)
    normed_grad = dot(project_grad, qkv_full, ((1,), (1,)))
    unused, first_back = jax.vjp(layer_norm, flowing, gain_one, bias_one)
    flowing_part, gain_one_grad, bias_one_grad = first_back(normed_grad)
    head_grad = dot(normed_all, to_arrive, ((0,), (0,)))
    shifts = (
        gain_one_grad,
        bias_one_grad,
        query_shift_grad,
        value_shift_grad,
        out_shift_grad,
        gain_two_grad,
        bias_two_grad,
        down_shift_grad,
    )
    return middle_grad + flowing_part, (head_grad, up_grad, down_grad, up_shift_grad, shifts, out_grad)


def reduce_grads(core, grads):
    head_grad, up_grad, down_grad, up_shift_grad, shifts, out_grad = grads
    heads = head_grad.astype(BF16).reshape(S, 4, 24, 3 * HD).transpose(0, 2, 1, 3).reshape(S, 24, D)
    ups = up_grad.astype(BF16).reshape(S, 2, 48, 384)
    ups = jnp.concatenate([ups[:, 0], ups[:, 1]], axis=2)
    downs = down_grad.astype(BF16).reshape(S, 48, D)
    vectors = jnp.stack(shifts).reshape(8, S, 96).transpose(1, 0, 2).reshape(S, 1, D)
    hiddens = jnp.pad(up_shift_grad.reshape(S, 1, 48), ((0, 0), (0, 0), (0, D - 48)))
    rest = jnp.concatenate([vectors, hiddens, jnp.zeros((S, 6, D), F32)], axis=1).astype(BF16)
    packed = jnp.concatenate([heads, ups, downs, rest], axis=1)
    owned = jnp.sum(exchange(packed, "shard").astype(F32), axis=0)
    outs = jnp.sum(exchange(out_grad.reshape(C, 6, D), "ctx").astype(F32), axis=0)
    owned = jnp.concatenate([owned[:122], outs], axis=0).astype(BF16)
    own, other = gather_ctx(owned)
    every = jnp.where(core == 0, jnp.stack([own, other], 1), jnp.stack([other, own], 1))
    every = every.reshape(C, 128, D)
    qkv = every[:H, :24].reshape(H, 24, 4, 3, HD).transpose(2, 1, 3, 0, 4).reshape(96, 3 * D).astype(F32)
    halves = every.reshape(2, 8, 128, D)
    ups = halves[0, :, 24:72].astype(F32) + halves[1, :, 24:72].astype(F32)
    ups = ups.reshape(8, 48, 2, S, 48).transpose(2, 1, 3, 0, 4).reshape(96, FF)
    downs = (halves[0, :, 72:120].astype(F32) + halves[1, :, 72:120].astype(F32)).reshape(384, D)
    vectors = jnp.sum(every[:, 120].astype(F32), axis=0).reshape(8, 96)
    hiddens = (halves[0, :, 121, :48].astype(F32) + halves[1, :, 121, :48].astype(F32)).reshape(384)
    outs = every[:, 122:].reshape(96, D).astype(F32)
    return (
        vectors[0],
        vectors[1],
        qkv,
        vectors[2],
        vectors[3],
        outs,
        vectors[4],
        vectors[5],
        vectors[6],
        ups,
        hiddens,
        downs,
        vectors[7],
    )


def shards(
    states,
    cotangent,
    pair_order,
    norm1_gain,
    norm1_bias,
    qkv_weight,
    query_bias,
    value_bias,
    out_weight,
    out_bias,
    norm2_gain,
    norm2_bias,
    up_weight,
    up_bias,
    down_weight,
    down_bias,
):
    place = lax.axis_index("ctx")
    core = place % 2
    rank = place % 8
    head = jnp.minimum(place, H - 1)
    pairs = jnp.stack([pair_order, 2 * C - 1 - pair_order], axis=1)
    ctx_pos = pairs.reshape(-1)
    by_core = pairs.reshape(8, 2, 2).transpose(1, 0, 2)
    arrive_pos = jnp.where(core == 0, by_core, by_core[::-1]).reshape(-1)
    places = (arrive_pos, ctx_pos)

    vectors = jnp.stack(
        [norm1_gain, norm1_bias, query_bias, value_bias, out_bias, norm2_gain, norm2_bias, down_bias]
    )
    head_piece = lax.dynamic_slice_in_dim(qkv_weight.reshape(LAYERS, 96, 3, D), head * HD, HD, axis=3)
    packed = jnp.concatenate(
        [head_piece.reshape(LAYERS * 96 * 3 * HD // D, D), vectors.reshape(2, D), up_bias.reshape(1, D)], axis=0
    )
    packed = jnp.pad(packed, ((0, 13), (0, 0)))
    gathered = spread_to(packed, S, "shard")
    head_weights = gathered[:, :48].reshape(S, LAYERS, 96, 3 * HD)
    vectors = gathered[:, 48:50].reshape(S, 8, LAYERS, 96).transpose(2, 1, 0, 3).reshape(LAYERS, 8, D)
    vectors = vectors.astype(F32)
    up_shifts = gathered[:, 50].reshape(S, LAYERS, 8, 48)
    up_shifts = lax.dynamic_index_in_dim(up_shifts, rank, 2, False).transpose(1, 0, 2).reshape(LAYERS, 1, 384)
    up_shifts = up_shifts.astype(F32)
    head_shifts = jnp.concatenate(
        [
            lax.dynamic_slice_in_dim(vectors[:, 2], head * HD, HD, axis=1),
            jnp.zeros((LAYERS, HD), F32),
            lax.dynamic_slice_in_dim(vectors[:, 3], head * HD, HD, axis=1),
        ],
        axis=1,
    ).reshape(LAYERS, 1, 3 * HD)

    out_full = gather_halves(core, out_weight)
    unit = lax.broadcasted_iota(jnp.int32, (FF, 384), 0)
    column = lax.broadcasted_iota(jnp.int32, (FF, 384), 1)
    pick = (unit == (column // 48) * 384 + rank * 48 + column % 48).astype(BF16)
    up_piece = dot(up_weight.reshape(LAYERS * 96, FF), pick).astype(BF16).reshape(LAYERS, 96, 384)
    down_piece = lax.dynamic_slice_in_dim(down_weight, rank * 48, 48, axis=1)
    up_parts, down_parts = [], []
    for layer in range(LAYERS):
        up_parts.append(lax.all_gather(up_piece[layer], "shard", axis=0, tiled=True))
        down_parts.append(lax.all_gather(down_piece[layer], "shard", axis=0, tiled=True))
    qkv_full = gather_halves(core, qkv_weight)

    flowing = states.reshape(TOK, D).astype(F32)
    saved_all = []
    smalls = []
    for layer in range(LAYERS):
        small = (
            head_shifts[layer],
            [vectors[layer, member : member + 1] for member in range(8)],
            up_shifts[layer],
        )
        small = (small[0], [member.reshape(D) for member in small[1]], small[2])
        smalls.append(small)
        head_weight = head_weights[:, layer].reshape(D, 3 * HD)
        params = (head_weight, out_full[layer], up_parts[layer], down_parts[layer])
        flowing, saved = forward_layer(flowing, params, small, places)
        saved_all.append(saved)
    result = flowing.astype(BF16).reshape(states.shape)
    grad_flow = cotangent.reshape(TOK, D).astype(F32)
    collected = [None] * LAYERS
    for layer in range(LAYERS - 1, -1, -1):
        params = (qkv_full[layer], out_full[layer], up_parts[layer], down_parts[layer])
        grad_flow, grads = backward_layer(grad_flow, saved_all[layer], params, smalls[layer], places)
        collected[layer] = reduce_grads(core, grads)
    stacked = tuple(
        jnp.stack([collected[layer][member] for layer in range(LAYERS)]) for member in range(13)
    )
    return (result, grad_flow.astype(BF16).reshape(states.shape)) + stacked


def solution(mesh):
    matrix = P(None, "shard", None)
    vector = P(None, "shard")
    rows = P("shard", "ctx", None)
    params = (
        vector,
        vector,
        matrix,
        vector,
        vector,
        matrix,
        vector,
        vector,
        vector,
        matrix,
        vector,
        matrix,
        vector,
    )
    return jax.shard_map(
        shards,
        mesh=mesh,
        in_specs=(rows, rows, P()) + params,
        out_specs=(rows, rows) + params,
        check_vma=False,
    )
```

time: 2140 us -> 848 us (0.40)
  waiting for transfers between devices: 1580 us -> 205 us
  starting transfers between devices: 1.49 us -> 127 us
  matrix products: 169 us -> 50.5 us
  Pallas kernels: 0 us -> 35.7 us
  other arithmetic: 40.3 us -> 66.9 us
    all_gather x12 -> x2, waiting for transfers between devices: 689 us -> 0.02 us  [gather_halves(): own = lax.all_gather(piece, 'shard', axis=0)]
    reduce_scatter x8 -> x2, waiting for transfers between devices: 653 us -> 0.02 us  [backward_layer(): lax.psum_scatter(out_grad, 'shard', scatter_dimension=0, tiled=True)]
    unnamed x29 -> x4, waiting for transfers between devices: 201 us -> 0.07 us
    all_to_all x0 -> x19, waiting for transfers between devices: none -> 200 us  [exchange(): lax.all_to_all(parts, axis, 0, 0, tiled=True, axis_index_groups=groups)]
    dot_general x34 -> x23, matrix products: 151 us -> 50.5 us  [dot(): lax.dot_general(left, right, (dims, ((), ())), preferred_element_type=F32)]
    unnamed x281 -> x328, local copies, waits for them, and re-layouts: 123 us -> 29.7 us
    all_to_all x0 -> x19, starting transfers between devices: none -> 91.5 us  [exchange(): lax.all_to_all(parts, axis, 0, 0, tiled=True, axis_index_groups=groups)]
    all_gather x2 -> x4, blocking collectives: 39.2 us -> 109 us  [the longest x2 58.3 us: shards(): lax.all_gather(down_piece[layer], 'shard', axis=0, tiled=True)]
  transfers between devices with their start and end apart: 25 -> 37, of which waited for: 25 -> 20; matrix products, arithmetic and copies ran while one was open for 10% -> 23% of each run, Pallas kernels for 0% -> 4%
where the time goes in v1:
time: 848 us; the launch traced here: 836 us
  waiting for transfers between devices  205 us (24%)
  blocking collectives  174 us (21%)
  local copies, waits for them, and re-layouts  161 us (19%)
  starting transfers between devices  127 us (15%)
  other arithmetic  66.9 us (8%)
  matrix products  50.5 us (6%)
  Pallas kernels  35.7 us (4%)
  between operations  16 us (2%)
    all_to_all x19, waiting for transfers between devices, exchange(): lax.all_to_all(parts, axis, 0, 0, tiled=True, axis_index_groups=groups)  200 us
    all_to_all x19, starting transfers between devices, exchange(): lax.all_to_all(parts, axis, 0, 0, tiled=True, axis_index_groups=groups)  91.5 us
    all_to_all x4, blocking collectives, exchange(): lax.all_to_all(parts, axis, 0, 0, tiled=True, axis_index_groups=groups)  65 us
    all_gather x2, blocking collectives, shards(): lax.all_gather(down_piece[layer], 'shard', axis=0, tiled=True)  58.3 us
    all_gather x2, blocking collectives, shards(): lax.all_gather(up_piece[layer], 'shard', axis=0, tiled=True)  50.8 us
    dot_general x23, matrix products, dot(): lax.dot_general(left, right, (dims, ((), ())), preferred_element_type=F32)  50.5 us
    ppermute x14, starting transfers between devices, swap_core(): return lax.ppermute(part, 'ctx', SWAP)  35.2 us
    unnamed x328, local copies, waits for them, and re-layouts  29.7 us
  transfers between devices with their start and end apart: 37, of which 20 were waited for; matrix products, arithmetic and copies ran while one was open for 23% of the time, Pallas kernels for 4%

profile of v1, /device:TPU:1, one launch (start us, length us, event | category | flops | bytes accessed | tf_op | source)
XLA Modules:
  0.0 835.8 jit_solution(17698157892081792172)
XLA Ops:
  16.9 6.9 all-to-all-start
  24.1 11.3 %all-to-all-done = bf16[8,64,768]{2,1,0:T(8,128)(2,1)S(1)} async-done(((bf16[8,64,768]{2,1,0:T(8,128)(2,1)}), bf16[8,64,768]{2,1,0:T(8,128)(2,1)S(1)}, u32[]{:S(2)}, u32[]{:S(2)}) %all-to-all-start) | async-done | bytes 786464 | tf_op jit(solution)/shard_map/all_to_all | solution.py:39
  37.8 6.4 all-to-all-start.1
  50.2 16.9 %all-to-all-done.1 = bf16[8,128,768]{2,1,0:T(8,128)(2,1)S(1)} async-done(((bf16[8,128,768]{2,1,0:T(8,128)(2,1)}), bf16[8,128,768]{2,1,0:T(8,128)(2,1)S(1)}, u32[]{:S(2)}, u32[]{:S(2)}) %all-to-all-start.1) | async-done | bytes 1572896 | tf_op jit(solution)/shard_map/all_to_all | solution.py:39
  71.8 29.7 %all-gather.1 = bf16[1,384,768]{2,1,0:T(8,128)(2,1)} all-gather(bf16[1,48,768]{2,1,0:T(8,128)(2,1)} %get-tuple-element.92), channel_id=3, replica_groups=mesh['shard'=8,'ctx'=16] {'shard'}, dimensions={1}, use_global_device_ids=true | all-gather | bytes 663552 | tf_op jit(solution)/shard_map/all_gather | solution.py:396
  103.0 4.5 collective-permute-start.1
  115.2 6.4 shard_map.271
  124.2 7.0 all-to-all-start.2
  133.6 6.3 all-to-all-done.2
  144.1 3.5 all-to-all-start.3
  150.8 8.3 all-to-all-done.3
  162.4 24.1 %all_gather.26 = bf16[768,384]{1,0:T(8,128)(2,1)S(1)} all-gather(bf16[96,384]{1,0:T(8,128)(2,1)S(1)} %get-tuple-element.105), channel_id=1, replica_groups=mesh['shard'=8,'ctx'=16] {'shard'}, dimensions={0}, use_global_device_ids=true | all-gather | bytes 663552 | tf_op jit(solution)/shard_map/all_gather | solution.py:395
  192.1 6.2 collective-permute-start.3
  200.4 14.4 %all_to_all.115 = bf16[4,128,768]{2,1,0:T(8,128)(2,1)S(1)} all-to-all(bf16[4,128,768]{2,1,0:T(8,128)(2,1)S(1)} %add_convert_fusion.3), channel_id=1, replica_groups={{0,2,4,6},{1,3,5,7},{8,10,12,14},{9,11,13,15},{16,18,20,22},{17,19,21,2..., dimensions={0} | all-to-all | bytes 1572864 | tf_op jit(solution)/shard_map/all_to_all | solution.py:39
  216.0 24.1 %all_to_all.116 = bf16[8,128,768]{2,1,0:T(8,128)(2,1)S(1)} all-to-all(bf16[8,128,768]{2,1,0:T(8,128)(2,1)S(1)} %broadcast_in_dim.43), channel_id=1, replica_groups={{0,2,4,6,8,10,12,14},{1,3,5,7,9,11,13,15},{16,18,20,22,24,26,28,30},{17..., dimensions={0} | all-to-all | bytes 3145728 | tf_op jit(solution)/shard_map/all_to_all | solution.py:39
  247.7 6.4 shard_map.272
  258.7 12.2 %all_to_all.117 = bf16[16,128,64]{1,2,0:T(8,128)(2,1)} all-to-all(bf16[16,128,64]{1,2,0:T(8,128)(2,1)S(1)} %copy.108), channel_id=1, replica_groups=mesh['shard'=8,'ctx'=16] {'ctx'}, dimensions={0} | all-to-all | bytes 524288 | tf_op jit(solution)/shard_map/all_to_all | solution.py:39
  272.8 4.4 all-to-all-start.9
  282.5 6.3 all-to-all-done.9
  290.7 4.2 all-to-all-start.7
  296.7 8.9 %all-to-all-done.7 = bf16[4,128,768]{2,1,0:T(8,128)(2,1)} async-done(((bf16[4,128,768]{2,1,0:T(8,128)(2,1)}), bf16[4,128,768]{2,1,0:T(8,128)(2,1)}, u32[]{:S(2)}, u32[]{:S(2)}) %all-to-all-start.7) | async-done | bytes 786464 | tf_op jit(solution)/shard_map/all_to_all | solution.py:39
  308.2 28.7 %all-gather.2 = bf16[1,384,768]{2,1,0:T(8,128)(2,1)} all-gather(bf16[1,48,768]{2,1,0:T(8,128)(2,1)} %get-tuple-element.91), channel_id=4, replica_groups=mesh['shard'=8,'ctx'=16] {'shard'}, dimensions={1}, use_global_device_ids=true | all-gather | bytes 663552 | tf_op jit(solution)/shard_map/all_gather | solution.py:396
  336.8 26.7 %all_gather.28 = bf16[768,384]{1,0:T(8,128)(2,1)} all-gather(bf16[96,384]{1,0:T(8,128)(2,1)} %get-tuple-element.104), channel_id=1, replica_groups=mesh['shard'=8,'ctx'=16] {'shard'}, dimensions={0}, use_global_device_ids=true | all-gather | bytes 663552 | tf_op jit(solution)/shard_map/all_gather | solution.py:395
  371.4 11.6 %collective-permute-start.6 = (bf16[4,128,768]{2,1,0:T(8,128)(2,1)S(1)}, bf16[4,128,768]{2,1,0:T(8,128)(2,1)S(1)}, u32[]{:S(2)}, u32[]{:S(2)}) collective-permute-start(bf16[4,128,768]{2,1,0:T(8,128)(2,1)S(1)} %bitcast.322), channel_id=1, source_target_pairs={{0,1},{1,0},{2,3},{3,2},{4,5},{5,4},{6,7},{7,6},{8,9},{9,8},{10,11... | collective-permute-start | bytes 2359304 | tf_op jit(solution)/shard_map/ppermute | solution.py:47
  389.4 4.2 all-to-all-start.8
  397.3 8.8 %all-to-all-done.8 = bf16[4,128,768]{2,1,0:T(8,128)(2,1)} async-done(((bf16[4,128,768]{2,1,0:T(8,128)(2,1)}), bf16[4,128,768]{2,1,0:T(8,128)(2,1)}, u32[]{:S(2)}, u32[]{:S(2)}) %all-to-all-start.8) | async-done | bytes 786464 | tf_op jit(solution)/shard_map/all_to_all | solution.py:39
  406.1 4.2 all-to-all-start.10
  412.4 9.6 %all-to-all-done.10 = bf16[4,128,768]{2,1,0:T(8,128)(2,1)} async-done(((bf16[4,128,768]{2,1,0:T(8,128)(2,1)}), bf16[4,128,768]{2,1,0:T(8,128)(2,1)}, u32[]{:S(2)}, u32[]{:S(2)}) %all-to-all-start.10) | async-done | bytes 786464 | tf_op jit(solution)/shard_map/all_to_all | solution.py:39
  433.6 14.2 %all_to_all.118 = bf16[16,128,64]{1,2,0:T(8,128)(2,1)} all-to-all(bf16[16,128,64]{1,2,0:T(8,128)(2,1)S(1)} %concatenate.132), channel_id=1, replica_groups=mesh['shard'=8,'ctx'=16] {'ctx'}, dimensions={0} | all-to-all | bytes 524288 | tf_op jit(solution)/shard_map/all_to_all | solution.py:39
  454.0 11.4 %shard_map.273 = (bf16[2048,192]{1,0:T(8,128)(2,1)S(1)}, bf16[2048,192]{1,0:T(8,128)(2,1)S(1)}) custom-call(s32[32]{0:T(128)S(1)} %reshape.724.arrive_pos, s32[32]{0:T(128)S(1)} %reshape.725.ctx_pos, bf16[2048,64]{1,0:T(8,128)(2,1)S(1)} %copy-done.17, bf16[2048,64]{1,0:T(8,128)(2,1)S(1)} %copy-done.19, bf16[2048,64]{1,0:T(8,128)(2,1)S(1)} %copy-done.21, ...), custom_call_target="tpu_custom_call" | custom-call | flops 4000000000 | bytes 5000000 | tf_op jit(solution)/shard_map/pallas_call | solution.py:190
  469.6 5.2 all-to-all-start.12
  474.8 4.1 fusion.111
  478.9 4.1 fusion.112
  483.0 6.4 all-to-all-done.12
  491.0 4.3 multiply_reduce_fusion.1
  497.3 4.2 all-to-all-start.13
  506.7 6.5 all-to-all-done.13
  520.1 3.7 convolution_convert_fusion.2
  548.7 3.6 all-to-all-start.14
  553.8 6.1 concatenate.147
  559.9 3.8 convolution_convert_fusion.4
  568.3 4.4 all-to-all-start.15
  576.0 5.3 all-to-all-done.15
  583.7 11.4 %shard_map.274 = (bf16[2048,192]{1,0:T(8,128)(2,1)S(1)}, bf16[2048,192]{1,0:T(8,128)(2,1)S(1)}) custom-call(s32[32]{0:T(128)S(1)} %reshape.724.arrive_pos, s32[32]{0:T(128)S(1)} %reshape.725.ctx_pos, bf16[2048,64]{1,0:T(8,128)(2,1)S(1)} %copy-done.11, bf16[2048,64]{1,0:T(8,128)(2,1)S(1)} %copy-done.13, bf16[2048,64]{1,0:T(8,128)(2,1)S(1)} %copy-done.15, ...), custom_call_target="tpu_custom_call" | custom-call | flops 4000000000 | bytes 5000000 | tf_op jit(solution)/shard_map/pallas_call | solution.py:190
  596.5 5.4 all-to-all-start.16
  612.5 4.1 all-to-all-done.16
  616.6 3.6 all-to-all-start.20
  621.8 4.6 fusion.101
  627.5 30.9 %all-to-all-done.20 = bf16[8,128,768]{2,1,0:T(8,128)(2,1)S(1)} async-done(((bf16[8,128,768]{2,1,0:T(8,128)(2,1)}), bf16[8,128,768]{2,1,0:T(8,128)(2,1)S(1)}, u32[]{:S(2)}, u32[]{:S(2)}) %all-to-all-start.20) | async-done | bytes 1572896 | tf_op jit(solution)/shard_map/all_to_all | solution.py:39
  658.4 4.7 all-to-all-start.21
  663.3 9.3 %concatenate.144 = bf16[8,128,768]{2,1,0:T(8,128)(2,1)} concatenate(bf16[8,24,768]{2,1,0:T(8,128)(2,1)} %reshape.756, bf16[8,48,768]{2,1,0:T(8,128)(2,1)S(1)} %copy-done.55, bf16[8,48,768]{2,1,0:T(8,128)(2,1)} %bitcast.338, bf16[8,1,768]{2,1,0:T(2,128)(2,1)S(1)} %reshape.776, bf16[8,1,768]{2,1,0:T(2,128)(2,1)S(1)} %copy-done.95, bf16[8,6,768]{2,1,0:T(8,128)(2,1)S(1)} %copy-done.76), dimensions={1} | concatenate | bytes 3145728 | tf_op jit(solution)/shard_map/concatenate | solution.py:303
  673.3 3.6 all-to-all-start.17
  678.6 19.5 %all-to-all-done.17 = bf16[8,128,768]{2,1,0:T(8,128)(2,1)S(1)} async-done(((bf16[8,128,768]{2,1,0:T(8,128)(2,1)}), bf16[8,128,768]{2,1,0:T(8,128)(2,1)S(1)}, u32[]{:S(2)}, u32[]{:S(2)}) %all-to-all-start.17) | async-done | bytes 1572896 | tf_op jit(solution)/shard_map/all_to_all | solution.py:39
  698.1 8.0 all-to-all-start.18
  708.0 6.3 all-to-all-done.18
  715.6 3.6 all-to-all-start.22
  720.4 21.7 %all-to-all-done.22 = bf16[8,128,768]{2,1,0:T(8,128)(2,1)S(1)} async-done(((bf16[8,128,768]{2,1,0:T(8,128)(2,1)}), bf16[8,128,768]{2,1,0:T(8,128)(2,1)S(1)}, u32[]{:S(2)}, u32[]{:S(2)}) %all-to-all-start.22) | async-done | bytes 1572896 | tf_op jit(solution)/shard_map/all_to_all | solution.py:39
  743.5 4.4 all-to-all-start.19
  748.8 22.1 %all-to-all-done.19 = bf16[8,128,768]{2,1,0:T(8,128)(2,1)} async-done(((bf16[8,128,768]{2,1,0:T(8,128)(2,1)}), bf16[8,128,768]{2,1,0:T(8,128)(2,1)}, u32[]{:S(2)}, u32[]{:S(2)}) %all-to-all-start.19) | async-done | bytes 1572896 | tf_op jit(solution)/shard_map/all_to_all | solution.py:39
  776.4 3.5 convert_element_type.468
  790.3 3.5 copy.140
  793.9 4.5 stack_reshape.5
  811.2 3.5 copy.141
  814.6 3.8 stack_reshape.4
  (607 shorter events, 238.3 us)
Async XLA Ops:
  7.2 141.2 %copy-start = (bf16[2,96,3072]{2,1,0:T(8,128)(2,1)S(1)}, bf16[2,96,3072]{2,1,0:T(8,128)(2,1)}, u32[]{:S(2)}) copy-start(bf16[2,96,3072]{2,1,0:T(8,128)(2,1)} %param.28) | copy-start | bytes 3538948
  16.9 18.6 %all-to-all-start = ((bf16[8,64,768]{2,1,0:T(8,128)(2,1)}), bf16[8,64,768]{2,1,0:T(8,128)(2,1)S(1)}, u32[]{:S(2)}, u32[]{:S(2)}) async-start(bf16[8,64,768]{2,1,0:T(8,128)(2,1)} %broadcast_in_dim.38), calls=%async_computation | async-start | bytes 1572864 | tf_op jit(solution)/shard_map/all_to_all | solution.py:39
  23.9 14.0 %copy-start.106 = (f32[128]{0:T(128)}, f32[128]{0:T(128)S(1)}, u32[]{:S(2)}) copy-start(f32[128]{0:T(128)S(1)} %broadcast_multiply_fusion.3) | copy-start | bytes 1540
  24.1 13.7 %copy-start.122 = (f32[128]{0:T(128)}, f32[128]{0:T(128)S(1)}, u32[]{:S(2)}) copy-start(f32[128]{0:T(128)S(1)} %fusion.88) | copy-start | bytes 1540
  37.8 29.3 %all-to-all-start.1 = ((bf16[8,128,768]{2,1,0:T(8,128)(2,1)}), bf16[8,128,768]{2,1,0:T(8,128)(2,1)S(1)}, u32[]{:S(2)}, u32[]{:S(2)}) async-start(bf16[8,128,768]{2,1,0:T(8,128)(2,1)} %broadcast_in_dim.40), calls=%async_computation.1 | async-start | bytes 3145728 | tf_op jit(solution)/shard_map/all_to_all | solution.py:39
  44.2 64.6 %slice-start.2 = ((bf16[8,64,768]{2,1,0:T(8,128)(2,1)}), bf16[8,48,768]{2,1,0:T(8,128)(2,1)S(1)}, s32[]{:S(2)}) async-start(bf16[8,64,768]{2,1,0:T(8,128)(2,1)} %copy-done.48), calls=%async_computation.31 | async-start | bytes 1179648 | tf_op jit(solution)/shard_map/slice | solution.py:372
  44.2 58.8 %all-gather.7.cloned.1.call-start = ((), (), s32[]{:S(2)}) async-start(), calls=%async_computation.27 | async-start | bytes 1327104 | tf_op jit(solution)/shard_map/all_gather | solution.py:216
  67.2 46.4 %collective-permute-start = (bf16[8,128,768]{2,1,0:T(8,128)(2,1)S(1)}, bf16[8,128,768]{2,1,0:T(8,128)(2,1)}, u32[]{:S(2)}, u32[]{:S(2)}) collective-permute-start(bf16[8,128,768]{2,1,0:T(8,128)(2,1)S(1)} %all-to-all-done.1), channel_id=1, source_target_pairs={{0,1},{1,0},{2,3},{3,2},{4,5},{5,4},{6,7},{7,6},{8,9},{9,8},{10,11... | collective-permute-start | bytes 4718600 | tf_op jit(solution)/shard_map/ppermute | solution.py:47
  103.0 28.2 %collective-permute-start.1 = (bf16[8,2,96,384]{3,2,1,0:T(8,128)(2,1)}, bf16[8,2,96,384]{3,2,1,0:T(8,128)(2,1)}, u32[]{:S(2)}, u32[]{:S(2)}) collective-permute-start(bf16[8,2,96,384]{3,2,1,0:T(8,128)(2,1)} %bitcast.316), channel_id=1, source_target_pairs={{0,1},{1,0},{2,3},{3,2},{4,5},{5,4},{6,7},{7,6},{8,9},{9,8},{10,11... | collective-permute-start | bytes 3538952 | tf_op jit(solution)/shard_map/ppermute | solution.py:47
  124.2 15.7 %copy-start.130 = (f32[768]{0:T(1024)S(1)}, f32[768]{0:T(1024)}, u32[]{:S(2)}) copy-start(f32[768]{0:T(1024)} %get-tuple-element.63) | copy-start | bytes 9220
  124.2 15.7 %all-to-all-start.2 = ((bf16[16,128,64]{1,2,0:T(8,128)(2,1)}), bf16[16,128,64]{1,2,0:T(8,128)(2,1)S(1)}, u32[]{:S(2)}, u32[]{:S(2)}) async-start(bf16[16,128,64]{1,2,0:T(8,128)(2,1)} %copy.107), calls=%async_computation.2 | async-start | bytes 524288 | tf_op jit(solution)/shard_map/all_to_all | solution.py:39
  142.2 72.7 %copy-start.23 = (f32[128,768]{1,0:T(8,128)}, f32[128,768]{1,0:T(8,128)S(1)}, u32[]{:S(2)}) copy-start(f32[128,768]{1,0:T(8,128)S(1)} %get-tuple-element.129) | copy-start | bytes 1179652
  144.1 15.0 %all-to-all-start.3 = ((bf16[4,128,768]{2,1,0:T(8,128)(2,1)}), bf16[4,128,768]{2,1,0:T(8,128)(2,1)S(1)}, u32[]{:S(2)}, u32[]{:S(2)}) async-start(bf16[4,128,768]{2,1,0:T(8,128)(2,1)} %broadcast_in_dim.42), calls=%async_computation.3 | async-start | bytes 1572864 | tf_op jit(solution)/shard_map/all_to_all | solution.py:39
  147.6 246.0 %all-gather.9.cloned.1.call-start = ((), (), s32[]{:S(2)}) async-start(), calls=%async_computation.28 | async-start | bytes 3981312 | tf_op jit(solution)/shard_map/all_gather | solution.py:216
  148.4 38.1 %copy-start.49 = (bf16[8,64,768]{2,1,0:T(8,128)(2,1)S(1)}, bf16[8,64,768]{2,1,0:T(8,128)(2,1)}, u32[]{:S(2)}) copy-start(bf16[8,64,768]{2,1,0:T(8,128)(2,1)} %copy-done.48) | copy-start | bytes 2359300
  159.1 28.8 %collective-permute-start.2 = (bf16[4,128,768]{2,1,0:T(8,128)(2,1)S(1)}, bf16[4,128,768]{2,1,0:T(8,128)(2,1)}, u32[]{:S(2)}, u32[]{:S(2)}) collective-permute-start(bf16[4,128,768]{2,1,0:T(8,128)(2,1)S(1)} %all-to-all-done.3), channel_id=1, source_target_pairs={{0,1},{1,0},{2,3},{3,2},{4,5},{5,4},{6,7},{7,6},{8,9},{9,8},{10,11... | collective-permute-start | bytes 2359304 | tf_op jit(solution)/shard_map/ppermute | solution.py:47
  192.1 8.1 collective-permute-start.3
  200.4 14.6 %copy-start.104 = (f32[768]{0:T(1024)S(1)}, f32[768]{0:T(1024)}, u32[]{:S(2)}) copy-start(f32[768]{0:T(1024)} %get-tuple-element.60) | copy-start | bytes 9220
  215.1 25.0 %copy-start.31 = (f32[128,768]{1,0:T(8,128)}, f32[128,768]{1,0:T(8,128)S(1)}, u32[]{:S(2)}) copy-start(f32[128,768]{1,0:T(8,128)S(1)} %get-tuple-element.82) | copy-start | bytes 1179652
  216.0 26.4 %copy-start.58 = (bf16[2,96,2304]{2,1,0:T(8,128)(2,1)S(1)}, bf16[2,96,2304]{2,1,0:T(8,128)(2,1)}, u32[]{:S(2)}) copy-start(bf16[2,96,2304]{2,1,0:T(8,128)(2,1)} %param.21) | copy-start | bytes 2654212
  240.1 5.5 collective-permute-start.4
  272.8 16.0 %all-to-all-start.9 = ((bf16[4,128,768]{2,1,0:T(8,128)(2,1)}), bf16[4,128,768]{2,1,0:T(8,128)(2,1)}, u32[]{:S(2)}, u32[]{:S(2)}) async-start(bf16[4,128,768]{2,1,0:T(8,128)(2,1)} %broadcast_in_dim.45), calls=%async_computation.9 | async-start | bytes 1572864 | tf_op jit(solution)/shard_map/all_to_all | solution.py:39
  290.7 14.9 %all-to-all-start.7 = ((bf16[4,128,768]{2,1,0:T(8,128)(2,1)}), bf16[4,128,768]{2,1,0:T(8,128)(2,1)}, u32[]{:S(2)}, u32[]{:S(2)}) async-start(bf16[4,128,768]{2,1,0:T(8,128)(2,1)} %broadcast_in_dim.44), calls=%async_computation.7 | async-start | bytes 1572864 | tf_op jit(solution)/shard_map/all_to_all | solution.py:39
  294.9 70.0 %collective-permute-start.7 = (bf16[4,128,768]{2,1,0:T(8,128)(2,1)}, bf16[4,128,768]{2,1,0:T(8,128)(2,1)}, u32[]{:S(2)}, u32[]{:S(2)}) collective-permute-start(bf16[4,128,768]{2,1,0:T(8,128)(2,1)} %all-to-all-done.9), channel_id=1, source_target_pairs={{0,1},{1,0},{2,3},{3,2},{4,5},{5,4},{6,7},{7,6},{8,9},{9,8},{10,11... | collective-permute-start | bytes 2359304 | tf_op jit(solution)/shard_map/ppermute | solution.py:47
  305.5 60.9 %collective-permute-start.5 = (bf16[4,128,768]{2,1,0:T(8,128)(2,1)}, bf16[4,128,768]{2,1,0:T(8,128)(2,1)}, u32[]{:S(2)}, u32[]{:S(2)}) collective-permute-start(bf16[4,128,768]{2,1,0:T(8,128)(2,1)} %all-to-all-done.7), channel_id=1, source_target_pairs={{0,1},{1,0},{2,3},{3,2},{4,5},{5,4},{6,7},{7,6},{8,9},{9,8},{10,11... | collective-permute-start | bytes 2359304 | tf_op jit(solution)/shard_map/ppermute | solution.py:47
  366.4 16.5 %copy-start.65 = (bf16[8,128,768]{2,1,0:T(8,128)(2,1)}, bf16[8,128,768]{2,1,0:T(8,128)(2,1)S(1)}, u32[]{:S(2)}) copy-start(bf16[8,128,768]{2,1,0:T(8,128)(2,1)S(1)} %pad_maximum_fusion.6) | copy-start | bytes 4718596
  371.4 17.0 %collective-permute-start.6 = (bf16[4,128,768]{2,1,0:T(8,128)(2,1)S(1)}, bf16[4,128,768]{2,1,0:T(8,128)(2,1)S(1)}, u32[]{:S(2)}, u32[]{:S(2)}) collective-permute-start(bf16[4,128,768]{2,1,0:T(8,128)(2,1)S(1)} %bitcast.322), channel_id=1, source_target_pairs={{0,1},{1,0},{2,3},{3,2},{4,5},{5,4},{6,7},{7,6},{8,9},{9,8},{10,11... | collective-permute-start | bytes 2359304 | tf_op jit(solution)/shard_map/ppermute | solution.py:47
  387.4 6.3 collective-permute-start.8
  389.4 16.7 %all-to-all-start.8 = ((bf16[4,128,768]{2,1,0:T(8,128)(2,1)}), bf16[4,128,768]{2,1,0:T(8,128)(2,1)}, u32[]{:S(2)}, u32[]{:S(2)}) async-start(bf16[4,128,768]{2,1,0:T(8,128)(2,1)} %add_convert_fusion.2), calls=%async_computation.8 | async-start | bytes 1572864 | tf_op jit(solution)/shard_map/all_to_all | solution.py:39
  393.7 85.3 %collective-permute-start.9 = (bf16[8,2,96,1152]{3,2,1,0:T(8,128)(2,1)}, bf16[8,2,96,1152]{3,2,1,0:T(8,128)(2,1)}, u32[]{:S(2)}, u32[]{:S(2)}) collective-permute-start(bf16[8,2,96,1152]{3,2,1,0:T(8,128)(2,1)} %bitcast.293), channel_id=1, source_target_pairs={{0,1},{1,0},{2,3},{3,2},{4,5},{5,4},{6,7},{7,6},{8,9},{9,8},{10,11... | collective-permute-start | bytes 10616840 | tf_op jit(solution)/shard_map/ppermute | solution.py:47
  406.1 15.8 %all-to-all-start.10 = ((bf16[4,128,768]{2,1,0:T(8,128)(2,1)}), bf16[4,128,768]{2,1,0:T(8,128)(2,1)}, u32[]{:S(2)}, u32[]{:S(2)}) async-start(bf16[4,128,768]{2,1,0:T(8,128)(2,1)} %add_convert_fusion.1), calls=%async_computation.10 | async-start | bytes 1572864 | tf_op jit(solution)/shard_map/all_to_all | solution.py:39
  469.6 19.8 %all-to-all-start.12 = ((bf16[16,128,192]{1,2,0:T(8,128)(2,1)}), bf16[16,128,192]{1,2,0:T(8,128)(2,1)}, u32[]{:S(2)}, u32[]{:S(2)}) async-start(bf16[16,128,192]{1,2,0:T(8,128)(2,1)} %copy.111), calls=%async_computation.12 | async-start | bytes 1572864 | tf_op jit(solution)/shard_map/all_to_all | solution.py:39
  496.3 69.6 %copy-start.40 = (f32[128,768]{1,0:T(8,128)}, f32[128,768]{1,0:T(8,128)S(1)}, u32[]{:S(2)}) copy-start(f32[128,768]{1,0:T(8,128)S(1)} %get-tuple-element.70) | copy-start | bytes 1179652
  497.3 15.9 %all-to-all-start.13 = ((bf16[4,128,768]{2,1,0:T(8,128)(2,1)}), bf16[4,128,768]{2,1,0:T(8,128)(2,1)}, u32[]{:S(2)}, u32[]{:S(2)}) async-start(bf16[4,128,768]{2,1,0:T(8,128)(2,1)} %broadcast_in_dim.50), calls=%async_computation.13 | async-start | bytes 1572864 | tf_op jit(solution)/shard_map/all_to_all | solution.py:39
  501.5 101.2 %reduce-scatter.5.cloned.1.call-start = ((), (), s32[]{:S(2)}) async-start(), calls=%async_computation.26 | async-start | bytes 1327104 | tf_op jit(solution)/shard_map/reduce_scatter | solution.py:271
  513.2 18.4 %collective-permute-start.10 = (bf16[4,128,768]{2,1,0:T(8,128)(2,1)}, bf16[4,128,768]{2,1,0:T(8,128)(2,1)}, u32[]{:S(2)}, u32[]{:S(2)}) collective-permute-start(bf16[4,128,768]{2,1,0:T(8,128)(2,1)} %all-to-all-done.13), channel_id=1, source_target_pairs={{0,1},{1,0},{2,3},{3,2},{4,5},{5,4},{6,7},{7,6},{8,9},{9,8},{10,11... | collective-permute-start | bytes 2359304 | tf_op jit(solution)/shard_map/ppermute | solution.py:47
  540.5 4.5 collective-permute-start.11
  548.7 16.0 %all-to-all-start.14 = ((bf16[4,128,768]{2,1,0:T(8,128)(2,1)}), bf16[4,128,768]{2,1,0:T(8,128)(2,1)S(1)}, u32[]{:S(2)}, u32[]{:S(2)}) async-start(bf16[4,128,768]{2,1,0:T(8,128)(2,1)} %add_convert_fusion), calls=%async_computation.14 | async-start | bytes 1572864 | tf_op jit(solution)/shard_map/all_to_all | solution.py:39
  568.3 13.1 %all-to-all-start.15 = ((bf16[16,128,64]{1,2,0:T(8,128)(2,1)}), bf16[16,128,64]{1,2,0:T(8,128)(2,1)S(1)}, u32[]{:S(2)}, u32[]{:S(2)}) async-start(bf16[16,128,64]{1,2,0:T(8,128)(2,1)} %concatenate.138), calls=%async_computation.15 | async-start | bytes 524288 | tf_op jit(solution)/shard_map/all_to_all | solution.py:39
  596.5 20.1 %all-to-all-start.16 = ((bf16[16,128,192]{1,2,0:T(8,128)(2,1)}), bf16[16,128,192]{1,2,0:T(8,128)(2,1)}, u32[]{:S(2)}, u32[]{:S(2)}) async-start(bf16[16,128,192]{1,2,0:T(8,128)(2,1)} %copy.115), calls=%async_computation.16 | async-start | bytes 1572864 | tf_op jit(solution)/shard_map/all_to_all | solution.py:39
  601.9 75.0 %reduce-scatter.3.cloned.1.call-start = ((), (), s32[]{:S(2)}) async-start(), calls=%async_computation.25 | async-start | bytes 1327104 | tf_op jit(solution)/shard_map/reduce_scatter | solution.py:271
  616.6 41.8 %all-to-all-start.20 = ((bf16[8,128,768]{2,1,0:T(8,128)(2,1)}), bf16[8,128,768]{2,1,0:T(8,128)(2,1)S(1)}, u32[]{:S(2)}, u32[]{:S(2)}) async-start(bf16[8,128,768]{2,1,0:T(8,128)(2,1)} %concatenate.147), calls=%async_computation.21 | async-start | bytes 3145728 | tf_op jit(solution)/shard_map/all_to_all | solution.py:39
  621.7 41.4 %copy-start.115 = (bf16[1,8,96]{2,1,0:T(8,128)(2,1)S(1)}, bf16[1,8,96]{2,1,0:T(8,128)(2,1)}, u32[]{:S(2)}) copy-start(bf16[1,8,96]{2,1,0:T(8,128)(2,1)} %stack.194) | copy-start | bytes 4612
  621.7 41.4 %copy-start.113 = (bf16[1,8,96]{2,1,0:T(8,128)(2,1)S(1)}, bf16[1,8,96]{2,1,0:T(8,128)(2,1)}, u32[]{:S(2)}) copy-start(bf16[1,8,96]{2,1,0:T(8,128)(2,1)} %stack.195) | copy-start | bytes 4612
  621.7 41.5 %copy-start.55 = (bf16[8,48,768]{2,1,0:T(8,128)(2,1)S(1)}, bf16[8,48,768]{2,1,0:T(8,128)(2,1)}, u32[]{:S(2)}) copy-start(bf16[8,48,768]{2,1,0:T(8,128)(2,1)} %pad_maximum_fusion.8) | copy-start | bytes 1769476
  621.7 41.5 %copy-start.76 = (bf16[8,6,768]{2,1,0:T(8,128)(2,1)S(1)}, bf16[8,6,768]{2,1,0:T(8,128)(2,1)}, u32[]{:S(2)}) copy-start(bf16[8,6,768]{2,1,0:T(8,128)(2,1)} %copy-done.75) | copy-start | bytes 221188
  621.7 41.5 %copy-start.95 = (bf16[8,1,768]{2,1,0:T(2,128)(2,1)S(1)}, bf16[8,1,768]{2,1,0:T(2,128)(2,1)}, u32[]{:S(2)}) copy-start(bf16[8,1,768]{2,1,0:T(2,128)(2,1)} %pad.16.clone) | copy-start | bytes 36868
  626.3 46.3 %copy-start.68 = (f32[128,768]{1,0:T(8,128)}, f32[128,768]{1,0:T(8,128)S(1)}, u32[]{:S(2)}) copy-start(f32[128,768]{1,0:T(8,128)S(1)} %get-tuple-element.133) | copy-start | bytes 1179652
  658.4 14.2 %all-to-all-start.21 = ((bf16[16,6,768]{2,1,0:T(8,128)(2,1)}), bf16[16,6,768]{2,1,0:T(8,128)(2,1)S(1)}, u32[]{:S(2)}, u32[]{:S(2)}) async-start(bf16[16,6,768]{2,1,0:T(8,128)(2,1)} %reshape.768), calls=%async_computation.23 | async-start | bytes 393216 | tf_op jit(solution)/shard_map/all_to_all | solution.py:39
  673.3 24.8 %all-to-all-start.17 = ((bf16[8,128,768]{2,1,0:T(8,128)(2,1)}), bf16[8,128,768]{2,1,0:T(8,128)(2,1)S(1)}, u32[]{:S(2)}, u32[]{:S(2)}) async-start(bf16[8,128,768]{2,1,0:T(8,128)(2,1)} %concatenate.144), calls=%async_computation.17 | async-start | bytes 3145728 | tf_op jit(solution)/shard_map/all_to_all | solution.py:39
  676.9 30.1 %copy-start.84 = (bf16[16,6,768]{2,1,0:T(8,128)(2,1)S(1)}, bf16[16,6,768]{2,1,0:T(8,128)(2,1)}, u32[]{:S(2)}) copy-start(bf16[16,6,768]{2,1,0:T(8,128)(2,1)} %copy-done.83) | copy-start | bytes 442372
  698.1 16.2 %all-to-all-start.18 = ((bf16[16,6,768]{2,1,0:T(8,128)(2,1)}), bf16[16,6,768]{2,1,0:T(8,128)(2,1)}, u32[]{:S(2)}, u32[]{:S(2)}) async-start(bf16[16,6,768]{2,1,0:T(8,128)(2,1)} %reshape.761), calls=%async_computation.19 | async-start | bytes 393216 | tf_op jit(solution)/shard_map/all_to_all | solution.py:39
  715.6 26.5 %all-to-all-start.22 = ((bf16[8,128,768]{2,1,0:T(8,128)(2,1)}), bf16[8,128,768]{2,1,0:T(8,128)(2,1)S(1)}, u32[]{:S(2)}, u32[]{:S(2)}) async-start(bf16[8,128,768]{2,1,0:T(8,128)(2,1)} %broadcast_in_dim.56), calls=%async_computation.24 | async-start | bytes 3145728 | tf_op jit(solution)/shard_map/all_to_all | solution.py:39
  743.5 28.5 %copy-start.151 = (f32[128]{0:T(128)S(1)}, f32[128]{0:T(128)}, u32[]{:S(2)}) copy-start(f32[128]{0:T(128)} %get-tuple-element.46) | copy-start | bytes 1540
  743.5 28.5 %copy-start.41 = (f32[128,768]{1,0:T(8,128)S(1)}, f32[128,768]{1,0:T(8,128)}, u32[]{:S(2)}) copy-start(f32[128,768]{1,0:T(8,128)} %copy-done.40) | copy-start | bytes 1179652
  743.5 28.5 %copy-start.43 = (f32[128,768]{1,0:T(8,128)S(1)}, f32[128,768]{1,0:T(8,128)}, u32[]{:S(2)}) copy-start(f32[128,768]{1,0:T(8,128)} %copy-done.42) | copy-start | bytes 1179652
  743.5 28.5 %copy-start.69 = (f32[128,768]{1,0:T(8,128)S(1)}, f32[128,768]{1,0:T(8,128)}, u32[]{:S(2)}) copy-start(f32[128,768]{1,0:T(8,128)} %copy-done.68) | copy-start | bytes 1179652
  743.5 28.5 %copy-start.108 = (f32[128]{0:T(128)S(1)}, f32[128]{0:T(128)}, u32[]{:S(2)}) copy-start(f32[128]{0:T(128)} %copy-done.106) | copy-start | bytes 1540
  743.5 28.5 %copy-start.124 = (f32[128]{0:T(128)S(1)}, f32[128]{0:T(128)}, u32[]{:S(2)}) copy-start(f32[128]{0:T(128)} %copy-done.122) | copy-start | bytes 1540
  743.5 28.5 %copy-start.132 = (f32[128]{0:T(128)S(1)}, f32[128]{0:T(128)}, u32[]{:S(2)}) copy-start(f32[128]{0:T(128)} %copy-done.131) | copy-start | bytes 1540
  743.5 28.5 %copy-start.136 = (f32[128]{0:T(128)S(1)}, f32[128]{0:T(128)}, u32[]{:S(2)}) copy-start(f32[128]{0:T(128)} %copy-done.135) | copy-start | bytes 1540
  743.5 27.4 %all-to-all-start.19 = ((bf16[8,128,768]{2,1,0:T(8,128)(2,1)}), bf16[8,128,768]{2,1,0:T(8,128)(2,1)}, u32[]{:S(2)}, u32[]{:S(2)}) async-start(bf16[8,128,768]{2,1,0:T(8,128)(2,1)} %broadcast_in_dim.55), calls=%async_computation.20 | async-start | bytes 3145728 | tf_op jit(solution)/shard_map/all_to_all | solution.py:39
  748.0 24.9 %collective-permute-start.13 = (bf16[8,128,768]{2,1,0:T(8,128)(2,1)S(1)}, bf16[8,128,768]{2,1,0:T(8,128)(2,1)}, u32[]{:S(2)}, u32[]{:S(2)}) collective-permute-start(bf16[8,128,768]{2,1,0:T(8,128)(2,1)S(1)} %all-to-all-done.22), channel_id=1, source_target_pairs={{0,1},{1,0},{2,3},{3,2},{4,5},{5,4},{6,7},{7,6},{8,9},{9,8},{10,11... | collective-permute-start | bytes 4718600 | tf_op jit(solution)/shard_map/ppermute | solution.py:47
  770.9 28.5 %collective-permute-start.12 = (bf16[8,128,768]{2,1,0:T(8,128)(2,1)}, bf16[8,128,768]{2,1,0:T(8,128)(2,1)}, u32[]{:S(2)}, u32[]{:S(2)}) collective-permute-start(bf16[8,128,768]{2,1,0:T(8,128)(2,1)} %all-to-all-done.19), channel_id=1, source_target_pairs={{0,1},{1,0},{2,3},{3,2},{4,5},{5,4},{6,7},{7,6},{8,9},{9,8},{10,11... | collective-permute-start | bytes 4718600 | tf_op jit(solution)/shard_map/ppermute | solution.py:47
  (129 other events, 414.1 us)
Sparse Core Ops, SparseCore 0:
  47.3 48.0 all-gather.6
  243.3 80.0 all-gather.8
  531.7 31.6 reduce-scatter.4
  609.2 51.4 reduce-scatter.2

commit v2 on v1

v2 whole, which is shorter than its diff:
```python
import functools

import jax
import jax.numpy as jnp
from jax import lax
from jax.experimental import pallas as pl
from jax.experimental.pallas import tpu as pltpu
from jax.sharding import PartitionSpec as P

H = 12
HD = 64
D = 768
FF = 3072
LAYERS = 2
S = 8
C = 16
TOK = 128
LEN = TOK * C
BLK = TOK // 2
ROWS = 256
EPSILON = 1e-05
NEGATIVE = -1e30
F32 = jnp.float32
BF16 = jnp.bfloat16

CHIP_GROUPS = [[2 * q + core for q in range(8)] for core in range(2)]
X_GROUPS = [[8 * y + 2 * x + core for x in range(4)] for y in range(2) for core in range(2)]
SWAP = [(i, i ^ 1) for i in range(C)]


def layer_norm(states, gain, shift):
    average = jnp.mean(states, axis=-1, keepdims=True)
    centered = states - average
    spread = jnp.mean(centered * centered, axis=-1, keepdims=True)
    return centered * lax.rsqrt(spread + EPSILON) * gain + shift


def exchange(parts, axis, groups=None):
    return lax.all_to_all(parts, axis, 0, 0, tiled=True, axis_index_groups=groups)


def spread_to(part, count, axis, groups=None):
    return exchange(jnp.broadcast_to(part[None], (count,) + part.shape), axis, groups)


def swap_core(part):
    return lax.ppermute(part, "ctx", SWAP)


def gather_ctx(part):
    own = spread_to(part, 8, "ctx", CHIP_GROUPS)
    return own, swap_core(own)


def gather_x(part):
    own = spread_to(part, 4, "ctx", X_GROUPS)
    return jnp.concatenate([own, swap_core(own)], axis=0)


def scatter(near, far, groups):
    mine = near.astype(F32) + swap_core(far.astype(BF16)).astype(F32)
    parts = exchange(mine.astype(BF16), "ctx", groups)
    return jnp.sum(parts.astype(F32), axis=0)


def scatter_x(partial):
    return scatter(partial[:4], partial[4:], X_GROUPS)


def dot(left, right, dims=((1,), (0,))):
    return lax.dot_general(left, right, (dims, ((), ())), preferred_element_type=F32)


def rows_of(block):
    return pl.ds(pl.multiple_of(block * BLK, BLK), BLK)


def attend_kernel(fresh, arrive_pos, ctx_pos, own_ref, other_ref, weight_ref, shift_ref, *rest):
    if fresh:
        gain_ref, bias_ref, mixed_ref, q_ref, k_ref, v_ref, own_normed, other_normed, out_ref = rest
    else:
        mixed_ref, q_ref, k_ref, v_ref, out_ref = rest
    for step in range(LEN // ROWS):
        half = LEN // ROWS // 2
        source = own_ref if step < half else other_ref
        rows = slice(step % half * ROWS, (step % half + 1) * ROWS)
        normed = source[rows, :]
        if fresh:
            normed = layer_norm(normed.astype(F32), gain_ref[...], bias_ref[...]).astype(BF16)
            (own_normed if step < half else other_normed)[rows, :] = normed
        piece = dot(normed, weight_ref[...]) + shift_ref[...]
        for part in range(ROWS // BLK):
            rows = rows_of(arrive_pos[step * (ROWS // BLK) + part])
            block = piece[part * BLK : (part + 1) * BLK, :]
            q_ref[rows, :] = (block[:, :HD].astype(BF16).astype(F32) * 0.125).astype(BF16)
            k_ref[rows, :] = block[:, HD : 2 * HD].astype(BF16)
            v_ref[rows, :] = block[:, 2 * HD :].astype(BF16)
    keep = lax.broadcasted_iota(jnp.int32, (ROWS, ROWS), 0) >= lax.broadcasted_iota(
        jnp.int32, (ROWS, ROWS), 1
    )
    for step in range(LEN // ROWS):
        start = step * ROWS
        queries = q_ref[start : start + ROWS, :]
        near = dot(queries, k_ref[start : start + ROWS, :], ((1,), (1,)))
        near = jnp.where(keep, near, NEGATIVE)
        highest = jnp.max(near, axis=1, keepdims=True)
        if step:
            far = dot(queries, k_ref[:start, :], ((1,), (1,)))
            highest = jnp.maximum(highest, jnp.max(far, axis=1, keepdims=True))
        weights = jnp.exp(near - highest)
        total = jnp.sum(weights, axis=1, keepdims=True)
        mixed = dot(weights.astype(BF16), v_ref[start : start + ROWS, :])
        if step:
            weights = jnp.exp(far - highest)
            total = total + jnp.sum(weights, axis=1, keepdims=True)
            mixed = mixed + dot(weights.astype(BF16), v_ref[:start, :])
        out_ref[start : start + ROWS, :] = (mixed / total).astype(BF16)
    for block in range(LEN // BLK):
        mixed_ref[block * BLK : (block + 1) * BLK, :] = out_ref[rows_of(ctx_pos[block]), :]


def attend_back_kernel(
    arrive_pos, ctx_pos, q_ref, k_ref, v_ref, grad_ref, weight_ref,
    to_arrive_ref, near_ref, far_ref, sums_ref, do_ref, dk_ref, dv_ref, all_ref
):
    for block in range(LEN // BLK):
        do_ref[rows_of(ctx_pos[block]), :] = grad_ref[block * BLK : (block + 1) * BLK, :]
    keep = lax.broadcasted_iota(jnp.int32, (ROWS, ROWS), 0) <= lax.broadcasted_iota(
        jnp.int32, (ROWS, ROWS), 1
    )
    for step in range(LEN // ROWS - 1, -1, -1):
        start = step * ROWS
        end = start + ROWS
        queries = q_ref[start:end, :]
        grads = do_ref[start:end, :]
        near_keys, near_values = k_ref[start:end, :], v_ref[start:end, :]
        near = jnp.where(keep, dot(near_keys, queries, ((1,), (1,))), NEGATIVE)
        highest = jnp.max(near, axis=0, keepdims=True)
        if step:
            far_keys, far_values = k_ref[:start, :], v_ref[:start, :]
            far = dot(far_keys, queries, ((1,), (1,)))
            highest = jnp.maximum(highest, jnp.max(far, axis=0, keepdims=True))
        near = jnp.exp(near - highest)
        total = jnp.sum(near, axis=0, keepdims=True)
        if step:
            far = jnp.exp(far - highest)
            total = total + jnp.sum(far, axis=0, keepdims=True)
        inverse = 1.0 / total
        near = near * inverse
        near_grad = dot(near_values, grads, ((1,), (1,)))
        inner = jnp.sum(near * near_grad, axis=0, keepdims=True)
        if step:
            far = far * inverse
            far_grad = dot(far_values, grads, ((1,), (1,)))
            inner = inner + jnp.sum(far * far_grad, axis=0, keepdims=True)
        near_scores = (near * (near_grad - inner)).astype(BF16)
        near_dk = dot(near_scores, queries)
        near_dv = dot(near.astype(BF16), grads)
        query_grad = dot(near_scores, near_keys, ((0,), (0,)))
        if step == LEN // ROWS - 1:
            dk_ref[start:end, :] = near_dk
            dv_ref[start:end, :] = near_dv
        else:
            dk_ref[start:end, :] += near_dk
            dv_ref[start:end, :] += near_dv
        if step:
            far_scores = (far * (far_grad - inner)).astype(BF16)
            far_dk = dot(far_scores, queries)
            far_dv = dot(far.astype(BF16), grads)
            query_grad = query_grad + dot(far_scores, far_keys, ((0,), (0,)))
            if step == LEN // ROWS - 1:
                dk_ref[:start, :] = far_dk
                dv_ref[:start, :] = far_dv
            else:
                dk_ref[:start, :] += far_dk
                dv_ref[:start, :] += far_dv
        all_ref[start:end, :] = jnp.concatenate(
            [query_grad * 0.125, dk_ref[start:end, :], dv_ref[start:end, :]], axis=1
        ).astype(BF16)
    for block in range(LEN // BLK):
        to_arrive_ref[block * BLK : (block + 1) * BLK, : 3 * HD] = all_ref[rows_of(arrive_pos[block]), :]
    to_arrive_ref[:, 3 * HD :] = jnp.zeros((LEN, HD), BF16)
    sums_ref[...] = jnp.sum(all_ref[...].astype(F32), axis=0, keepdims=True)
    for step in range(LEN // ROWS):
        rows = slice(step * ROWS, (step + 1) * ROWS)
        part = dot(to_arrive_ref[rows, : 3 * HD], weight_ref[...], ((1,), (1,))).astype(BF16)
        if step * ROWS < LEN // 2:
            near_ref[rows, :] = part
        else:
            far_ref[step * ROWS - LEN // 2 : (step + 1) * ROWS - LEN // 2, :] = part


SMEM = pl.BlockSpec(memory_space=pltpu.SMEM)
VMEM = pl.BlockSpec(memory_space=pltpu.VMEM)
VMEM_BYTES = 48 * 2**20


def attend(arrive_pos, ctx_pos, own, other, weight, shift, norm=None):
    head = jax.ShapeDtypeStruct((LEN, HD), BF16)
    fresh = norm is not None
    outs = (head,) * 4
    extra = ()
    if fresh:
        outs = outs + (jax.ShapeDtypeStruct((LEN // 2, D), BF16),) * 2
        extra = tuple(member.reshape(1, D) for member in norm)
    return pl.pallas_call(
        functools.partial(attend_kernel, fresh),
        out_shape=outs,
        in_specs=[SMEM, SMEM] + [VMEM] * (4 + len(extra)),
        out_specs=(VMEM,) * len(outs),
        scratch_shapes=[pltpu.VMEM((LEN, HD), BF16)],
        compiler_params=pltpu.CompilerParams(vmem_limit_bytes=VMEM_BYTES),
        cost_estimate=pl.CostEstimate(flops=2 * 10**9, bytes_accessed=5 * 10**6, transcendentals=2 * 10**6),
    )(arrive_pos, ctx_pos, own, other, weight, shift, *extra)


def attend_back(arrive_pos, ctx_pos, queries, keys, values, grads, weight):
    return pl.pallas_call(
        attend_back_kernel,
        out_shape=(
            jax.ShapeDtypeStruct((LEN, 4 * HD), BF16),
            jax.ShapeDtypeStruct((LEN // 2, D), BF16),
            jax.ShapeDtypeStruct((LEN // 2, D), BF16),
            jax.ShapeDtypeStruct((1, 3 * HD), F32),
        ),
        in_specs=[SMEM, SMEM] + [VMEM] * 5,
        out_specs=(VMEM,) * 4,
        scratch_shapes=[
            pltpu.VMEM((LEN, HD), BF16),
            pltpu.VMEM((LEN, HD), F32),
            pltpu.VMEM((LEN, HD), F32),
            pltpu.VMEM((LEN, 3 * HD), BF16),
        ],
        compiler_params=pltpu.CompilerParams(vmem_limit_bytes=VMEM_BYTES),
        cost_estimate=pl.CostEstimate(flops=4 * 10**9, bytes_accessed=5 * 10**6, transcendentals=2 * 10**6),
    )(arrive_pos, ctx_pos, queries, keys, values, grads, weight)


HEADS, UPS, DOWNS, SMALL, OUTS, PACKED = 0, 32, 80, 128, 144, 240


def weight_grads_kernel(
    own_ref, other_ref, arrive_ref, second_ref, hidden_ref, active_ref, down_ref, mixed_ref, attended_ref, small_ref, out_ref
):
    both = ((0,), (0,))
    half = LEN // 2
    heads = dot(own_ref[...], arrive_ref[:half, :], both) + dot(other_ref[...], arrive_ref[half:, :], both)
    heads = heads.astype(BF16)
    for owner in range(S):
        for part in range(3):
            first = owner * 96 + part * 32
            out_ref[owner, HEADS:UPS, part * 256 : (part + 1) * 256] = heads[first : first + 32, :]
    ups = dot(second_ref[...], hidden_ref[...], both).astype(BF16)
    for owner in range(S):
        for part in range(2):
            first = owner * 96 + part * 48
            out_ref[owner, UPS:DOWNS, part * 384 : (part + 1) * 384] = ups[first : first + 48, :]
    downs = dot(active_ref[...], down_ref[...], both).astype(BF16)
    for owner in range(S):
        out_ref[owner, DOWNS:SMALL, :] = downs[owner * 48 : (owner + 1) * 48, :]
        out_ref[owner, SMALL:OUTS, :] = small_ref[owner]
    outs = dot(mixed_ref[...], attended_ref[...], both).astype(BF16)
    for owner in range(S):
        out_ref[owner, OUTS:PACKED, :] = outs[owner * 96 : (owner + 1) * 96, :]


def weight_grads(*parts):
    return pl.pallas_call(
        weight_grads_kernel,
        out_shape=jax.ShapeDtypeStruct((S, PACKED, D), BF16),
        in_specs=[VMEM] * len(parts),
        out_specs=VMEM,
        compiler_params=pltpu.CompilerParams(vmem_limit_bytes=VMEM_BYTES),
        cost_estimate=pl.CostEstimate(flops=2 * 10**9, bytes_accessed=12 * 10**6, transcendentals=0),
    )(*parts)


def unpack_kernel(slots, first_ref, second_ref, qkv_ref, out_ref, up_ref, down_ref, up_shift_ref, *vector_refs):
    for layer, source in enumerate((first_ref, second_ref)):
        def slot(place, layer=layer):
            return slots[layer * C + place]

        for head in range(H):
            block = source[slot(head), HEADS:UPS, :].astype(F32)
            for part in range(3):
                for kind in range(3):
                    lane = part * 256 + kind * HD
                    column = kind * D + head * HD
                    qkv_ref[layer, part * 32 : (part + 1) * 32, column : column + HD] = block[:, lane : lane + HD]
        for rank in range(8):
            low, high = slot(rank), slot(rank + 8)
            block = source[low, UPS:DOWNS, :].astype(F32) + source[high, UPS:DOWNS, :].astype(F32)
            for part in range(2):
                for owner in range(S):
                    lane = part * 384 + owner * 48
                    column = owner * 384 + rank * 48
                    up_ref[layer, part * 48 : (part + 1) * 48, column : column + 48] = block[:, lane : lane + 48]
            block = source[low, DOWNS:SMALL, :].astype(F32) + source[high, DOWNS:SMALL, :].astype(F32)
            down_ref[layer, rank * 48 : (rank + 1) * 48, :] = block
            small = source[low, SMALL:OUTS, :].astype(F32) + source[high, SMALL:OUTS, :].astype(F32)
            up_shift_ref[layer : layer + 1, rank * 48 : (rank + 1) * 48] = small[1:2, :48]
            vectors = small[0:1, :] if rank == 0 else vectors + small[0:1, :]
        for member, ref in enumerate(vector_refs):
            ref[layer : layer + 1, :] = vectors[:, member * 96 : (member + 1) * 96]
    for place in range(C):
        small = first_ref[slots[place], SMALL:OUTS, :].astype(F32)
        for layer in range(LAYERS):
            out_ref[layer, place * 6 : (place + 1) * 6, :] = small[2 + 6 * layer : 8 + 6 * layer, :]


def unpack(slots, first, second):
    shapes = [(96, 3 * D), (96, D), (96, FF), (384, D), (384,)] + [(96,)] * 8
    return pl.pallas_call(
        unpack_kernel,
        out_shape=tuple(jax.ShapeDtypeStruct((LAYERS,) + shape, F32) for shape in shapes),
        in_specs=[SMEM, VMEM, VMEM],
        out_specs=(VMEM,) * len(shapes),
        compiler_params=pltpu.CompilerParams(vmem_limit_bytes=VMEM_BYTES),
        cost_estimate=pl.CostEstimate(flops=10**6, bytes_accessed=14 * 10**6, transcendentals=0),
    )(slots, first, second)


def join_cores(core, own, other, axis):
    return jnp.where(
        core == 0, jnp.concatenate([own, other], axis=axis), jnp.concatenate([other, own], axis=axis)
    )


def forward_layer(flowing, params, small, places, gathered=None, carried=None):
    arrive_pos, ctx_pos = places
    head_weight, out_full, up_part, down_part = params
    head_shift, vectors, up_shift = small
    gain_one, bias_one, unused, unused, out_shift, gain_two, bias_two, down_shift = vectors
    if gathered is not None:
        mixed_head, queries, keys, values, own, other = attend(
            arrive_pos, ctx_pos, *gathered, head_weight, head_shift, (gain_one, bias_one)
        )
    else:
        normed = layer_norm(flowing, gain_one, bias_one).astype(BF16)
        own, other = (part.reshape(LEN // 2, D) for part in gather_ctx(normed))
        mixed_head, queries, keys, values = attend(arrive_pos, ctx_pos, own, other, head_weight, head_shift)
    mixed = exchange(mixed_head.reshape(C, TOK, HD), "ctx")[:H]
    mixed = mixed.transpose(1, 0, 2).reshape(TOK, D)
    middle = flowing + dot(mixed, out_full) + out_shift
    second = layer_norm(middle, gain_two, bias_two).astype(BF16)
    if carried is not None:
        both = gather_x(jnp.concatenate([second, carried], axis=0))
        second_all = both[:, :TOK].reshape(8 * TOK, D)
        carried = both[:, TOK:].reshape(8 * TOK, D)
    else:
        second_all = gather_x(second).reshape(8 * TOK, D)
    hidden = dot(second_all, up_part) + up_shift
    activated = jax.nn.gelu(hidden, approximate=True).astype(BF16)
    partial = dot(activated, down_part).reshape(8, TOK, D)
    output = middle + scatter_x(partial) + down_shift
    saved = (flowing, own, other, queries, keys, values, mixed, middle, second_all, hidden, activated)
    return output, saved, carried


def backward_layer(grad_out, down_all, saved, params, small, places, head, running=None):
    arrive_pos, ctx_pos = places
    head_weight, out_full, up_part, down_part = params
    unused, vectors, unused = small
    gain_one, bias_one, unused, unused, unused, gain_two, bias_two, unused = vectors
    flowing, own, other, queries, keys, values, mixed, middle, second_all, hidden, activated = saved
    down_in = grad_out.astype(BF16)
    down_shift_grad = jnp.sum(down_in.astype(F32), axis=0)
    if down_all is None:
        down_all = gather_x(down_in).reshape(8 * TOK, D)
    activated_grad = dot(down_all, down_part, ((1,), (1,)))
    unused, gelu_back = jax.vjp(lambda inner: jax.nn.gelu(inner, approximate=True), hidden)
    hidden_grad = gelu_back(activated_grad)[0].astype(BF16)
    second_grad = scatter_x(dot(hidden_grad, up_part, ((1,), (1,))).reshape(8, TOK, D))
    up_shift_grad = jnp.sum(hidden_grad.astype(F32), axis=0)
    unused, norm_back = jax.vjp(layer_norm, middle, gain_two, bias_two)
    middle_part, gain_two_grad, bias_two_grad = norm_back(second_grad)
    middle_grad = grad_out + middle_part
    attended_in = middle_grad.astype(BF16)
    out_shift_grad = jnp.sum(attended_in.astype(F32), axis=0)
    mixed_grad = dot(attended_in, out_full, ((1,), (1,))).astype(BF16)
    mixed_grad = mixed_grad.reshape(TOK, H, HD).transpose(1, 0, 2)
    mixed_grad = jnp.concatenate([mixed_grad, jnp.zeros((C - H, TOK, HD), BF16)], axis=0)
    mixed_grad = exchange(mixed_grad, "ctx").reshape(LEN, HD)
    if running is not None:
        mixed_grad, running = lax.optimization_barrier((mixed_grad, running))
    to_arrive, near, far, sums = attend_back(
        arrive_pos, ctx_pos, queries, keys, values, mixed_grad, head_weight
    )
    normed_grad = scatter(near.reshape(8, TOK, D), far.reshape(8, TOK, D), CHIP_GROUPS)
    sums = jnp.where(lax.axis_index("ctx") < H, sums[0], 0.0)
    query_shift_grad = lax.dynamic_update_slice_in_dim(jnp.zeros((D,), F32), sums[:HD], head * HD, 0)
    value_shift_grad = lax.dynamic_update_slice_in_dim(jnp.zeros((D,), F32), sums[2 * HD :], head * HD, 0)
    unused, first_back = jax.vjp(layer_norm, flowing, gain_one, bias_one)
    flowing_part, gain_one_grad, bias_one_grad = first_back(normed_grad)
    shifts = (
        gain_one_grad,
        bias_one_grad,
        query_shift_grad,
        value_shift_grad,
        out_shift_grad,
        gain_two_grad,
        bias_two_grad,
        down_shift_grad,
    )
    vectors = jnp.stack(shifts).reshape(8, S, 96).transpose(1, 0, 2).reshape(S, 1, D)
    hiddens = jnp.pad(up_shift_grad.reshape(S, 1, 48), ((0, 0), (0, 0), (0, D - 48)))
    rest = jnp.concatenate([vectors, hiddens, jnp.zeros((S, 14, D), F32)], axis=1).astype(BF16)
    packed = weight_grads(
        own, other, to_arrive, second_all, hidden_grad, activated, down_all, mixed, attended_in, rest
    )
    return middle_grad + flowing_part, packed, running


def shards(
    states,
    cotangent,
    pair_order,
    norm1_gain,
    norm1_bias,
    qkv_weight,
    query_bias,
    value_bias,
    out_weight,
    out_bias,
    norm2_gain,
    norm2_bias,
    up_weight,
    up_bias,
    down_weight,
    down_bias,
):
    place = lax.axis_index("ctx")
    core = place % 2
    rank = place % 8
    head = jnp.minimum(place, H - 1)
    pairs = jnp.stack([pair_order, 2 * C - 1 - pair_order], axis=1)
    ctx_pos = pairs.reshape(-1)
    by_core = pairs.reshape(8, 2, 2).transpose(1, 0, 2)
    arrive_pos = jnp.where(core == 0, by_core, by_core[::-1]).reshape(-1)
    places = (arrive_pos, ctx_pos)

    states_all = tuple(part.reshape(LEN // 2, D) for part in gather_ctx(states.reshape(TOK, D)))

    unit = lax.broadcasted_iota(jnp.int32, (FF, 384), 0)
    column = lax.broadcasted_iota(jnp.int32, (FF, 384), 1)
    pick = (unit == (column // 48) * 384 + rank * 48 + column % 48).astype(BF16)
    up_piece = dot(up_weight.reshape(LAYERS * 96, FF), pick).astype(BF16).reshape(LAYERS, 96, 384)
    down_piece = lax.dynamic_slice_in_dim(down_weight, rank * 48, 48, axis=1)
    out_piece = lax.dynamic_slice_in_dim(out_weight, core * 384, 384, axis=2)

    def beside(piece):
        return jnp.concatenate([piece[:48], piece[48:]], axis=1)

    def apart(piece):
        return jnp.concatenate([piece[..., :384], piece[..., 384:]], axis=1).reshape(D, 384)

    def split(rows):
        own = apart(rows[:, :48])
        out_full = join_cores(core, own, swap_core(own), 1)
        return out_full, apart(rows[:, 48:96]), rows[:, 96:].reshape(384, D)

    layer_pieces = [
        jnp.concatenate([beside(out_piece[layer]), beside(up_piece[layer]), down_piece[layer]], axis=0)
        for layer in range(LAYERS)
    ]

    vectors = jnp.stack(
        [norm1_gain, norm1_bias, query_bias, value_bias, out_bias, norm2_gain, norm2_bias, down_bias]
    )
    head_piece = lax.dynamic_slice_in_dim(qkv_weight.reshape(LAYERS, 96, 3, D), head * HD, HD, axis=3)
    head_piece = jnp.where(place < H, head_piece, jnp.zeros_like(head_piece))
    packed = jnp.concatenate(
        [
            head_piece.reshape(LAYERS * 96 * 3 * HD // D, D),
            vectors.reshape(2, D),
            up_bias.reshape(1, D),
            jnp.zeros((13, D), BF16),
            layer_pieces[0],
            layer_pieces[1],
        ],
        axis=0,
    )
    gathered = spread_to(packed, S, "shard")
    layer_weights = [split(gathered[:, 64:208]), split(gathered[:, 208:])]
    head_weights = gathered[:, :48].reshape(S, LAYERS, 96, 3 * HD)
    vectors = gathered[:, 48:50].reshape(S, 8, LAYERS, 96).transpose(2, 1, 0, 3).reshape(LAYERS, 8, D)
    vectors = vectors.astype(F32)
    up_shifts = gathered[:, 50].reshape(S, LAYERS, 8, 48)
    up_shifts = lax.dynamic_index_in_dim(up_shifts, rank, 2, False).transpose(1, 0, 2).reshape(LAYERS, 1, 384)
    up_shifts = up_shifts.astype(F32)
    head_shifts = jnp.concatenate(
        [
            lax.dynamic_slice_in_dim(vectors[:, 2], head * HD, HD, axis=1),
            jnp.zeros((LAYERS, HD), F32),
            lax.dynamic_slice_in_dim(vectors[:, 3], head * HD, HD, axis=1),
        ],
        axis=1,
    ).reshape(LAYERS, 1, 3 * HD)

    flowing = states.reshape(TOK, D).astype(F32)
    saved_all = []
    smalls = []
    all_params = []
    for layer in range(LAYERS):
        small = (
            head_shifts[layer],
            [vectors[layer, member : member + 1] for member in range(8)],
            up_shifts[layer],
        )
        small = (small[0], [member.reshape(D) for member in small[1]], small[2])
        smalls.append(small)
        params = (head_weights[:, layer].reshape(D, 3 * HD),) + layer_weights[layer]
        all_params.append(params)
        flowing, saved, carried = forward_layer(
            flowing,
            params,
            small,
            places,
            gathered=states_all if layer == 0 else None,
            carried=cotangent.reshape(TOK, D) if layer == LAYERS - 1 else None,
        )
        saved_all.append(saved)
    result = flowing.astype(BF16).reshape(states.shape)
    grad_flow = cotangent.reshape(TOK, D).astype(F32)
    grad_flow, packed, unused = backward_layer(
        grad_flow, carried, saved_all[1], all_params[1], smalls[1], places, head
    )
    grad_flow, packed = lax.optimization_barrier((grad_flow, packed))
    owned_last = lax.psum_scatter(packed.reshape(S * PACKED, D), "shard", scatter_dimension=0, tiled=True)
    grad_flow, packed, owned_last = backward_layer(
        grad_flow, None, saved_all[0], all_params[0], smalls[0], places, head, owned_last
    )
    every_last = lax.all_gather(owned_last[:OUTS], "ctx", axis=0)
    owned = jnp.sum(exchange(packed, "shard").astype(F32), axis=0).astype(BF16)
    outs = jnp.stack([owned[OUTS:], owned_last[OUTS:]]).reshape(LAYERS, C, 6, D)
    outs = outs.transpose(1, 0, 2, 3).reshape(C, 12, D)
    outs = exchange(jnp.pad(outs, ((0, 0), (0, 4), (0, 0))), "ctx").astype(F32)
    outs = jnp.sum(outs, axis=0)[:12].astype(BF16)
    owned = jnp.concatenate([owned[: SMALL + 2], outs, jnp.zeros((2, D), BF16)], axis=0)
    every = jnp.concatenate(gather_ctx(owned), axis=0)
    places_of = jnp.arange(C, dtype=jnp.int32)
    slots = jnp.concatenate([places_of // 2 + 8 * (places_of % 2 != core).astype(jnp.int32), places_of])
    qkv, outs, ups, downs, hiddens, *vectors = unpack(slots, every, every_last)
    return (
        result,
        grad_flow.astype(BF16).reshape(states.shape),
        vectors[0],
        vectors[1],
        qkv,
        vectors[2],
        vectors[3],
        outs,
        vectors[4],
        vectors[5],
        vectors[6],
        ups,
        hiddens,
        downs,
        vectors[7],
    )


def solution(mesh):
    matrix = P(None, "shard", None)
    vector = P(None, "shard")
    rows = P("shard", "ctx", None)
    params = (
        vector,
        vector,
        matrix,
        vector,
        vector,
        matrix,
        vector,
        vector,
        vector,
        matrix,
        vector,
        matrix,
        vector,
    )
    return jax.shard_map(
        shards,
        mesh=mesh,
        in_specs=(rows, rows, P()) + params,
        out_specs=(rows, rows) + params,
        check_vma=False,
    )
```

time: 848 us -> 668 us (0.79)
  local copies, waits for them, and re-layouts: 161 us -> 83.2 us
  starting transfers between devices: 127 us -> 57.2 us
  Pallas kernels: 35.7 us -> 63.9 us
  matrix products: 50.5 us -> 23 us
  other arithmetic: 66.9 us -> 46.4 us
  waiting for transfers between devices: 205 us -> 185 us
  blocking collectives: 174 us -> 186 us
    all_to_all x4 -> x11, blocking collectives: 65 us -> 186 us  [exchange(): lax.all_to_all(parts, axis, 0, 0, tiled=True, axis_index_groups=groups)]
    all_gather x4 -> x0, blocking collectives: 109 us -> none  [the longest x2 58.3 us: shards(): lax.all_gather(down_piece[layer], 'shard', axis=0, tiled=True)]
    all_to_all x19 -> x8, starting transfers between devices: 91.5 us -> 40.8 us  [exchange(): lax.all_to_all(parts, axis, 0, 0, tiled=True, axis_index_groups=groups)]
    all_to_all x19 -> x8, waiting for transfers between devices: 200 us -> 156 us  [exchange(): lax.all_to_all(parts, axis, 0, 0, tiled=True, axis_index_groups=groups)]
    pallas_call x4 -> x7, Pallas kernels: 35.7 us -> 63.9 us  [the longest x2 27.3 us: attend_back(): pl.pallas_call(attend_back_kernel, out_shape=(jax.ShapeDtypeStruct((LEN,...]
    dot_general x23 -> x13, matrix products: 50.5 us -> 23 us  [dot(): lax.dot_general(left, right, (dims, ((), ())), preferred_element_type=F32)]
    ppermute x14, starting transfers between devices: 35.2 us -> 16.3 us  [swap_core(): return lax.ppermute(part, 'ctx', SWAP)]
    slice x27 -> x21, local copies, waits for them, and re-layouts: 24.7 us -> 9.88 us  [the longest x9 2.89 us: scatter_x(): return scatter(partial[:4], partial[4:], X_GROUPS)]
  transfers between devices with their start and end apart: 37 -> 24, of which waited for: 20 -> 18; matrix products, arithmetic and copies ran while one was open for 23% -> 9% of each run, Pallas kernels for 4% -> 2%
where the time goes in v2:
time: 668 us; the launch traced here: 661 us
  blocking collectives  186 us (28%)
  waiting for transfers between devices  185 us (28%)
  local copies, waits for them, and re-layouts  83.2 us (12%)
  Pallas kernels  63.9 us (10%)
  starting transfers between devices  57.2 us (9%)
  other arithmetic  46.4 us (7%)
  matrix products  23 us (3%)
  between operations  16 us (2%)
    all_to_all x11, blocking collectives, exchange(): lax.all_to_all(parts, axis, 0, 0, tiled=True, axis_index_groups=groups)  186 us
    all_to_all x8, waiting for transfers between devices, exchange(): lax.all_to_all(parts, axis, 0, 0, tiled=True, axis_index_groups=groups)  156 us
    all_to_all x8, starting transfers between devices, exchange(): lax.all_to_all(parts, axis, 0, 0, tiled=True, axis_index_groups=groups)  40.8 us
    unnamed x240, local copies, waits for them, and re-layouts  34.4 us
    pallas_call x2, Pallas kernels, attend_back(): pl.pallas_call(attend_back_kernel, out_shape=(jax.ShapeDtypeStruct((LEN,...  27.3 us
    dot_general x13, matrix products, dot(): lax.dot_general(left, right, (dims, ((), ())), preferred_element_type=F32)  23 us
    ppermute x14, waiting for transfers between devices, swap_core(): return lax.ppermute(part, 'ctx', SWAP)  18.4 us
    ppermute x14, starting transfers between devices, swap_core(): return lax.ppermute(part, 'ctx', SWAP)  16.3 us
  transfers between devices with their start and end apart: 24, of which 18 were waited for; matrix products, arithmetic and copies ran while one was open for 9% of the time, Pallas kernels for 2%

profile of v2, /device:TPU:1, one launch (start us, length us, event | category | flops | bytes accessed | tf_op | source)
XLA Modules:
  0.0 660.9 jit_solution(16733302484473791482)
XLA Ops:
  7.2 2.3 broadcast_in_dim.43
  9.5 7.6 %all-to-all-start = ((bf16[8,128,768]{2,1,0:T(8,128)(2,1)}), bf16[8,128,768]{2,1,0:T(8,128)(2,1)}, u32[]{:S(2)}, u32[]{:S(2)}) async-start(bf16[8,128,768]{2,1,0:T(8,128)(2,1)} %broadcast_in_dim.43), calls=%async_computation | async-start | bytes 3145728 | tf_op jit(solution)/shard_map/all_to_all | solution.py:39
  20.7 19.4 %all-to-all-done = bf16[8,128,768]{2,1,0:T(8,128)(2,1)} async-done(((bf16[8,128,768]{2,1,0:T(8,128)(2,1)}), bf16[8,128,768]{2,1,0:T(8,128)(2,1)}, u32[]{:S(2)}, u32[]{:S(2)}) %all-to-all-start) | async-done | bytes 1572896 | tf_op jit(solution)/shard_map/all_to_all | solution.py:39
  40.1 2.3 broadcast_in_dim.46
  42.5 5.3 all-to-all-start.1
  49.7 47.9 %all-to-all-done.1 = bf16[8,352,768]{2,1,0:T(8,128)(2,1)} async-done(((bf16[8,352,768]{2,1,0:T(8,128)(2,1)}), bf16[8,352,768]{2,1,0:T(8,128)(2,1)}, u32[]{:S(2)}, u32[]{:S(2)}) %all-to-all-start.1) | async-done | bytes 4325408 | tf_op jit(solution)/shard_map/all_to_all | solution.py:39
  98.5 2.8 fusion.80
  102.5 2.3 collective-permute-start.1
  104.8 2.6 fusion.79
  109.2 9.5 %shard_map.271 = (bf16[2048,64]{1,0:T(8,128)(2,1)S(1)}, bf16[2048,64]{1,0:T(8,128)(2,1)S(1)}, bf16[2048,64]{1,0:T(8,128)(2,1)S(1)}, bf16[2048,64]{1,0:T(8,128)(2...) custom-call(s32[32]{0:T(128)S(1)} %reshape.445.arrive_pos, s32[32]{0:T(128)S(1)} %reshape.446.ctx_pos, ...), custom_call_target="tpu_custom_call" | custom-call | flops 2000000000 | bytes 5000000 | tf_op jit(solution)/shard_map/pallas_call | solution.py:206
  123.7 12.1 %all_to_all.95 = bf16[16,128,64]{1,2,0:T(8,128)(2,1)S(1)} all-to-all(bf16[16,128,64]{1,2,0:T(8,128)(2,1)S(1)} %copy.79), channel_id=1, replica_groups=mesh['shard'=8,'ctx'=16] {'ctx'}, dimensions={0} | all-to-all | bytes 524288 | tf_op jit(solution)/shard_map/all_to_all | solution.py:39
  135.8 2.2 fusion.88
  138.6 13.7 %all_to_all.96 = bf16[4,128,768]{2,1,0:T(8,128)(2,1)S(1)} all-to-all(bf16[4,128,768]{2,1,0:T(8,128)(2,1)S(1)} %broadcast_in_dim.48), channel_id=1, replica_groups={{0,2,4,6},{1,3,5,7},{8,10,12,14},{9,11,13,15},{16,18,20,22},{17,19,21,2..., dimensions={0} | all-to-all | bytes 1572864 | tf_op jit(solution)/shard_map/all_to_all | solution.py:39
  152.3 2.2 collective-permute-start.2
  157.9 2.4 multiply_convert_fusion.1
  163.9 14.5 %all_to_all.97 = bf16[4,128,768]{2,1,0:T(8,128)(2,1)S(1)} all-to-all(bf16[4,128,768]{2,1,0:T(8,128)(2,1)S(1)} %add_convert_fusion.3), channel_id=1, replica_groups={{0,2,4,6},{1,3,5,7},{8,10,12,14},{9,11,13,15},{16,18,20,22},{17,19,21,2..., dimensions={0} | all-to-all | bytes 1572864 | tf_op jit(solution)/shard_map/all_to_all | solution.py:39
  179.7 24.0 %all_to_all.98 = bf16[8,128,768]{2,1,0:T(8,128)(2,1)S(1)} all-to-all(bf16[8,128,768]{2,1,0:T(8,128)(2,1)S(1)} %broadcast_in_dim.49), channel_id=1, replica_groups={{0,2,4,6,8,10,12,14},{1,3,5,7,9,11,13,15},{16,18,20,22,24,26,28,30},{17..., dimensions={0} | all-to-all | bytes 3145728 | tf_op jit(solution)/shard_map/all_to_all | solution.py:39
  203.7 2.4 collective-permute-start.4
  207.1 2.1 collective-permute-done.4
  209.2 6.4 shard_map.272
  218.2 11.6 %all_to_all.99 = bf16[16,128,64]{1,2,0:T(8,128)(2,1)S(1)} all-to-all(bf16[16,128,64]{1,2,0:T(8,128)(2,1)S(1)} %copy.80), channel_id=1, replica_groups=mesh['shard'=8,'ctx'=16] {'ctx'}, dimensions={0} | all-to-all | bytes 524288 | tf_op jit(solution)/shard_map/all_to_all | solution.py:39
  229.9 2.3 fusion.89
  232.9 23.1 %all_to_all.100 = bf16[4,256,768]{2,1,0:T(8,128)(2,1)} all-to-all(bf16[4,256,768]{2,1,0:T(8,128)(2,1)S(1)} %broadcast_in_dim.50), channel_id=1, replica_groups={{0,2,4,6},{1,3,5,7},{8,10,12,14},{9,11,13,15},{16,18,20,22},{17,19,21,2..., dimensions={0} | all-to-all | bytes 3145728 | tf_op jit(solution)/shard_map/all_to_all | solution.py:39
  256.0 2.4 collective-permute-start.6
  265.2 2.4 fusion.74
  274.1 4.2 all-to-all-start.9
  279.7 2.2 add_convert_fusion.2
  281.9 8.4 %all-to-all-done.9 = bf16[4,128,768]{2,1,0:T(8,128)(2,1)} async-done(((bf16[4,128,768]{2,1,0:T(8,128)(2,1)}), bf16[4,128,768]{2,1,0:T(8,128)(2,1)}, u32[]{:S(2)}, u32[]{:S(2)}) %all-to-all-start.9) | async-done | bytes 786464 | tf_op jit(solution)/shard_map/all_to_all | solution.py:39
  290.4 4.2 all-to-all-start.8
  299.3 6.5 all-to-all-done.8
  307.1 1.8 fusion.77
  310.4 2.9 convolution_convert_fusion.1
  314.4 14.1 %all_to_all.101 = bf16[16,128,64]{1,2,0:T(8,128)(2,1)} all-to-all(bf16[16,128,64]{1,2,0:T(8,128)(2,1)S(1)} %concatenate.100), channel_id=1, replica_groups=mesh['shard'=8,'ctx'=16] {'ctx'}, dimensions={0} | all-to-all | bytes 524288 | tf_op jit(solution)/shard_map/all_to_all | solution.py:39
  328.5 2.0 copy.82
  335.6 13.6 %shard_map.273 = (bf16[2048,256]{1,0:T(8,128)(2,1)S(1)}, bf16[1024,768]{1,0:T(8,128)(2,1)S(1)}, bf16[1024,768]{1,0:T(8,128)(2,1)}, f32[1,192]{1,0:T(1,128)S(1)}) custom-call(s32[32]{0:T(128)S(1)} %reshape.445.arrive_pos, s32[32]{0:T(128)S(1)} %reshape.446.ctx_pos, bf16[2048,64]{1,0:T(8,128)(2,1)S(1)} %copy-done.23, bf16[2048,64]{1,0:T(8,128)(2,1)S(1)} %copy-done.25, ...), custom_call_target="tpu_custom_call" | custom-call | flops 4000000000 | bytes 5000000 | tf_op jit(solution)/shard_map/pallas_call | solution.py:218
  351.3 3.2 collective-permute-done.9
  356.1 4.4 all-to-all-start.11
  365.6 1.9 reduce.7
  377.6 6.0 all-to-all-done.11
  383.6 2.3 reduce.5
  392.6 2.0 fusion.76
  402.0 2.1 add_add_fusion.5
  406.3 6.7 %shard_map.274 = bf16[8,240,768]{2,1,0:T(8,128)(2,1)} custom-call(bf16[1024,768]{1,0:T(8,128)(2,1)S(1)} %bitcast.147, bf16[1024,768]{1,0:T(8,128)(2,1)} %bitcast.149, bf16[2048,256]{1,0:T(8,128)(2,1)S(1)} %copy-done.10, bf16[1024,768]{1,0:T(8,128)(2,1)} %bitcast.167, bf16[1024,384]{1,0:T(8,128)(2,1)S(1)} %copy-done.4, ...), custom_call_target="tpu_custom_call" | custom-call | flops 2000000000 | bytes 12000000 | tf_op jit(solution)/shard_map/pallas_call | solution.py:268
  414.6 13.8 %all_to_all.102 = bf16[4,128,768]{2,1,0:T(8,128)(2,1)S(1)} all-to-all(bf16[4,128,768]{2,1,0:T(8,128)(2,1)S(1)} %broadcast_in_dim.109), channel_id=1, replica_groups={{0,2,4,6},{1,3,5,7},{8,10,12,14},{9,11,13,15},{16,18,20,22},{17,19,21,2..., dimensions={0} | all-to-all | bytes 1572864 | tf_op jit(solution)/shard_map/all_to_all | solution.py:39
  430.3 1.9 collective-permute-done.10
  432.4 2.4 fusion.69
  438.5 14.7 %all_to_all.103 = bf16[4,128,768]{2,1,0:T(8,128)(2,1)S(1)} all-to-all(bf16[4,128,768]{2,1,0:T(8,128)(2,1)S(1)} %add_convert_fusion), channel_id=1, replica_groups={{0,2,4,6},{1,3,5,7},{8,10,12,14},{9,11,13,15},{16,18,20,22},{17,19,21,2..., dimensions={0} | all-to-all | bytes 1572864 | tf_op jit(solution)/shard_map/all_to_all | solution.py:39
  454.9 2.2 convolution_convert_fusion
  457.3 14.2 %all_to_all.104 = bf16[16,128,64]{1,2,0:T(8,128)(2,1)S(1)} all-to-all(bf16[16,128,64]{1,2,0:T(8,128)(2,1)S(1)} %concatenate.103), channel_id=1, replica_groups=mesh['shard'=8,'ctx'=16] {'ctx'}, dimensions={0} | all-to-all | bytes 524288 | tf_op jit(solution)/shard_map/all_to_all | solution.py:39
  471.7 10.6 %reduce-scatter.2.cloned.1.call-done = bf16[240,768]{1,0:T(8,128)(2,1)} async-done(((bf16[1920,768]{1,0:T(8,128)(2,1)}), bf16[240,768]{1,0:T(8,128)(2,1)}) %reduce-scatter.2.cloned.1.call-update) | async-done | bytes 368656 | tf_op jit(solution)/shard_map/reduce_scatter | solution.py:529
  486.5 13.6 %shard_map.275 = (bf16[2048,256]{1,0:T(8,128)(2,1)S(1)}, bf16[1024,768]{1,0:T(8,128)(2,1)S(1)}, bf16[1024,768]{1,0:T(8,128)(2,1)}, f32[1,192]{1,0:T(1,128)S(1)}) custom-call(s32[32]{0:T(128)S(1)} %reshape.445.arrive_pos, s32[32]{0:T(128)S(1)} %reshape.446.ctx_pos, bf16[2048,64]{1,0:T(8,128)(2,1)S(1)} %copy-done.17, bf16[2048,64]{1,0:T(8,128)(2,1)S(1)} %copy-done.19, ...), custom_call_target="tpu_custom_call" | custom-call | flops 4000000000 | bytes 5000000 | tf_op jit(solution)/shard_map/pallas_call | solution.py:218
  501.1 3.2 collective-permute-done.12
  506.0 6.2 all-to-all-start.15
  515.0 20.3 %all-to-all-done.15 = bf16[8,128,768]{2,1,0:T(8,128)(2,1)} async-done(((bf16[8,128,768]{2,1,0:T(8,128)(2,1)}), bf16[8,128,768]{2,1,0:T(8,128)(2,1)}, u32[]{:S(2)}, u32[]{:S(2)}) %all-to-all-start.15) | async-done | bytes 1572896 | tf_op jit(solution)/shard_map/all_to_all | solution.py:39
  542.2 6.7 %shard_map.276 = bf16[8,240,768]{2,1,0:T(8,128)(2,1)} custom-call(bf16[1024,768]{1,0:T(8,128)(2,1)S(1)} %copy-done.6, bf16[1024,768]{1,0:T(8,128)(2,1)} %copy-done.7, bf16[2048,256]{1,0:T(8,128)(2,1)S(1)} %get-tuple-element.69.arrive_ref, bf16[1024,768]{1,0:T(8,128)(2,1)} %bitcast.163, bf16[1024,384]{1,0:T(8,128)(2,1)S(1)} %get-tuple-element.113.hidden_ref, ...), custom_call_target="tpu_custom_call" | custom-call | flops 2000000000 | bytes 12000000 | tf_op jit(solution)/shard_map/pallas_call | solution.py:268
  549.0 3.8 all-to-all-start.16
  553.6 36.8 %all-to-all-done.16 = bf16[8,240,768]{2,1,0:T(8,128)(2,1)S(1)} async-done(((bf16[8,240,768]{2,1,0:T(8,128)(2,1)}), bf16[8,240,768]{2,1,0:T(8,128)(2,1)S(1)}, u32[]{:S(2)}, u32[]{:S(2)}) %all-to-all-start.16) | async-done | bytes 2949152 | tf_op jit(solution)/shard_map/all_to_all | solution.py:39
  592.1 5.0 all-to-all-start.17
  597.3 10.6 %all-to-all-done.17 = bf16[16,16,768]{2,1,0:T(8,128)(2,1)S(1)} async-done(((bf16[16,16,768]{2,1,0:T(8,128)(2,1)}), bf16[16,16,768]{2,1,0:T(8,128)(2,1)S(1)}, u32[]{:S(2)}, u32[]{:S(2)}) %all-to-all-start.17) | async-done | bytes 393248 | tf_op jit(solution)/shard_map/all_to_all | solution.py:39
  608.2 30.6 %all_to_all.105 = bf16[8,144,768]{2,1,0:T(8,128)(2,1)S(1)} all-to-all(bf16[8,144,768]{2,1,0:T(8,128)(2,1)S(1)} %broadcast_in_dim.115), channel_id=1, replica_groups={{0,2,4,6,8,10,12,14},{1,3,5,7,9,11,13,15},{16,18,20,22,24,26,28,30},{17..., dimensions={0} | all-to-all | bytes 3538944 | tf_op jit(solution)/shard_map/all_to_all | solution.py:39
  640.2 2.3 collective-permute-done.13
  642.5 2.1 pad_maximum_fusion.first_ref
  644.7 2.0 copy-done.2
  646.7 7.2 %shard_map.277 = (f32[2,96,2304]{2,1,0:T(8,128)}, f32[2,96,768]{2,1,0:T(8,128)}, f32[2,96,3072]{2,1,0:T(8,128)}, f32[2,384,768]{2,1,0:T(8,128)}, f32[2,384]{1,0:...) custom-call(s32[32]{0:T(128)S(1)} %pad_add_fusion.1.slots, ...), custom_call_target="tpu_custom_call" | custom-call | flops 1000000 | bytes 14000000 | tf_op jit(solution)/shard_map/pallas_call | solution.py:313
  (459 shorter events, 120.0 us)
Async XLA Ops:
  7.2 11.2 %copy-start = (bf16[2,96,3072]{2,1,0:T(8,128)(2,1)S(1)}, bf16[2,96,3072]{2,1,0:T(8,128)(2,1)}, u32[]{:S(2)}) copy-start(bf16[2,96,3072]{2,1,0:T(8,128)(2,1)} %param.28) | copy-start | bytes 3538948
  9.5 7.7 %copy-start.99 = (bf16[2,96]{1,0:T(2,128)(2,1)S(1)}, bf16[2,96]{1,0:T(2,128)(2,1)}, u32[]{:S(2)}) copy-start(bf16[2,96]{1,0:T(2,128)(2,1)} %param.19) | copy-start | bytes 1156
  9.5 7.8 %copy-start.66 = (bf16[2,96,2304]{2,1,0:T(8,128)(2,1)S(1)}, bf16[2,96,2304]{2,1,0:T(8,128)(2,1)}, u32[]{:S(2)}) copy-start(bf16[2,96,2304]{2,1,0:T(8,128)(2,1)} %param.21) | copy-start | bytes 2654212
  9.5 30.7 %all-to-all-start = ((bf16[8,128,768]{2,1,0:T(8,128)(2,1)}), bf16[8,128,768]{2,1,0:T(8,128)(2,1)}, u32[]{:S(2)}, u32[]{:S(2)}) async-start(bf16[8,128,768]{2,1,0:T(8,128)(2,1)} %broadcast_in_dim.43), calls=%async_computation | async-start | bytes 3145728 | tf_op jit(solution)/shard_map/all_to_all | solution.py:39
  42.5 55.1 %all-to-all-start.1 = ((bf16[8,352,768]{2,1,0:T(8,128)(2,1)}), bf16[8,352,768]{2,1,0:T(8,128)(2,1)}, u32[]{:S(2)}, u32[]{:S(2)}) async-start(bf16[8,352,768]{2,1,0:T(8,128)(2,1)} %broadcast_in_dim.46), calls=%async_computation.1 | async-start | bytes 8650752 | tf_op jit(solution)/shard_map/all_to_all | solution.py:39
  48.6 60.6 %collective-permute-start = (bf16[8,128,768]{2,1,0:T(8,128)(2,1)}, bf16[8,128,768]{2,1,0:T(8,128)(2,1)}, u32[]{:S(2)}, u32[]{:S(2)}) collective-permute-start(bf16[8,128,768]{2,1,0:T(8,128)(2,1)} %all-to-all-done), channel_id=1, source_target_pairs={{0,1},{1,0},{2,3},{3,2},{4,5},{5,4},{6,7},{7,6},{8,9},{9,8},{10,11... | collective-permute-start | bytes 4718600 | tf_op jit(solution)/shard_map/ppermute | solution.py:47
  102.5 33.4 %collective-permute-start.1 = (bf16[768,384]{1,0:T(8,128)(2,1)}, bf16[768,384]{1,0:T(8,128)(2,1)}, u32[]{:S(2)}, u32[]{:S(2)}) collective-permute-start(bf16[768,384]{1,0:T(8,128)(2,1)} %bitcast.31), channel_id=1, source_target_pairs={{0,1},{1,0},{2,3},{3,2},{4,5},{5,4},{6,7},{7,6},{8,9},{9,8},{10,11... | collective-permute-start | bytes 1769480 | tf_op jit(solution)/shard_map/ppermute | solution.py:47
  108.4 10.4 %copy-start.12 = (bf16[8,1,96,192]{3,2,1,0:T(8,128)(2,1)}, bf16[8,1,96,192]{3,2,1,0:T(8,128)(2,1)S(1)}, u32[]{:S(2)}) copy-start(bf16[8,1,96,192]{3,2,1,0:T(8,128)(2,1)S(1)} %get-tuple-element.142) | copy-start | bytes 884740
  108.4 100.8 %copy-start.14 = (bf16[8,1,96,192]{3,2,1,0:T(8,128)(2,1)}, bf16[8,1,96,192]{3,2,1,0:T(8,128)(2,1)S(1)}, u32[]{:S(2)}) copy-start(bf16[8,1,96,192]{3,2,1,0:T(8,128)(2,1)S(1)} %get-tuple-element.141) | copy-start | bytes 884740
  109.2 29.2 %copy-start.72 = (f32[768]{0:T(1024)}, f32[768]{0:T(1024)S(1)}, u32[]{:S(2)}) copy-start(f32[768]{0:T(1024)S(1)} %get-tuple-element.104) | copy-start | bytes 9220
  109.2 69.7 %copy-start.74 = (f32[768]{0:T(1024)}, f32[768]{0:T(1024)S(1)}, u32[]{:S(2)}) copy-start(f32[768]{0:T(1024)S(1)} %get-tuple-element.101) | copy-start | bytes 9220
  123.5 12.3 %copy-start.45 = (bf16[1,128,768]{2,1,0:T(8,128)(2,1)S(1)}, bf16[1,128,768]{2,1,0:T(8,128)(2,1)}, u32[]{:S(2)}) copy-start(bf16[1,128,768]{2,1,0:T(8,128)(2,1)} %param.16) | copy-start | bytes 589828
  138.1 40.4 %copy-start.28 = (f32[128,768]{1,0:T(8,128)}, f32[128,768]{1,0:T(8,128)S(1)}, u32[]{:S(2)}) copy-start(f32[128,768]{1,0:T(8,128)S(1)} %get-tuple-element.167) | copy-start | bytes 1179652
  138.1 14.2 %copy-start.80 = (f32[128]{0:T(128)}, f32[128]{0:T(128)S(1)}, u32[]{:S(2)}) copy-start(f32[128]{0:T(128)S(1)} %broadcast_multiply_fusion.3) | copy-start | bytes 1540
  138.3 14.0 %copy-start.95 = (f32[128]{0:T(128)}, f32[128]{0:T(128)S(1)}, u32[]{:S(2)}) copy-start(f32[128]{0:T(128)S(1)} %multiply_reduce_fusion.8) | copy-start | bytes 1540
  138.3 14.0 %copy-start.84 = (f32[128]{0:T(128)}, f32[128]{0:T(128)S(1)}, u32[]{:S(2)}) copy-start(f32[128]{0:T(128)S(1)} %fusion.55) | copy-start | bytes 1540
  152.3 4.3 collective-permute-start.2
  161.4 2.4 collective-permute-start.3
  178.7 25.1 %copy-start.82 = (f32[128]{0:T(128)}, f32[128]{0:T(128)S(1)}, u32[]{:S(2)}) copy-start(f32[128]{0:T(128)S(1)} %broadcast_multiply_fusion.2) | copy-start | bytes 1540
  178.9 24.9 %copy-start.97 = (f32[128]{0:T(128)}, f32[128]{0:T(128)S(1)}, u32[]{:S(2)}) copy-start(f32[128]{0:T(128)S(1)} %multiply_reduce_fusion.7) | copy-start | bytes 1540
  178.9 24.8 %copy-start.86 = (f32[128]{0:T(128)}, f32[128]{0:T(128)S(1)}, u32[]{:S(2)}) copy-start(f32[128]{0:T(128)S(1)} %fusion.56) | copy-start | bytes 1540
  179.7 26.5 %copy-start.64 = (bf16[8,48,384]{2,1,0:T(8,128)(2,1)S(1)}, bf16[8,48,384]{2,1,0:T(8,128)(2,1)}, u32[]{:S(2)}) copy-start(bf16[8,48,384]{2,1,0:T(8,128)(2,1)} %get-tuple-element.131) | copy-start | bytes 884740
  179.7 26.5 %copy-start.65 = (bf16[8,48,384]{2,1,0:T(8,128)(2,1)S(1)}, bf16[8,48,384]{2,1,0:T(8,128)(2,1)}, u32[]{:S(2)}) copy-start(bf16[8,48,384]{2,1,0:T(8,128)(2,1)} %get-tuple-element.132) | copy-start | bytes 884740
  203.7 5.4 collective-permute-start.4
  207.0 22.8 %collective-permute-start.5 = (bf16[768,384]{1,0:T(8,128)(2,1)}, bf16[768,384]{1,0:T(8,128)(2,1)}, u32[]{:S(2)}, u32[]{:S(2)}) collective-permute-start(bf16[768,384]{1,0:T(8,128)(2,1)} %bitcast.45), channel_id=1, source_target_pairs={{0,1},{1,0},{2,3},{3,2},{4,5},{5,4},{6,7},{7,6},{8,9},{9,8},{10,11... | collective-permute-start | bytes 1769480 | tf_op jit(solution)/shard_map/ppermute | solution.py:47
  209.2 6.5 copy-start.8
  218.0 11.9 %copy-start.31 = (f32[128,768]{1,0:T(8,128)S(1)}, f32[128,768]{1,0:T(8,128)}, u32[]{:S(2)}) copy-start(f32[128,768]{1,0:T(8,128)} %copy-done.30) | copy-start | bytes 1179652
  232.9 25.5 %copy-start.77 = (f32[8,48]{1,0:T(8,128)S(1)}, f32[8,48]{1,0:T(8,128)}, u32[]{:S(2)}) copy-start(f32[8,48]{1,0:T(8,128)} %get-tuple-element.106) | copy-start | bytes 4612
  232.9 25.5 %copy-start.62 = (bf16[8,48,384]{2,1,0:T(8,128)(2,1)S(1)}, bf16[8,48,384]{2,1,0:T(8,128)(2,1)}, u32[]{:S(2)}) copy-start(bf16[8,48,384]{2,1,0:T(8,128)(2,1)} %get-tuple-element.129) | copy-start | bytes 884740
  232.9 25.5 %copy-start.63 = (bf16[8,48,384]{2,1,0:T(8,128)(2,1)S(1)}, bf16[8,48,384]{2,1,0:T(8,128)(2,1)}, u32[]{:S(2)}) copy-start(bf16[8,48,384]{2,1,0:T(8,128)(2,1)} %get-tuple-element.130) | copy-start | bytes 884740
  256.0 5.7 collective-permute-start.6
  268.7 4.3 collective-permute-start.8
  272.8 5.5 collective-permute-start.7
  274.1 16.3 %all-to-all-start.9 = ((bf16[4,128,768]{2,1,0:T(8,128)(2,1)}), bf16[4,128,768]{2,1,0:T(8,128)(2,1)}, u32[]{:S(2)}, u32[]{:S(2)}) async-start(bf16[4,128,768]{2,1,0:T(8,128)(2,1)} %add_convert_fusion.1), calls=%async_computation.9 | async-start | bytes 1572864 | tf_op jit(solution)/shard_map/all_to_all | solution.py:39
  281.9 14.7 %copy-start.42 = (f32[128,768]{1,0:T(8,128)S(1)}, f32[128,768]{1,0:T(8,128)}, u32[]{:S(2)}) copy-start(f32[128,768]{1,0:T(8,128)} %copy-done.41) | copy-start | bytes 1179652
  290.4 15.4 %all-to-all-start.8 = ((bf16[4,128,768]{2,1,0:T(8,128)(2,1)}), bf16[4,128,768]{2,1,0:T(8,128)(2,1)}, u32[]{:S(2)}, u32[]{:S(2)}) async-start(bf16[4,128,768]{2,1,0:T(8,128)(2,1)} %add_convert_fusion.2), calls=%async_computation.8 | async-start | bytes 1572864 | tf_op jit(solution)/shard_map/all_to_all | solution.py:39
  350.3 4.3 collective-permute-start.9
  356.1 27.5 %all-to-all-start.11 = ((bf16[8,128,768]{2,1,0:T(8,128)(2,1)}), bf16[8,128,768]{2,1,0:T(8,128)(2,1)}, u32[]{:S(2)}, u32[]{:S(2)}) async-start(bf16[8,128,768]{2,1,0:T(8,128)(2,1)} %fusion.2), calls=%async_computation.11 | async-start | bytes 3145728 | tf_op jit(solution)/shard_map/all_to_all | solution.py:39
  360.6 121.8 %reduce-scatter.2.cloned.1.call-start = ((), (), s32[]{:S(2)}) async-start(), calls=%async_computation.20 | async-start | bytes 3317760 | tf_op jit(solution)/shard_map/reduce_scatter | solution.py:529
  377.6 11.4 %copy-start.75 = (f32[768]{0:T(1024)S(1)}, f32[768]{0:T(1024)}, u32[]{:S(2)}) copy-start(f32[768]{0:T(1024)} %copy-done.74) | copy-start | bytes 9220
  428.5 3.7 collective-permute-start.10
  435.9 2.4 collective-permute-start.11
  438.4 14.9 %copy-start.29 = (f32[128,768]{1,0:T(8,128)S(1)}, f32[128,768]{1,0:T(8,128)}, u32[]{:S(2)}) copy-start(f32[128,768]{1,0:T(8,128)} %copy-done.28) | copy-start | bytes 1179652
  438.4 14.9 %copy-start.73 = (f32[768]{0:T(1024)S(1)}, f32[768]{0:T(1024)}, u32[]{:S(2)}) copy-start(f32[768]{0:T(1024)} %copy-done.72) | copy-start | bytes 9220
  438.4 14.9 %copy-start.81 = (f32[128]{0:T(128)S(1)}, f32[128]{0:T(128)}, u32[]{:S(2)}) copy-start(f32[128]{0:T(128)} %copy-done.80) | copy-start | bytes 1540
  438.4 14.9 %copy-start.85 = (f32[128]{0:T(128)S(1)}, f32[128]{0:T(128)}, u32[]{:S(2)}) copy-start(f32[128]{0:T(128)} %copy-done.84) | copy-start | bytes 1540
  438.5 15.6 %copy-start.96 = (f32[128]{0:T(128)S(1)}, f32[128]{0:T(128)}, u32[]{:S(2)}) copy-start(f32[128]{0:T(128)} %copy-done.95) | copy-start | bytes 1540
  500.1 4.2 collective-permute-start.12
  506.0 6.3 copy-start.46
  506.0 6.4 copy-start.68
  506.0 6.6 copy-start.78
  506.0 6.7 %copy-start.94 = (bf16[384]{0:T(512)(128)(2,1)S(1)}, bf16[384]{0:T(512)(128)(2,1)}, u32[]{:S(2)}) copy-start(bf16[384]{0:T(512)(128)(2,1)} %get-tuple-element.112) | copy-start | bytes 2308
  506.0 8.1 %copy-start.79 = (bf16[768]{0:T(1024)(128)(2,1)S(1)}, bf16[768]{0:T(1024)(128)(2,1)}, u32[]{:S(2)}) copy-start(bf16[768]{0:T(1024)(128)(2,1)} %get-tuple-element.85) | copy-start | bytes 4612
  506.0 29.3 %all-to-all-start.15 = ((bf16[8,128,768]{2,1,0:T(8,128)(2,1)}), bf16[8,128,768]{2,1,0:T(8,128)(2,1)}, u32[]{:S(2)}, u32[]{:S(2)}) async-start(bf16[8,128,768]{2,1,0:T(8,128)(2,1)} %fusion.1), calls=%async_computation.16 | async-start | bytes 3145728 | tf_op jit(solution)/shard_map/all_to_all | solution.py:39
  549.0 41.5 %all-to-all-start.16 = ((bf16[8,240,768]{2,1,0:T(8,128)(2,1)}), bf16[8,240,768]{2,1,0:T(8,128)(2,1)S(1)}, u32[]{:S(2)}, u32[]{:S(2)}) async-start(bf16[8,240,768]{2,1,0:T(8,128)(2,1)} %shard_map.276), calls=%async_computation.17 | async-start | bytes 5898240 | tf_op jit(solution)/shard_map/all_to_all | solution.py:39
  552.7 91.9 %all-gather.3.cloned.1.call-start = ((), (), s32[]{:S(2)}) async-start(), calls=%async_computation.21 | async-start | bytes 3760128 | tf_op jit(solution)/shard_map/all_gather | solution.py:533
  592.1 15.7 %all-to-all-start.17 = ((bf16[16,16,768]{2,1,0:T(8,128)(2,1)}), bf16[16,16,768]{2,1,0:T(8,128)(2,1)S(1)}, u32[]{:S(2)}, u32[]{:S(2)}) async-start(bf16[16,16,768]{2,1,0:T(8,128)(2,1)} %pad.17.clone), calls=%async_computation.18 | async-start | bytes 786432 | tf_op jit(solution)/shard_map/all_to_all | solution.py:39
  608.1 31.2 %copy-start.40 = (f32[128,768]{1,0:T(8,128)S(1)}, f32[128,768]{1,0:T(8,128)}, u32[]{:S(2)}) copy-start(f32[128,768]{1,0:T(8,128)} %add_add_fusion.5) | copy-start | bytes 1179652
  608.1 31.2 %copy-start.44 = (f32[128,768]{1,0:T(8,128)S(1)}, f32[128,768]{1,0:T(8,128)}, u32[]{:S(2)}) copy-start(f32[128,768]{1,0:T(8,128)} %copy-done.43) | copy-start | bytes 1179652
  608.2 31.2 %copy-start.48 = (bf16[1,128,768]{2,1,0:T(8,128)(2,1)S(1)}, bf16[1,128,768]{2,1,0:T(8,128)(2,1)}, u32[]{:S(2)}) copy-start(bf16[1,128,768]{2,1,0:T(8,128)(2,1)} %param.16) | copy-start | bytes 589828
  608.2 31.2 %copy-start.50 = (f32[128,768]{1,0:T(8,128)S(1)}, f32[128,768]{1,0:T(8,128)}, u32[]{:S(2)}) copy-start(f32[128,768]{1,0:T(8,128)} %copy-done.49) | copy-start | bytes 1179652
  608.2 31.2 %copy-start.89 = (f32[128]{0:T(128)S(1)}, f32[128]{0:T(128)}, u32[]{:S(2)}) copy-start(f32[128]{0:T(128)} %copy-done.88) | copy-start | bytes 1540
  638.7 3.8 collective-permute-start.13
  646.7 7.2 %copy-start.1 = (bf16[2,96,3072]{2,1,0:T(8,128)(2,1)S(1)}, bf16[2,96,3072]{2,1,0:T(8,128)(2,1)}, u32[]{:S(2)}) copy-start(bf16[2,96,3072]{2,1,0:T(8,128)(2,1)} %param.28) | copy-start | bytes 3538948
  (69 other events, 114.1 us)
Sparse Core Ops, SparseCore 0:
  413.1 69.2 reduce-scatter.1
  556.9 56.0 all-gather.2

commit v3 on v2

--- a/solution.py
+++ b/solution.py
@@ -191,7 +191,7 @@
 
 
 SMEM = pl.BlockSpec(memory_space=pltpu.SMEM)
-VMEM = pl.BlockSpec(memory_space=pltpu.VMEM)
+WHOLE = pl.BlockSpec()
 VMEM_BYTES = 48 * 2**20
 
 
@@ -202,12 +202,12 @@
     extra = ()
     if fresh:
         outs = outs + (jax.ShapeDtypeStruct((LEN // 2, D), BF16),) * 2
-        extra = tuple(member.reshape(1, D) for member in norm)
+        extra = tuple(norm)
     return pl.pallas_call(
         functools.partial(attend_kernel, fresh),
         out_shape=outs,
-        in_specs=[SMEM, SMEM] + [VMEM] * (4 + len(extra)),
-        out_specs=(VMEM,) * len(outs),
+        in_specs=[SMEM, SMEM] + [WHOLE] * (4 + len(extra)),
+        out_specs=(WHOLE,) * len(outs),
         scratch_shapes=[pltpu.VMEM((LEN, HD), BF16)],
         compiler_params=pltpu.CompilerParams(vmem_limit_bytes=VMEM_BYTES),
         cost_estimate=pl.CostEstimate(flops=2 * 10**9, bytes_accessed=5 * 10**6, transcendentals=2 * 10**6),
@@ -223,8 +223,8 @@
             jax.ShapeDtypeStruct((LEN // 2, D), BF16),
             jax.ShapeDtypeStruct((1, 3 * HD), F32),
         ),
-        in_specs=[SMEM, SMEM] + [VMEM] * 5,
-        out_specs=(VMEM,) * 4,
+        in_specs=[SMEM, SMEM] + [WHOLE] * 5,
+        out_specs=(WHOLE,) * 4,
         scratch_shapes=[
             pltpu.VMEM((LEN, HD), BF16),
             pltpu.VMEM((LEN, HD), F32),
@@ -236,88 +236,117 @@
     )(arrive_pos, ctx_pos, queries, keys, values, grads, weight)
 
 
-HEADS, UPS, DOWNS, SMALL, OUTS, PACKED = 0, 32, 80, 128, 144, 240
-
-
-def weight_grads_kernel(
-    own_ref, other_ref, arrive_ref, second_ref, hidden_ref, active_ref, down_ref, mixed_ref, attended_ref, small_ref, out_ref
-):
-    both = ((0,), (0,))
-    half = LEN // 2
-    heads = dot(own_ref[...], arrive_ref[:half, :], both) + dot(other_ref[...], arrive_ref[half:, :], both)
-    heads = heads.astype(BF16)
-    for owner in range(S):
-        for part in range(3):
-            first = owner * 96 + part * 32
-            out_ref[owner, HEADS:UPS, part * 256 : (part + 1) * 256] = heads[first : first + 32, :]
-    ups = dot(second_ref[...], hidden_ref[...], both).astype(BF16)
+UPS, DOWNS, OUTS, FIRST = 0, 48, 96, 192
+HEADS, SMALL, SECOND = 0, 32, 48
+BOTH_ROWS = ((0,), (0,))
+
+
+def first_grads_kernel(second_ref, hidden_ref, active_ref, down_ref, mixed_ref, attended_ref, out_ref):
+    ups = dot(second_ref[...], hidden_ref[...], BOTH_ROWS).astype(BF16)
     for owner in range(S):
         for part in range(2):
             first = owner * 96 + part * 48
             out_ref[owner, UPS:DOWNS, part * 384 : (part + 1) * 384] = ups[first : first + 48, :]
-    downs = dot(active_ref[...], down_ref[...], both).astype(BF16)
+    downs = dot(active_ref[...], down_ref[...], BOTH_ROWS).astype(BF16)
     for owner in range(S):
-        out_ref[owner, DOWNS:SMALL, :] = downs[owner * 48 : (owner + 1) * 48, :]
-        out_ref[owner, SMALL:OUTS, :] = small_ref[owner]
-    outs = dot(mixed_ref[...], attended_ref[...], both).astype(BF16)
+        out_ref[owner, DOWNS:OUTS, :] = downs[owner * 48 : (owner + 1) * 48, :]
+    outs = dot(mixed_ref[...], attended_ref[...], BOTH_ROWS).astype(BF16)
     for owner in range(S):
-        out_ref[owner, OUTS:PACKED, :] = outs[owner * 96 : (owner + 1) * 96, :]
-
-
-def weight_grads(*parts):
+        out_ref[owner, OUTS:FIRST, :] = outs[owner * 96 : (owner + 1) * 96, :]
+
+
+def first_grads(*parts):
     return pl.pallas_call(
-        weight_grads_kernel,
-        out_shape=jax.ShapeDtypeStruct((S, PACKED, D), BF16),
-        in_specs=[VMEM] * len(parts),
-        out_specs=VMEM,
+        first_grads_kernel,
+        out_shape=jax.ShapeDtypeStruct((S, FIRST, D), BF16),
+        in_specs=[WHOLE] * len(parts),
+        out_specs=WHOLE,
         compiler_params=pltpu.CompilerParams(vmem_limit_bytes=VMEM_BYTES),
-        cost_estimate=pl.CostEstimate(flops=2 * 10**9, bytes_accessed=12 * 10**6, transcendentals=0),
+        cost_estimate=pl.CostEstimate(flops=2 * 10**9, bytes_accessed=9 * 10**6, transcendentals=0),
     )(*parts)
 
 
-def unpack_kernel(slots, first_ref, second_ref, qkv_ref, out_ref, up_ref, down_ref, up_shift_ref, *vector_refs):
-    for layer, source in enumerate((first_ref, second_ref)):
-        def slot(place, layer=layer):
-            return slots[layer * C + place]
+def second_grads_kernel(head, own_ref, other_ref, arrive_ref, sums_ref, hidden_sum_ref, *rest):
+    vector_refs, out_ref = rest[:-1], rest[-1]
+    half = LEN // 2
+    heads = dot(own_ref[...], arrive_ref[:half, :], BOTH_ROWS) + dot(other_ref[...], arrive_ref[half:, :], BOTH_ROWS)
+    heads = heads.astype(BF16)
+    here = lax.broadcasted_iota(jnp.int32, (1, D), 1) // HD == head[0]
+    queries = jnp.where(here, jnp.concatenate([sums_ref[:, :HD]] * H, axis=1), 0.0)
+    values = jnp.where(here, jnp.concatenate([sums_ref[:, 2 * HD : 3 * HD]] * H, axis=1), 0.0)
+    vectors = [ref[...] for ref in vector_refs]
+    vectors = vectors[:2] + [queries, values] + vectors[2:]
+    row = lax.broadcasted_iota(jnp.int32, (SECOND - SMALL, D), 0)
+    for owner in range(S):
+        for part in range(3):
+            first = owner * 96 + part * 32
+            out_ref[owner, HEADS:SMALL, part * 256 : (part + 1) * 256] = heads[first : first + 32, :]
+        mine = jnp.concatenate([member[:, owner * 96 : (owner + 1) * 96] for member in vectors], axis=1)
+        hidden = jnp.concatenate(
+            [hidden_sum_ref[:, owner * 48 : (owner + 1) * 48], jnp.zeros((1, D - 48), F32)], axis=1
+        )
+        block = jnp.where(row == 0, mine, jnp.where(row == 1, hidden, 0.0))
+        out_ref[owner, SMALL:SECOND, :] = block.astype(BF16)
+
+
+def second_grads(head, *parts):
+    return pl.pallas_call(
+        second_grads_kernel,
+        out_shape=jax.ShapeDtypeStruct((S, SECOND, D), BF16),
+        in_specs=[SMEM] + [WHOLE] * len(parts),
+        out_specs=WHOLE,
+        compiler_params=pltpu.CompilerParams(vmem_limit_bytes=VMEM_BYTES),
+        cost_estimate=pl.CostEstimate(flops=10**9, bytes_accessed=5 * 10**6, transcendentals=0),
+    )(head, *parts)
+
+
+def unpack_kernel(slots, first_ref, second_ref, last_ref, qkv_ref, out_ref, up_ref, down_ref, up_shift_ref, *vector_refs):
+    layers = (
+        ((first_ref, 0, lambda place: place), (second_ref, 0, lambda place: slots[place])),
+        ((last_ref, 0, lambda place: place), (last_ref, OUTS, lambda place: place)),
+    )
+    for layer, (wide, late) in enumerate(layers):
+        def rows(source, place, start, end):
+            ref, base, slot = source
+            return ref[slot(place), base + start : base + end, :].astype(F32)
 
         for head in range(H):
-            block = source[slot(head), HEADS:UPS, :].astype(F32)
+            block = rows(late, head, HEADS, SMALL)
             for part in range(3):
                 for kind in range(3):
                     lane = part * 256 + kind * HD
                     column = kind * D + head * HD
                     qkv_ref[layer, part * 32 : (part + 1) * 32, column : column + HD] = block[:, lane : lane + HD]
         for rank in range(8):
-            low, high = slot(rank), slot(rank + 8)
-            block = source[low, UPS:DOWNS, :].astype(F32) + source[high, UPS:DOWNS, :].astype(F32)
+            block = rows(wide, rank, UPS, DOWNS) + rows(wide, rank + 8, UPS, DOWNS)
             for part in range(2):
                 for owner in range(S):
                     lane = part * 384 + owner * 48
                     column = owner * 384 + rank * 48
                     up_ref[layer, part * 48 : (part + 1) * 48, column : column + 48] = block[:, lane : lane + 48]
-            block = source[low, DOWNS:SMALL, :].astype(F32) + source[high, DOWNS:SMALL, :].astype(F32)
+            block = rows(wide, rank, DOWNS, OUTS) + rows(wide, rank + 8, DOWNS, OUTS)
             down_ref[layer, rank * 48 : (rank + 1) * 48, :] = block
-            small = source[low, SMALL:OUTS, :].astype(F32) + source[high, SMALL:OUTS, :].astype(F32)
+            small = rows(late, rank, SMALL, SECOND) + rows(late, rank + 8, SMALL, SECOND)
             up_shift_ref[layer : layer + 1, rank * 48 : (rank + 1) * 48] = small[1:2, :48]
             vectors = small[0:1, :] if rank == 0 else vectors + small[0:1, :]
         for member, ref in enumerate(vector_refs):
             ref[layer : layer + 1, :] = vectors[:, member * 96 : (member + 1) * 96]
     for place in range(C):
-        small = first_ref[slots[place], SMALL:OUTS, :].astype(F32)
+        small = second_ref[slots[place], SMALL:SECOND, :].astype(F32)
         for layer in range(LAYERS):
             out_ref[layer, place * 6 : (place + 1) * 6, :] = small[2 + 6 * layer : 8 + 6 * layer, :]
 
 
-def unpack(slots, first, second):
+def unpack(slots, first, second, last):
     shapes = [(96, 3 * D), (96, D), (96, FF), (384, D), (384,)] + [(96,)] * 8
     return pl.pallas_call(
         unpack_kernel,
         out_shape=tuple(jax.ShapeDtypeStruct((LAYERS,) + shape, F32) for shape in shapes),
-        in_specs=[SMEM, VMEM, VMEM],
-        out_specs=(VMEM,) * len(shapes),
+        in_specs=[SMEM] + [WHOLE] * 3,
+        out_specs=(WHOLE,) * len(shapes),
         compiler_params=pltpu.CompilerParams(vmem_limit_bytes=VMEM_BYTES),
         cost_estimate=pl.CostEstimate(flops=10**6, bytes_accessed=14 * 10**6, transcendentals=0),
-    )(slots, first, second)
+    )(slots, first, second, last)
 
 
 def join_cores(core, own, other, axis):
@@ -326,9 +355,8 @@
     )
 
 
-def forward_layer(flowing, params, small, places, gathered=None, carried=None):
+def forward_layer(flowing, head_weight, layer_rows, split, small, places, gathered=None, carried=None):
     arrive_pos, ctx_pos = places
-    head_weight, out_full, up_part, down_part = params
     head_shift, vectors, up_shift = small
     gain_one, bias_one, unused, unused, out_shift, gain_two, bias_two, down_shift = vectors
     if gathered is not None:
@@ -337,8 +365,10 @@
         )
     else:
         normed = layer_norm(flowing, gain_one, bias_one).astype(BF16)
+        normed, layer_rows = lax.optimization_barrier((normed, layer_rows))
         own, other = (part.reshape(LEN // 2, D) for part in gather_ctx(normed))
         mixed_head, queries, keys, values = attend(arrive_pos, ctx_pos, own, other, head_weight, head_shift)
+    out_full, up_part, down_part = split(layer_rows)
     mixed = exchange(mixed_head.reshape(C, TOK, HD), "ctx")[:H]
     mixed = mixed.transpose(1, 0, 2).reshape(TOK, D)
     middle = flowing + dot(mixed, out_full) + out_shift
@@ -354,61 +384,62 @@
     partial = dot(activated, down_part).reshape(8, TOK, D)
     output = middle + scatter_x(partial) + down_shift
     saved = (flowing, own, other, queries, keys, values, mixed, middle, second_all, hidden, activated)
-    return output, saved, carried
-
-
-def backward_layer(grad_out, down_all, saved, params, small, places, head, running=None):
+    return output, saved, carried, (head_weight, out_full, up_part, down_part)
+
+
+def backward_layer(grad_out, down_all, saved, params, small, places, head, last):
     arrive_pos, ctx_pos = places
     head_weight, out_full, up_part, down_part = params
     unused, vectors, unused = small
     gain_one, bias_one, unused, unused, unused, gain_two, bias_two, unused = vectors
     flowing, own, other, queries, keys, values, mixed, middle, second_all, hidden, activated = saved
     down_in = grad_out.astype(BF16)
-    down_shift_grad = jnp.sum(down_in.astype(F32), axis=0)
+    down_shift_grad = jnp.sum(down_in.astype(F32), axis=0, keepdims=True)
     if down_all is None:
         down_all = gather_x(down_in).reshape(8 * TOK, D)
     activated_grad = dot(down_all, down_part, ((1,), (1,)))
     unused, gelu_back = jax.vjp(lambda inner: jax.nn.gelu(inner, approximate=True), hidden)
     hidden_grad = gelu_back(activated_grad)[0].astype(BF16)
     second_grad = scatter_x(dot(hidden_grad, up_part, ((1,), (1,))).reshape(8, TOK, D))
-    up_shift_grad = jnp.sum(hidden_grad.astype(F32), axis=0)
+    up_shift_grad = jnp.sum(hidden_grad.astype(F32), axis=0, keepdims=True)
     unused, norm_back = jax.vjp(layer_norm, middle, gain_two, bias_two)
     middle_part, gain_two_grad, bias_two_grad = norm_back(second_grad)
     middle_grad = grad_out + middle_part
     attended_in = middle_grad.astype(BF16)
-    out_shift_grad = jnp.sum(attended_in.astype(F32), axis=0)
+    out_shift_grad = jnp.sum(attended_in.astype(F32), axis=0, keepdims=True)
     mixed_grad = dot(attended_in, out_full, ((1,), (1,))).astype(BF16)
     mixed_grad = mixed_grad.reshape(TOK, H, HD).transpose(1, 0, 2)
     mixed_grad = jnp.concatenate([mixed_grad, jnp.zeros((C - H, TOK, HD), BF16)], axis=0)
     mixed_grad = exchange(mixed_grad, "ctx").reshape(LEN, HD)
-    if running is not None:
-        mixed_grad, running = lax.optimization_barrier((mixed_grad, running))
+    packed = first_grads(second_all, hidden_grad, activated, down_all, mixed, attended_in)
+    if last is not None:
+        mixed_grad, last, packed = lax.optimization_barrier((mixed_grad, last, packed))
+        owned = jnp.sum(exchange(packed, "shard").astype(F32), axis=0).astype(BF16)
+    else:
+        owned = lax.psum_scatter(packed.reshape(S * FIRST, D), "shard", scatter_dimension=0, tiled=True)
     to_arrive, near, far, sums = attend_back(
         arrive_pos, ctx_pos, queries, keys, values, mixed_grad, head_weight
     )
+    if last is not None:
+        near, far, owned = lax.optimization_barrier((near, far, owned))
     normed_grad = scatter(near.reshape(8, TOK, D), far.reshape(8, TOK, D), CHIP_GROUPS)
-    sums = jnp.where(lax.axis_index("ctx") < H, sums[0], 0.0)
-    query_shift_grad = lax.dynamic_update_slice_in_dim(jnp.zeros((D,), F32), sums[:HD], head * HD, 0)
-    value_shift_grad = lax.dynamic_update_slice_in_dim(jnp.zeros((D,), F32), sums[2 * HD :], head * HD, 0)
     unused, first_back = jax.vjp(layer_norm, flowing, gain_one, bias_one)
     flowing_part, gain_one_grad, bias_one_grad = first_back(normed_grad)
-    shifts = (
+    late = second_grads(
+        head,
+        own,
+        other,
+        to_arrive,
+        sums,
+        up_shift_grad,
         gain_one_grad,
         bias_one_grad,
-        query_shift_grad,
-        value_shift_grad,
         out_shift_grad,
         gain_two_grad,
         bias_two_grad,
         down_shift_grad,
     )
-    vectors = jnp.stack(shifts).reshape(8, S, 96).transpose(1, 0, 2).reshape(S, 1, D)
-    hiddens = jnp.pad(up_shift_grad.reshape(S, 1, 48), ((0, 0), (0, 0), (0, D - 48)))
-    rest = jnp.concatenate([vectors, hiddens, jnp.zeros((S, 14, D), F32)], axis=1).astype(BF16)
-    packed = weight_grads(
-        own, other, to_arrive, second_all, hidden_grad, activated, down_all, mixed, attended_in, rest
-    )
-    return middle_grad + flowing_part, packed, running
+    return middle_grad + flowing_part, owned, late, last
 
 
 def shards(
@@ -476,12 +507,11 @@
             up_bias.reshape(1, D),
             jnp.zeros((13, D), BF16),
             layer_pieces[0],
-            layer_pieces[1],
         ],
         axis=0,
     )
     gathered = spread_to(packed, S, "shard")
-    layer_weights = [split(gathered[:, 64:208]), split(gathered[:, 208:])]
+    layer_rows = [gathered[:, 64:], lax.all_gather(layer_pieces[1], "shard", axis=0)]
     head_weights = gathered[:, :48].reshape(S, LAYERS, 96, 3 * HD)
     vectors = gathered[:, 48:50].reshape(S, 8, LAYERS, 96).transpose(2, 1, 0, 3).reshape(LAYERS, 8, D)
     vectors = vectors.astype(F32)
@@ -507,40 +537,43 @@
             [vectors[layer, member : member + 1] for member in range(8)],
             up_shifts[layer],
         )
-        small = (small[0], [member.reshape(D) for member in small[1]], small[2])
         smalls.append(small)
-        params = (head_weights[:, layer].reshape(D, 3 * HD),) + layer_weights[layer]
-        all_params.append(params)
-        flowing, saved, carried = forward_layer(
+        flowing, saved, carried, params = forward_layer(
             flowing,
-            params,
+            head_weights[:, layer].reshape(D, 3 * HD),
+            layer_rows[layer],
+            split,
             small,
             places,
             gathered=states_all if layer == 0 else None,
             carried=cotangent.reshape(TOK, D) if layer == LAYERS - 1 else None,
         )
         saved_all.append(saved)
+        all_params.append(params)
     result = flowing.astype(BF16).reshape(states.shape)
     grad_flow = cotangent.reshape(TOK, D).astype(F32)
-    grad_flow, packed, unused = backward_layer(
-        grad_flow, carried, saved_all[1], all_params[1], smalls[1], places, head
-    )
-    grad_flow, packed = lax.optimization_barrier((grad_flow, packed))
-    owned_last = lax.psum_scatter(packed.reshape(S * PACKED, D), "shard", scatter_dimension=0, tiled=True)
-    grad_flow, packed, owned_last = backward_layer(
-        grad_flow, None, saved_all[0], all_params[0], smalls[0], places, head, owned_last
-    )
-    every_last = lax.all_gather(owned_last[:OUTS], "ctx", axis=0)
-    owned = jnp.sum(exchange(packed, "shard").astype(F32), axis=0).astype(BF16)
-    outs = jnp.stack([owned[OUTS:], owned_last[OUTS:]]).reshape(LAYERS, C, 6, D)
+    held = jnp.where(place < H, place, -1).reshape(1)
+    grad_flow, first_last, late, unused = backward_layer(
+        grad_flow, carried, saved_all[1], all_params[1], smalls[1], places, held, None
+    )
+    grad_flow, late = lax.optimization_barrier((grad_flow, late))
+    late_last = lax.psum_scatter(late.reshape(S * SECOND, D), "shard", scatter_dimension=0, tiled=True)
+    grad_flow, first, late, last = backward_layer(
+        grad_flow, None, saved_all[0], all_params[0], smalls[0], places, held, (first_last, late_last)
+    )
+    first_last, late_last = last
+    every_last = lax.all_gather(jnp.concatenate([first_last[:OUTS], late_last], axis=0), "ctx", axis=0)
+    every_first = lax.all_gather(first[:OUTS], "ctx", axis=0)
+    outs = jnp.stack([first[OUTS:], first_last[OUTS:]]).reshape(LAYERS, C, 6, D)
     outs = outs.transpose(1, 0, 2, 3).reshape(C, 12, D)
     outs = exchange(jnp.pad(outs, ((0, 0), (0, 4), (0, 0))), "ctx").astype(F32)
     outs = jnp.sum(outs, axis=0)[:12].astype(BF16)
-    owned = jnp.concatenate([owned[: SMALL + 2], outs, jnp.zeros((2, D), BF16)], axis=0)
-    every = jnp.concatenate(gather_ctx(owned), axis=0)
+    late = jnp.sum(exchange(late, "shard").astype(F32), axis=0).astype(BF16)
+    late = jnp.concatenate([late[: SMALL + 2], outs, jnp.zeros((2, D), BF16)], axis=0)
+    every_late = jnp.concatenate(gather_ctx(late), axis=0)
     places_of = jnp.arange(C, dtype=jnp.int32)
-    slots = jnp.concatenate([places_of // 2 + 8 * (places_of % 2 != core).astype(jnp.int32), places_of])
-    qkv, outs, ups, downs, hiddens, *vectors = unpack(slots, every, every_last)
+    slots = places_of // 2 + 8 * (places_of % 2 != core).astype(jnp.int32)
+    qkv, outs, ups, downs, hiddens, *vectors = unpack(slots, every_first, every_late, every_last)
     return (
         result,
         grad_flow.astype(BF16).reshape(states.shape),

time: 668 us -> 666 us (level)
  waiting for transfers between devices: 185 us -> 223 us
  blocking collectives: 186 us -> 163 us
  local copies, waits for them, and re-layouts: 83.2 us -> 63.9 us
  starting transfers between devices: 57.2 us -> 71.3 us
    all_gather x1 -> x3, waiting for transfers between devices: 0.01 us -> 47 us  [the longest x1 30.9 us: shards(): lax.all_gather(jnp.concatenate([first_last[:OUTS], late_last], axis=0), '...]
    all_to_all x11 -> x10, blocking collectives: 186 us -> 163 us  [exchange(): lax.all_to_all(parts, axis, 0, 0, tiled=True, axis_index_groups=groups)]
    all_to_all x8 -> x10, waiting for transfers between devices: 156 us -> 135 us  [exchange(): lax.all_to_all(parts, axis, 0, 0, tiled=True, axis_index_groups=groups)]
    reduce_scatter x1 -> x2, waiting for transfers between devices: 10.6 us -> 27.8 us  [the longest x1 27.7 us: backward_layer(): lax.psum_scatter(packed.reshape(S * FIRST, D), 'shard', scatter_dimension...]
    another operation x29 -> x2, local copies, waits for them, and re-layouts: 13.4 us -> 0.11 us  [shards(): outs = jnp.stack([first[OUTS:], first_last[OUTS:]]).reshape(LAYERS, C, 6, D)]
    all_to_all x8 -> x10, starting transfers between devices: 40.8 us -> 51.9 us  [exchange(): lax.all_to_all(parts, axis, 0, 0, tiled=True, axis_index_groups=groups)]
    unnamed x240 -> x272, local copies, waits for them, and re-layouts: 34.4 us -> 29.5 us
    pallas_call x2 -> x4, Pallas kernels: 13.4 us -> 9.66 us  [the longest x2 6.71 us: first_grads(): pl.pallas_call(first_grads_kernel, out_shape=jax.ShapeDtypeStruct((S, FIR...]
  transfers between devices with their start and end apart: 24 -> 29, of which waited for: 18 -> 19; matrix products, arithmetic and copies ran while one was open for 9% -> 10% of each run, Pallas kernels for 2% -> 6%
where the time goes in v3:
time: 666 us; the launch traced here: 659 us
  waiting for transfers between devices  223 us (33%)
  blocking collectives  163 us (24%)
  starting transfers between devices  71.3 us (11%)
  local copies, waits for them, and re-layouts  63.9 us (10%)
  Pallas kernels  60 us (9%)
  other arithmetic  39.9 us (6%)
  matrix products  22.9 us (3%)
  between operations  16.1 us (2%)
    all_to_all x10, blocking collectives, exchange(): lax.all_to_all(parts, axis, 0, 0, tiled=True, axis_index_groups=groups)  163 us
    all_to_all x10, waiting for transfers between devices, exchange(): lax.all_to_all(parts, axis, 0, 0, tiled=True, axis_index_groups=groups)  135 us
    all_to_all x10, starting transfers between devices, exchange(): lax.all_to_all(parts, axis, 0, 0, tiled=True, axis_index_groups=groups)  51.9 us
    all_gather x1, waiting for transfers between devices, shards(): lax.all_gather(jnp.concatenate([first_last[:OUTS], late_last], axis=0), '...  30.9 us
    unnamed x272, local copies, waits for them, and re-layouts  29.5 us
    reduce_scatter x1, waiting for transfers between devices, backward_layer(): lax.psum_scatter(packed.reshape(S * FIRST, D), 'shard', scatter_dimension...  27.7 us
    pallas_call x2, Pallas kernels, attend_back(): pl.pallas_call(attend_back_kernel, out_shape=(jax.ShapeDtypeStruct((LEN,...  27.2 us
    dot_general x13, matrix products, dot(): lax.dot_general(left, right, (dims, ((), ())), preferred_element_type=F32)  22.9 us
  transfers between devices with their start and end apart: 29, of which 19 were waited for; matrix products, arithmetic and copies ran while one was open for 10% of the time, Pallas kernels for 6%

profile of v3, /device:TPU:1, one launch (start us, length us, event | category | flops | bytes accessed | tf_op | source)
XLA Modules:
  0.0 659.4 jit_solution(1939293251726597614)
XLA Ops:
  7.2 2.3 broadcast_in_dim.50
  9.5 7.6 %all-to-all-start = ((bf16[8,128,768]{2,1,0:T(8,128)(2,1)}), bf16[8,128,768]{2,1,0:T(8,128)(2,1)}, u32[]{:S(2)}, u32[]{:S(2)}) async-start(bf16[8,128,768]{2,1,0:T(8,128)(2,1)} %broadcast_in_dim.50), calls=%async_computation | async-start | bytes 3145728 | tf_op jit(solution)/shard_map/all_to_all | solution.py:39
  22.5 17.6 %all-to-all-done = bf16[8,128,768]{2,1,0:T(8,128)(2,1)} async-done(((bf16[8,128,768]{2,1,0:T(8,128)(2,1)}), bf16[8,128,768]{2,1,0:T(8,128)(2,1)}, u32[]{:S(2)}, u32[]{:S(2)}) %all-to-all-start) | async-done | bytes 1572896 | tf_op jit(solution)/shard_map/all_to_all | solution.py:39
  41.7 5.3 all-to-all-start.1
  49.0 28.8 %all-to-all-done.1 = bf16[8,208,768]{2,1,0:T(8,128)(2,1)S(1)} async-done(((bf16[8,208,768]{2,1,0:T(8,128)(2,1)}), bf16[8,208,768]{2,1,0:T(8,128)(2,1)S(1)}, u32[]{:S(2)}, u32[]{:S(2)}) %all-to-all-start.1) | async-done | bytes 2555936 | tf_op jit(solution)/shard_map/all_to_all | solution.py:39
  80.1 2.3 collective-permute-start.1
  86.5 9.5 %shard_map.271 = (bf16[2048,64]{1,0:T(8,128)(2,1)S(1)}, bf16[2048,64]{1,0:T(8,128)(2,1)S(1)}, bf16[2048,64]{1,0:T(8,128)(2,1)S(1)}, bf16[2048,64]{1,0:T(8,128)(2...) custom-call(s32[32]{0:T(128)S(1)} %reshape.367.arrive_pos, s32[32]{0:T(128)S(1)} %reshape.368.ctx_pos, ...), custom_call_target="tpu_custom_call" | custom-call | flops 2000000000 | bytes 5000000 | tf_op jit(solution)/shard_map/pallas_call | solution.py:206
  101.1 12.2 %all_to_all.100 = bf16[16,128,64]{1,2,0:T(8,128)(2,1)S(1)} all-to-all(bf16[16,128,64]{1,2,0:T(8,128)(2,1)S(1)} %copy.67), channel_id=1, replica_groups=mesh['shard'=8,'ctx'=16] {'ctx'}, dimensions={0} | all-to-all | bytes 524288 | tf_op jit(solution)/shard_map/all_to_all | solution.py:39
  115.8 13.9 %all_to_all.101 = bf16[4,128,768]{2,1,0:T(8,128)(2,1)S(1)} all-to-all(bf16[4,128,768]{2,1,0:T(8,128)(2,1)S(1)} %broadcast_in_dim.55), channel_id=1, replica_groups={{0,2,4,6},{1,3,5,7},{8,10,12,14},{9,11,13,15},{16,18,20,22},{17,19,21,2..., dimensions={0} | all-to-all | bytes 1572864 | tf_op jit(solution)/shard_map/all_to_all | solution.py:39
  129.7 2.2 collective-permute-start.2
  136.3 2.4 multiply_convert_fusion.1
  140.0 2.1 collective-permute-done.3
  142.4 14.8 %all_to_all.102 = bf16[4,128,768]{2,1,0:T(8,128)(2,1)S(1)} all-to-all(bf16[4,128,768]{2,1,0:T(8,128)(2,1)S(1)} %add_convert_fusion.3), channel_id=1, replica_groups={{0,2,4,6},{1,3,5,7},{8,10,12,14},{9,11,13,15},{16,18,20,22},{17,19,21,2..., dimensions={0} | all-to-all | bytes 1572864 | tf_op jit(solution)/shard_map/all_to_all | solution.py:39
  158.0 16.1 %all-gather.7.cloned.1.call-done = bf16[1152,768]{1,0:T(8,128)(2,1)} async-done(((bf16[144,768]{1,0:T(8,128)(2,1)}), bf16[1152,768]{1,0:T(8,128)(2,1)}) %all-gather.7.cloned.1.call-update) | async-done | bytes 1769488 | tf_op jit(solution)/shard_map/all_gather | solution.py:514
  174.2 27.7 %all_to_all.103 = bf16[8,128,768]{2,1,0:T(8,128)(2,1)S(1)} all-to-all(bf16[8,128,768]{2,1,0:T(8,128)(2,1)S(1)} %broadcast_in_dim.56), channel_id=1, replica_groups={{0,2,4,6,8,10,12,14},{1,3,5,7,9,11,13,15},{16,18,20,22,24,26,28,30},{17..., dimensions={0} | all-to-all | bytes 3145728 | tf_op jit(solution)/shard_map/all_to_all | solution.py:39
  202.0 2.2 collective-permute-start.4
  207.2 6.4 shard_map.272
  215.5 11.7 %all_to_all.104 = bf16[16,128,64]{1,2,0:T(8,128)(2,1)S(1)} all-to-all(bf16[16,128,64]{1,2,0:T(8,128)(2,1)S(1)} %copy.68), channel_id=1, replica_groups=mesh['shard'=8,'ctx'=16] {'ctx'}, dimensions={0} | all-to-all | bytes 524288 | tf_op jit(solution)/shard_map/all_to_all | solution.py:39
  227.3 2.2 fusion.78
  230.4 22.2 %all_to_all.105 = bf16[4,256,768]{2,1,0:T(8,128)(2,1)S(1)} all-to-all(bf16[4,256,768]{2,1,0:T(8,128)(2,1)S(1)} %broadcast_in_dim.57), channel_id=1, replica_groups={{0,2,4,6},{1,3,5,7},{8,10,12,14},{9,11,13,15},{16,18,20,22},{17,19,21,2..., dimensions={0} | all-to-all | bytes 3145728 | tf_op jit(solution)/shard_map/all_to_all | solution.py:39
  252.6 2.4 collective-permute-start.6
  261.6 2.6 convert_reduce_fusion.9
  270.7 4.2 all-to-all-start.9
  276.3 2.3 add_convert_fusion.2
  278.6 8.8 %all-to-all-done.9 = bf16[4,128,768]{2,1,0:T(8,128)(2,1)} async-done(((bf16[4,128,768]{2,1,0:T(8,128)(2,1)}), bf16[4,128,768]{2,1,0:T(8,128)(2,1)}, u32[]{:S(2)}, u32[]{:S(2)}) %all-to-all-start.9) | async-done | bytes 786464 | tf_op jit(solution)/shard_map/all_to_all | solution.py:39
  287.4 4.2 all-to-all-start.8
  291.6 2.1 convert_reduce_fusion.6
  297.2 6.1 all-to-all-done.8
  307.9 2.8 convolution_convert_fusion.1
  311.9 13.7 %all_to_all.106 = bf16[16,128,64]{1,2,0:T(8,128)(2,1)} all-to-all(bf16[16,128,64]{1,2,0:T(8,128)(2,1)S(1)} %concatenate.92), channel_id=1, replica_groups=mesh['shard'=8,'ctx'=16] {'ctx'}, dimensions={0} | all-to-all | bytes 524288 | tf_op jit(solution)/shard_map/all_to_all | solution.py:39
  325.5 2.0 copy.70
  332.7 13.6 %shard_map.273 = (bf16[2048,256]{1,0:T(8,128)(2,1)S(1)}, bf16[1024,768]{1,0:T(8,128)(2,1)S(1)}, bf16[1024,768]{1,0:T(8,128)(2,1)}, f32[1,192]{1,0:T(1,128)S(1)}) custom-call(s32[32]{0:T(128)S(1)} %reshape.367.arrive_pos, s32[32]{0:T(128)S(1)} %reshape.368.ctx_pos, bf16[2048,64]{1,0:T(8,128)(2,1)S(1)} %copy-done.36, bf16[2048,64]{1,0:T(8,128)(2,1)S(1)} %copy-done.38, ...), custom_call_target="tpu_custom_call" | custom-call | flops 4000000000 | bytes 5000000 | tf_op jit(solution)/shard_map/pallas_call | solution.py:218
  348.5 3.2 collective-permute-done.9
  353.4 4.3 all-to-all-start.11
  357.9 22.8 %all-to-all-done.11 = bf16[8,128,768]{2,1,0:T(8,128)(2,1)} async-done(((bf16[8,128,768]{2,1,0:T(8,128)(2,1)}), bf16[8,128,768]{2,1,0:T(8,128)(2,1)}, u32[]{:S(2)}, u32[]{:S(2)}) %all-to-all-start.11) | async-done | bytes 1572896 | tf_op jit(solution)/shard_map/all_to_all | solution.py:39
  380.7 2.1 convert_reduce_fusion.2
  388.6 14.4 %all_to_all.107 = bf16[4,128,768]{2,1,0:T(8,128)(2,1)} all-to-all(bf16[4,128,768]{2,1,0:T(8,128)(2,1)S(1)} %broadcast_in_dim.124), channel_id=1, replica_groups={{0,2,4,6},{1,3,5,7},{8,10,12,14},{9,11,13,15},{16,18,20,22},{17,19,21,2..., dimensions={0} | all-to-all | bytes 1572864 | tf_op jit(solution)/shard_map/all_to_all | solution.py:39
  403.0 1.9 collective-permute-start.10
  409.7 3.4 shard_map.275
  415.1 2.4 convert_reduce_fusion.8
  418.9 2.2 collective-permute-done.11
  421.2 14.5 %all_to_all.108 = bf16[4,128,768]{2,1,0:T(8,128)(2,1)S(1)} all-to-all(bf16[4,128,768]{2,1,0:T(8,128)(2,1)S(1)} %add_convert_fusion), channel_id=1, replica_groups={{0,2,4,6},{1,3,5,7},{8,10,12,14},{9,11,13,15},{16,18,20,22},{17,19,21,2..., dimensions={0} | all-to-all | bytes 1572864 | tf_op jit(solution)/shard_map/all_to_all | solution.py:39
  438.5 2.5 convolution_convert_fusion
  442.8 5.2 all-to-all-start.14
  451.3 3.4 shard_map.276
  454.7 2.2 all-to-all-done.14
  458.1 27.7 %reduce-scatter.3.cloned.1.call-done = bf16[192,768]{1,0:T(8,128)(2,1)} async-done(((bf16[1536,768]{1,0:T(8,128)(2,1)}), bf16[192,768]{1,0:T(8,128)(2,1)}) %reduce-scatter.3.cloned.1.call-update) | async-done | bytes 294928 | tf_op jit(solution)/shard_map/reduce_scatter | solution.py:419
  485.8 4.5 all-to-all-start.15
  493.7 13.5 %shard_map.277 = (bf16[2048,256]{1,0:T(8,128)(2,1)S(1)}, bf16[1024,768]{1,0:T(8,128)(2,1)S(1)}, bf16[1024,768]{1,0:T(8,128)(2,1)}, f32[1,192]{1,0:T(1,128)S(1)}) custom-call(s32[32]{0:T(128)S(1)} %reshape.367.arrive_pos, s32[32]{0:T(128)S(1)} %reshape.368.ctx_pos, bf16[2048,64]{1,0:T(8,128)(2,1)S(1)} %copy-done.30, bf16[2048,64]{1,0:T(8,128)(2,1)S(1)} %copy-done.32, ...), custom_call_target="tpu_custom_call" | custom-call | flops 4000000000 | bytes 5000000 | tf_op jit(solution)/shard_map/pallas_call | solution.py:218
  507.2 12.1 %all-to-all-done.15 = bf16[8,192,768]{2,1,0:T(8,128)(2,1)} async-done(((bf16[8,192,768]{2,1,0:T(8,128)(2,1)}), bf16[8,192,768]{2,1,0:T(8,128)(2,1)}, u32[]{:S(2)}, u32[]{:S(2)}) %all-to-all-start.15) | async-done | bytes 2359328 | tf_op jit(solution)/shard_map/all_to_all | solution.py:39
  519.4 2.3 reduce_sum.437
  525.0 3.2 collective-permute-done.12
  529.9 6.3 all-to-all-start.16
  537.6 23.0 %all-to-all-done.16 = bf16[8,128,768]{2,1,0:T(8,128)(2,1)} async-done(((bf16[8,128,768]{2,1,0:T(8,128)(2,1)}), bf16[8,128,768]{2,1,0:T(8,128)(2,1)}, u32[]{:S(2)}, u32[]{:S(2)}) %all-to-all-start.16) | async-done | bytes 1572896 | tf_op jit(solution)/shard_map/all_to_all | solution.py:39
  560.5 6.8 %all-to-all-start.18 = ((bf16[16,16,768]{2,1,0:T(8,128)(2,1)}), bf16[16,16,768]{2,1,0:T(8,128)(2,1)S(1)}, u32[]{:S(2)}, u32[]{:S(2)}) async-start(bf16[16,16,768]{2,1,0:T(8,128)(2,1)} %pad.6.clone), calls=%async_computation.20 | async-start | bytes 786432 | tf_op jit(solution)/shard_map/all_to_all | solution.py:39
  567.3 2.1 convert_reduce_fusion
  570.0 1.9 shard_map.278
  571.9 5.6 all-to-all-done.18
  577.5 3.5 all-to-all-start.17
  582.2 8.4 %all-to-all-done.17 = bf16[8,48,768]{2,1,0:T(8,128)(2,1)S(1)} async-done(((bf16[8,48,768]{2,1,0:T(8,128)(2,1)}), bf16[8,48,768]{2,1,0:T(8,128)(2,1)S(1)}, u32[]{:S(2)}, u32[]{:S(2)}) %all-to-all-start.17) | async-done | bytes 589856 | tf_op jit(solution)/shard_map/all_to_all | solution.py:39
  590.9 17.4 %all_to_all.109 = bf16[8,48,768]{2,1,0:T(8,128)(2,1)S(1)} all-to-all(bf16[8,48,768]{2,1,0:T(8,128)(2,1)S(1)} %broadcast_in_dim.133), channel_id=1, replica_groups={{0,2,4,6,8,10,12,14},{1,3,5,7,9,11,13,15},{16,18,20,22,24,26,28,30},{17..., dimensions={0} | all-to-all | bytes 1179648 | tf_op jit(solution)/shard_map/all_to_all | solution.py:39
  608.3 2.7 collective-permute-start.13
  612.8 30.9 %all-gather.11.cloned.1.call-done = bf16[2304,768]{1,0:T(8,128)(2,1)} async-done(((bf16[144,768]{1,0:T(8,128)(2,1)}), bf16[2304,768]{1,0:T(8,128)(2,1)}) %all-gather.11.cloned.1.call-update) | async-done | bytes 3538960 | tf_op jit(solution)/shard_map/all_gather | solution.py:565
  645.4 7.2 %shard_map.279 = (f32[2,96,2304]{2,1,0:T(8,128)}, f32[2,96,768]{2,1,0:T(8,128)}, f32[2,96,3072]{2,1,0:T(8,128)}, f32[2,384,768]{2,1,0:T(8,128)}, f32[2,384]{1,0:...) custom-call(s32[16]{0:T(128)S(1)} %fusion.47.slots, ...), custom_call_target="tpu_custom_call" | custom-call | flops 1000000 | bytes 14000000 | tf_op jit(solution)/shard_map/pallas_call | solution.py:342
  (471 shorter events, 105.1 us)
Async XLA Ops:
  9.5 30.7 %all-to-all-start = ((bf16[8,128,768]{2,1,0:T(8,128)(2,1)}), bf16[8,128,768]{2,1,0:T(8,128)(2,1)}, u32[]{:S(2)}, u32[]{:S(2)}) async-start(bf16[8,128,768]{2,1,0:T(8,128)(2,1)} %broadcast_in_dim.50), calls=%async_computation | async-start | bytes 3145728 | tf_op jit(solution)/shard_map/all_to_all | solution.py:39
  41.7 36.1 %all-to-all-start.1 = ((bf16[8,208,768]{2,1,0:T(8,128)(2,1)}), bf16[8,208,768]{2,1,0:T(8,128)(2,1)S(1)}, u32[]{:S(2)}, u32[]{:S(2)}) async-start(bf16[8,208,768]{2,1,0:T(8,128)(2,1)} %broadcast_in_dim.53), calls=%async_computation.1 | async-start | bytes 5111808 | tf_op jit(solution)/shard_map/all_to_all | solution.py:39
  47.0 127.1 %all-gather.7.cloned.1.call-start = ((), (), s32[]{:S(2)}) async-start(), calls=%async_computation.24 | async-start | bytes 1990656 | tf_op jit(solution)/shard_map/all_gather | solution.py:514
  47.9 38.6 %collective-permute-start = (bf16[8,128,768]{2,1,0:T(8,128)(2,1)}, bf16[8,128,768]{2,1,0:T(8,128)(2,1)}, u32[]{:S(2)}, u32[]{:S(2)}) collective-permute-start(bf16[8,128,768]{2,1,0:T(8,128)(2,1)} %all-to-all-done), channel_id=1, source_target_pairs={{0,1},{1,0},{2,3},{3,2},{4,5},{5,4},{6,7},{7,6},{8,9},{9,8},{10,11... | collective-permute-start | bytes 4718600 | tf_op jit(solution)/shard_map/ppermute | solution.py:47
  80.1 33.2 %collective-permute-start.1 = (bf16[768,384]{1,0:T(8,128)(2,1)}, bf16[768,384]{1,0:T(8,128)(2,1)}, u32[]{:S(2)}, u32[]{:S(2)}) collective-permute-start(bf16[768,384]{1,0:T(8,128)(2,1)} %bitcast.201), channel_id=1, source_target_pairs={{0,1},{1,0},{2,3},{3,2},{4,5},{5,4},{6,7},{7,6},{8,9},{9,8},{10,11... | collective-permute-start | bytes 1769480 | tf_op jit(solution)/shard_map/ppermute | solution.py:47
  85.7 121.5 %copy-start.27 = (bf16[8,1,96,192]{3,2,1,0:T(8,128)(2,1)}, bf16[8,1,96,192]{3,2,1,0:T(8,128)(2,1)S(1)}, u32[]{:S(2)}) copy-start(bf16[8,1,96,192]{3,2,1,0:T(8,128)(2,1)S(1)} %get-tuple-element.163) | copy-start | bytes 884740
  100.8 12.5 %copy-start.50 = (bf16[1,128,768]{2,1,0:T(8,128)(2,1)S(1)}, bf16[1,128,768]{2,1,0:T(8,128)(2,1)}, u32[]{:S(2)}) copy-start(bf16[1,128,768]{2,1,0:T(8,128)(2,1)} %param.16) | copy-start | bytes 589828
  100.8 12.5 %copy-start.72 = (bf16[8,96,384]{2,1,0:T(8,128)(2,1)S(1)}, bf16[8,96,384]{2,1,0:T(8,128)(2,1)}, u32[]{:S(2)}) copy-start(bf16[8,96,384]{2,1,0:T(8,128)(2,1)} %pad_maximum_fusion.3) | copy-start | bytes 1769476
  115.2 42.0 %copy-start.41 = (f32[128,768]{1,0:T(8,128)}, f32[128,768]{1,0:T(8,128)S(1)}, u32[]{:S(2)}) copy-start(f32[128,768]{1,0:T(8,128)S(1)} %get-tuple-element.190) | copy-start | bytes 1179652
  115.3 14.4 %copy-start.97 = (f32[128]{0:T(128)}, f32[128]{0:T(128)S(1)}, u32[]{:S(2)}) copy-start(f32[128]{0:T(128)S(1)} %broadcast_multiply_fusion.3) | copy-start | bytes 1540
  115.5 14.2 %copy-start.117 = (f32[128]{0:T(128)}, f32[128]{0:T(128)S(1)}, u32[]{:S(2)}) copy-start(f32[128]{0:T(128)S(1)} %multiply_reduce_fusion.8) | copy-start | bytes 1540
  115.5 14.2 %copy-start.102 = (f32[128]{0:T(128)}, f32[128]{0:T(128)S(1)}, u32[]{:S(2)}) copy-start(f32[128]{0:T(128)S(1)} %fusion.48) | copy-start | bytes 1540
  115.5 16.4 %copy-start.76 = (bf16[48,768]{1,0:T(8,128)(2,1)S(1)}, bf16[48,768]{1,0:T(8,128)(2,1)}, u32[]{:S(2)}) copy-start(bf16[48,768]{1,0:T(8,128)(2,1)} %get-tuple-element.161) | copy-start | bytes 221188
  115.5 16.4 %copy-start.77 = (bf16[48,384]{1,0:T(8,128)(2,1)S(1)}, bf16[48,384]{1,0:T(8,128)(2,1)}, u32[]{:S(2)}) copy-start(bf16[48,384]{1,0:T(8,128)(2,1)} %get-tuple-element.175) | copy-start | bytes 110596
  115.5 16.4 %copy-start.78 = (bf16[48,384]{1,0:T(8,128)(2,1)S(1)}, bf16[48,384]{1,0:T(8,128)(2,1)}, u32[]{:S(2)}) copy-start(bf16[48,384]{1,0:T(8,128)(2,1)} %get-tuple-element.176) | copy-start | bytes 110596
  115.5 16.4 %copy-start.79 = (bf16[48,384]{1,0:T(8,128)(2,1)S(1)}, bf16[48,384]{1,0:T(8,128)(2,1)}, u32[]{:S(2)}) copy-start(bf16[48,384]{1,0:T(8,128)(2,1)} %get-tuple-element.170) | copy-start | bytes 110596
  115.5 16.4 %copy-start.80 = (bf16[48,384]{1,0:T(8,128)(2,1)S(1)}, bf16[48,384]{1,0:T(8,128)(2,1)}, u32[]{:S(2)}) copy-start(bf16[48,384]{1,0:T(8,128)(2,1)} %get-tuple-element.173) | copy-start | bytes 110596
  115.7 18.8 %copy-start.67 = (bf16[8,48,384]{2,1,0:T(8,128)(2,1)S(1)}, bf16[8,48,384]{2,1,0:T(8,128)(2,1)}, u32[]{:S(2)}) copy-start(bf16[8,48,384]{2,1,0:T(8,128)(2,1)} %get-tuple-element.152) | copy-start | bytes 884740
  115.7 18.8 %copy-start.68 = (bf16[8,48,384]{2,1,0:T(8,128)(2,1)S(1)}, bf16[8,48,384]{2,1,0:T(8,128)(2,1)}, u32[]{:S(2)}) copy-start(bf16[8,48,384]{2,1,0:T(8,128)(2,1)} %get-tuple-element.153) | copy-start | bytes 884740
  129.7 4.9 collective-permute-start.2
  139.8 2.4 collective-permute-start.3
  142.3 14.9 %copy-start.88 = (f32[768]{0:T(1024)S(1)}, f32[768]{0:T(1024)}, u32[]{:S(2)}) copy-start(f32[768]{0:T(1024)} %get-tuple-element.124) | copy-start | bytes 9220
  157.4 44.5 %copy-start.43 = (f32[128,768]{1,0:T(8,128)}, f32[128,768]{1,0:T(8,128)S(1)}, u32[]{:S(2)}) copy-start(f32[128,768]{1,0:T(8,128)S(1)} %get-tuple-element.147) | copy-start | bytes 1179652
  157.4 44.5 %copy-start.99 = (f32[128]{0:T(128)}, f32[128]{0:T(128)S(1)}, u32[]{:S(2)}) copy-start(f32[128]{0:T(128)S(1)} %broadcast_multiply_fusion.2) | copy-start | bytes 1540
  157.6 44.3 %copy-start.119 = (f32[128]{0:T(128)}, f32[128]{0:T(128)S(1)}, u32[]{:S(2)}) copy-start(f32[128]{0:T(128)S(1)} %multiply_reduce_fusion.7) | copy-start | bytes 1540
  157.7 44.3 %copy-start.104 = (f32[128]{0:T(128)}, f32[128]{0:T(128)S(1)}, u32[]{:S(2)}) copy-start(f32[128]{0:T(128)S(1)} %fusion.49) | copy-start | bytes 1540
  174.2 30.0 %copy-start.62 = (bf16[1152,768]{1,0:T(8,128)(2,1)S(1)}, bf16[1152,768]{1,0:T(8,128)(2,1)}, u32[]{:S(2)}) copy-start(bf16[1152,768]{1,0:T(8,128)(2,1)} %all-gather.7.cloned.1.call-done) | copy-start | bytes 5308420
  202.0 5.2 collective-permute-start.4
  206.0 21.3 %collective-permute-start.5 = (bf16[768,384]{1,0:T(8,128)(2,1)}, bf16[768,384]{1,0:T(8,128)(2,1)}, u32[]{:S(2)}, u32[]{:S(2)}) collective-permute-start(bf16[768,384]{1,0:T(8,128)(2,1)} %bitcast.46), channel_id=1, source_target_pairs={{0,1},{1,0},{2,3},{3,2},{4,5},{5,4},{6,7},{7,6},{8,9},{9,8},{10,11... | collective-permute-start | bytes 1769480 | tf_op jit(solution)/shard_map/ppermute | solution.py:47
  215.3 14.3 %copy-start.35 = (bf16[2048,64]{1,0:T(8,128)(2,1)}, bf16[2048,64]{1,0:T(8,128)(2,1)S(1)}, u32[]{:S(2)}) copy-start(bf16[2048,64]{1,0:T(8,128)(2,1)S(1)} %get-tuple-element.61.q_ref) | copy-start | bytes 786436
  252.6 6.0 collective-permute-start.6
  265.4 4.3 collective-permute-start.8
  269.0 5.9 collective-permute-start.7
  270.7 16.7 %all-to-all-start.9 = ((bf16[4,128,768]{2,1,0:T(8,128)(2,1)}), bf16[4,128,768]{2,1,0:T(8,128)(2,1)}, u32[]{:S(2)}, u32[]{:S(2)}) async-start(bf16[4,128,768]{2,1,0:T(8,128)(2,1)} %add_convert_fusion.1), calls=%async_computation.9 | async-start | bytes 1572864 | tf_op jit(solution)/shard_map/all_to_all | solution.py:39
  287.4 15.8 %all-to-all-start.8 = ((bf16[4,128,768]{2,1,0:T(8,128)(2,1)}), bf16[4,128,768]{2,1,0:T(8,128)(2,1)}, u32[]{:S(2)}, u32[]{:S(2)}) async-start(bf16[4,128,768]{2,1,0:T(8,128)(2,1)} %add_convert_fusion.2), calls=%async_computation.8 | async-start | bytes 1572864 | tf_op jit(solution)/shard_map/all_to_all | solution.py:39
  347.3 4.5 collective-permute-start.9
  353.4 27.4 %all-to-all-start.11 = ((bf16[8,128,768]{2,1,0:T(8,128)(2,1)}), bf16[8,128,768]{2,1,0:T(8,128)(2,1)}, u32[]{:S(2)}, u32[]{:S(2)}) async-start(bf16[8,128,768]{2,1,0:T(8,128)(2,1)} %fusion.2), calls=%async_computation.11 | async-start | bytes 3145728 | tf_op jit(solution)/shard_map/all_to_all | solution.py:39
  357.7 25.2 %copy-start.84 = (f32[768]{0:T(1024)S(1)}, f32[768]{0:T(1024)}, u32[]{:S(2)}) copy-start(f32[768]{0:T(1024)} %get-tuple-element.123) | copy-start | bytes 9220
  357.7 25.2 %copy-start.100 = (f32[128]{0:T(128)S(1)}, f32[128]{0:T(128)}, u32[]{:S(2)}) copy-start(f32[128]{0:T(128)} %copy-done.99) | copy-start | bytes 1540
  357.7 25.2 %copy-start.105 = (f32[128]{0:T(128)S(1)}, f32[128]{0:T(128)}, u32[]{:S(2)}) copy-start(f32[128]{0:T(128)} %copy-done.104) | copy-start | bytes 1540
  357.7 25.4 %copy-start.120 = (f32[128]{0:T(128)S(1)}, f32[128]{0:T(128)}, u32[]{:S(2)}) copy-start(f32[128]{0:T(128)} %copy-done.119) | copy-start | bytes 1540
  357.7 100.3 %reduce-scatter.5.cloned.1.call-start = ((), (), s32[]{:S(2)}) async-start(), calls=%async_computation.23 | async-start | bytes 663552 | tf_op jit(solution)/shard_map/reduce_scatter | solution.py:560
  357.9 25.5 %copy-start.115 = (f32[128]{0:T(128)S(1)}, f32[128]{0:T(128)}, u32[]{:S(2)}) copy-start(f32[128]{0:T(128)} %copy-done.114) | copy-start | bytes 1540
  386.8 99.0 %reduce-scatter.3.cloned.1.call-start = ((), (), s32[]{:S(2)}) async-start(), calls=%async_computation.22 | async-start | bytes 2654208 | tf_op jit(solution)/shard_map/reduce_scatter | solution.py:419
  403.0 10.1 %collective-permute-start.10 = (bf16[4,128,768]{2,1,0:T(8,128)(2,1)}, bf16[4,128,768]{2,1,0:T(8,128)(2,1)}, u32[]{:S(2)}, u32[]{:S(2)}) collective-permute-start(bf16[4,128,768]{2,1,0:T(8,128)(2,1)} %all_to_all.107), channel_id=1, source_target_pairs={{0,1},{1,0},{2,3},{3,2},{4,5},{5,4},{6,7},{7,6},{8,9},{9,8},{10,11... | collective-permute-start | bytes 2359304 | tf_op jit(solution)/shard_map/ppermute | solution.py:47
  418.7 2.4 collective-permute-start.11
  421.2 15.5 %copy-start.42 = (f32[128,768]{1,0:T(8,128)S(1)}, f32[128,768]{1,0:T(8,128)}, u32[]{:S(2)}) copy-start(f32[128,768]{1,0:T(8,128)} %copy-done.41) | copy-start | bytes 1179652
  421.2 15.5 %copy-start.98 = (f32[128]{0:T(128)S(1)}, f32[128]{0:T(128)}, u32[]{:S(2)}) copy-start(f32[128]{0:T(128)} %copy-done.97) | copy-start | bytes 1540
  421.2 15.5 %copy-start.103 = (f32[128]{0:T(128)S(1)}, f32[128]{0:T(128)}, u32[]{:S(2)}) copy-start(f32[128]{0:T(128)} %copy-done.102) | copy-start | bytes 1540
  421.2 16.2 %copy-start.118 = (f32[128]{0:T(128)S(1)}, f32[128]{0:T(128)}, u32[]{:S(2)}) copy-start(f32[128]{0:T(128)} %copy-done.117) | copy-start | bytes 1540
  442.8 14.0 %all-to-all-start.14 = ((bf16[16,128,64]{1,2,0:T(8,128)(2,1)}), bf16[16,128,64]{1,2,0:T(8,128)(2,1)}, u32[]{:S(2)}, u32[]{:S(2)}) async-start(bf16[16,128,64]{1,2,0:T(8,128)(2,1)} %concatenate.94), calls=%async_computation.14 | async-start | bytes 524288 | tf_op jit(solution)/shard_map/all_to_all | solution.py:39
  485.8 33.5 %all-to-all-start.15 = ((bf16[8,192,768]{2,1,0:T(8,128)(2,1)}), bf16[8,192,768]{2,1,0:T(8,128)(2,1)}, u32[]{:S(2)}, u32[]{:S(2)}) async-start(bf16[8,192,768]{2,1,0:T(8,128)(2,1)} %shard_map.276), calls=%async_computation.17 | async-start | bytes 4718592 | tf_op jit(solution)/shard_map/all_to_all | solution.py:39
  490.3 122.5 %all-gather.9.cloned.1.call-start = ((), (), s32[]{:S(2)}) async-start(), calls=%async_computation.25 | async-start | bytes 2506752 | tf_op jit(solution)/shard_map/all_gather | solution.py:566
  507.2 15.2 %copy-start.75 = (bf16[192,768]{1,0:T(8,128)(2,1)S(1)}, bf16[192,768]{1,0:T(8,128)(2,1)}, u32[]{:S(2)}) copy-start(bf16[192,768]{1,0:T(8,128)(2,1)} %reduce-scatter.3.cloned.1.call-done) | copy-start | bytes 884740
  507.2 15.3 %copy-start.81 = (bf16[48,768]{1,0:T(8,128)(2,1)S(1)}, bf16[48,768]{1,0:T(8,128)(2,1)}, u32[]{:S(2)}) copy-start(bf16[48,768]{1,0:T(8,128)(2,1)} %reduce-scatter.5.cloned.1.call-done) | copy-start | bytes 221188
  522.4 121.4 %all-gather.11.cloned.1.call-start = ((), (), s32[]{:S(2)}) async-start(), calls=%async_computation.26 | async-start | bytes 3760128 | tf_op jit(solution)/shard_map/all_gather | solution.py:565
  523.2 5.1 collective-permute-start.12
  529.9 30.6 %all-to-all-start.16 = ((bf16[8,128,768]{2,1,0:T(8,128)(2,1)}), bf16[8,128,768]{2,1,0:T(8,128)(2,1)}, u32[]{:S(2)}, u32[]{:S(2)}) async-start(bf16[8,128,768]{2,1,0:T(8,128)(2,1)} %fusion.1), calls=%async_computation.18 | async-start | bytes 3145728 | tf_op jit(solution)/shard_map/all_to_all | solution.py:39
  560.5 16.9 %all-to-all-start.18 = ((bf16[16,16,768]{2,1,0:T(8,128)(2,1)}), bf16[16,16,768]{2,1,0:T(8,128)(2,1)S(1)}, u32[]{:S(2)}, u32[]{:S(2)}) async-start(bf16[16,16,768]{2,1,0:T(8,128)(2,1)} %pad.6.clone), calls=%async_computation.20 | async-start | bytes 786432 | tf_op jit(solution)/shard_map/all_to_all | solution.py:39
  577.5 13.2 %all-to-all-start.17 = ((bf16[8,48,768]{2,1,0:T(8,128)(2,1)}), bf16[8,48,768]{2,1,0:T(8,128)(2,1)S(1)}, u32[]{:S(2)}, u32[]{:S(2)}) async-start(bf16[8,48,768]{2,1,0:T(8,128)(2,1)} %shard_map.278), calls=%async_computation.19 | async-start | bytes 1179648 | tf_op jit(solution)/shard_map/all_to_all | solution.py:39
  581.1 30.0 %copy-start.49 = (f32[128,768]{1,0:T(8,128)S(1)}, f32[128,768]{1,0:T(8,128)}, u32[]{:S(2)}) copy-start(f32[128,768]{1,0:T(8,128)} %add_add_fusion.5) | copy-start | bytes 1179652
  581.1 30.0 %copy-start.53 = (f32[128,768]{1,0:T(8,128)S(1)}, f32[128,768]{1,0:T(8,128)}, u32[]{:S(2)}) copy-start(f32[128,768]{1,0:T(8,128)} %copy-done.52) | copy-start | bytes 1179652
  581.1 30.0 %copy-start.109 = (f32[128]{0:T(128)S(1)}, f32[128]{0:T(128)}, u32[]{:S(2)}) copy-start(f32[128]{0:T(128)} %copy-done.108) | copy-start | bytes 1540
  608.3 4.4 collective-permute-start.13
  (97 other events, 272.4 us)
Sparse Core Ops, SparseCore 0:
  132.8 41.2 all-gather.6
  387.0 32.1 reduce-scatter.4
  422.1 63.6 reduce-scatter.2
  522.5 67.4 all-gather.8
  592.9 50.8 all-gather.10

commit v4 on v3

--- a/solution.py
+++ b/solution.py
@@ -192,7 +192,7 @@
 
 SMEM = pl.BlockSpec(memory_space=pltpu.SMEM)
 WHOLE = pl.BlockSpec()
-VMEM_BYTES = 48 * 2**20
+VMEM_BYTES = 60 * 2**20
 
 
 def attend(arrive_pos, ctx_pos, own, other, weight, shift, norm=None):
@@ -237,7 +237,7 @@
 
 
 UPS, DOWNS, OUTS, FIRST = 0, 48, 96, 192
-HEADS, SMALL, SECOND = 0, 32, 48
+HEADS, SMALL, SECOND = 0, 64, 80
 BOTH_ROWS = ((0,), (0,))
 
 
@@ -266,8 +266,8 @@
     )(*parts)
 
 
-def second_grads_kernel(head, own_ref, other_ref, arrive_ref, sums_ref, hidden_sum_ref, *rest):
-    vector_refs, out_ref = rest[:-1], rest[-1]
+def second_grads_kernel(layer, head, own_ref, other_ref, arrive_ref, sums_ref, hidden_sum_ref, *rest):
+    vector_refs, prior_refs, out_ref = rest[:6], rest[6:-1], rest[-1]
     half = LEN // 2
     heads = dot(own_ref[...], arrive_ref[:half, :], BOTH_ROWS) + dot(other_ref[...], arrive_ref[half:, :], BOTH_ROWS)
     heads = heads.astype(BF16)
@@ -280,18 +280,23 @@
     for owner in range(S):
         for part in range(3):
             first = owner * 96 + part * 32
-            out_ref[owner, HEADS:SMALL, part * 256 : (part + 1) * 256] = heads[first : first + 32, :]
+            out_ref[owner, layer * 32 : (layer + 1) * 32, part * 256 : (part + 1) * 256] = heads[first : first + 32, :]
         mine = jnp.concatenate([member[:, owner * 96 : (owner + 1) * 96] for member in vectors], axis=1)
         hidden = jnp.concatenate(
             [hidden_sum_ref[:, owner * 48 : (owner + 1) * 48], jnp.zeros((1, D - 48), F32)], axis=1
         )
-        block = jnp.where(row == 0, mine, jnp.where(row == 1, hidden, 0.0))
+        block = jnp.where(row == 2 * layer, mine, jnp.where(row == 2 * layer + 1, hidden, 0.0))
+        for prior_ref in prior_refs:
+            block = block + prior_ref[owner, SMALL:SECOND, :].astype(F32)
+            out_ref[owner, 32:SMALL, :] = prior_ref[owner, 32:SMALL, :]
+        if not prior_refs:
+            out_ref[owner, :32, :] = jnp.zeros((32, D), BF16)
         out_ref[owner, SMALL:SECOND, :] = block.astype(BF16)
 
 
-def second_grads(head, *parts):
+def second_grads(layer, head, *parts):
     return pl.pallas_call(
-        second_grads_kernel,
+        functools.partial(second_grads_kernel, layer),
         out_shape=jax.ShapeDtypeStruct((S, SECOND, D), BF16),
         in_specs=[SMEM] + [WHOLE] * len(parts),
         out_specs=WHOLE,
@@ -300,44 +305,43 @@
     )(head, *parts)
 
 
-def unpack_kernel(slots, first_ref, second_ref, last_ref, qkv_ref, out_ref, up_ref, down_ref, up_shift_ref, *vector_refs):
-    layers = (
-        ((first_ref, 0, lambda place: place), (second_ref, 0, lambda place: slots[place])),
-        ((last_ref, 0, lambda place: place), (last_ref, OUTS, lambda place: place)),
-    )
-    for layer, (wide, late) in enumerate(layers):
-        def rows(source, place, start, end):
-            ref, base, slot = source
-            return ref[slot(place), base + start : base + end, :].astype(F32)
+def unpack_kernel(slots, late_ref, first_ref, last_ref, qkv_ref, out_ref, up_ref, down_ref, up_shift_ref, *vector_refs):
+    for layer, wide_ref in enumerate((first_ref, last_ref)):
+        def late(place, start, end):
+            return late_ref[slots[place], start:end, :].astype(F32)
+
+        def wide(place, start, end, wide_ref=wide_ref):
+            return wide_ref[place, start:end, :].astype(F32)
 
         for head in range(H):
-            block = rows(late, head, HEADS, SMALL)
+            block = late(head, layer * 32, (layer + 1) * 32)
             for part in range(3):
                 for kind in range(3):
                     lane = part * 256 + kind * HD
                     column = kind * D + head * HD
                     qkv_ref[layer, part * 32 : (part + 1) * 32, column : column + HD] = block[:, lane : lane + HD]
         for rank in range(8):
-            block = rows(wide, rank, UPS, DOWNS) + rows(wide, rank + 8, UPS, DOWNS)
+            block = wide(rank, UPS, DOWNS) + wide(rank + 8, UPS, DOWNS)
             for part in range(2):
                 for owner in range(S):
                     lane = part * 384 + owner * 48
                     column = owner * 384 + rank * 48
                     up_ref[layer, part * 48 : (part + 1) * 48, column : column + 48] = block[:, lane : lane + 48]
-            block = rows(wide, rank, DOWNS, OUTS) + rows(wide, rank + 8, DOWNS, OUTS)
+            block = wide(rank, DOWNS, OUTS) + wide(rank + 8, DOWNS, OUTS)
             down_ref[layer, rank * 48 : (rank + 1) * 48, :] = block
-            small = rows(late, rank, SMALL, SECOND) + rows(late, rank + 8, SMALL, SECOND)
-            up_shift_ref[layer : layer + 1, rank * 48 : (rank + 1) * 48] = small[1:2, :48]
-            vectors = small[0:1, :] if rank == 0 else vectors + small[0:1, :]
+            small = late(rank, SMALL, SECOND) + late(rank + 8, SMALL, SECOND)
+            up_shift_ref[layer : layer + 1, rank * 48 : (rank + 1) * 48] = small[2 * layer + 1 : 2 * layer + 2, :48]
+            mine = small[2 * layer : 2 * layer + 1, :]
+            vectors = mine if rank == 0 else vectors + mine
         for member, ref in enumerate(vector_refs):
             ref[layer : layer + 1, :] = vectors[:, member * 96 : (member + 1) * 96]
     for place in range(C):
-        small = second_ref[slots[place], SMALL:SECOND, :].astype(F32)
+        small = late_ref[slots[place], SMALL:SECOND, :].astype(F32)
         for layer in range(LAYERS):
-            out_ref[layer, place * 6 : (place + 1) * 6, :] = small[2 + 6 * layer : 8 + 6 * layer, :]
-
-
-def unpack(slots, first, second, last):
+            out_ref[layer, place * 6 : (place + 1) * 6, :] = small[4 + 6 * layer : 10 + 6 * layer, :]
+
+
+def unpack(slots, late, first, last):
     shapes = [(96, 3 * D), (96, D), (96, FF), (384, D), (384,)] + [(96,)] * 8
     return pl.pallas_call(
         unpack_kernel,
@@ -346,7 +350,7 @@
         out_specs=(WHOLE,) * len(shapes),
         compiler_params=pltpu.CompilerParams(vmem_limit_bytes=VMEM_BYTES),
         cost_estimate=pl.CostEstimate(flops=10**6, bytes_accessed=14 * 10**6, transcendentals=0),
-    )(slots, first, second, last)
+    )(slots, late, first, last)
 
 
 def join_cores(core, own, other, axis):
@@ -363,6 +367,7 @@
         mixed_head, queries, keys, values, own, other = attend(
             arrive_pos, ctx_pos, *gathered, head_weight, head_shift, (gain_one, bias_one)
         )
+        mixed_head, layer_rows = lax.optimization_barrier((mixed_head, layer_rows))
     else:
         normed = layer_norm(flowing, gain_one, bias_one).astype(BF16)
         normed, layer_rows = lax.optimization_barrier((normed, layer_rows))
@@ -387,7 +392,7 @@
     return output, saved, carried, (head_weight, out_full, up_part, down_part)
 
 
-def backward_layer(grad_out, down_all, saved, params, small, places, head, last):
+def backward_layer(grad_out, down_all, saved, params, small, places, head, layer, prior, spread):
     arrive_pos, ctx_pos = places
     head_weight, out_full, up_part, down_part = params
     unused, vectors, unused = small
@@ -400,7 +405,8 @@
     activated_grad = dot(down_all, down_part, ((1,), (1,)))
     unused, gelu_back = jax.vjp(lambda inner: jax.nn.gelu(inner, approximate=True), hidden)
     hidden_grad = gelu_back(activated_grad)[0].astype(BF16)
-    second_grad = scatter_x(dot(hidden_grad, up_part, ((1,), (1,))).reshape(8, TOK, D))
+    second_part = dot(hidden_grad, up_part, ((1,), (1,))).reshape(8, TOK, D)
+    second_grad = scatter_x(second_part)
     up_shift_grad = jnp.sum(hidden_grad.astype(F32), axis=0, keepdims=True)
     unused, norm_back = jax.vjp(layer_norm, middle, gain_two, bias_two)
     middle_part, gain_two_grad, bias_two_grad = norm_back(second_grad)
@@ -412,20 +418,17 @@
     mixed_grad = jnp.concatenate([mixed_grad, jnp.zeros((C - H, TOK, HD), BF16)], axis=0)
     mixed_grad = exchange(mixed_grad, "ctx").reshape(LEN, HD)
     packed = first_grads(second_all, hidden_grad, activated, down_all, mixed, attended_in)
-    if last is not None:
-        mixed_grad, last, packed = lax.optimization_barrier((mixed_grad, last, packed))
-        owned = jnp.sum(exchange(packed, "shard").astype(F32), axis=0).astype(BF16)
-    else:
-        owned = lax.psum_scatter(packed.reshape(S * FIRST, D), "shard", scatter_dimension=0, tiled=True)
+    mixed_grad, packed = lax.optimization_barrier((mixed_grad, packed))
+    owned = jnp.sum(exchange(packed, "shard").astype(F32), axis=0).astype(BF16)
     to_arrive, near, far, sums = attend_back(
         arrive_pos, ctx_pos, queries, keys, values, mixed_grad, head_weight
     )
-    if last is not None:
-        near, far, owned = lax.optimization_barrier((near, far, owned))
+    near, far, owned, spread = lax.optimization_barrier((near, far, owned, spread))
     normed_grad = scatter(near.reshape(8, TOK, D), far.reshape(8, TOK, D), CHIP_GROUPS)
     unused, first_back = jax.vjp(layer_norm, flowing, gain_one, bias_one)
     flowing_part, gain_one_grad, bias_one_grad = first_back(normed_grad)
     late = second_grads(
+        layer,
         head,
         own,
         other,
@@ -438,8 +441,9 @@
         gain_two_grad,
         bias_two_grad,
         down_shift_grad,
-    )
-    return middle_grad + flowing_part, owned, late, last
+        *prior,
+    )
+    return middle_grad + flowing_part, owned, late, spread
 
 
 def shards(
@@ -506,12 +510,12 @@
             vectors.reshape(2, D),
             up_bias.reshape(1, D),
             jnp.zeros((13, D), BF16),
-            layer_pieces[0],
         ],
         axis=0,
     )
     gathered = spread_to(packed, S, "shard")
-    layer_rows = [gathered[:, 64:], lax.all_gather(layer_pieces[1], "shard", axis=0)]
+    gathered, first_piece = lax.optimization_barrier((gathered, layer_pieces[0]))
+    layer_rows = [spread_to(first_piece, S, "shard"), lax.all_gather(layer_pieces[1], "shard", axis=0)]
     head_weights = gathered[:, :48].reshape(S, LAYERS, 96, 3 * HD)
     vectors = gathered[:, 48:50].reshape(S, 8, LAYERS, 96).transpose(2, 1, 0, 3).reshape(LAYERS, 8, D)
     vectors = vectors.astype(F32)
@@ -553,27 +557,25 @@
     result = flowing.astype(BF16).reshape(states.shape)
     grad_flow = cotangent.reshape(TOK, D).astype(F32)
     held = jnp.where(place < H, place, -1).reshape(1)
-    grad_flow, first_last, late, unused = backward_layer(
-        grad_flow, carried, saved_all[1], all_params[1], smalls[1], places, held, None
+    grad_flow, owned_last, late, unused = backward_layer(
+        grad_flow, carried, saved_all[1], all_params[1], smalls[1], places, held, 1, (), ()
     )
     grad_flow, late = lax.optimization_barrier((grad_flow, late))
-    late_last = lax.psum_scatter(late.reshape(S * SECOND, D), "shard", scatter_dimension=0, tiled=True)
-    grad_flow, first, late, last = backward_layer(
-        grad_flow, None, saved_all[0], all_params[0], smalls[0], places, held, (first_last, late_last)
-    )
-    first_last, late_last = last
-    every_last = lax.all_gather(jnp.concatenate([first_last[:OUTS], late_last], axis=0), "ctx", axis=0)
-    every_first = lax.all_gather(first[:OUTS], "ctx", axis=0)
-    outs = jnp.stack([first[OUTS:], first_last[OUTS:]]).reshape(LAYERS, C, 6, D)
+    every_last = lax.all_gather(owned_last[:OUTS], "ctx", axis=0)
+    grad_flow, owned, late, every_last = backward_layer(
+        grad_flow, None, saved_all[0], all_params[0], smalls[0], places, held, 0, (late,), every_last
+    )
+    every_first = lax.all_gather(owned[:OUTS], "ctx", axis=0)
+    outs = jnp.stack([owned[OUTS:], owned_last[OUTS:]]).reshape(LAYERS, C, 6, D)
     outs = outs.transpose(1, 0, 2, 3).reshape(C, 12, D)
     outs = exchange(jnp.pad(outs, ((0, 0), (0, 4), (0, 0))), "ctx").astype(F32)
     outs = jnp.sum(outs, axis=0)[:12].astype(BF16)
     late = jnp.sum(exchange(late, "shard").astype(F32), axis=0).astype(BF16)
-    late = jnp.concatenate([late[: SMALL + 2], outs, jnp.zeros((2, D), BF16)], axis=0)
+    late = jnp.concatenate([late[: SMALL + 4], outs], axis=0)
     every_late = jnp.concatenate(gather_ctx(late), axis=0)
     places_of = jnp.arange(C, dtype=jnp.int32)
     slots = places_of // 2 + 8 * (places_of % 2 != core).astype(jnp.int32)
-    qkv, outs, ups, downs, hiddens, *vectors = unpack(slots, every_first, every_late, every_last)
+    qkv, outs, ups, downs, hiddens, *vectors = unpack(slots, every_late, every_first, every_last)
     return (
         result,
         grad_flow.astype(BF16).reshape(states.shape),

time: 666 us -> 601 us (0.902)
  waiting for transfers between devices: 223 us -> 163 us
  Pallas kernels: 60 us -> 76.9 us
  local copies, waits for them, and re-layouts: 63.9 us -> 52.1 us
  starting transfers between devices: 71.3 us -> 79.4 us
  blocking collectives: 163 us -> 155 us
  other arithmetic: 39.9 us -> 32.1 us
    all_gather x2, waiting for transfers between devices: 30.9 us -> 0.02 us  [the longest x1 0.02 us: shards(): every_last = lax.all_gather(owned_last[:OUTS], 'ctx', axis=0)]
    reduce_scatter x2 -> x0, waiting for transfers between devices: 27.8 us -> none  [the longest x1 27.7 us: backward_layer(): lax.psum_scatter(packed.reshape(S * FIRST, D), 'shard', scatter_dimension...]
    unnamed x272 -> x186, local copies, waits for them, and re-layouts: 29.5 us -> 7.21 us
    all_to_all x10 -> x9, blocking collectives: 163 us -> 155 us  [exchange(): lax.all_to_all(parts, axis, 0, 0, tiled=True, axis_index_groups=groups)]
    all_to_all x10 -> x13, starting transfers between devices: 51.9 us -> 59 us  [exchange(): lax.all_to_all(parts, axis, 0, 0, tiled=True, axis_index_groups=groups)]
    all_to_all x10 -> x13, waiting for transfers between devices: 135 us -> 137 us  [exchange(): lax.all_to_all(parts, axis, 0, 0, tiled=True, axis_index_groups=groups)]
  transfers between devices with their start and end apart: 29 -> 30, of which waited for: 19 -> 22; matrix products, arithmetic and copies ran while one was open for 10% -> 10% of each run, Pallas kernels for 6% -> 11%
where the time goes in v4:
time: 601 us; the launch traced here: 596 us
  waiting for transfers between devices  163 us (27%)
  blocking collectives  155 us (26%)
  starting transfers between devices  79.4 us (13%)
  Pallas kernels  76.9 us (13%)
  local copies, waits for them, and re-layouts  52.1 us (9%)
  other arithmetic  32.1 us (5%)
  matrix products  22.4 us (4%)
  between operations  15.4 us (3%)
    all_to_all x9, blocking collectives, exchange(): lax.all_to_all(parts, axis, 0, 0, tiled=True, axis_index_groups=groups)  155 us
    all_to_all x13, waiting for transfers between devices, exchange(): lax.all_to_all(parts, axis, 0, 0, tiled=True, axis_index_groups=groups)  137 us
    all_to_all x13, starting transfers between devices, exchange(): lax.all_to_all(parts, axis, 0, 0, tiled=True, axis_index_groups=groups)  59 us
    pallas_call x2, Pallas kernels, attend_back(): pl.pallas_call(attend_back_kernel, out_shape=(jax.ShapeDtypeStruct((LEN,...  29.4 us
    dot_general x13, matrix products, dot(): lax.dot_general(left, right, (dims, ((), ())), preferred_element_type=F32)  22.4 us
    ppermute x14, starting transfers between devices, swap_core(): return lax.ppermute(part, 'ctx', SWAP)  20.1 us
    pallas_call x2, Pallas kernels, attend(): pl.pallas_call(functools.partial(attend_kernel, fresh), out_shape=outs, i...  18.9 us
    ppermute x14, waiting for transfers between devices, swap_core(): return lax.ppermute(part, 'ctx', SWAP)  13.9 us
  transfers between devices with their start and end apart: 30, of which 22 were waited for; matrix products, arithmetic and copies ran while one was open for 10% of the time, Pallas kernels for 11%

profile of v4, /device:TPU:1, one launch (start us, length us, event | category | flops | bytes accessed | tf_op | source)
XLA Modules:
  0.0 596.1 jit_solution(13798367827870871572)
XLA Ops:
  7.2 2.3 broadcast_in_dim.50
  9.6 7.6 %all-to-all-start = ((bf16[8,128,768]{2,1,0:T(8,128)(2,1)}), bf16[8,128,768]{2,1,0:T(8,128)(2,1)}, u32[]{:S(2)}, u32[]{:S(2)}) async-start(bf16[8,128,768]{2,1,0:T(8,128)(2,1)} %broadcast_in_dim.50), calls=%async_computation | async-start | bytes 3145728 | tf_op jit(solution)/shard_map/all_to_all | solution.py:39
  23.1 17.1 %all-to-all-done = bf16[8,128,768]{2,1,0:T(8,128)(2,1)} async-done(((bf16[8,128,768]{2,1,0:T(8,128)(2,1)}), bf16[8,128,768]{2,1,0:T(8,128)(2,1)}, u32[]{:S(2)}, u32[]{:S(2)}) %all-to-all-start) | async-done | bytes 1572896 | tf_op jit(solution)/shard_map/all_to_all | solution.py:39
  41.2 5.1 all-to-all-start.1
  49.1 8.7 %all-to-all-done.1 = bf16[8,64,768]{2,1,0:T(8,128)(2,1)S(1)} async-done(((bf16[8,64,768]{2,1,0:T(8,128)(2,1)}), bf16[8,64,768]{2,1,0:T(8,128)(2,1)S(1)}, u32[]{:S(2)}, u32[]{:S(2)}) %all-to-all-start.1) | async-done | bytes 786464 | tf_op jit(solution)/shard_map/all_to_all | solution.py:39
  59.3 3.8 all-to-all-start.2
  68.2 10.3 %shard_map.271 = (bf16[2048,64]{1,0:T(8,128)(2,1)}, bf16[2048,64]{1,0:T(8,128)(2,1)}, bf16[2048,64]{1,0:T(8,128)(2,1)}, bf16[2048,64]{1,0:T(8,128)(2,1)}, bf16[1...) custom-call(s32[32]{0:T(128)} %reshape.362.arrive_pos, s32[32]{0:T(128)} %reshape.363.ctx_pos, ...), custom_call_target="tpu_custom_call" | custom-call | flops 2000000000 | bytes 5000000 | tf_op jit(solution)/shard_map/pallas_call | solution.py:206
  78.5 5.7 all-to-all-done.2
  85.2 3.3 collective-permute-start.1
  89.7 12.5 %all_to_all.110 = bf16[16,128,64]{1,2,0:T(8,128)(2,1)S(1)} all-to-all(bf16[16,128,64]{1,2,0:T(8,128)(2,1)S(1)} %copy.69), channel_id=1, replica_groups=mesh['shard'=8,'ctx'=16] {'ctx'}, dimensions={0} | all-to-all | bytes 524288 | tf_op jit(solution)/shard_map/all_to_all | solution.py:39
  102.3 2.3 fusion.76
  105.4 13.7 %all_to_all.111 = bf16[4,128,768]{2,1,0:T(8,128)(2,1)S(1)} all-to-all(bf16[4,128,768]{2,1,0:T(8,128)(2,1)S(1)} %broadcast_in_dim.56), channel_id=1, replica_groups={{0,2,4,6},{1,3,5,7},{8,10,12,14},{9,11,13,15},{16,18,20,22},{17,19,21,2..., dimensions={0} | all-to-all | bytes 1572864 | tf_op jit(solution)/shard_map/all_to_all | solution.py:39
  119.2 2.1 collective-permute-start.2
  129.6 2.4 multiply_convert_fusion.1
  133.3 2.1 collective-permute-done.3
  135.6 14.4 %all_to_all.112 = bf16[4,128,768]{2,1,0:T(8,128)(2,1)S(1)} all-to-all(bf16[4,128,768]{2,1,0:T(8,128)(2,1)S(1)} %add_convert_fusion.3), channel_id=1, replica_groups={{0,2,4,6},{1,3,5,7},{8,10,12,14},{9,11,13,15},{16,18,20,22},{17,19,21,2..., dimensions={0} | all-to-all | bytes 1572864 | tf_op jit(solution)/shard_map/all_to_all | solution.py:39
  150.8 12.0 %all-gather.7.cloned.1.call-done = bf16[1152,768]{1,0:T(8,128)(2,1)} async-done(((bf16[144,768]{1,0:T(8,128)(2,1)}), bf16[1152,768]{1,0:T(8,128)(2,1)}) %all-gather.7.cloned.1.call-update) | async-done | bytes 1769488 | tf_op jit(solution)/shard_map/all_gather | solution.py:518
  163.0 27.7 %all_to_all.113 = bf16[8,128,768]{2,1,0:T(8,128)(2,1)S(1)} all-to-all(bf16[8,128,768]{2,1,0:T(8,128)(2,1)S(1)} %broadcast_in_dim.57), channel_id=1, replica_groups={{0,2,4,6,8,10,12,14},{1,3,5,7,9,11,13,15},{16,18,20,22,24,26,28,30},{17..., dimensions={0} | all-to-all | bytes 3145728 | tf_op jit(solution)/shard_map/all_to_all | solution.py:39
  190.7 2.2 collective-permute-start.4
  197.1 8.6 %shard_map.272 = (bf16[2048,64]{1,0:T(8,128)(2,1)}, bf16[2048,64]{1,0:T(8,128)(2,1)}, bf16[2048,64]{1,0:T(8,128)(2,1)}, bf16[2048,64]{1,0:T(8,128)(2,1)}) custom-call(s32[32]{0:T(128)} %reshape.362.arrive_pos, s32[32]{0:T(128)} %reshape.363.ctx_pos, bf16[1024,768]{1,0:T(8,128)(2,1)} %bitcast.159, bf16[1024,768]{1,0:T(8,128)(2,1)} %bitcast.175, ...), custom_call_target="tpu_custom_call" | custom-call | flops 2000000000 | bytes 5000000 | tf_op jit(solution)/shard_map/pallas_call | solution.py:206
  207.0 11.6 %all_to_all.114 = bf16[16,128,64]{1,2,0:T(8,128)(2,1)S(1)} all-to-all(bf16[16,128,64]{1,2,0:T(8,128)(2,1)S(1)} %copy.70), channel_id=1, replica_groups=mesh['shard'=8,'ctx'=16] {'ctx'}, dimensions={0} | all-to-all | bytes 524288 | tf_op jit(solution)/shard_map/all_to_all | solution.py:39
  218.6 2.3 fusion.77
  221.6 22.3 %all_to_all.115 = bf16[4,256,768]{2,1,0:T(8,128)(2,1)S(1)} all-to-all(bf16[4,256,768]{2,1,0:T(8,128)(2,1)S(1)} %broadcast_in_dim.58), channel_id=1, replica_groups={{0,2,4,6},{1,3,5,7},{8,10,12,14},{9,11,13,15},{16,18,20,22},{17,19,21,2..., dimensions={0} | all-to-all | bytes 3145728 | tf_op jit(solution)/shard_map/all_to_all | solution.py:39
  244.0 2.3 collective-permute-start.6
  252.9 2.6 convert_reduce_fusion.9
  260.8 3.5 all-to-all-start.10
  265.7 2.2 add_convert_fusion.2
  267.9 8.6 %all-to-all-done.10 = bf16[4,128,768]{2,1,0:T(8,128)(2,1)S(1)} async-done(((bf16[4,128,768]{2,1,0:T(8,128)(2,1)}), bf16[4,128,768]{2,1,0:T(8,128)(2,1)S(1)}, u32[]{:S(2)}, u32[]{:S(2)}) %all-to-all-start.10) | async-done | bytes 786464 | tf_op jit(solution)/shard_map/all_to_all | solution.py:39
  276.5 3.5 all-to-all-start.9
  283.1 8.2 %all-to-all-done.9 = bf16[4,128,768]{2,1,0:T(8,128)(2,1)S(1)} async-done(((bf16[4,128,768]{2,1,0:T(8,128)(2,1)}), bf16[4,128,768]{2,1,0:T(8,128)(2,1)S(1)}, u32[]{:S(2)}, u32[]{:S(2)}) %all-to-all-start.9) | async-done | bytes 786464 | tf_op jit(solution)/shard_map/all_to_all | solution.py:39
  293.8 2.3 convolution_convert_fusion.1
  297.0 5.2 all-to-all-start.11
  303.0 5.8 shard_map.273
  308.7 2.2 all-to-all-done.11
  311.9 3.8 all-to-all-start.12
  315.7 14.7 %shard_map.274 = (bf16[2048,256]{1,0:T(8,128)(2,1)}, bf16[1024,768]{1,0:T(8,128)(2,1)}, bf16[1024,768]{1,0:T(8,128)(2,1)}, f32[1,192]{1,0:T(1,128)}) custom-call(s32[32]{0:T(128)} %reshape.362.arrive_pos, s32[32]{0:T(128)} %reshape.363.ctx_pos, bf16[2048,64]{1,0:T(8,128)(2,1)} %get-tuple-element.73.q_ref, bf16[2048,64]{1,0:T(8,128)(2,1)} %get-tuple-element.74.k_ref, ...), custom_call_target="tpu_custom_call" | custom-call | flops 4000000000 | bytes 5000000 | tf_op jit(solution)/shard_map/pallas_call | solution.py:218
  330.4 14.3 %all-to-all-done.12 = bf16[8,192,768]{2,1,0:T(8,128)(2,1)S(1)} async-done(((bf16[8,192,768]{2,1,0:T(8,128)(2,1)}), bf16[8,192,768]{2,1,0:T(8,128)(2,1)S(1)}, u32[]{:S(2)}, u32[]{:S(2)}) %all-to-all-start.12) | async-done | bytes 2359328 | tf_op jit(solution)/shard_map/all_to_all | solution.py:39
  347.7 3.2 collective-permute-done.9
  350.9 3.0 fusion.2
  353.9 4.6 all-to-all-start.13
  361.6 20.0 %all-to-all-done.13 = bf16[8,128,768]{2,1,0:T(8,128)(2,1)S(1)} async-done(((bf16[8,128,768]{2,1,0:T(8,128)(2,1)}), bf16[8,128,768]{2,1,0:T(8,128)(2,1)S(1)}, u32[]{:S(2)}, u32[]{:S(2)}) %all-to-all-start.13) | async-done | bytes 1572896 | tf_op jit(solution)/shard_map/all_to_all | solution.py:39
  383.9 4.3 shard_map.275.rest_6_
  388.3 13.7 %all_to_all.116 = bf16[4,128,768]{2,1,0:T(8,128)(2,1)S(1)} all-to-all(bf16[4,128,768]{2,1,0:T(8,128)(2,1)S(1)} %broadcast_in_dim.128), channel_id=1, replica_groups={{0,2,4,6},{1,3,5,7},{8,10,12,14},{9,11,13,15},{16,18,20,22},{17,19,21,2..., dimensions={0} | all-to-all | bytes 1572864 | tf_op jit(solution)/shard_map/all_to_all | solution.py:39
  406.0 2.4 convert_reduce_fusion.8
  414.4 16.4 %all_to_all.117 = bf16[4,128,768]{2,1,0:T(8,128)(2,1)S(1)} all-to-all(bf16[4,128,768]{2,1,0:T(8,128)(2,1)S(1)} %add_convert_fusion), channel_id=1, replica_groups={{0,2,4,6},{1,3,5,7},{8,10,12,14},{9,11,13,15},{16,18,20,22},{17,19,21,2..., dimensions={0} | all-to-all | bytes 1572864 | tf_op jit(solution)/shard_map/all_to_all | solution.py:39
  432.9 2.2 convolution_convert_fusion
  436.1 4.8 all-to-all-start.16
  441.8 5.8 shard_map.276
  447.5 2.4 all-to-all-done.16
  450.9 4.0 all-to-all-start.17
  455.0 14.7 %shard_map.277 = (bf16[2048,256]{1,0:T(8,128)(2,1)}, bf16[1024,768]{1,0:T(8,128)(2,1)}, bf16[1024,768]{1,0:T(8,128)(2,1)}, f32[1,192]{1,0:T(1,128)}) custom-call(s32[32]{0:T(128)} %reshape.362.arrive_pos, s32[32]{0:T(128)} %reshape.363.ctx_pos, bf16[2048,64]{1,0:T(8,128)(2,1)} %get-tuple-element.85.q_ref, bf16[2048,64]{1,0:T(8,128)(2,1)} %get-tuple-element.86.k_ref, ...), custom_call_target="tpu_custom_call" | custom-call | flops 4000000000 | bytes 5000000 | tf_op jit(solution)/shard_map/pallas_call | solution.py:218
  469.7 14.1 %all-to-all-done.17 = bf16[8,192,768]{2,1,0:T(8,128)(2,1)S(1)} async-done(((bf16[8,192,768]{2,1,0:T(8,128)(2,1)}), bf16[8,192,768]{2,1,0:T(8,128)(2,1)S(1)}, u32[]{:S(2)}, u32[]{:S(2)}) %all-to-all-start.17) | async-done | bytes 2359328 | tf_op jit(solution)/shard_map/all_to_all | solution.py:39
  484.2 2.1 collective-permute-start.12
  486.3 3.2 collective-permute-done.12
  489.6 3.0 fusion.1
  492.6 4.4 all-to-all-start.18
  502.0 18.9 %all-to-all-done.18 = bf16[8,128,768]{2,1,0:T(8,128)(2,1)S(1)} async-done(((bf16[8,128,768]{2,1,0:T(8,128)(2,1)}), bf16[8,128,768]{2,1,0:T(8,128)(2,1)S(1)}, u32[]{:S(2)}, u32[]{:S(2)}) %all-to-all-start.18) | async-done | bytes 1572896 | tf_op jit(solution)/shard_map/all_to_all | solution.py:39
  520.9 5.0 all-to-all-start.20
  528.1 4.5 shard_map.278
  532.7 3.0 all-to-all-done.20
  535.7 3.6 all-to-all-start.19
  539.4 13.6 %all-to-all-done.19 = bf16[8,80,768]{2,1,0:T(8,128)(2,1)S(1)} async-done(((bf16[8,80,768]{2,1,0:T(8,128)(2,1)}), bf16[8,80,768]{2,1,0:T(8,128)(2,1)S(1)}, u32[]{:S(2)}, u32[]{:S(2)}) %all-to-all-start.19) | async-done | bytes 983072 | tf_op jit(solution)/shard_map/all_to_all | solution.py:39
  553.2 22.6 %all_to_all.118 = bf16[8,80,768]{2,1,0:T(8,128)(2,1)S(1)} all-to-all(bf16[8,80,768]{2,1,0:T(8,128)(2,1)S(1)} %broadcast_in_dim.136), channel_id=1, replica_groups={{0,2,4,6,8,10,12,14},{1,3,5,7,9,11,13,15},{16,18,20,22,24,26,28,30},{17..., dimensions={0} | all-to-all | bytes 1966080 | tf_op jit(solution)/shard_map/all_to_all | solution.py:39
  581.2 8.2 %shard_map.279 = (f32[2,96,2304]{2,1,0:T(8,128)}, f32[2,96,768]{2,1,0:T(8,128)}, f32[2,96,3072]{2,1,0:T(8,128)}, f32[2,384,768]{2,1,0:T(8,128)}, f32[2,384]{1,0:...) custom-call(s32[16]{0:T(128)} %fusion.47.slots, ...), custom_call_target="tpu_custom_call" | custom-call | flops 1000000 | bytes 14000000 | tf_op jit(solution)/shard_map/pallas_call | solution.py:346
  (386 shorter events, 93.4 us)
Async XLA Ops:
  7.2 39.1 %copy-start = (bf16[2,96,3072]{2,1,0:T(8,128)(2,1)S(1)}, bf16[2,96,3072]{2,1,0:T(8,128)(2,1)}, u32[]{:S(2)}) copy-start(bf16[2,96,3072]{2,1,0:T(8,128)(2,1)} %param.28) | copy-start | bytes 3538948
  9.5 7.8 %copy-start.85 = (bf16[2,96]{1,0:T(2,128)(2,1)S(1)}, bf16[2,96]{1,0:T(2,128)(2,1)}, u32[]{:S(2)}) copy-start(bf16[2,96]{1,0:T(2,128)(2,1)} %param.27) | copy-start | bytes 1156
  9.5 7.8 %copy-start.86 = (bf16[2,96]{1,0:T(2,128)(2,1)S(1)}, bf16[2,96]{1,0:T(2,128)(2,1)}, u32[]{:S(2)}) copy-start(bf16[2,96]{1,0:T(2,128)(2,1)} %param.31) | copy-start | bytes 1156
  9.5 8.0 %copy-start.73 = (bf16[2,384]{1,0:T(2,128)(2,1)S(1)}, bf16[2,384]{1,0:T(2,128)(2,1)}, u32[]{:S(2)}) copy-start(bf16[2,384]{1,0:T(2,128)(2,1)} %param.29) | copy-start | bytes 4612
  9.6 9.7 %copy-start.29 = (bf16[2,96,2304]{2,1,0:T(8,128)(2,1)S(1)}, bf16[2,96,2304]{2,1,0:T(8,128)(2,1)}, u32[]{:S(2)}) copy-start(bf16[2,96,2304]{2,1,0:T(8,128)(2,1)} %param.21) | copy-start | bytes 2654212
  9.6 30.7 %all-to-all-start = ((bf16[8,128,768]{2,1,0:T(8,128)(2,1)}), bf16[8,128,768]{2,1,0:T(8,128)(2,1)}, u32[]{:S(2)}, u32[]{:S(2)}) async-start(bf16[8,128,768]{2,1,0:T(8,128)(2,1)} %broadcast_in_dim.50), calls=%async_computation | async-start | bytes 3145728 | tf_op jit(solution)/shard_map/all_to_all | solution.py:39
  41.2 16.7 %all-to-all-start.1 = ((bf16[8,64,768]{2,1,0:T(8,128)(2,1)}), bf16[8,64,768]{2,1,0:T(8,128)(2,1)S(1)}, u32[]{:S(2)}, u32[]{:S(2)}) async-start(bf16[8,64,768]{2,1,0:T(8,128)(2,1)} %broadcast_in_dim.53), calls=%async_computation.1 | async-start | bytes 1572864 | tf_op jit(solution)/shard_map/all_to_all | solution.py:39
  48.0 20.2 %collective-permute-start = (bf16[8,128,768]{2,1,0:T(8,128)(2,1)}, bf16[8,128,768]{2,1,0:T(8,128)(2,1)}, u32[]{:S(2)}, u32[]{:S(2)}) collective-permute-start(bf16[8,128,768]{2,1,0:T(8,128)(2,1)} %all-to-all-done), channel_id=1, source_target_pairs={{0,1},{1,0},{2,3},{3,2},{4,5},{5,4},{6,7},{7,6},{8,9},{9,8},{10,11... | collective-permute-start | bytes 4718600 | tf_op jit(solution)/shard_map/ppermute | solution.py:47
  59.3 24.9 %all-to-all-start.2 = ((bf16[8,144,768]{2,1,0:T(8,128)(2,1)}), bf16[8,144,768]{2,1,0:T(8,128)(2,1)S(1)}, u32[]{:S(2)}, u32[]{:S(2)}) async-start(bf16[8,144,768]{2,1,0:T(8,128)(2,1)} %broadcast_in_dim.55), calls=%async_computation.2 | async-start | bytes 3538944 | tf_op jit(solution)/shard_map/all_to_all | solution.py:39
  63.1 99.7 %all-gather.7.cloned.1.call-start = ((), (), s32[]{:S(2)}) async-start(), calls=%async_computation.22 | async-start | bytes 1990656 | tf_op jit(solution)/shard_map/all_gather | solution.py:518
  84.3 18.0 %copy-start.9 = (bf16[1,128,768]{2,1,0:T(8,128)(2,1)S(1)}, bf16[1,128,768]{2,1,0:T(8,128)(2,1)}, u32[]{:S(2)}) copy-start(bf16[1,128,768]{2,1,0:T(8,128)(2,1)} %param.16) | copy-start | bytes 589828
  85.2 17.1 %collective-permute-start.1 = (bf16[768,384]{1,0:T(8,128)(2,1)}, bf16[768,384]{1,0:T(8,128)(2,1)}, u32[]{:S(2)}, u32[]{:S(2)}) collective-permute-start(bf16[768,384]{1,0:T(8,128)(2,1)} %bitcast.28), channel_id=1, source_target_pairs={{0,1},{1,0},{2,3},{3,2},{4,5},{5,4},{6,7},{7,6},{8,9},{9,8},{10,11... | collective-permute-start | bytes 1769480 | tf_op jit(solution)/shard_map/ppermute | solution.py:47
  104.8 16.4 %copy-start.35 = (bf16[48,768]{1,0:T(8,128)(2,1)S(1)}, bf16[48,768]{1,0:T(8,128)(2,1)}, u32[]{:S(2)}) copy-start(bf16[48,768]{1,0:T(8,128)(2,1)} %get-tuple-element.175) | copy-start | bytes 221188
  104.8 16.4 %copy-start.36 = (bf16[48,384]{1,0:T(8,128)(2,1)S(1)}, bf16[48,384]{1,0:T(8,128)(2,1)}, u32[]{:S(2)}) copy-start(bf16[48,384]{1,0:T(8,128)(2,1)} %get-tuple-element.184) | copy-start | bytes 110596
  104.9 16.4 %copy-start.37 = (bf16[48,384]{1,0:T(8,128)(2,1)S(1)}, bf16[48,384]{1,0:T(8,128)(2,1)}, u32[]{:S(2)}) copy-start(bf16[48,384]{1,0:T(8,128)(2,1)} %get-tuple-element.187) | copy-start | bytes 110596
  104.9 16.4 %copy-start.38 = (bf16[48,384]{1,0:T(8,128)(2,1)S(1)}, bf16[48,384]{1,0:T(8,128)(2,1)}, u32[]{:S(2)}) copy-start(bf16[48,384]{1,0:T(8,128)(2,1)} %get-tuple-element.189) | copy-start | bytes 110596
  104.9 16.4 %copy-start.39 = (bf16[48,384]{1,0:T(8,128)(2,1)S(1)}, bf16[48,384]{1,0:T(8,128)(2,1)}, u32[]{:S(2)}) copy-start(bf16[48,384]{1,0:T(8,128)(2,1)} %get-tuple-element.190) | copy-start | bytes 110596
  119.2 8.7 %collective-permute-start.2 = (bf16[4,128,768]{2,1,0:T(8,128)(2,1)S(1)}, bf16[4,128,768]{2,1,0:T(8,128)(2,1)}, u32[]{:S(2)}, u32[]{:S(2)}) collective-permute-start(bf16[4,128,768]{2,1,0:T(8,128)(2,1)S(1)} %all_to_all.111), channel_id=1, source_target_pairs={{0,1},{1,0},{2,3},{3,2},{4,5},{5,4},{6,7},{7,6},{8,9},{9,8},{10,11... | collective-permute-start | bytes 2359304 | tf_op jit(solution)/shard_map/ppermute | solution.py:47
  133.1 2.4 collective-permute-start.3
  135.6 14.5 %copy-start.44 = (f32[768]{0:T(1024)S(1)}, f32[768]{0:T(1024)}, u32[]{:S(2)}) copy-start(f32[768]{0:T(1024)} %get-tuple-element.140) | copy-start | bytes 9220
  150.3 40.4 %copy-start.53 = (f32[128]{0:T(128)}, f32[128]{0:T(128)S(1)}, u32[]{:S(2)}) copy-start(f32[128]{0:T(128)S(1)} %broadcast_multiply_fusion.2) | copy-start | bytes 1540
  150.5 40.3 %copy-start.76 = (f32[128]{0:T(128)}, f32[128]{0:T(128)S(1)}, u32[]{:S(2)}) copy-start(f32[128]{0:T(128)S(1)} %multiply_reduce_fusion.7) | copy-start | bytes 1540
  150.5 40.2 %copy-start.59 = (f32[128]{0:T(128)}, f32[128]{0:T(128)S(1)}, u32[]{:S(2)}) copy-start(f32[128]{0:T(128)S(1)} %fusion.49) | copy-start | bytes 1540
  163.0 29.9 %copy-start.24 = (bf16[1152,768]{1,0:T(8,128)(2,1)S(1)}, bf16[1152,768]{1,0:T(8,128)(2,1)}, u32[]{:S(2)}) copy-start(bf16[1152,768]{1,0:T(8,128)(2,1)} %all-gather.7.cloned.1.call-done) | copy-start | bytes 5308420
  190.7 5.2 collective-permute-start.4
  194.6 23.9 %collective-permute-start.5 = (bf16[768,384]{1,0:T(8,128)(2,1)}, bf16[768,384]{1,0:T(8,128)(2,1)}, u32[]{:S(2)}, u32[]{:S(2)}) collective-permute-start(bf16[768,384]{1,0:T(8,128)(2,1)} %bitcast.46), channel_id=1, source_target_pairs={{0,1},{1,0},{2,3},{3,2},{4,5},{5,4},{6,7},{7,6},{8,9},{9,8},{10,11... | collective-permute-start | bytes 1769480 | tf_op jit(solution)/shard_map/ppermute | solution.py:47
  205.7 12.9 %copy-start.63 = (f32[768]{0:T(1024)S(1)}, f32[768]{0:T(1024)}, u32[]{:S(2)}) copy-start(f32[768]{0:T(1024)} %get-tuple-element.137) | copy-start | bytes 9220
  221.6 24.6 %copy-start.50 = (f32[8,48]{1,0:T(8,128)S(1)}, f32[8,48]{1,0:T(8,128)}, u32[]{:S(2)}) copy-start(f32[8,48]{1,0:T(8,128)} %get-tuple-element.144) | copy-start | bytes 4612
  244.0 5.5 collective-permute-start.6
  256.6 3.1 collective-permute-start.8
  258.2 6.1 %collective-permute-start.7 = (bf16[4,128,768]{2,1,0:T(8,128)(2,1)S(1)}, bf16[4,128,768]{2,1,0:T(8,128)(2,1)}, u32[]{:S(2)}, u32[]{:S(2)}) collective-permute-start(bf16[4,128,768]{2,1,0:T(8,128)(2,1)S(1)} %bitcast.180), channel_id=1, source_target_pairs={{0,1},{1,0},{2,3},{3,2},{4,5},{5,4},{6,7},{7,6},{8,9},{9,8},{10,11... | collective-permute-start | bytes 2359304 | tf_op jit(solution)/shard_map/ppermute | solution.py:47
  260.8 15.8 %all-to-all-start.10 = ((bf16[4,128,768]{2,1,0:T(8,128)(2,1)}), bf16[4,128,768]{2,1,0:T(8,128)(2,1)S(1)}, u32[]{:S(2)}, u32[]{:S(2)}) async-start(bf16[4,128,768]{2,1,0:T(8,128)(2,1)} %add_convert_fusion.1), calls=%async_computation.10 | async-start | bytes 1572864 | tf_op jit(solution)/shard_map/all_to_all | solution.py:39
  276.5 14.8 %all-to-all-start.9 = ((bf16[4,128,768]{2,1,0:T(8,128)(2,1)}), bf16[4,128,768]{2,1,0:T(8,128)(2,1)S(1)}, u32[]{:S(2)}, u32[]{:S(2)}) async-start(bf16[4,128,768]{2,1,0:T(8,128)(2,1)} %add_convert_fusion.2), calls=%async_computation.9 | async-start | bytes 1572864 | tf_op jit(solution)/shard_map/all_to_all | solution.py:39
  280.9 10.6 %copy-start.41 = (f32[768]{0:T(1024)S(1)}, f32[768]{0:T(1024)}, u32[]{:S(2)}) copy-start(f32[768]{0:T(1024)} %get-tuple-element.134) | copy-start | bytes 9220
  280.9 10.6 %copy-start.56 = (f32[128]{0:T(128)S(1)}, f32[128]{0:T(128)}, u32[]{:S(2)}) copy-start(f32[128]{0:T(128)} %copy-done.55) | copy-start | bytes 1540
  280.9 10.6 %copy-start.62 = (f32[128]{0:T(128)S(1)}, f32[128]{0:T(128)}, u32[]{:S(2)}) copy-start(f32[128]{0:T(128)} %copy-done.61) | copy-start | bytes 1540
  297.0 13.9 %all-to-all-start.11 = ((bf16[16,128,64]{1,2,0:T(8,128)(2,1)}), bf16[16,128,64]{1,2,0:T(8,128)(2,1)S(1)}, u32[]{:S(2)}, u32[]{:S(2)}) async-start(bf16[16,128,64]{1,2,0:T(8,128)(2,1)} %concatenate.93), calls=%async_computation.11 | async-start | bytes 524288 | tf_op jit(solution)/shard_map/all_to_all | solution.py:39
  311.9 32.8 %all-to-all-start.12 = ((bf16[8,192,768]{2,1,0:T(8,128)(2,1)}), bf16[8,192,768]{2,1,0:T(8,128)(2,1)S(1)}, u32[]{:S(2)}, u32[]{:S(2)}) async-start(bf16[8,192,768]{2,1,0:T(8,128)(2,1)} %shard_map.273), calls=%async_computation.12 | async-start | bytes 4718592 | tf_op jit(solution)/shard_map/all_to_all | solution.py:39
  345.8 5.2 collective-permute-start.9
  353.9 27.6 %all-to-all-start.13 = ((bf16[8,128,768]{2,1,0:T(8,128)(2,1)}), bf16[8,128,768]{2,1,0:T(8,128)(2,1)S(1)}, u32[]{:S(2)}, u32[]{:S(2)}) async-start(bf16[8,128,768]{2,1,0:T(8,128)(2,1)} %fusion.2), calls=%async_computation.13 | async-start | bytes 3145728 | tf_op jit(solution)/shard_map/all_to_all | solution.py:39
  358.5 24.1 %copy-start.54 = (f32[128]{0:T(128)S(1)}, f32[128]{0:T(128)}, u32[]{:S(2)}) copy-start(f32[128]{0:T(128)} %copy-done.53) | copy-start | bytes 1540
  358.5 24.1 %copy-start.60 = (f32[128]{0:T(128)S(1)}, f32[128]{0:T(128)}, u32[]{:S(2)}) copy-start(f32[128]{0:T(128)} %copy-done.59) | copy-start | bytes 1540
  358.6 24.9 %copy-start.77 = (f32[128]{0:T(128)S(1)}, f32[128]{0:T(128)}, u32[]{:S(2)}) copy-start(f32[128]{0:T(128)} %copy-done.76) | copy-start | bytes 1540
  358.6 125.6 %all-gather.9.cloned.1.call-start = ((), (), s32[]{:S(2)}) async-start(), calls=%async_computation.23 | async-start | bytes 2506752 | tf_op jit(solution)/shard_map/all_gather | solution.py:564
  361.5 22.2 %copy-start.14 = (f32[128,768]{1,0:T(8,128)S(1)}, f32[128,768]{1,0:T(8,128)}, u32[]{:S(2)}) copy-start(f32[128,768]{1,0:T(8,128)} %copy-done.13) | copy-start | bytes 1179652
  361.6 22.2 %copy-start.26 = (bf16[1,128,768]{2,1,0:T(8,128)(2,1)S(1)}, bf16[1,128,768]{2,1,0:T(8,128)(2,1)}, u32[]{:S(2)}) copy-start(bf16[1,128,768]{2,1,0:T(8,128)(2,1)} %param.17) | copy-start | bytes 589828
  361.6 22.2 %copy-start.72 = (f32[128]{0:T(128)S(1)}, f32[128]{0:T(128)}, u32[]{:S(2)}) copy-start(f32[128]{0:T(128)} %copy-done.71) | copy-start | bytes 1540
  402.0 3.8 collective-permute-start.10
  411.2 2.4 collective-permute-start.11
  414.4 16.8 %copy-start.52 = (f32[128]{0:T(128)S(1)}, f32[128]{0:T(128)}, u32[]{:S(2)}) copy-start(f32[128]{0:T(128)} %copy-done.51) | copy-start | bytes 1540
  414.4 16.8 %copy-start.58 = (f32[128]{0:T(128)S(1)}, f32[128]{0:T(128)}, u32[]{:S(2)}) copy-start(f32[128]{0:T(128)} %copy-done.57) | copy-start | bytes 1540
  414.4 17.5 %copy-start.75 = (f32[128]{0:T(128)S(1)}, f32[128]{0:T(128)}, u32[]{:S(2)}) copy-start(f32[128]{0:T(128)} %copy-done.74) | copy-start | bytes 1540
  432.9 8.0 %copy-start.31 = (bf16[12,128,64]{1,2,0:T(8,128)(2,1)S(1)}, bf16[12,128,64]{1,2,0:T(8,128)(2,1)}, u32[]{:S(2)}) copy-start(bf16[12,128,64]{1,2,0:T(8,128)(2,1)} %copy-done.30) | copy-start | bytes 589828
  436.1 13.8 %all-to-all-start.16 = ((bf16[16,128,64]{1,2,0:T(8,128)(2,1)}), bf16[16,128,64]{1,2,0:T(8,128)(2,1)S(1)}, u32[]{:S(2)}, u32[]{:S(2)}) async-start(bf16[16,128,64]{1,2,0:T(8,128)(2,1)} %concatenate.95), calls=%async_computation.16 | async-start | bytes 524288 | tf_op jit(solution)/shard_map/all_to_all | solution.py:39
  450.9 32.8 %all-to-all-start.17 = ((bf16[8,192,768]{2,1,0:T(8,128)(2,1)}), bf16[8,192,768]{2,1,0:T(8,128)(2,1)S(1)}, u32[]{:S(2)}, u32[]{:S(2)}) async-start(bf16[8,192,768]{2,1,0:T(8,128)(2,1)} %shard_map.276), calls=%async_computation.17 | async-start | bytes 4718592 | tf_op jit(solution)/shard_map/all_to_all | solution.py:39
  484.2 5.4 collective-permute-start.12
  492.6 28.3 %all-to-all-start.18 = ((bf16[8,128,768]{2,1,0:T(8,128)(2,1)}), bf16[8,128,768]{2,1,0:T(8,128)(2,1)S(1)}, u32[]{:S(2)}, u32[]{:S(2)}) async-start(bf16[8,128,768]{2,1,0:T(8,128)(2,1)} %fusion.1), calls=%async_computation.18 | async-start | bytes 3145728 | tf_op jit(solution)/shard_map/all_to_all | solution.py:39
  497.0 84.2 %all-gather.11.cloned.1.call-start = ((), (), s32[]{:S(2)}) async-start(), calls=%async_computation.24 | async-start | bytes 2506752 | tf_op jit(solution)/shard_map/all_gather | solution.py:568
  520.9 14.8 %all-to-all-start.20 = ((bf16[16,16,768]{2,1,0:T(8,128)(2,1)}), bf16[16,16,768]{2,1,0:T(8,128)(2,1)S(1)}, u32[]{:S(2)}, u32[]{:S(2)}) async-start(bf16[16,16,768]{2,1,0:T(8,128)(2,1)} %pad.6.clone), calls=%async_computation.20 | async-start | bytes 786432 | tf_op jit(solution)/shard_map/all_to_all | solution.py:39
  535.7 17.2 %all-to-all-start.19 = ((bf16[8,80,768]{2,1,0:T(8,128)(2,1)}), bf16[8,80,768]{2,1,0:T(8,128)(2,1)S(1)}, u32[]{:S(2)}, u32[]{:S(2)}) async-start(bf16[8,80,768]{2,1,0:T(8,128)(2,1)} %shard_map.278), calls=%async_computation.19 | async-start | bytes 1966080 | tf_op jit(solution)/shard_map/all_to_all | solution.py:39
  553.1 25.0 %copy-start.12 = (f32[128,768]{1,0:T(8,128)S(1)}, f32[128,768]{1,0:T(8,128)}, u32[]{:S(2)}) copy-start(f32[128,768]{1,0:T(8,128)} %copy-done.11) | copy-start | bytes 1179652
  553.1 25.0 %copy-start.66 = (f32[128]{0:T(128)S(1)}, f32[128]{0:T(128)}, u32[]{:S(2)}) copy-start(f32[128]{0:T(128)} %copy-done.65) | copy-start | bytes 1540
  575.8 3.9 collective-permute-start.13
  581.2 8.2 %copy-start.1 = (bf16[2,96,3072]{2,1,0:T(8,128)(2,1)S(1)}, bf16[2,96,3072]{2,1,0:T(8,128)(2,1)}, u32[]{:S(2)}) copy-start(bf16[2,96,3072]{2,1,0:T(8,128)(2,1)} %param.28) | copy-start | bytes 3538948
  (57 other events, 186.1 us)
Sparse Core Ops, SparseCore 0:
  122.1 40.6 all-gather.6
  412.9 48.9 all-gather.8
  500.8 53.2 all-gather.10

commit v5 on v4

--- a/solution.py
+++ b/solution.py
@@ -1,4 +1,5 @@
 import functools
+import math
 
 import jax
 import jax.numpy as jnp
@@ -54,7 +55,7 @@
 
 def gather_x(part):
     own = spread_to(part, 4, "ctx", X_GROUPS)
-    return jnp.concatenate([own, swap_core(own)], axis=0)
+    return own.reshape(4 * TOK, D), swap_core(own).reshape(4 * TOK, D)
 
 
 def scatter(near, far, groups):
@@ -63,8 +64,8 @@
     return jnp.sum(parts.astype(F32), axis=0)
 
 
-def scatter_x(partial):
-    return scatter(partial[:4], partial[4:], X_GROUPS)
+def scatter_x(near, far):
+    return scatter(near.reshape(4, TOK, D), far.reshape(4, TOK, D), X_GROUPS)
 
 
 def dot(left, right, dims=((1,), (0,))):
@@ -236,18 +237,105 @@
     )(arrive_pos, ctx_pos, queries, keys, values, grads, weight)
 
 
+GELU_SCALE = math.sqrt(2.0 / math.pi)
+GELU_CUBE = 0.044715
+
+
+def load_feed(rows_ref, up_ref, down_ref):
+    for owner in range(S):
+        for part in range(2):
+            first = owner * 96 + part * 48
+            up_ref[first : first + 48, :] = rows_ref[owner, 48:96, part * 384 : (part + 1) * 384]
+        down_ref[owner * 48 : (owner + 1) * 48, :] = rows_ref[owner, 96:144, :]
+
+
+def feed_kernel(own_ref, other_ref, rows_ref, shift_ref, hidden_ref, active_ref, near_ref, far_ref, up_ref, down_ref):
+    load_feed(rows_ref, up_ref, down_ref)
+    for side, (source, target) in enumerate(((own_ref, near_ref), (other_ref, far_ref))):
+        for step in range(4 * TOK // ROWS):
+            rows = slice(step * ROWS, (step + 1) * ROWS)
+            saved = slice(side * 4 * TOK + step * ROWS, side * 4 * TOK + (step + 1) * ROWS)
+            hidden = dot(source[rows, :], up_ref[...]) + shift_ref[...]
+            hidden_ref[saved, :] = hidden
+            inner = GELU_SCALE * (hidden + GELU_CUBE * hidden * hidden * hidden)
+            active = (hidden * (0.5 * (1.0 + jnp.tanh(inner)))).astype(BF16)
+            active_ref[saved, :] = active
+            target[rows, :] = dot(active, down_ref[...]).astype(BF16)
+
+
+def feed_back_kernel(own_ref, other_ref, rows_ref, hidden_ref, grad_ref, near_ref, far_ref, sums_ref, up_ref, down_ref):
+    load_feed(rows_ref, up_ref, down_ref)
+    sums = jnp.zeros((1, 384), F32)
+    for side, (source, target) in enumerate(((own_ref, near_ref), (other_ref, far_ref))):
+        for step in range(4 * TOK // ROWS):
+            rows = slice(step * ROWS, (step + 1) * ROWS)
+            saved = slice(side * 4 * TOK + step * ROWS, side * 4 * TOK + (step + 1) * ROWS)
+            active_grad = dot(source[rows, :], down_ref[...], ((1,), (1,)))
+            hidden = hidden_ref[saved, :]
+            square = hidden * hidden
+            bend = jnp.tanh(GELU_SCALE * (hidden + GELU_CUBE * square * hidden))
+            slope = GELU_SCALE * (1.0 + 3.0 * GELU_CUBE * square)
+            slope = 0.5 * (1.0 + bend) + 0.5 * hidden * (1.0 - bend * bend) * slope
+            grad = (active_grad * slope).astype(BF16)
+            grad_ref[saved, :] = grad
+            sums = sums + jnp.sum(grad.astype(F32), axis=0, keepdims=True)
+            target[rows, :] = dot(grad, up_ref[...], ((1,), (1,))).astype(BF16)
+    sums_ref[...] = sums
+
+
+def feed(own, other, rows, shift):
+    half = jax.ShapeDtypeStruct((4 * TOK, D), BF16)
+    return pl.pallas_call(
+        feed_kernel,
+        out_shape=(
+            jax.ShapeDtypeStruct((8 * TOK, 384), F32),
+            jax.ShapeDtypeStruct((8 * TOK, 384), BF16),
+            half,
+            half,
+        ),
+        in_specs=[WHOLE] * 4,
+        out_specs=(WHOLE,) * 4,
+        scratch_shapes=[pltpu.VMEM((D, 384), BF16), pltpu.VMEM((384, D), BF16)],
+        compiler_params=pltpu.CompilerParams(vmem_limit_bytes=VMEM_BYTES),
+        cost_estimate=pl.CostEstimate(flops=12 * 10**8, bytes_accessed=7 * 10**6, transcendentals=4 * 10**5),
+    )(own, other, rows, shift)
+
+
+def feed_back(own, other, rows, hidden):
+    half = jax.ShapeDtypeStruct((4 * TOK, D), BF16)
+    return pl.pallas_call(
+        feed_back_kernel,
+        out_shape=(
+            jax.ShapeDtypeStruct((8 * TOK, 384), BF16),
+            half,
+            half,
+            jax.ShapeDtypeStruct((1, 384), F32),
+        ),
+        in_specs=[WHOLE] * 4,
+        out_specs=(WHOLE,) * 4,
+        scratch_shapes=[pltpu.VMEM((D, 384), BF16), pltpu.VMEM((384, D), BF16)],
+        compiler_params=pltpu.CompilerParams(vmem_limit_bytes=VMEM_BYTES),
+        cost_estimate=pl.CostEstimate(flops=12 * 10**8, bytes_accessed=7 * 10**6, transcendentals=4 * 10**5),
+    )(own, other, rows, hidden)
+
+
 UPS, DOWNS, OUTS, FIRST = 0, 48, 96, 192
 HEADS, SMALL, SECOND = 0, 64, 80
 BOTH_ROWS = ((0,), (0,))
 
 
-def first_grads_kernel(second_ref, hidden_ref, active_ref, down_ref, mixed_ref, attended_ref, out_ref):
-    ups = dot(second_ref[...], hidden_ref[...], BOTH_ROWS).astype(BF16)
+def first_grads_kernel(
+    own_ref, other_ref, hidden_ref, active_ref, own_down_ref, other_down_ref, mixed_ref, attended_ref, out_ref
+):
+    half = 4 * TOK
+    ups = dot(own_ref[...], hidden_ref[:half, :], BOTH_ROWS) + dot(other_ref[...], hidden_ref[half:, :], BOTH_ROWS)
+    ups = ups.astype(BF16)
     for owner in range(S):
         for part in range(2):
             first = owner * 96 + part * 48
             out_ref[owner, UPS:DOWNS, part * 384 : (part + 1) * 384] = ups[first : first + 48, :]
-    downs = dot(active_ref[...], down_ref[...], BOTH_ROWS).astype(BF16)
+    downs = dot(active_ref[:half, :], own_down_ref[...], BOTH_ROWS)
+    downs = (downs + dot(active_ref[half:, :], other_down_ref[...], BOTH_ROWS)).astype(BF16)
     for owner in range(S):
         out_ref[owner, DOWNS:OUTS, :] = downs[owner * 48 : (owner + 1) * 48, :]
     outs = dot(mixed_ref[...], attended_ref[...], BOTH_ROWS).astype(BF16)
@@ -359,7 +447,7 @@
     )
 
 
-def forward_layer(flowing, head_weight, layer_rows, split, small, places, gathered=None, carried=None):
+def forward_layer(flowing, head_weight, layer_rows, join_out, small, places, gathered=None, carried=None):
     arrive_pos, ctx_pos = places
     head_shift, vectors, up_shift = small
     gain_one, bias_one, unused, unused, out_shift, gain_two, bias_two, down_shift = vectors
@@ -372,42 +460,36 @@
         normed = layer_norm(flowing, gain_one, bias_one).astype(BF16)
         normed, layer_rows = lax.optimization_barrier((normed, layer_rows))
         own, other = (part.reshape(LEN // 2, D) for part in gather_ctx(normed))
+        own, other, carried = lax.optimization_barrier((own, other, carried))
+        carried = spread_to(carried, 4, "ctx", X_GROUPS)
         mixed_head, queries, keys, values = attend(arrive_pos, ctx_pos, own, other, head_weight, head_shift)
-    out_full, up_part, down_part = split(layer_rows)
+        mixed_head, carried = lax.optimization_barrier((mixed_head, carried))
+        carried = (carried.reshape(4 * TOK, D), swap_core(carried).reshape(4 * TOK, D))
+    out_full = join_out(layer_rows)
     mixed = exchange(mixed_head.reshape(C, TOK, HD), "ctx")[:H]
     mixed = mixed.transpose(1, 0, 2).reshape(TOK, D)
     middle = flowing + dot(mixed, out_full) + out_shift
     second = layer_norm(middle, gain_two, bias_two).astype(BF16)
-    if carried is not None:
-        both = gather_x(jnp.concatenate([second, carried], axis=0))
-        second_all = both[:, :TOK].reshape(8 * TOK, D)
-        carried = both[:, TOK:].reshape(8 * TOK, D)
-    else:
-        second_all = gather_x(second).reshape(8 * TOK, D)
-    hidden = dot(second_all, up_part) + up_shift
-    activated = jax.nn.gelu(hidden, approximate=True).astype(BF16)
-    partial = dot(activated, down_part).reshape(8, TOK, D)
-    output = middle + scatter_x(partial) + down_shift
+    second_all = gather_x(second)
+    hidden, activated, near, far = feed(*second_all, layer_rows, up_shift)
+    output = middle + scatter_x(near, far) + down_shift
     saved = (flowing, own, other, queries, keys, values, mixed, middle, second_all, hidden, activated)
-    return output, saved, carried, (head_weight, out_full, up_part, down_part)
+    return output, saved, carried, (head_weight, out_full, layer_rows)
 
 
 def backward_layer(grad_out, down_all, saved, params, small, places, head, layer, prior, spread):
     arrive_pos, ctx_pos = places
-    head_weight, out_full, up_part, down_part = params
+    head_weight, out_full, layer_rows = params
     unused, vectors, unused = small
     gain_one, bias_one, unused, unused, unused, gain_two, bias_two, unused = vectors
     flowing, own, other, queries, keys, values, mixed, middle, second_all, hidden, activated = saved
     down_in = grad_out.astype(BF16)
     down_shift_grad = jnp.sum(down_in.astype(F32), axis=0, keepdims=True)
     if down_all is None:
-        down_all = gather_x(down_in).reshape(8 * TOK, D)
-    activated_grad = dot(down_all, down_part, ((1,), (1,)))
-    unused, gelu_back = jax.vjp(lambda inner: jax.nn.gelu(inner, approximate=True), hidden)
-    hidden_grad = gelu_back(activated_grad)[0].astype(BF16)
-    second_part = dot(hidden_grad, up_part, ((1,), (1,))).reshape(8, TOK, D)
-    second_grad = scatter_x(second_part)
-    up_shift_grad = jnp.sum(hidden_grad.astype(F32), axis=0, keepdims=True)
+        down_all = gather_x(down_in)
+    hidden_grad, near, far, up_shift_grad = feed_back(*down_all, layer_rows, hidden)
+    near, far, prior = lax.optimization_barrier((near, far, prior))
+    second_grad = scatter_x(near, far)
     unused, norm_back = jax.vjp(layer_norm, middle, gain_two, bias_two)
     middle_part, gain_two_grad, bias_two_grad = norm_back(second_grad)
     middle_grad = grad_out + middle_part
@@ -417,7 +499,7 @@
     mixed_grad = mixed_grad.reshape(TOK, H, HD).transpose(1, 0, 2)
     mixed_grad = jnp.concatenate([mixed_grad, jnp.zeros((C - H, TOK, HD), BF16)], axis=0)
     mixed_grad = exchange(mixed_grad, "ctx").reshape(LEN, HD)
-    packed = first_grads(second_all, hidden_grad, activated, down_all, mixed, attended_in)
+    packed = first_grads(*second_all, hidden_grad, activated, *down_all, mixed, attended_in)
     mixed_grad, packed = lax.optimization_barrier((mixed_grad, packed))
     owned = jnp.sum(exchange(packed, "shard").astype(F32), axis=0).astype(BF16)
     to_arrive, near, far, sums = attend_back(
@@ -489,10 +571,9 @@
     def apart(piece):
         return jnp.concatenate([piece[..., :384], piece[..., 384:]], axis=1).reshape(D, 384)
 
-    def split(rows):
+    def join_out(rows):
         own = apart(rows[:, :48])
-        out_full = join_cores(core, own, swap_core(own), 1)
-        return out_full, apart(rows[:, 48:96]), rows[:, 96:].reshape(384, D)
+        return join_cores(core, own, swap_core(own), 1)
 
     layer_pieces = [
         jnp.concatenate([beside(out_piece[layer]), beside(up_piece[layer]), down_piece[layer]], axis=0)
@@ -546,7 +627,7 @@
             flowing,
             head_weights[:, layer].reshape(D, 3 * HD),
             layer_rows[layer],
-            split,
+            join_out,
             small,
             places,
             gathered=states_all if layer == 0 else None,
@@ -560,7 +641,6 @@
     grad_flow, owned_last, late, unused = backward_layer(
         grad_flow, carried, saved_all[1], all_params[1], smalls[1], places, held, 1, (), ()
     )
-    grad_flow, late = lax.optimization_barrier((grad_flow, late))
     every_last = lax.all_gather(owned_last[:OUTS], "ctx", axis=0)
     grad_flow, owned, late, every_last = backward_layer(
         grad_flow, None, saved_all[0], all_params[0], smalls[0], places, held, 0, (late,), every_last

time: 601 us -> 601 us (level)
  Pallas kernels: 76.9 us -> 99.6 us
  blocking collectives: 155 us -> 175 us
  matrix products: 22.4 us -> 5.96 us
  waiting for transfers between devices: 163 us -> 147 us
    pallas_call x0 -> x4, Pallas kernels: none -> 22.8 us  [the longest x2 11.5 us: feed(): pl.pallas_call(feed_kernel, out_shape=(jax.ShapeDtypeStruct((8 * TOK, 384...]
    all_to_all x13, waiting for transfers between devices: 137 us -> 117 us  [exchange(): lax.all_to_all(parts, axis, 0, 0, tiled=True, axis_index_groups=groups)]
    all_to_all x9 -> x10, blocking collectives: 155 us -> 175 us  [exchange(): lax.all_to_all(parts, axis, 0, 0, tiled=True, axis_index_groups=groups)]
    dot_general x13 -> x5, matrix products: 22.4 us -> 5.96 us  [dot(): lax.dot_general(left, right, (dims, ((), ())), preferred_element_type=F32)]
    ppermute x14 -> x15, waiting for transfers between devices: 13.9 us -> 16.9 us  [swap_core(): return lax.ppermute(part, 'ctx', SWAP)]
    ppermute x14 -> x15, starting transfers between devices: 20.1 us -> 20.4 us  [swap_core(): return lax.ppermute(part, 'ctx', SWAP)]
  transfers between devices with their start and end apart: 30 -> 31, of which waited for: 22 -> 22; matrix products, arithmetic and copies ran while one was open for 10% -> 9% of each run, Pallas kernels for 11% -> 13%
where the time goes in v5:
time: 601 us; the launch traced here: 596 us
  blocking collectives  175 us (29%)
  waiting for transfers between devices  147 us (24%)
  Pallas kernels  99.6 us (17%)
  starting transfers between devices  78.1 us (13%)
  local copies, waits for them, and re-layouts  47.9 us (8%)
  other arithmetic  27 us (4%)
  between operations  15.3 us (3%)
    all_to_all x10, blocking collectives, exchange(): lax.all_to_all(parts, axis, 0, 0, tiled=True, axis_index_groups=groups)  175 us
    all_to_all x13, waiting for transfers between devices, exchange(): lax.all_to_all(parts, axis, 0, 0, tiled=True, axis_index_groups=groups)  117 us
    all_to_all x13, starting transfers between devices, exchange(): lax.all_to_all(parts, axis, 0, 0, tiled=True, axis_index_groups=groups)  56.7 us
    pallas_call x2, Pallas kernels, attend_back(): pl.pallas_call(attend_back_kernel, out_shape=(jax.ShapeDtypeStruct((LEN,...  29.4 us
    ppermute x15, starting transfers between devices, swap_core(): return lax.ppermute(part, 'ctx', SWAP)  20.4 us
    pallas_call x2, Pallas kernels, attend(): pl.pallas_call(functools.partial(attend_kernel, fresh), out_shape=outs, i...  18.9 us
    ppermute x15, waiting for transfers between devices, swap_core(): return lax.ppermute(part, 'ctx', SWAP)  16.9 us
    all_gather x1, waiting for transfers between devices, shards(): lax.all_gather(layer_pieces[1], 'shard', axis=0)  13.3 us
  transfers between devices with their start and end apart: 31, of which 22 were waited for; matrix products, arithmetic and copies ran while one was open for 9% of the time, Pallas kernels for 13%

profile of v5, /device:TPU:1, one launch (start us, length us, event | category | flops | bytes accessed | tf_op | source)
XLA Modules:
  0.0 595.8 jit_solution(9556089676627250402)
XLA Ops:
  7.2 2.3 broadcast_in_dim.48
  9.5 7.6 %all-to-all-start = ((bf16[8,128,768]{2,1,0:T(8,128)(2,1)}), bf16[8,128,768]{2,1,0:T(8,128)(2,1)}, u32[]{:S(2)}, u32[]{:S(2)}) async-start(bf16[8,128,768]{2,1,0:T(8,128)(2,1)} %broadcast_in_dim.48), calls=%async_computation | async-start | bytes 3145728 | tf_op jit(solution)/shard_map/all_to_all | solution.py:40
  26.9 13.2 %all-to-all-done = bf16[8,128,768]{2,1,0:T(8,128)(2,1)} async-done(((bf16[8,128,768]{2,1,0:T(8,128)(2,1)}), bf16[8,128,768]{2,1,0:T(8,128)(2,1)}, u32[]{:S(2)}, u32[]{:S(2)}) %all-to-all-start) | async-done | bytes 1572896 | tf_op jit(solution)/shard_map/all_to_all | solution.py:40
  41.1 5.1 all-to-all-start.1
  49.0 8.7 %all-to-all-done.1 = bf16[8,64,768]{2,1,0:T(8,128)(2,1)S(1)} async-done(((bf16[8,64,768]{2,1,0:T(8,128)(2,1)}), bf16[8,64,768]{2,1,0:T(8,128)(2,1)S(1)}, u32[]{:S(2)}, u32[]{:S(2)}) %all-to-all-start.1) | async-done | bytes 786464 | tf_op jit(solution)/shard_map/all_to_all | solution.py:40
  59.2 3.8 all-to-all-start.2
  68.4 10.3 %shard_map.271 = (bf16[2048,64]{1,0:T(8,128)(2,1)}, bf16[2048,64]{1,0:T(8,128)(2,1)}, bf16[2048,64]{1,0:T(8,128)(2,1)}, bf16[2048,64]{1,0:T(8,128)(2,1)}, bf16[1...) custom-call(s32[32]{0:T(128)} %reshape.369.arrive_pos, s32[32]{0:T(128)} %reshape.370.ctx_pos, ...), custom_call_target="tpu_custom_call" | custom-call | flops 2000000000 | bytes 5000000 | tf_op jit(solution)/shard_map/pallas_call | solution.py:207
  78.7 5.3 all-to-all-done.2.rows_ref
  84.2 3.4 collective-permute-start.1
  88.8 13.0 %all_to_all.115 = bf16[16,128,64]{1,2,0:T(8,128)(2,1)S(1)} all-to-all(bf16[16,128,64]{1,2,0:T(8,128)(2,1)S(1)} %copy.69), channel_id=1, replica_groups=mesh['shard'=8,'ctx'=16] {'ctx'}, dimensions={0} | all-to-all | bytes 524288 | tf_op jit(solution)/shard_map/all_to_all | solution.py:40
  104.6 13.9 %all_to_all.116 = bf16[4,128,768]{2,1,0:T(8,128)(2,1)S(1)} all-to-all(bf16[4,128,768]{2,1,0:T(8,128)(2,1)S(1)} %broadcast_in_dim.54), channel_id=1, replica_groups={{0,2,4,6},{1,3,5,7},{8,10,12,14},{9,11,13,15},{16,18,20,22},{17,19,21,2..., dimensions={0} | all-to-all | bytes 1572864 | tf_op jit(solution)/shard_map/all_to_all | solution.py:40
  118.5 2.1 collective-permute-start.2
  123.7 5.8 shard_map.272
  129.5 2.5 collective-permute-done.3
  133.3 14.7 %all_to_all.117 = bf16[4,128,768]{2,1,0:T(8,128)(2,1)S(1)} all-to-all(bf16[4,128,768]{2,1,0:T(8,128)(2,1)S(1)} %fusion.14), channel_id=1, replica_groups={{0,2,4,6},{1,3,5,7},{8,10,12,14},{9,11,13,15},{16,18,20,22},{17,19,21,2..., dimensions={0} | all-to-all | bytes 1572864 | tf_op jit(solution)/shard_map/all_to_all | solution.py:40
  148.8 13.3 %all-gather.7.cloned.1.call-done = bf16[1152,768]{1,0:T(8,128)(2,1)} async-done(((bf16[144,768]{1,0:T(8,128)(2,1)}), bf16[1152,768]{1,0:T(8,128)(2,1)}) %all-gather.7.cloned.1.call-update) | async-done | bytes 1769488 | tf_op jit(solution)/shard_map/all_gather | solution.py:599
  162.2 27.7 %all_to_all.118 = bf16[8,128,768]{2,1,0:T(8,128)(2,1)S(1)} all-to-all(bf16[8,128,768]{2,1,0:T(8,128)(2,1)S(1)} %broadcast_in_dim.55), channel_id=1, replica_groups={{0,2,4,6,8,10,12,14},{1,3,5,7,9,11,13,15},{16,18,20,22,24,26,28,30},{17..., dimensions={0} | all-to-all | bytes 3145728 | tf_op jit(solution)/shard_map/all_to_all | solution.py:40
  190.0 2.2 collective-permute-start.4
  192.2 3.0 collective-permute-done.4
  197.4 3.5 all-to-all-start.7
  202.6 8.6 %shard_map.273 = (bf16[2048,64]{1,0:T(8,128)(2,1)}, bf16[2048,64]{1,0:T(8,128)(2,1)}, bf16[2048,64]{1,0:T(8,128)(2,1)}, bf16[2048,64]{1,0:T(8,128)(2,1)}) custom-call(s32[32]{0:T(128)} %reshape.369.arrive_pos, s32[32]{0:T(128)} %reshape.370.ctx_pos, bf16[1024,768]{1,0:T(8,128)(2,1)} %bitcast.140, bf16[1024,768]{1,0:T(8,128)(2,1)} %bitcast.157, ...), custom_call_target="tpu_custom_call" | custom-call | flops 2000000000 | bytes 5000000 | tf_op jit(solution)/shard_map/pallas_call | solution.py:207
  214.4 12.4 %all_to_all.119 = bf16[16,128,64]{1,2,0:T(8,128)(2,1)S(1)} all-to-all(bf16[16,128,64]{1,2,0:T(8,128)(2,1)S(1)} %copy.70), channel_id=1, replica_groups=mesh['shard'=8,'ctx'=16] {'ctx'}, dimensions={0} | all-to-all | bytes 524288 | tf_op jit(solution)/shard_map/all_to_all | solution.py:40
  228.6 13.8 %all_to_all.120 = bf16[4,128,768]{2,1,0:T(8,128)(2,1)S(1)} all-to-all(bf16[4,128,768]{2,1,0:T(8,128)(2,1)S(1)} %broadcast_in_dim.57), channel_id=1, replica_groups={{0,2,4,6},{1,3,5,7},{8,10,12,14},{9,11,13,15},{16,18,20,22},{17,19,21,2..., dimensions={0} | all-to-all | bytes 1572864 | tf_op jit(solution)/shard_map/all_to_all | solution.py:40
  246.3 5.7 shard_map.274
  253.0 5.6 shard_map.275
  259.1 2.0 collective-permute-done.9
  261.1 2.3 fusion.12
  263.4 3.5 all-to-all-start.11
  266.9 2.2 fusion.13
  269.1 9.7 %all-to-all-done.11 = bf16[4,128,768]{2,1,0:T(8,128)(2,1)S(1)} async-done(((bf16[4,128,768]{2,1,0:T(8,128)(2,1)}), bf16[4,128,768]{2,1,0:T(8,128)(2,1)S(1)}, u32[]{:S(2)}, u32[]{:S(2)}) %all-to-all-start.11) | async-done | bytes 786464 | tf_op jit(solution)/shard_map/all_to_all | solution.py:40
  278.9 3.5 all-to-all-start.10
  284.0 9.4 %all-to-all-done.10 = bf16[4,128,768]{2,1,0:T(8,128)(2,1)S(1)} async-done(((bf16[4,128,768]{2,1,0:T(8,128)(2,1)}), bf16[4,128,768]{2,1,0:T(8,128)(2,1)S(1)}, u32[]{:S(2)}, u32[]{:S(2)}) %all-to-all-start.10) | async-done | bytes 786464 | tf_op jit(solution)/shard_map/all_to_all | solution.py:40
  297.4 5.4 all-to-all-start.12
  303.7 5.8 shard_map.276
  309.4 2.2 all-to-all-done.12
  312.6 3.6 all-to-all-start.13
  316.7 14.7 %shard_map.277 = (bf16[2048,256]{1,0:T(8,128)(2,1)}, bf16[1024,768]{1,0:T(8,128)(2,1)}, bf16[1024,768]{1,0:T(8,128)(2,1)}, f32[1,192]{1,0:T(1,128)}) custom-call(s32[32]{0:T(128)} %reshape.369.arrive_pos, s32[32]{0:T(128)} %reshape.370.ctx_pos, bf16[2048,64]{1,0:T(8,128)(2,1)} %get-tuple-element.111.q_ref, bf16[2048,64]{1,0:T(8,128)(2,1)} %get-tuple-element.112.k_ref, ...), custom_call_target="tpu_custom_call" | custom-call | flops 4000000000 | bytes 5000000 | tf_op jit(solution)/shard_map/pallas_call | solution.py:219
  331.4 13.8 %all-to-all-done.13 = bf16[8,192,768]{2,1,0:T(8,128)(2,1)S(1)} async-done(((bf16[8,192,768]{2,1,0:T(8,128)(2,1)}), bf16[8,192,768]{2,1,0:T(8,128)(2,1)S(1)}, u32[]{:S(2)}, u32[]{:S(2)}) %all-to-all-start.13) | async-done | bytes 2359328 | tf_op jit(solution)/shard_map/all_to_all | solution.py:40
  348.2 3.2 collective-permute-done.10
  353.2 26.5 %all_to_all.121 = bf16[8,128,768]{2,1,0:T(8,128)(2,1)S(1)} all-to-all(bf16[8,128,768]{2,1,0:T(8,128)(2,1)S(1)} %fusion.2), channel_id=1, replica_groups={{0,2,4,6,8,10,12,14},{1,3,5,7,9,11,13,15},{16,18,20,22,24,26,28,30},{17..., dimensions={0} | all-to-all | bytes 3145728 | tf_op jit(solution)/shard_map/all_to_all | solution.py:40
  381.2 13.1 %all_to_all.122 = bf16[4,128,768]{2,1,0:T(8,128)(2,1)S(1)} all-to-all(bf16[4,128,768]{2,1,0:T(8,128)(2,1)S(1)} %broadcast_in_dim.62), channel_id=1, replica_groups={{0,2,4,6},{1,3,5,7},{8,10,12,14},{9,11,13,15},{16,18,20,22},{17,19,21,2..., dimensions={0} | all-to-all | bytes 1572864 | tf_op jit(solution)/shard_map/all_to_all | solution.py:40
  394.3 2.5 collective-permute-start.11
  400.4 4.3 shard_map.279.rest_6_
  405.5 5.6 shard_map.278
  415.0 17.5 %all_to_all.123 = bf16[4,128,768]{2,1,0:T(8,128)(2,1)S(1)} all-to-all(bf16[4,128,768]{2,1,0:T(8,128)(2,1)S(1)} %fusion.11), channel_id=1, replica_groups={{0,2,4,6},{1,3,5,7},{8,10,12,14},{9,11,13,15},{16,18,20,22},{17,19,21,2..., dimensions={0} | all-to-all | bytes 1572864 | tf_op jit(solution)/shard_map/all_to_all | solution.py:40
  434.0 1.9 convolution_convert_fusion
  436.9 3.7 all-to-all-start.17
  441.4 5.8 shard_map.280
  447.2 2.4 all-to-all-done.17
  450.6 3.8 all-to-all-start.18
  454.4 14.7 %shard_map.281 = (bf16[2048,256]{1,0:T(8,128)(2,1)}, bf16[1024,768]{1,0:T(8,128)(2,1)}, bf16[1024,768]{1,0:T(8,128)(2,1)}, f32[1,192]{1,0:T(1,128)}) custom-call(s32[32]{0:T(128)} %reshape.369.arrive_pos, s32[32]{0:T(128)} %reshape.370.ctx_pos, bf16[2048,64]{1,0:T(8,128)(2,1)} %get-tuple-element.130.q_ref, bf16[2048,64]{1,0:T(8,128)(2,1)} %get-tuple-element.131.k_ref, ...), custom_call_target="tpu_custom_call" | custom-call | flops 4000000000 | bytes 5000000 | tf_op jit(solution)/shard_map/pallas_call | solution.py:219
  469.1 13.9 %all-to-all-done.18 = bf16[8,192,768]{2,1,0:T(8,128)(2,1)S(1)} async-done(((bf16[8,192,768]{2,1,0:T(8,128)(2,1)}), bf16[8,192,768]{2,1,0:T(8,128)(2,1)S(1)}, u32[]{:S(2)}, u32[]{:S(2)}) %all-to-all-start.18) | async-done | bytes 2359328 | tf_op jit(solution)/shard_map/all_to_all | solution.py:40
  483.6 2.3 collective-permute-start.13
  485.9 3.2 collective-permute-done.13
  489.1 3.0 fusion.1
  492.1 4.4 all-to-all-start.19
  501.0 19.5 %all-to-all-done.19 = bf16[8,128,768]{2,1,0:T(8,128)(2,1)S(1)} async-done(((bf16[8,128,768]{2,1,0:T(8,128)(2,1)}), bf16[8,128,768]{2,1,0:T(8,128)(2,1)S(1)}, u32[]{:S(2)}, u32[]{:S(2)}) %all-to-all-start.19) | async-done | bytes 1572896 | tf_op jit(solution)/shard_map/all_to_all | solution.py:40
  520.5 5.0 all-to-all-start.21
  527.7 4.5 shard_map.282
  532.2 3.0 all-to-all-done.21
  535.3 3.6 all-to-all-start.20
  538.9 13.6 %all-to-all-done.20 = bf16[8,80,768]{2,1,0:T(8,128)(2,1)S(1)} async-done(((bf16[8,80,768]{2,1,0:T(8,128)(2,1)}), bf16[8,80,768]{2,1,0:T(8,128)(2,1)S(1)}, u32[]{:S(2)}, u32[]{:S(2)}) %all-to-all-start.20) | async-done | bytes 983072 | tf_op jit(solution)/shard_map/all_to_all | solution.py:40
  552.8 22.6 %all_to_all.124 = bf16[8,80,768]{2,1,0:T(8,128)(2,1)S(1)} all-to-all(bf16[8,80,768]{2,1,0:T(8,128)(2,1)S(1)} %broadcast_in_dim.135), channel_id=1, replica_groups={{0,2,4,6,8,10,12,14},{1,3,5,7,9,11,13,15},{16,18,20,22,24,26,28,30},{17..., dimensions={0} | all-to-all | bytes 1966080 | tf_op jit(solution)/shard_map/all_to_all | solution.py:40
  580.8 8.2 %shard_map.283 = (f32[2,96,2304]{2,1,0:T(8,128)}, f32[2,96,768]{2,1,0:T(8,128)}, f32[2,96,3072]{2,1,0:T(8,128)}, f32[2,384,768]{2,1,0:T(8,128)}, f32[2,384]{1,0:...) custom-call(s32[16]{0:T(128)} %fusion.37.slots, ...), custom_call_target="tpu_custom_call" | custom-call | flops 1000000 | bytes 14000000 | tf_op jit(solution)/shard_map/pallas_call | solution.py:434
  (353 shorter events, 82.8 us)
Async XLA Ops:
  7.2 39.0 %copy-start = (bf16[2,96,3072]{2,1,0:T(8,128)(2,1)S(1)}, bf16[2,96,3072]{2,1,0:T(8,128)(2,1)}, u32[]{:S(2)}) copy-start(bf16[2,96,3072]{2,1,0:T(8,128)(2,1)} %param.28) | copy-start | bytes 3538948
  9.5 30.7 %all-to-all-start = ((bf16[8,128,768]{2,1,0:T(8,128)(2,1)}), bf16[8,128,768]{2,1,0:T(8,128)(2,1)}, u32[]{:S(2)}, u32[]{:S(2)}) async-start(bf16[8,128,768]{2,1,0:T(8,128)(2,1)} %broadcast_in_dim.48), calls=%async_computation | async-start | bytes 3145728 | tf_op jit(solution)/shard_map/all_to_all | solution.py:40
  41.1 16.7 %all-to-all-start.1 = ((bf16[8,64,768]{2,1,0:T(8,128)(2,1)}), bf16[8,64,768]{2,1,0:T(8,128)(2,1)S(1)}, u32[]{:S(2)}, u32[]{:S(2)}) async-start(bf16[8,64,768]{2,1,0:T(8,128)(2,1)} %broadcast_in_dim.51), calls=%async_computation.1 | async-start | bytes 1572864 | tf_op jit(solution)/shard_map/all_to_all | solution.py:40
  47.8 20.6 %collective-permute-start = (bf16[8,128,768]{2,1,0:T(8,128)(2,1)}, bf16[8,128,768]{2,1,0:T(8,128)(2,1)}, u32[]{:S(2)}, u32[]{:S(2)}) collective-permute-start(bf16[8,128,768]{2,1,0:T(8,128)(2,1)} %all-to-all-done), channel_id=1, source_target_pairs={{0,1},{1,0},{2,3},{3,2},{4,5},{5,4},{6,7},{7,6},{8,9},{9,8},{10,11... | collective-permute-start | bytes 4718600 | tf_op jit(solution)/shard_map/ppermute | solution.py:48
  59.2 24.9 %all-to-all-start.2 = ((bf16[8,144,768]{2,1,0:T(8,128)(2,1)}), bf16[8,144,768]{2,1,0:T(8,128)(2,1)S(1)}, u32[]{:S(2)}, u32[]{:S(2)}) async-start(bf16[8,144,768]{2,1,0:T(8,128)(2,1)} %broadcast_in_dim.53), calls=%async_computation.2 | async-start | bytes 3538944 | tf_op jit(solution)/shard_map/all_to_all | solution.py:40
  63.0 99.1 %all-gather.7.cloned.1.call-start = ((), (), s32[]{:S(2)}) async-start(), calls=%async_computation.23 | async-start | bytes 1990656 | tf_op jit(solution)/shard_map/all_gather | solution.py:599
  84.1 17.8 %copy-start.6 = (bf16[1,128,768]{2,1,0:T(8,128)(2,1)S(1)}, bf16[1,128,768]{2,1,0:T(8,128)(2,1)}, u32[]{:S(2)}) copy-start(bf16[1,128,768]{2,1,0:T(8,128)(2,1)} %param.16) | copy-start | bytes 589828
  84.2 19.6 %copy-start.34 = (bf16[8,96,384]{2,1,0:T(8,128)(2,1)}, bf16[8,96,384]{2,1,0:T(8,128)(2,1)S(1)}, u32[]{:S(2)}) copy-start(bf16[8,96,384]{2,1,0:T(8,128)(2,1)S(1)} %pad_maximum_fusion.1) | copy-start | bytes 1769476
  84.2 17.7 %collective-permute-start.1 = (bf16[768,384]{1,0:T(8,128)(2,1)S(1)}, bf16[768,384]{1,0:T(8,128)(2,1)}, u32[]{:S(2)}, u32[]{:S(2)}) collective-permute-start(bf16[768,384]{1,0:T(8,128)(2,1)S(1)} %bitcast.174), channel_id=1, source_target_pairs={{0,1},{1,0},{2,3},{3,2},{4,5},{5,4},{6,7},{7,6},{8,9},{9,8},{10,11... | collective-permute-start | bytes 1769480 | tf_op jit(solution)/shard_map/ppermute | solution.py:48
  104.0 16.5 %copy-start.39 = (bf16[48,768]{1,0:T(8,128)(2,1)S(1)}, bf16[48,768]{1,0:T(8,128)(2,1)}, u32[]{:S(2)}) copy-start(bf16[48,768]{1,0:T(8,128)(2,1)} %get-tuple-element.213) | copy-start | bytes 221188
  104.0 16.5 %copy-start.40 = (bf16[48,384]{1,0:T(8,128)(2,1)S(1)}, bf16[48,384]{1,0:T(8,128)(2,1)}, u32[]{:S(2)}) copy-start(bf16[48,384]{1,0:T(8,128)(2,1)} %get-tuple-element.222) | copy-start | bytes 110596
  104.0 16.5 %copy-start.41 = (bf16[48,384]{1,0:T(8,128)(2,1)S(1)}, bf16[48,384]{1,0:T(8,128)(2,1)}, u32[]{:S(2)}) copy-start(bf16[48,384]{1,0:T(8,128)(2,1)} %get-tuple-element.225) | copy-start | bytes 110596
  104.1 16.5 %copy-start.42 = (bf16[48,384]{1,0:T(8,128)(2,1)S(1)}, bf16[48,384]{1,0:T(8,128)(2,1)}, u32[]{:S(2)}) copy-start(bf16[48,384]{1,0:T(8,128)(2,1)} %get-tuple-element.227) | copy-start | bytes 110596
  104.1 16.5 %copy-start.43 = (bf16[48,384]{1,0:T(8,128)(2,1)S(1)}, bf16[48,384]{1,0:T(8,128)(2,1)}, u32[]{:S(2)}) copy-start(bf16[48,384]{1,0:T(8,128)(2,1)} %get-tuple-element.228) | copy-start | bytes 110596
  104.5 16.8 %copy-start.19 = (bf16[8,64,768]{2,1,0:T(8,128)(2,1)S(1)}, bf16[8,64,768]{2,1,0:T(8,128)(2,1)}, u32[]{:S(2)}) copy-start(bf16[8,64,768]{2,1,0:T(8,128)(2,1)} %copy-done.18) | copy-start | bytes 2359300
  118.5 4.3 collective-permute-start.2
  129.5 2.5 collective-permute-start.3
  133.3 14.8 %copy-start.48 = (f32[768]{0:T(1024)S(1)}, f32[768]{0:T(1024)}, u32[]{:S(2)}) copy-start(f32[768]{0:T(1024)} %get-tuple-element.188) | copy-start | bytes 9220
  148.2 41.8 %copy-start.55 = (f32[128]{0:T(128)}, f32[128]{0:T(128)S(1)}, u32[]{:S(2)}) copy-start(f32[128]{0:T(128)S(1)} %broadcast_multiply_fusion.2) | copy-start | bytes 1540
  148.4 41.6 %copy-start.75 = (f32[128]{0:T(128)}, f32[128]{0:T(128)S(1)}, u32[]{:S(2)}) copy-start(f32[128]{0:T(128)S(1)} %multiply_reduce_fusion.7) | copy-start | bytes 1540
  148.4 41.5 %copy-start.61 = (f32[128]{0:T(128)}, f32[128]{0:T(128)S(1)}, u32[]{:S(2)}) copy-start(f32[128]{0:T(128)S(1)} %fusion.39) | copy-start | bytes 1540
  162.2 34.2 %copy-start.20 = (bf16[1,128,768]{2,1,0:T(8,128)(2,1)S(1)}, bf16[1,128,768]{2,1,0:T(8,128)(2,1)}, u32[]{:S(2)}) copy-start(bf16[1,128,768]{2,1,0:T(8,128)(2,1)} %param.17) | copy-start | bytes 589828
  190.0 12.0 %copy-start.5 = (bf16[8,128,768]{2,1,0:T(8,128)(2,1)}, bf16[8,128,768]{2,1,0:T(8,128)(2,1)S(1)}, u32[]{:S(2)}) copy-start(bf16[8,128,768]{2,1,0:T(8,128)(2,1)S(1)} %all_to_all.118) | copy-start | bytes 4718596
  190.0 5.2 collective-permute-start.4
  197.4 15.5 %all-to-all-start.7 = ((bf16[4,128,768]{2,1,0:T(8,128)(2,1)}), bf16[4,128,768]{2,1,0:T(8,128)(2,1)S(1)}, u32[]{:S(2)}, u32[]{:S(2)}) async-start(bf16[4,128,768]{2,1,0:T(8,128)(2,1)} %broadcast_in_dim.56), calls=%async_computation.7 | async-start | bytes 1572864 | tf_op jit(solution)/shard_map/all_to_all | solution.py:40
  202.1 24.8 %copy-start.36 = (bf16[8,96,384]{2,1,0:T(8,128)(2,1)}, bf16[8,96,384]{2,1,0:T(8,128)(2,1)S(1)}, u32[]{:S(2)}) copy-start(bf16[8,96,384]{2,1,0:T(8,128)(2,1)S(1)} %pad_maximum_fusion.2) | copy-start | bytes 1769476
  202.1 24.7 %collective-permute-start.5 = (bf16[768,384]{1,0:T(8,128)(2,1)S(1)}, bf16[768,384]{1,0:T(8,128)(2,1)S(1)}, u32[]{:S(2)}, u32[]{:S(2)}) collective-permute-start(bf16[768,384]{1,0:T(8,128)(2,1)S(1)} %bitcast.177), channel_id=1, source_target_pairs={{0,1},{1,0},{2,3},{3,2},{4,5},{5,4},{6,7},{7,6},{8,9},{9,8},{10,11... | collective-permute-start | bytes 1769480 | tf_op jit(solution)/shard_map/ppermute | solution.py:48
  211.1 15.7 %copy-start.65 = (f32[768]{0:T(1024)S(1)}, f32[768]{0:T(1024)}, u32[]{:S(2)}) copy-start(f32[768]{0:T(1024)} %get-tuple-element.185) | copy-start | bytes 9220
  212.9 31.4 %copy-start.3 = (bf16[4,128,768]{2,1,0:T(8,128)(2,1)}, bf16[4,128,768]{2,1,0:T(8,128)(2,1)S(1)}, u32[]{:S(2)}) copy-start(bf16[4,128,768]{2,1,0:T(8,128)(2,1)S(1)} %all-to-all-done.7) | copy-start | bytes 2359300
  242.4 3.9 collective-permute-start.6
  244.3 7.8 %collective-permute-start.8 = (bf16[4,128,768]{2,1,0:T(8,128)(2,1)S(1)}, bf16[4,128,768]{2,1,0:T(8,128)(2,1)S(1)}, u32[]{:S(2)}, u32[]{:S(2)}) collective-permute-start(bf16[4,128,768]{2,1,0:T(8,128)(2,1)S(1)} %all-to-all-done.7), channel_id=1, source_target_pairs={{0,1},{1,0},{2,3},{3,2},{4,5},{5,4},{6,7},{7,6},{8,9},{9,8},{10,11... | collective-permute-start | bytes 2359304 | tf_op jit(solution)/shard_map/ppermute | solution.py:48
  258.6 2.5 collective-permute-start.9
  259.0 7.9 %collective-permute-start.7 = (bf16[4,128,768]{2,1,0:T(8,128)(2,1)}, bf16[4,128,768]{2,1,0:T(8,128)(2,1)}, u32[]{:S(2)}, u32[]{:S(2)}) collective-permute-start(bf16[4,128,768]{2,1,0:T(8,128)(2,1)} %bitcast.51), channel_id=1, source_target_pairs={{0,1},{1,0},{2,3},{3,2},{4,5},{5,4},{6,7},{7,6},{8,9},{9,8},{10,11... | collective-permute-start | bytes 2359304 | tf_op jit(solution)/shard_map/ppermute | solution.py:48
  263.4 15.5 %all-to-all-start.11 = ((bf16[4,128,768]{2,1,0:T(8,128)(2,1)}), bf16[4,128,768]{2,1,0:T(8,128)(2,1)S(1)}, u32[]{:S(2)}, u32[]{:S(2)}) async-start(bf16[4,128,768]{2,1,0:T(8,128)(2,1)} %fusion.12), calls=%async_computation.11 | async-start | bytes 1572864 | tf_op jit(solution)/shard_map/all_to_all | solution.py:40
  269.1 14.2 %copy-start.58 = (f32[128]{0:T(128)S(1)}, f32[128]{0:T(128)}, u32[]{:S(2)}) copy-start(f32[128]{0:T(128)} %copy-done.57) | copy-start | bytes 1540
  269.1 14.2 %copy-start.64 = (f32[128]{0:T(128)S(1)}, f32[128]{0:T(128)}, u32[]{:S(2)}) copy-start(f32[128]{0:T(128)} %copy-done.63) | copy-start | bytes 1540
  269.1 14.9 %copy-start.78 = (f32[128]{0:T(128)S(1)}, f32[128]{0:T(128)}, u32[]{:S(2)}) copy-start(f32[128]{0:T(128)} %copy-done.77) | copy-start | bytes 1540
  278.9 14.6 %all-to-all-start.10 = ((bf16[4,128,768]{2,1,0:T(8,128)(2,1)}), bf16[4,128,768]{2,1,0:T(8,128)(2,1)S(1)}, u32[]{:S(2)}, u32[]{:S(2)}) async-start(bf16[4,128,768]{2,1,0:T(8,128)(2,1)} %fusion.13), calls=%async_computation.10 | async-start | bytes 1572864 | tf_op jit(solution)/shard_map/all_to_all | solution.py:40
  282.4 11.2 %copy-start.45 = (f32[768]{0:T(1024)S(1)}, f32[768]{0:T(1024)}, u32[]{:S(2)}) copy-start(f32[768]{0:T(1024)} %get-tuple-element.182) | copy-start | bytes 9220
  284.0 11.2 %copy-start.21 = (bf16[1,128,768]{2,1,0:T(8,128)(2,1)S(1)}, bf16[1,128,768]{2,1,0:T(8,128)(2,1)}, u32[]{:S(2)}) copy-start(bf16[1,128,768]{2,1,0:T(8,128)(2,1)} %param.17) | copy-start | bytes 589828
  297.4 14.2 %all-to-all-start.12 = ((bf16[16,128,64]{1,2,0:T(8,128)(2,1)}), bf16[16,128,64]{1,2,0:T(8,128)(2,1)S(1)}, u32[]{:S(2)}, u32[]{:S(2)}) async-start(bf16[16,128,64]{1,2,0:T(8,128)(2,1)} %concatenate.70), calls=%async_computation.12 | async-start | bytes 524288 | tf_op jit(solution)/shard_map/all_to_all | solution.py:40
  312.6 32.6 %all-to-all-start.13 = ((bf16[8,192,768]{2,1,0:T(8,128)(2,1)}), bf16[8,192,768]{2,1,0:T(8,128)(2,1)S(1)}, u32[]{:S(2)}, u32[]{:S(2)}) async-start(bf16[8,192,768]{2,1,0:T(8,128)(2,1)} %shard_map.276), calls=%async_computation.13 | async-start | bytes 4718592 | tf_op jit(solution)/shard_map/all_to_all | solution.py:40
  316.2 167.3 %all-gather.9.cloned.1.call-start = ((), (), s32[]{:S(2)}) async-start(), calls=%async_computation.24 | async-start | bytes 2506752 | tf_op jit(solution)/shard_map/all_gather | solution.py:644
  346.3 5.1 collective-permute-start.10
  381.1 52.8 %copy-start.8 = (f32[128,768]{1,0:T(8,128)}, f32[128,768]{1,0:T(8,128)S(1)}, u32[]{:S(2)}) copy-start(f32[128,768]{1,0:T(8,128)S(1)} %get-tuple-element.196) | copy-start | bytes 1179652
  381.1 15.7 %copy-start.52 = (f32[768]{0:T(1024)S(1)}, f32[768]{0:T(1024)}, u32[]{:S(2)}) copy-start(f32[768]{0:T(1024)} %get-tuple-element.226) | copy-start | bytes 9220
  381.1 16.9 %copy-start.50 = (f32[768]{0:T(1024)S(1)}, f32[768]{0:T(1024)}, u32[]{:S(2)}) copy-start(f32[768]{0:T(1024)} %get-tuple-element.169) | copy-start | bytes 9220
  381.1 17.5 %copy-start.49 = (f32[768]{0:T(1024)S(1)}, f32[768]{0:T(1024)}, u32[]{:S(2)}) copy-start(f32[768]{0:T(1024)} %get-tuple-element.175) | copy-start | bytes 9220
  394.3 10.3 %collective-permute-start.11 = (bf16[4,128,768]{2,1,0:T(8,128)(2,1)S(1)}, bf16[4,128,768]{2,1,0:T(8,128)(2,1)S(1)}, u32[]{:S(2)}, u32[]{:S(2)}) collective-permute-start(bf16[4,128,768]{2,1,0:T(8,128)(2,1)S(1)} %all_to_all.122), channel_id=1, source_target_pairs={{0,1},{1,0},{2,3},{3,2},{4,5},{5,4},{6,7},{7,6},{8,9},{9,8},{10,11... | collective-permute-start | bytes 2359304 | tf_op jit(solution)/shard_map/ppermute | solution.py:48
  411.2 2.5 collective-permute-start.12
  415.0 17.8 %copy-start.54 = (f32[128]{0:T(128)S(1)}, f32[128]{0:T(128)}, u32[]{:S(2)}) copy-start(f32[128]{0:T(128)} %copy-done.53) | copy-start | bytes 1540
  415.0 17.8 %copy-start.60 = (f32[128]{0:T(128)S(1)}, f32[128]{0:T(128)}, u32[]{:S(2)}) copy-start(f32[128]{0:T(128)} %copy-done.59) | copy-start | bytes 1540
  415.0 18.6 %copy-start.74 = (f32[128]{0:T(128)S(1)}, f32[128]{0:T(128)}, u32[]{:S(2)}) copy-start(f32[128]{0:T(128)} %copy-done.73) | copy-start | bytes 1540
  436.9 12.7 %all-to-all-start.17 = ((bf16[16,128,64]{1,2,0:T(8,128)(2,1)}), bf16[16,128,64]{1,2,0:T(8,128)(2,1)S(1)}, u32[]{:S(2)}, u32[]{:S(2)}) async-start(bf16[16,128,64]{1,2,0:T(8,128)(2,1)} %concatenate.71), calls=%async_computation.17 | async-start | bytes 524288 | tf_op jit(solution)/shard_map/all_to_all | solution.py:40
  450.6 32.5 %all-to-all-start.18 = ((bf16[8,192,768]{2,1,0:T(8,128)(2,1)}), bf16[8,192,768]{2,1,0:T(8,128)(2,1)S(1)}, u32[]{:S(2)}, u32[]{:S(2)}) async-start(bf16[8,192,768]{2,1,0:T(8,128)(2,1)} %shard_map.280), calls=%async_computation.18 | async-start | bytes 4718592 | tf_op jit(solution)/shard_map/all_to_all | solution.py:40
  483.6 5.6 collective-permute-start.13
  492.1 28.4 %all-to-all-start.19 = ((bf16[8,128,768]{2,1,0:T(8,128)(2,1)}), bf16[8,128,768]{2,1,0:T(8,128)(2,1)S(1)}, u32[]{:S(2)}, u32[]{:S(2)}) async-start(bf16[8,128,768]{2,1,0:T(8,128)(2,1)} %fusion.1), calls=%async_computation.19 | async-start | bytes 3145728 | tf_op jit(solution)/shard_map/all_to_all | solution.py:40
  496.5 84.2 %all-gather.11.cloned.1.call-start = ((), (), s32[]{:S(2)}) async-start(), calls=%async_computation.25 | async-start | bytes 2506752 | tf_op jit(solution)/shard_map/all_gather | solution.py:648
  520.5 14.8 %all-to-all-start.21 = ((bf16[16,16,768]{2,1,0:T(8,128)(2,1)}), bf16[16,16,768]{2,1,0:T(8,128)(2,1)S(1)}, u32[]{:S(2)}, u32[]{:S(2)}) async-start(bf16[16,16,768]{2,1,0:T(8,128)(2,1)} %pad.6.clone), calls=%async_computation.21 | async-start | bytes 786432 | tf_op jit(solution)/shard_map/all_to_all | solution.py:40
  535.3 17.2 %all-to-all-start.20 = ((bf16[8,80,768]{2,1,0:T(8,128)(2,1)}), bf16[8,80,768]{2,1,0:T(8,128)(2,1)S(1)}, u32[]{:S(2)}, u32[]{:S(2)}) async-start(bf16[8,80,768]{2,1,0:T(8,128)(2,1)} %shard_map.282), calls=%async_computation.20 | async-start | bytes 1966080 | tf_op jit(solution)/shard_map/all_to_all | solution.py:40
  552.6 25.0 %copy-start.9 = (f32[128,768]{1,0:T(8,128)S(1)}, f32[128,768]{1,0:T(8,128)}, u32[]{:S(2)}) copy-start(f32[128,768]{1,0:T(8,128)} %copy-done.8) | copy-start | bytes 1179652
  552.7 25.0 %copy-start.11 = (f32[128,768]{1,0:T(8,128)S(1)}, f32[128,768]{1,0:T(8,128)}, u32[]{:S(2)}) copy-start(f32[128,768]{1,0:T(8,128)} %copy-done.10) | copy-start | bytes 1179652
  552.7 24.9 %copy-start.68 = (f32[128]{0:T(128)S(1)}, f32[128]{0:T(128)}, u32[]{:S(2)}) copy-start(f32[128]{0:T(128)} %copy-done.67) | copy-start | bytes 1540
  575.4 3.9 collective-permute-start.14
  (51 other events, 142.5 us)
Sparse Core Ops, SparseCore 0:
  121.4 40.6 all-gather.6
  412.1 49.5 all-gather.8
  500.4 53.2 all-gather.10

commit v6 on v5

--- a/solution.py
+++ b/solution.py
@@ -53,19 +53,25 @@
     return own, swap_core(own)
 
 
-def gather_x(part):
+def gather_x(part, beside=()):
     own = spread_to(part, 4, "ctx", X_GROUPS)
-    return own.reshape(4 * TOK, D), swap_core(own).reshape(4 * TOK, D)
-
-
-def scatter(near, far, groups):
+    own, beside = lax.optimization_barrier((own, beside))
+    return (own.reshape(4 * TOK, D), swap_core(own).reshape(4 * TOK, D)), beside
+
+
+def scatter(near, far, groups, run=None):
     mine = near.astype(F32) + swap_core(far.astype(BF16)).astype(F32)
-    parts = exchange(mine.astype(BF16), "ctx", groups)
-    return jnp.sum(parts.astype(F32), axis=0)
-
-
-def scatter_x(near, far):
-    return scatter(near.reshape(4, TOK, D), far.reshape(4, TOK, D), X_GROUPS)
+    mine = mine.astype(BF16)
+    if run is None:
+        return jnp.sum(exchange(mine, "ctx", groups).astype(F32), axis=0)
+    start, ready = run
+    mine, start = lax.optimization_barrier((mine, start))
+    parts, result = lax.optimization_barrier((exchange(mine, "ctx", groups), ready(start)))
+    return jnp.sum(parts.astype(F32), axis=0), result
+
+
+def scatter_x(near, far, run=None):
+    return scatter(near.reshape(4, TOK, D), far.reshape(4, TOK, D), X_GROUPS, run)
 
 
 def dot(left, right, dims=((1,), (0,))):
@@ -297,7 +303,7 @@
         out_specs=(WHOLE,) * 4,
         scratch_shapes=[pltpu.VMEM((D, 384), BF16), pltpu.VMEM((384, D), BF16)],
         compiler_params=pltpu.CompilerParams(vmem_limit_bytes=VMEM_BYTES),
-        cost_estimate=pl.CostEstimate(flops=12 * 10**8, bytes_accessed=7 * 10**6, transcendentals=4 * 10**5),
+        cost_estimate=pl.CostEstimate(flops=10**6, bytes_accessed=10**5, transcendentals=0),
     )(own, other, rows, shift)
 
 
@@ -393,21 +399,11 @@
     )(head, *parts)
 
 
-def unpack_kernel(slots, late_ref, first_ref, last_ref, qkv_ref, out_ref, up_ref, down_ref, up_shift_ref, *vector_refs):
+def unpack_wide_kernel(first_ref, last_ref, up_ref, down_ref):
     for layer, wide_ref in enumerate((first_ref, last_ref)):
-        def late(place, start, end):
-            return late_ref[slots[place], start:end, :].astype(F32)
-
         def wide(place, start, end, wide_ref=wide_ref):
             return wide_ref[place, start:end, :].astype(F32)
 
-        for head in range(H):
-            block = late(head, layer * 32, (layer + 1) * 32)
-            for part in range(3):
-                for kind in range(3):
-                    lane = part * 256 + kind * HD
-                    column = kind * D + head * HD
-                    qkv_ref[layer, part * 32 : (part + 1) * 32, column : column + HD] = block[:, lane : lane + HD]
         for rank in range(8):
             block = wide(rank, UPS, DOWNS) + wide(rank + 8, UPS, DOWNS)
             for part in range(2):
@@ -417,28 +413,58 @@
                     up_ref[layer, part * 48 : (part + 1) * 48, column : column + 48] = block[:, lane : lane + 48]
             block = wide(rank, DOWNS, OUTS) + wide(rank + 8, DOWNS, OUTS)
             down_ref[layer, rank * 48 : (rank + 1) * 48, :] = block
-            small = late(rank, SMALL, SECOND) + late(rank + 8, SMALL, SECOND)
+
+
+def unpack_late_kernel(slots, late_ref, qkv_ref, out_ref, up_shift_ref, *vector_refs):
+    def late(place, start, end):
+        return late_ref[slots[place], start:end, :].astype(F32)
+
+    for layer in range(LAYERS):
+        for head in range(H):
+            block = late(head, layer * 32, (layer + 1) * 32)
+            for part in range(3):
+                for kind in range(3):
+                    lane = part * 256 + kind * HD
+                    column = kind * D + head * HD
+                    qkv_ref[layer, part * 32 : (part + 1) * 32, column : column + HD] = block[:, lane : lane + HD]
+    totals = [None] * LAYERS
+    for rank in range(8):
+        low, high = late(rank, SMALL, SECOND), late(rank + 8, SMALL, SECOND)
+        small = low + high
+        for layer in range(LAYERS):
             up_shift_ref[layer : layer + 1, rank * 48 : (rank + 1) * 48] = small[2 * layer + 1 : 2 * layer + 2, :48]
             mine = small[2 * layer : 2 * layer + 1, :]
-            vectors = mine if rank == 0 else vectors + mine
+            totals[layer] = mine if rank == 0 else totals[layer] + mine
+            rows = slice(4 + 6 * layer, 10 + 6 * layer)
+            out_ref[layer, rank * 6 : (rank + 1) * 6, :] = low[rows, :]
+            out_ref[layer, (rank + 8) * 6 : (rank + 9) * 6, :] = high[rows, :]
+    for layer in range(LAYERS):
         for member, ref in enumerate(vector_refs):
-            ref[layer : layer + 1, :] = vectors[:, member * 96 : (member + 1) * 96]
-    for place in range(C):
-        small = late_ref[slots[place], SMALL:SECOND, :].astype(F32)
-        for layer in range(LAYERS):
-            out_ref[layer, place * 6 : (place + 1) * 6, :] = small[4 + 6 * layer : 10 + 6 * layer, :]
-
-
-def unpack(slots, late, first, last):
-    shapes = [(96, 3 * D), (96, D), (96, FF), (384, D), (384,)] + [(96,)] * 8
+            ref[layer : layer + 1, :] = totals[layer][:, member * 96 : (member + 1) * 96]
+
+
+def unpack_wide(first, last):
+    shapes = [(96, FF), (384, D)]
     return pl.pallas_call(
-        unpack_kernel,
+        unpack_wide_kernel,
         out_shape=tuple(jax.ShapeDtypeStruct((LAYERS,) + shape, F32) for shape in shapes),
-        in_specs=[SMEM] + [WHOLE] * 3,
+        in_specs=[WHOLE] * 2,
         out_specs=(WHOLE,) * len(shapes),
         compiler_params=pltpu.CompilerParams(vmem_limit_bytes=VMEM_BYTES),
-        cost_estimate=pl.CostEstimate(flops=10**6, bytes_accessed=14 * 10**6, transcendentals=0),
-    )(slots, late, first, last)
+        cost_estimate=pl.CostEstimate(flops=10**6, bytes_accessed=10 * 10**6, transcendentals=0),
+    )(first, last)
+
+
+def unpack_late(slots, late):
+    shapes = [(96, 3 * D), (96, D), (384,)] + [(96,)] * 8
+    return pl.pallas_call(
+        unpack_late_kernel,
+        out_shape=tuple(jax.ShapeDtypeStruct((LAYERS,) + shape, F32) for shape in shapes),
+        in_specs=[SMEM, WHOLE],
+        out_specs=(WHOLE,) * len(shapes),
+        compiler_params=pltpu.CompilerParams(vmem_limit_bytes=VMEM_BYTES),
+        cost_estimate=pl.CostEstimate(flops=10**6, bytes_accessed=5 * 10**6, transcendentals=0),
+    )(slots, late)
 
 
 def join_cores(core, own, other, axis):
@@ -470,14 +496,20 @@
     mixed = mixed.transpose(1, 0, 2).reshape(TOK, D)
     middle = flowing + dot(mixed, out_full) + out_shift
     second = layer_norm(middle, gain_two, bias_two).astype(BF16)
-    second_all = gather_x(second)
+    second_all, unused = gather_x(second)
     hidden, activated, near, far = feed(*second_all, layer_rows, up_shift)
-    output = middle + scatter_x(near, far) + down_shift
+    if carried is None:
+        summed = scatter_x(near, far)
+    else:
+        run = ((carried, layer_rows, hidden), lambda start: feed_back(*start[0], start[1], start[2]))
+        summed, begun = scatter_x(near, far, run)
+        carried = (carried, begun)
+    output = middle + summed + down_shift
     saved = (flowing, own, other, queries, keys, values, mixed, middle, second_all, hidden, activated)
     return output, saved, carried, (head_weight, out_full, layer_rows)
 
 
-def backward_layer(grad_out, down_all, saved, params, small, places, head, layer, prior, spread):
+def backward_layer(grad_out, begun, saved, params, small, places, head, layer, prior, spread):
     arrive_pos, ctx_pos = places
     head_weight, out_full, layer_rows = params
     unused, vectors, unused = small
@@ -485,10 +517,12 @@
     flowing, own, other, queries, keys, values, mixed, middle, second_all, hidden, activated = saved
     down_in = grad_out.astype(BF16)
     down_shift_grad = jnp.sum(down_in.astype(F32), axis=0, keepdims=True)
-    if down_all is None:
-        down_all = gather_x(down_in)
-    hidden_grad, near, far, up_shift_grad = feed_back(*down_all, layer_rows, hidden)
-    near, far, prior = lax.optimization_barrier((near, far, prior))
+    if begun is None:
+        down_all, prior = gather_x(down_in, prior)
+        begun = feed_back(*down_all, layer_rows, hidden)
+    else:
+        down_all, begun = begun
+    hidden_grad, near, far, up_shift_grad = begun
     second_grad = scatter_x(near, far)
     unused, norm_back = jax.vjp(layer_norm, middle, gain_two, bias_two)
     middle_part, gain_two_grad, bias_two_grad = norm_back(second_grad)
@@ -652,10 +686,13 @@
     outs = jnp.sum(outs, axis=0)[:12].astype(BF16)
     late = jnp.sum(exchange(late, "shard").astype(F32), axis=0).astype(BF16)
     late = jnp.concatenate([late[: SMALL + 4], outs], axis=0)
-    every_late = jnp.concatenate(gather_ctx(late), axis=0)
+    near = spread_to(late, 8, "ctx", CHIP_GROUPS)
+    near, wide = lax.optimization_barrier((near, unpack_wide(every_first, every_last)))
+    ups, downs = wide
+    every_late = jnp.concatenate([near, swap_core(near)], axis=0)
     places_of = jnp.arange(C, dtype=jnp.int32)
     slots = places_of // 2 + 8 * (places_of % 2 != core).astype(jnp.int32)
-    qkv, outs, ups, downs, hiddens, *vectors = unpack(slots, every_late, every_first, every_last)
+    qkv, outs, hiddens, *vectors = unpack_late(slots, every_late)
     return (
         result,
         grad_flow.astype(BF16).reshape(states.shape),

time: 601 us -> 596 us (level)
  blocking collectives: 175 us -> 139 us
  waiting for transfers between devices: 147 us -> 170 us
  starting transfers between devices: 78.1 us -> 86.5 us
    all_to_all x10 -> x8, blocking collectives: 175 us -> 139 us  [exchange(): lax.all_to_all(parts, axis, 0, 0, tiled=True, axis_index_groups=groups)]
    all_to_all x13 -> x15, waiting for transfers between devices: 117 us -> 136 us  [exchange(): lax.all_to_all(parts, axis, 0, 0, tiled=True, axis_index_groups=groups)]
    all_to_all x13 -> x15, starting transfers between devices: 56.7 us -> 65 us  [exchange(): lax.all_to_all(parts, axis, 0, 0, tiled=True, axis_index_groups=groups)]
  transfers between devices with their start and end apart: 31 -> 33, of which waited for: 22 -> 26; matrix products, arithmetic and copies ran while one was open for 9% -> 9% of each run, Pallas kernels for 13% -> 15%
where the time goes in v6:
time: 596 us; the launch traced here: 591 us
  waiting for transfers between devices  170 us (29%)
  blocking collectives  139 us (23%)
  Pallas kernels  101 us (17%)
  starting transfers between devices  86.5 us (15%)
  local copies, waits for them, and re-layouts  45.8 us (8%)
  other arithmetic  26.9 us (5%)
  between operations  15.4 us (3%)
    all_to_all x8, blocking collectives, exchange(): lax.all_to_all(parts, axis, 0, 0, tiled=True, axis_index_groups=groups)  139 us
    all_to_all x15, waiting for transfers between devices, exchange(): lax.all_to_all(parts, axis, 0, 0, tiled=True, axis_index_groups=groups)  136 us
    all_to_all x15, starting transfers between devices, exchange(): lax.all_to_all(parts, axis, 0, 0, tiled=True, axis_index_groups=groups)  65 us
    pallas_call x2, Pallas kernels, attend_back(): pl.pallas_call(attend_back_kernel, out_shape=(jax.ShapeDtypeStruct((LEN,...  29.4 us
    ppermute x15, starting transfers between devices, swap_core(): return lax.ppermute(part, 'ctx', SWAP)  20.6 us
    ppermute x15, waiting for transfers between devices, swap_core(): return lax.ppermute(part, 'ctx', SWAP)  20 us
    pallas_call x2, Pallas kernels, attend(): pl.pallas_call(functools.partial(attend_kernel, fresh), out_shape=outs, i...  18.9 us
    all_gather x1, waiting for transfers between devices, shards(): lax.all_gather(layer_pieces[1], 'shard', axis=0)  13.3 us
  transfers between devices with their start and end apart: 33, of which 26 were waited for; matrix products, arithmetic and copies ran while one was open for 9% of the time, Pallas kernels for 15%

profile of v6, /device:TPU:1, one launch (start us, length us, event | category | flops | bytes accessed | tf_op | source)
XLA Modules:
  0.0 590.9 jit_solution(9088768126705272583)
XLA Ops:
  7.2 2.3 broadcast_in_dim.48
  9.6 7.6 %all-to-all-start = ((bf16[8,128,768]{2,1,0:T(8,128)(2,1)}), bf16[8,128,768]{2,1,0:T(8,128)(2,1)}, u32[]{:S(2)}, u32[]{:S(2)}) async-start(bf16[8,128,768]{2,1,0:T(8,128)(2,1)} %broadcast_in_dim.48), calls=%async_computation | async-start | bytes 3145728 | tf_op jit(solution)/shard_map/all_to_all | solution.py:40
  23.1 17.1 %all-to-all-done = bf16[8,128,768]{2,1,0:T(8,128)(2,1)} async-done(((bf16[8,128,768]{2,1,0:T(8,128)(2,1)}), bf16[8,128,768]{2,1,0:T(8,128)(2,1)}, u32[]{:S(2)}, u32[]{:S(2)}) %all-to-all-start) | async-done | bytes 1572896 | tf_op jit(solution)/shard_map/all_to_all | solution.py:40
  41.2 5.1 all-to-all-start.1
  49.1 8.7 %all-to-all-done.1 = bf16[8,64,768]{2,1,0:T(8,128)(2,1)S(1)} async-done(((bf16[8,64,768]{2,1,0:T(8,128)(2,1)}), bf16[8,64,768]{2,1,0:T(8,128)(2,1)S(1)}, u32[]{:S(2)}, u32[]{:S(2)}) %all-to-all-start.1) | async-done | bytes 786464 | tf_op jit(solution)/shard_map/all_to_all | solution.py:40
  59.3 3.8 all-to-all-start.2
  68.6 10.3 %shard_map.271 = (bf16[2048,64]{1,0:T(8,128)(2,1)}, bf16[2048,64]{1,0:T(8,128)(2,1)}, bf16[2048,64]{1,0:T(8,128)(2,1)}, bf16[2048,64]{1,0:T(8,128)(2,1)}, bf16[1...) custom-call(s32[32]{0:T(128)} %reshape.369.arrive_pos, s32[32]{0:T(128)} %reshape.370.ctx_pos, ...), custom_call_target="tpu_custom_call" | custom-call | flops 2000000000 | bytes 5000000 | tf_op jit(solution)/shard_map/pallas_call | solution.py:213
  78.8 5.3 all-to-all-done.2.rows_ref
  84.3 3.4 collective-permute-start.1
  89.0 13.0 %all_to_all.115 = bf16[16,128,64]{1,2,0:T(8,128)(2,1)S(1)} all-to-all(bf16[16,128,64]{1,2,0:T(8,128)(2,1)S(1)} %copy.69), channel_id=1, replica_groups=mesh['shard'=8,'ctx'=16] {'ctx'}, dimensions={0} | all-to-all | bytes 524288 | tf_op jit(solution)/shard_map/all_to_all | solution.py:40
  104.7 13.9 %all_to_all.116 = bf16[4,128,768]{2,1,0:T(8,128)(2,1)S(1)} all-to-all(bf16[4,128,768]{2,1,0:T(8,128)(2,1)S(1)} %broadcast_in_dim.54), channel_id=1, replica_groups={{0,2,4,6},{1,3,5,7},{8,10,12,14},{9,11,13,15},{16,18,20,22},{17,19,21,2..., dimensions={0} | all-to-all | bytes 1572864 | tf_op jit(solution)/shard_map/all_to_all | solution.py:40
  123.8 5.8 shard_map.272
  129.6 2.5 collective-permute-done.3
  133.4 14.6 %all_to_all.117 = bf16[4,128,768]{2,1,0:T(8,128)(2,1)S(1)} all-to-all(bf16[4,128,768]{2,1,0:T(8,128)(2,1)S(1)} %fusion.14), channel_id=1, replica_groups={{0,2,4,6},{1,3,5,7},{8,10,12,14},{9,11,13,15},{16,18,20,22},{17,19,21,2..., dimensions={0} | all-to-all | bytes 1572864 | tf_op jit(solution)/shard_map/all_to_all | solution.py:40
  148.9 13.3 %all-gather.7.cloned.1.call-done = bf16[1152,768]{1,0:T(8,128)(2,1)} async-done(((bf16[144,768]{1,0:T(8,128)(2,1)}), bf16[1152,768]{1,0:T(8,128)(2,1)}) %all-gather.7.cloned.1.call-update) | async-done | bytes 1769488 | tf_op jit(solution)/shard_map/all_gather | solution.py:633
  162.3 27.7 %all_to_all.118 = bf16[8,128,768]{2,1,0:T(8,128)(2,1)S(1)} all-to-all(bf16[8,128,768]{2,1,0:T(8,128)(2,1)S(1)} %broadcast_in_dim.55), channel_id=1, replica_groups={{0,2,4,6,8,10,12,14},{1,3,5,7,9,11,13,15},{16,18,20,22,24,26,28,30},{17..., dimensions={0} | all-to-all | bytes 3145728 | tf_op jit(solution)/shard_map/all_to_all | solution.py:40
  190.1 2.2 collective-permute-start.4
  192.3 3.0 collective-permute-done.4
  197.5 3.5 all-to-all-start.7
  202.7 8.6 %shard_map.273 = (bf16[2048,64]{1,0:T(8,128)(2,1)}, bf16[2048,64]{1,0:T(8,128)(2,1)}, bf16[2048,64]{1,0:T(8,128)(2,1)}, bf16[2048,64]{1,0:T(8,128)(2,1)}) custom-call(s32[32]{0:T(128)} %reshape.369.arrive_pos, s32[32]{0:T(128)} %reshape.370.ctx_pos, bf16[1024,768]{1,0:T(8,128)(2,1)} %bitcast.147, bf16[1024,768]{1,0:T(8,128)(2,1)} %bitcast.161, ...), custom_call_target="tpu_custom_call" | custom-call | flops 2000000000 | bytes 5000000 | tf_op jit(solution)/shard_map/pallas_call | solution.py:213
  214.5 12.4 %all_to_all.119 = bf16[16,128,64]{1,2,0:T(8,128)(2,1)S(1)} all-to-all(bf16[16,128,64]{1,2,0:T(8,128)(2,1)S(1)} %copy.70), channel_id=1, replica_groups=mesh['shard'=8,'ctx'=16] {'ctx'}, dimensions={0} | all-to-all | bytes 524288 | tf_op jit(solution)/shard_map/all_to_all | solution.py:40
  228.6 13.8 %all_to_all.120 = bf16[4,128,768]{2,1,0:T(8,128)(2,1)S(1)} all-to-all(bf16[4,128,768]{2,1,0:T(8,128)(2,1)S(1)} %broadcast_in_dim.57), channel_id=1, replica_groups={{0,2,4,6},{1,3,5,7},{8,10,12,14},{9,11,13,15},{16,18,20,22},{17,19,21,2..., dimensions={0} | all-to-all | bytes 1572864 | tf_op jit(solution)/shard_map/all_to_all | solution.py:40
  247.2 5.7 shard_map.274
  255.5 2.2 fusion.13
  257.7 3.5 all-to-all-start.10
  261.2 5.7 shard_map.275
  266.9 6.3 %all-to-all-done.10 = bf16[4,128,768]{2,1,0:T(8,128)(2,1)S(1)} async-done(((bf16[4,128,768]{2,1,0:T(8,128)(2,1)}), bf16[4,128,768]{2,1,0:T(8,128)(2,1)S(1)}, u32[]{:S(2)}, u32[]{:S(2)}) %all-to-all-start.10) | async-done | bytes 786464 | tf_op jit(solution)/shard_map/all_to_all | solution.py:40
  274.4 2.1 collective-permute-done.9
  276.5 2.2 fusion.12
  278.7 3.5 all-to-all-start.11
  282.4 11.8 %all-to-all-done.11 = bf16[4,128,768]{2,1,0:T(8,128)(2,1)S(1)} async-done(((bf16[4,128,768]{2,1,0:T(8,128)(2,1)}), bf16[4,128,768]{2,1,0:T(8,128)(2,1)S(1)}, u32[]{:S(2)}, u32[]{:S(2)}) %all-to-all-start.11) | async-done | bytes 786464 | tf_op jit(solution)/shard_map/all_to_all | solution.py:40
  299.8 4.5 all-to-all-start.12
  305.2 5.8 shard_map.276
  310.9 2.2 all-to-all-done.12
  314.1 4.0 all-to-all-start.13
  318.1 14.7 %shard_map.277 = (bf16[2048,256]{1,0:T(8,128)(2,1)}, bf16[1024,768]{1,0:T(8,128)(2,1)}, bf16[1024,768]{1,0:T(8,128)(2,1)}, f32[1,192]{1,0:T(1,128)}) custom-call(s32[32]{0:T(128)} %reshape.369.arrive_pos, s32[32]{0:T(128)} %reshape.370.ctx_pos, bf16[2048,64]{1,0:T(8,128)(2,1)} %get-tuple-element.129.q_ref, bf16[2048,64]{1,0:T(8,128)(2,1)} %get-tuple-element.130.k_ref, ...), custom_call_target="tpu_custom_call" | custom-call | flops 4000000000 | bytes 5000000 | tf_op jit(solution)/shard_map/pallas_call | solution.py:225
  332.8 14.3 %all-to-all-done.13 = bf16[8,192,768]{2,1,0:T(8,128)(2,1)S(1)} async-done(((bf16[8,192,768]{2,1,0:T(8,128)(2,1)}), bf16[8,192,768]{2,1,0:T(8,128)(2,1)S(1)}, u32[]{:S(2)}, u32[]{:S(2)}) %all-to-all-start.13) | async-done | bytes 2359328 | tf_op jit(solution)/shard_map/all_to_all | solution.py:40
  350.0 3.2 collective-permute-done.10
  355.1 26.5 %all_to_all.121 = bf16[8,128,768]{2,1,0:T(8,128)(2,1)S(1)} all-to-all(bf16[8,128,768]{2,1,0:T(8,128)(2,1)S(1)} %fusion.2), channel_id=1, replica_groups={{0,2,4,6,8,10,12,14},{1,3,5,7,9,11,13,15},{16,18,20,22,24,26,28,30},{17..., dimensions={0} | all-to-all | bytes 3145728 | tf_op jit(solution)/shard_map/all_to_all | solution.py:40
  384.0 3.5 all-to-all-start.15
  391.1 4.3 shard_map.278.rest_6_
  395.4 2.9 all-to-all-done.15
  398.2 2.5 collective-permute-start.11
  403.5 5.7 shard_map.279
  413.1 17.4 %all_to_all.122 = bf16[4,128,768]{2,1,0:T(8,128)(2,1)S(1)} all-to-all(bf16[4,128,768]{2,1,0:T(8,128)(2,1)S(1)} %fusion.11), channel_id=1, replica_groups={{0,2,4,6},{1,3,5,7},{8,10,12,14},{9,11,13,15},{16,18,20,22},{17,19,21,2..., dimensions={0} | all-to-all | bytes 1572864 | tf_op jit(solution)/shard_map/all_to_all | solution.py:40
  434.9 3.8 all-to-all-start.17
  439.5 5.8 shard_map.280
  445.2 2.4 all-to-all-done.17
  448.6 3.7 all-to-all-start.18
  452.5 14.7 %shard_map.281 = (bf16[2048,256]{1,0:T(8,128)(2,1)}, bf16[1024,768]{1,0:T(8,128)(2,1)}, bf16[1024,768]{1,0:T(8,128)(2,1)}, f32[1,192]{1,0:T(1,128)}) custom-call(s32[32]{0:T(128)} %reshape.369.arrive_pos, s32[32]{0:T(128)} %reshape.370.ctx_pos, bf16[2048,64]{1,0:T(8,128)(2,1)} %get-tuple-element.147.q_ref, bf16[2048,64]{1,0:T(8,128)(2,1)} %get-tuple-element.148.k_ref, ...), custom_call_target="tpu_custom_call" | custom-call | flops 4000000000 | bytes 5000000 | tf_op jit(solution)/shard_map/pallas_call | solution.py:225
  467.3 14.0 %all-to-all-done.18 = bf16[8,192,768]{2,1,0:T(8,128)(2,1)S(1)} async-done(((bf16[8,192,768]{2,1,0:T(8,128)(2,1)}), bf16[8,192,768]{2,1,0:T(8,128)(2,1)S(1)}, u32[]{:S(2)}, u32[]{:S(2)}) %all-to-all-start.18) | async-done | bytes 2359328 | tf_op jit(solution)/shard_map/all_to_all | solution.py:40
  484.5 2.5 collective-permute-done.13
  487.1 2.9 fusion.1
  490.0 4.3 all-to-all-start.19
  498.0 20.8 %all-to-all-done.19 = bf16[8,128,768]{2,1,0:T(8,128)(2,1)S(1)} async-done(((bf16[8,128,768]{2,1,0:T(8,128)(2,1)}), bf16[8,128,768]{2,1,0:T(8,128)(2,1)S(1)}, u32[]{:S(2)}, u32[]{:S(2)}) %all-to-all-start.19) | async-done | bytes 1572896 | tf_op jit(solution)/shard_map/all_to_all | solution.py:40
  518.8 6.9 %all-to-all-start.21 = ((bf16[16,16,768]{2,1,0:T(8,128)(2,1)}), bf16[16,16,768]{2,1,0:T(8,128)(2,1)S(1)}, u32[]{:S(2)}, u32[]{:S(2)}) async-start(bf16[16,16,768]{2,1,0:T(8,128)(2,1)} %pad.6.clone), calls=%async_computation.21 | async-start | bytes 786432 | tf_op jit(solution)/shard_map/all_to_all | solution.py:40
  527.9 4.5 shard_map.282
  532.4 4.4 all-to-all-done.21
  536.9 3.6 all-to-all-start.20
  540.5 14.3 %all-to-all-done.20 = bf16[8,80,768]{2,1,0:T(8,128)(2,1)S(1)} async-done(((bf16[8,80,768]{2,1,0:T(8,128)(2,1)}), bf16[8,80,768]{2,1,0:T(8,128)(2,1)S(1)}, u32[]{:S(2)}, u32[]{:S(2)}) %all-to-all-start.20) | async-done | bytes 983072 | tf_op jit(solution)/shard_map/all_to_all | solution.py:40
  556.0 3.6 all-to-all-start.22
  559.7 6.5 %shard_map.283 = (f32[2,96,3072]{2,1,0:T(8,128)}, f32[2,384,768]{2,1,0:T(8,128)}) custom-call(bf16[16,96,768]{2,1,0:T(8,128)(2,1)} %bitcast.159, bf16[16,96,768]{2,1,0:T(8,128)(2,1)} %bitcast.158), custom_call_target="tpu_custom_call" | custom-call | flops 1000000 | bytes 10000000 | tf_op jit(solution)/shard_map/pallas_call | solution.py:448
  566.1 10.1 %all-to-all-done.22 = bf16[8,80,768]{2,1,0:T(8,128)(2,1)S(1)} async-done(((bf16[8,80,768]{2,1,0:T(8,128)(2,1)}), bf16[8,80,768]{2,1,0:T(8,128)(2,1)S(1)}, u32[]{:S(2)}, u32[]{:S(2)}) %all-to-all-start.22) | async-done | bytes 983072 | tf_op jit(solution)/shard_map/all_to_all | solution.py:40
  580.7 3.3 shard_map.284
  (368 shorter events, 90.9 us)
Async XLA Ops:
  7.2 39.1 %copy-start = (bf16[2,96,3072]{2,1,0:T(8,128)(2,1)S(1)}, bf16[2,96,3072]{2,1,0:T(8,128)(2,1)}, u32[]{:S(2)}) copy-start(bf16[2,96,3072]{2,1,0:T(8,128)(2,1)} %param.28) | copy-start | bytes 3538948
  9.5 8.0 %copy-start.72 = (bf16[2,384]{1,0:T(2,128)(2,1)S(1)}, bf16[2,384]{1,0:T(2,128)(2,1)}, u32[]{:S(2)}) copy-start(bf16[2,384]{1,0:T(2,128)(2,1)} %param.29) | copy-start | bytes 4612
  9.6 9.7 %copy-start.27 = (bf16[2,96,2304]{2,1,0:T(8,128)(2,1)S(1)}, bf16[2,96,2304]{2,1,0:T(8,128)(2,1)}, u32[]{:S(2)}) copy-start(bf16[2,96,2304]{2,1,0:T(8,128)(2,1)} %param.21) | copy-start | bytes 2654212
  9.6 30.7 %all-to-all-start = ((bf16[8,128,768]{2,1,0:T(8,128)(2,1)}), bf16[8,128,768]{2,1,0:T(8,128)(2,1)}, u32[]{:S(2)}, u32[]{:S(2)}) async-start(bf16[8,128,768]{2,1,0:T(8,128)(2,1)} %broadcast_in_dim.48), calls=%async_computation | async-start | bytes 3145728 | tf_op jit(solution)/shard_map/all_to_all | solution.py:40
  41.2 16.7 %all-to-all-start.1 = ((bf16[8,64,768]{2,1,0:T(8,128)(2,1)}), bf16[8,64,768]{2,1,0:T(8,128)(2,1)S(1)}, u32[]{:S(2)}, u32[]{:S(2)}) async-start(bf16[8,64,768]{2,1,0:T(8,128)(2,1)} %broadcast_in_dim.51), calls=%async_computation.1 | async-start | bytes 1572864 | tf_op jit(solution)/shard_map/all_to_all | solution.py:40
  48.0 20.6 %collective-permute-start = (bf16[8,128,768]{2,1,0:T(8,128)(2,1)}, bf16[8,128,768]{2,1,0:T(8,128)(2,1)}, u32[]{:S(2)}, u32[]{:S(2)}) collective-permute-start(bf16[8,128,768]{2,1,0:T(8,128)(2,1)} %all-to-all-done), channel_id=1, source_target_pairs={{0,1},{1,0},{2,3},{3,2},{4,5},{5,4},{6,7},{7,6},{8,9},{9,8},{10,11... | collective-permute-start | bytes 4718600 | tf_op jit(solution)/shard_map/ppermute | solution.py:48
  59.3 24.9 %all-to-all-start.2 = ((bf16[8,144,768]{2,1,0:T(8,128)(2,1)}), bf16[8,144,768]{2,1,0:T(8,128)(2,1)S(1)}, u32[]{:S(2)}, u32[]{:S(2)}) async-start(bf16[8,144,768]{2,1,0:T(8,128)(2,1)} %broadcast_in_dim.53), calls=%async_computation.2 | async-start | bytes 3538944 | tf_op jit(solution)/shard_map/all_to_all | solution.py:40
  63.1 99.1 %all-gather.7.cloned.1.call-start = ((), (), s32[]{:S(2)}) async-start(), calls=%async_computation.23 | async-start | bytes 1990656 | tf_op jit(solution)/shard_map/all_gather | solution.py:633
  84.2 17.8 %copy-start.8 = (bf16[1,128,768]{2,1,0:T(8,128)(2,1)S(1)}, bf16[1,128,768]{2,1,0:T(8,128)(2,1)}, u32[]{:S(2)}) copy-start(bf16[1,128,768]{2,1,0:T(8,128)(2,1)} %param.16) | copy-start | bytes 589828
  84.3 19.6 %copy-start.34 = (bf16[8,96,384]{2,1,0:T(8,128)(2,1)}, bf16[8,96,384]{2,1,0:T(8,128)(2,1)S(1)}, u32[]{:S(2)}) copy-start(bf16[8,96,384]{2,1,0:T(8,128)(2,1)S(1)} %pad_maximum_fusion.1) | copy-start | bytes 1769476
  84.3 17.7 %collective-permute-start.1 = (bf16[768,384]{1,0:T(8,128)(2,1)S(1)}, bf16[768,384]{1,0:T(8,128)(2,1)}, u32[]{:S(2)}, u32[]{:S(2)}) collective-permute-start(bf16[768,384]{1,0:T(8,128)(2,1)S(1)} %bitcast.176), channel_id=1, source_target_pairs={{0,1},{1,0},{2,3},{3,2},{4,5},{5,4},{6,7},{7,6},{8,9},{9,8},{10,11... | collective-permute-start | bytes 1769480 | tf_op jit(solution)/shard_map/ppermute | solution.py:48
  104.1 16.5 %copy-start.39 = (bf16[48,768]{1,0:T(8,128)(2,1)S(1)}, bf16[48,768]{1,0:T(8,128)(2,1)}, u32[]{:S(2)}) copy-start(bf16[48,768]{1,0:T(8,128)(2,1)} %get-tuple-element.233) | copy-start | bytes 221188
  104.1 16.5 %copy-start.40 = (bf16[48,384]{1,0:T(8,128)(2,1)S(1)}, bf16[48,384]{1,0:T(8,128)(2,1)}, u32[]{:S(2)}) copy-start(bf16[48,384]{1,0:T(8,128)(2,1)} %get-tuple-element.242) | copy-start | bytes 110596
  104.1 16.5 %copy-start.41 = (bf16[48,384]{1,0:T(8,128)(2,1)S(1)}, bf16[48,384]{1,0:T(8,128)(2,1)}, u32[]{:S(2)}) copy-start(bf16[48,384]{1,0:T(8,128)(2,1)} %get-tuple-element.245) | copy-start | bytes 110596
  104.1 16.5 %copy-start.42 = (bf16[48,384]{1,0:T(8,128)(2,1)S(1)}, bf16[48,384]{1,0:T(8,128)(2,1)}, u32[]{:S(2)}) copy-start(bf16[48,384]{1,0:T(8,128)(2,1)} %get-tuple-element.247) | copy-start | bytes 110596
  104.2 16.5 %copy-start.43 = (bf16[48,384]{1,0:T(8,128)(2,1)S(1)}, bf16[48,384]{1,0:T(8,128)(2,1)}, u32[]{:S(2)}) copy-start(bf16[48,384]{1,0:T(8,128)(2,1)} %get-tuple-element.248) | copy-start | bytes 110596
  104.6 16.8 %copy-start.21 = (bf16[8,64,768]{2,1,0:T(8,128)(2,1)S(1)}, bf16[8,64,768]{2,1,0:T(8,128)(2,1)}, u32[]{:S(2)}) copy-start(bf16[8,64,768]{2,1,0:T(8,128)(2,1)} %copy-done.20) | copy-start | bytes 2359300
  118.6 4.3 collective-permute-start.2
  129.6 2.5 collective-permute-start.3
  133.4 14.8 %copy-start.48 = (f32[768]{0:T(1024)S(1)}, f32[768]{0:T(1024)}, u32[]{:S(2)}) copy-start(f32[768]{0:T(1024)} %get-tuple-element.208) | copy-start | bytes 9220
  148.3 41.8 %copy-start.55 = (f32[128]{0:T(128)}, f32[128]{0:T(128)S(1)}, u32[]{:S(2)}) copy-start(f32[128]{0:T(128)S(1)} %broadcast_multiply_fusion.2) | copy-start | bytes 1540
  148.5 41.6 %copy-start.75 = (f32[128]{0:T(128)}, f32[128]{0:T(128)S(1)}, u32[]{:S(2)}) copy-start(f32[128]{0:T(128)S(1)} %multiply_reduce_fusion.7) | copy-start | bytes 1540
  148.5 41.5 %copy-start.61 = (f32[128]{0:T(128)}, f32[128]{0:T(128)S(1)}, u32[]{:S(2)}) copy-start(f32[128]{0:T(128)S(1)} %fusion.39) | copy-start | bytes 1540
  162.3 34.2 %copy-start.22 = (bf16[1,128,768]{2,1,0:T(8,128)(2,1)S(1)}, bf16[1,128,768]{2,1,0:T(8,128)(2,1)}, u32[]{:S(2)}) copy-start(bf16[1,128,768]{2,1,0:T(8,128)(2,1)} %param.17) | copy-start | bytes 589828
  190.1 12.0 %copy-start.7 = (bf16[8,128,768]{2,1,0:T(8,128)(2,1)}, bf16[8,128,768]{2,1,0:T(8,128)(2,1)S(1)}, u32[]{:S(2)}) copy-start(bf16[8,128,768]{2,1,0:T(8,128)(2,1)S(1)} %all_to_all.118) | copy-start | bytes 4718596
  190.1 5.2 collective-permute-start.4
  197.5 15.5 %all-to-all-start.7 = ((bf16[4,128,768]{2,1,0:T(8,128)(2,1)}), bf16[4,128,768]{2,1,0:T(8,128)(2,1)S(1)}, u32[]{:S(2)}, u32[]{:S(2)}) async-start(bf16[4,128,768]{2,1,0:T(8,128)(2,1)} %broadcast_in_dim.56), calls=%async_computation.7 | async-start | bytes 1572864 | tf_op jit(solution)/shard_map/all_to_all | solution.py:40
  202.2 24.8 %copy-start.36 = (bf16[8,96,384]{2,1,0:T(8,128)(2,1)}, bf16[8,96,384]{2,1,0:T(8,128)(2,1)S(1)}, u32[]{:S(2)}) copy-start(bf16[8,96,384]{2,1,0:T(8,128)(2,1)S(1)} %pad_maximum_fusion.2) | copy-start | bytes 1769476
  202.2 24.7 %collective-permute-start.5 = (bf16[768,384]{1,0:T(8,128)(2,1)S(1)}, bf16[768,384]{1,0:T(8,128)(2,1)S(1)}, u32[]{:S(2)}, u32[]{:S(2)}) collective-permute-start(bf16[768,384]{1,0:T(8,128)(2,1)S(1)} %bitcast.179), channel_id=1, source_target_pairs={{0,1},{1,0},{2,3},{3,2},{4,5},{5,4},{6,7},{7,6},{8,9},{9,8},{10,11... | collective-permute-start | bytes 1769480 | tf_op jit(solution)/shard_map/ppermute | solution.py:48
  211.2 15.7 %copy-start.65 = (f32[768]{0:T(1024)S(1)}, f32[768]{0:T(1024)}, u32[]{:S(2)}) copy-start(f32[768]{0:T(1024)} %get-tuple-element.205) | copy-start | bytes 9220
  213.0 40.3 %copy-start.3 = (bf16[4,128,768]{2,1,0:T(8,128)(2,1)}, bf16[4,128,768]{2,1,0:T(8,128)(2,1)S(1)}, u32[]{:S(2)}) copy-start(bf16[4,128,768]{2,1,0:T(8,128)(2,1)S(1)} %all-to-all-done.7) | copy-start | bytes 2359300
  242.3 4.0 collective-permute-start.6
  253.0 2.5 collective-permute-start.7
  253.3 4.3 collective-permute-start.8
  257.7 15.5 %all-to-all-start.10 = ((bf16[4,128,768]{2,1,0:T(8,128)(2,1)}), bf16[4,128,768]{2,1,0:T(8,128)(2,1)S(1)}, u32[]{:S(2)}, u32[]{:S(2)}) async-start(bf16[4,128,768]{2,1,0:T(8,128)(2,1)} %fusion.13), calls=%async_computation.10 | async-start | bytes 1572864 | tf_op jit(solution)/shard_map/all_to_all | solution.py:40
  273.2 3.3 collective-permute-start.9
  278.7 15.5 %all-to-all-start.11 = ((bf16[4,128,768]{2,1,0:T(8,128)(2,1)}), bf16[4,128,768]{2,1,0:T(8,128)(2,1)S(1)}, u32[]{:S(2)}, u32[]{:S(2)}) async-start(bf16[4,128,768]{2,1,0:T(8,128)(2,1)} %fusion.12), calls=%async_computation.11 | async-start | bytes 1572864 | tf_op jit(solution)/shard_map/all_to_all | solution.py:40
  282.2 12.9 %copy-start.58 = (f32[128]{0:T(128)S(1)}, f32[128]{0:T(128)}, u32[]{:S(2)}) copy-start(f32[128]{0:T(128)} %copy-done.57) | copy-start | bytes 1540
  282.2 12.9 %copy-start.64 = (f32[128]{0:T(128)S(1)}, f32[128]{0:T(128)}, u32[]{:S(2)}) copy-start(f32[128]{0:T(128)} %copy-done.63) | copy-start | bytes 1540
  282.2 13.7 %copy-start.78 = (f32[128]{0:T(128)S(1)}, f32[128]{0:T(128)}, u32[]{:S(2)}) copy-start(f32[128]{0:T(128)} %copy-done.77) | copy-start | bytes 1540
  282.2 13.7 %copy-start.45 = (f32[768]{0:T(1024)S(1)}, f32[768]{0:T(1024)}, u32[]{:S(2)}) copy-start(f32[768]{0:T(1024)} %get-tuple-element.202) | copy-start | bytes 9220
  299.8 13.3 %all-to-all-start.12 = ((bf16[16,128,64]{1,2,0:T(8,128)(2,1)}), bf16[16,128,64]{1,2,0:T(8,128)(2,1)S(1)}, u32[]{:S(2)}, u32[]{:S(2)}) async-start(bf16[16,128,64]{1,2,0:T(8,128)(2,1)} %concatenate.70), calls=%async_computation.12 | async-start | bytes 524288 | tf_op jit(solution)/shard_map/all_to_all | solution.py:40
  314.1 33.0 %all-to-all-start.13 = ((bf16[8,192,768]{2,1,0:T(8,128)(2,1)}), bf16[8,192,768]{2,1,0:T(8,128)(2,1)S(1)}, u32[]{:S(2)}, u32[]{:S(2)}) async-start(bf16[8,192,768]{2,1,0:T(8,128)(2,1)} %shard_map.276), calls=%async_computation.13 | async-start | bytes 4718592 | tf_op jit(solution)/shard_map/all_to_all | solution.py:40
  348.2 5.1 collective-permute-start.10
  383.0 48.8 %copy-start.10 = (f32[128,768]{1,0:T(8,128)}, f32[128,768]{1,0:T(8,128)S(1)}, u32[]{:S(2)}) copy-start(f32[128,768]{1,0:T(8,128)S(1)} %get-tuple-element.216) | copy-start | bytes 1179652
  384.0 14.2 %all-to-all-start.15 = ((bf16[4,128,768]{2,1,0:T(8,128)(2,1)}), bf16[4,128,768]{2,1,0:T(8,128)(2,1)S(1)}, u32[]{:S(2)}, u32[]{:S(2)}) async-start(bf16[4,128,768]{2,1,0:T(8,128)(2,1)} %broadcast_in_dim.62), calls=%async_computation.15 | async-start | bytes 1572864 | tf_op jit(solution)/shard_map/all_to_all | solution.py:40
  387.5 94.3 %all-gather.9.cloned.1.call-start = ((), (), s32[]{:S(2)}) async-start(), calls=%async_computation.24 | async-start | bytes 2506752 | tf_op jit(solution)/shard_map/all_gather | solution.py:678
  398.2 4.4 collective-permute-start.11
  409.2 2.5 collective-permute-start.12
  413.0 17.8 %copy-start.54 = (f32[128]{0:T(128)S(1)}, f32[128]{0:T(128)}, u32[]{:S(2)}) copy-start(f32[128]{0:T(128)} %copy-done.53) | copy-start | bytes 1540
  413.0 17.8 %copy-start.60 = (f32[128]{0:T(128)S(1)}, f32[128]{0:T(128)}, u32[]{:S(2)}) copy-start(f32[128]{0:T(128)} %copy-done.59) | copy-start | bytes 1540
  413.0 18.5 %copy-start.74 = (f32[128]{0:T(128)S(1)}, f32[128]{0:T(128)}, u32[]{:S(2)}) copy-start(f32[128]{0:T(128)} %copy-done.73) | copy-start | bytes 1540
  434.9 12.7 %all-to-all-start.17 = ((bf16[16,128,64]{1,2,0:T(8,128)(2,1)}), bf16[16,128,64]{1,2,0:T(8,128)(2,1)S(1)}, u32[]{:S(2)}, u32[]{:S(2)}) async-start(bf16[16,128,64]{1,2,0:T(8,128)(2,1)} %concatenate.71), calls=%async_computation.17 | async-start | bytes 524288 | tf_op jit(solution)/shard_map/all_to_all | solution.py:40
  448.6 32.7 %all-to-all-start.18 = ((bf16[8,192,768]{2,1,0:T(8,128)(2,1)}), bf16[8,192,768]{2,1,0:T(8,128)(2,1)S(1)}, u32[]{:S(2)}, u32[]{:S(2)}) async-start(bf16[8,192,768]{2,1,0:T(8,128)(2,1)} %shard_map.280), calls=%async_computation.18 | async-start | bytes 4718592 | tf_op jit(solution)/shard_map/all_to_all | solution.py:40
  452.3 107.3 %all-gather.11.cloned.1.call-start = ((), (), s32[]{:S(2)}) async-start(), calls=%async_computation.25 | async-start | bytes 2506752 | tf_op jit(solution)/shard_map/all_gather | solution.py:682
  481.8 5.3 collective-permute-start.13
  490.0 28.8 %all-to-all-start.19 = ((bf16[8,128,768]{2,1,0:T(8,128)(2,1)}), bf16[8,128,768]{2,1,0:T(8,128)(2,1)S(1)}, u32[]{:S(2)}, u32[]{:S(2)}) async-start(bf16[8,128,768]{2,1,0:T(8,128)(2,1)} %fusion.1), calls=%async_computation.19 | async-start | bytes 3145728 | tf_op jit(solution)/shard_map/all_to_all | solution.py:40
  518.8 18.1 %all-to-all-start.21 = ((bf16[16,16,768]{2,1,0:T(8,128)(2,1)}), bf16[16,16,768]{2,1,0:T(8,128)(2,1)S(1)}, u32[]{:S(2)}, u32[]{:S(2)}) async-start(bf16[16,16,768]{2,1,0:T(8,128)(2,1)} %pad.6.clone), calls=%async_computation.21 | async-start | bytes 786432 | tf_op jit(solution)/shard_map/all_to_all | solution.py:40
  536.9 17.9 %all-to-all-start.20 = ((bf16[8,80,768]{2,1,0:T(8,128)(2,1)}), bf16[8,80,768]{2,1,0:T(8,128)(2,1)S(1)}, u32[]{:S(2)}, u32[]{:S(2)}) async-start(bf16[8,80,768]{2,1,0:T(8,128)(2,1)} %shard_map.282), calls=%async_computation.20 | async-start | bytes 1966080 | tf_op jit(solution)/shard_map/all_to_all | solution.py:40
  556.0 20.2 %all-to-all-start.22 = ((bf16[8,80,768]{2,1,0:T(8,128)(2,1)}), bf16[8,80,768]{2,1,0:T(8,128)(2,1)S(1)}, u32[]{:S(2)}, u32[]{:S(2)}) async-start(bf16[8,80,768]{2,1,0:T(8,128)(2,1)} %broadcast_in_dim.135), calls=%async_computation.22 | async-start | bytes 1966080 | tf_op jit(solution)/shard_map/all_to_all | solution.py:40
  559.6 18.0 %copy-start.11 = (f32[128,768]{1,0:T(8,128)S(1)}, f32[128,768]{1,0:T(8,128)}, u32[]{:S(2)}) copy-start(f32[128,768]{1,0:T(8,128)} %copy-done.10) | copy-start | bytes 1179652
  559.6 18.0 %copy-start.13 = (f32[128,768]{1,0:T(8,128)S(1)}, f32[128,768]{1,0:T(8,128)}, u32[]{:S(2)}) copy-start(f32[128,768]{1,0:T(8,128)} %copy-done.12) | copy-start | bytes 1179652
  559.6 18.0 %copy-start.68 = (f32[128]{0:T(128)S(1)}, f32[128]{0:T(128)}, u32[]{:S(2)}) copy-start(f32[128]{0:T(128)} %copy-done.67) | copy-start | bytes 1540
  576.2 3.0 collective-permute-start.14
  (59 other events, 193.7 us)
Sparse Core Ops, SparseCore 0:
  121.5 40.6 all-gather.6
  410.5 49.3 all-gather.8
  484.6 64.3 all-gather.10

commit v7 on v6

--- a/solution.py
+++ b/solution.py
@@ -539,8 +539,10 @@
     to_arrive, near, far, sums = attend_back(
         arrive_pos, ctx_pos, queries, keys, values, mixed_grad, head_weight
     )
-    near, far, owned, spread = lax.optimization_barrier((near, far, owned, spread))
-    normed_grad = scatter(near.reshape(8, TOK, D), far.reshape(8, TOK, D), CHIP_GROUPS)
+    near, far = near.reshape(8, TOK, D), far.reshape(8, TOK, D)
+    near = (near.astype(F32) + swap_core(far).astype(F32)).astype(BF16)
+    near, owned, spread = lax.optimization_barrier((near, owned, spread))
+    normed_grad = jnp.sum(exchange(near, "ctx", CHIP_GROUPS).astype(F32), axis=0)
     unused, first_back = jax.vjp(layer_norm, flowing, gain_one, bias_one)
     flowing_part, gain_one_grad, bias_one_grad = first_back(normed_grad)
     late = second_grads(

time: 596 us -> 586 us (0.983)
  blocking collectives: 139 us -> 122 us
    all_to_all x8 -> x7, blocking collectives: 139 us -> 122 us  [exchange(): lax.all_to_all(parts, axis, 0, 0, tiled=True, axis_index_groups=groups)]
    all_to_all x15 -> x16, starting transfers between devices: 65 us -> 71.4 us  [exchange(): lax.all_to_all(parts, axis, 0, 0, tiled=True, axis_index_groups=groups)]
    all_to_all x15 -> x16, waiting for transfers between devices: 136 us -> 135 us  [exchange(): lax.all_to_all(parts, axis, 0, 0, tiled=True, axis_index_groups=groups)]
  transfers between devices with their start and end apart: 33 -> 34, of which waited for: 26 -> 27; matrix products, arithmetic and copies ran while one was open for 9% -> 9% of each run, Pallas kernels for 15% -> 15%
where the time goes in v7:
time: 586 us; the launch traced here: 581 us
  waiting for transfers between devices  169 us (29%)
  blocking collectives  122 us (21%)
  Pallas kernels  102 us (17%)
  starting transfers between devices  92 us (16%)
  local copies, waits for them, and re-layouts  45.7 us (8%)
  other arithmetic  29 us (5%)
  between operations  15.5 us (3%)
  matrix products  5.91 us (1%)
    all_to_all x16, waiting for transfers between devices, exchange(): lax.all_to_all(parts, axis, 0, 0, tiled=True, axis_index_groups=groups)  135 us
    all_to_all x7, blocking collectives, exchange(): lax.all_to_all(parts, axis, 0, 0, tiled=True, axis_index_groups=groups)  122 us
    all_to_all x16, starting transfers between devices, exchange(): lax.all_to_all(parts, axis, 0, 0, tiled=True, axis_index_groups=groups)  71.4 us
    pallas_call x2, Pallas kernels, attend_back(): pl.pallas_call(attend_back_kernel, out_shape=(jax.ShapeDtypeStruct((LEN,...  29.4 us
    ppermute x15, waiting for transfers between devices, swap_core(): return lax.ppermute(part, 'ctx', SWAP)  21.5 us
    ppermute x15, starting transfers between devices, swap_core(): return lax.ppermute(part, 'ctx', SWAP)  19.7 us
    pallas_call x2, Pallas kernels, attend(): pl.pallas_call(functools.partial(attend_kernel, fresh), out_shape=outs, i...  18.9 us
    all_gather x1, waiting for transfers between devices, shards(): lax.all_gather(layer_pieces[1], 'shard', axis=0)  13.3 us
  transfers between devices with their start and end apart: 34, of which 27 were waited for; matrix products, arithmetic and copies ran while one was open for 9% of the time, Pallas kernels for 15%

profile of v7, /device:TPU:1, one launch (start us, length us, event | category | flops | bytes accessed | tf_op | source)
XLA Modules:
  0.0 580.9 jit_solution(4971189318623350352)
XLA Ops:
  7.2 2.3 broadcast_in_dim.48
  9.6 7.6 %all-to-all-start = ((bf16[8,128,768]{2,1,0:T(8,128)(2,1)}), bf16[8,128,768]{2,1,0:T(8,128)(2,1)}, u32[]{:S(2)}, u32[]{:S(2)}) async-start(bf16[8,128,768]{2,1,0:T(8,128)(2,1)} %broadcast_in_dim.48), calls=%async_computation | async-start | bytes 3145728 | tf_op jit(solution)/shard_map/all_to_all | solution.py:40
  23.1 17.1 %all-to-all-done = bf16[8,128,768]{2,1,0:T(8,128)(2,1)} async-done(((bf16[8,128,768]{2,1,0:T(8,128)(2,1)}), bf16[8,128,768]{2,1,0:T(8,128)(2,1)}, u32[]{:S(2)}, u32[]{:S(2)}) %all-to-all-start) | async-done | bytes 1572896 | tf_op jit(solution)/shard_map/all_to_all | solution.py:40
  41.2 5.1 all-to-all-start.1
  49.1 8.7 %all-to-all-done.1 = bf16[8,64,768]{2,1,0:T(8,128)(2,1)S(1)} async-done(((bf16[8,64,768]{2,1,0:T(8,128)(2,1)}), bf16[8,64,768]{2,1,0:T(8,128)(2,1)S(1)}, u32[]{:S(2)}, u32[]{:S(2)}) %all-to-all-start.1) | async-done | bytes 786464 | tf_op jit(solution)/shard_map/all_to_all | solution.py:40
  59.3 3.8 all-to-all-start.2
  68.5 10.3 %shard_map.271 = (bf16[2048,64]{1,0:T(8,128)(2,1)}, bf16[2048,64]{1,0:T(8,128)(2,1)}, bf16[2048,64]{1,0:T(8,128)(2,1)}, bf16[2048,64]{1,0:T(8,128)(2,1)}, bf16[1...) custom-call(s32[32]{0:T(128)} %reshape.369.arrive_pos, s32[32]{0:T(128)} %reshape.370.ctx_pos, ...), custom_call_target="tpu_custom_call" | custom-call | flops 2000000000 | bytes 5000000 | tf_op jit(solution)/shard_map/pallas_call | solution.py:213
  78.8 5.3 all-to-all-done.2.rows_ref
  84.3 3.4 collective-permute-start.1
  89.0 13.0 %all_to_all.115 = bf16[16,128,64]{1,2,0:T(8,128)(2,1)S(1)} all-to-all(bf16[16,128,64]{1,2,0:T(8,128)(2,1)S(1)} %copy.69), channel_id=1, replica_groups=mesh['shard'=8,'ctx'=16] {'ctx'}, dimensions={0} | all-to-all | bytes 524288 | tf_op jit(solution)/shard_map/all_to_all | solution.py:40
  104.7 13.9 %all_to_all.116 = bf16[4,128,768]{2,1,0:T(8,128)(2,1)S(1)} all-to-all(bf16[4,128,768]{2,1,0:T(8,128)(2,1)S(1)} %broadcast_in_dim.54), channel_id=1, replica_groups={{0,2,4,6},{1,3,5,7},{8,10,12,14},{9,11,13,15},{16,18,20,22},{17,19,21,2..., dimensions={0} | all-to-all | bytes 1572864 | tf_op jit(solution)/shard_map/all_to_all | solution.py:40
  123.8 5.8 shard_map.272
  129.6 2.5 collective-permute-done.3
  133.4 14.7 %all_to_all.117 = bf16[4,128,768]{2,1,0:T(8,128)(2,1)S(1)} all-to-all(bf16[4,128,768]{2,1,0:T(8,128)(2,1)S(1)} %fusion.14), channel_id=1, replica_groups={{0,2,4,6},{1,3,5,7},{8,10,12,14},{9,11,13,15},{16,18,20,22},{17,19,21,2..., dimensions={0} | all-to-all | bytes 1572864 | tf_op jit(solution)/shard_map/all_to_all | solution.py:40
  148.9 13.3 %all-gather.7.cloned.1.call-done = bf16[1152,768]{1,0:T(8,128)(2,1)} async-done(((bf16[144,768]{1,0:T(8,128)(2,1)}), bf16[1152,768]{1,0:T(8,128)(2,1)}) %all-gather.7.cloned.1.call-update) | async-done | bytes 1769488 | tf_op jit(solution)/shard_map/all_gather | solution.py:635
  162.4 27.7 %all_to_all.118 = bf16[8,128,768]{2,1,0:T(8,128)(2,1)S(1)} all-to-all(bf16[8,128,768]{2,1,0:T(8,128)(2,1)S(1)} %broadcast_in_dim.55), channel_id=1, replica_groups={{0,2,4,6,8,10,12,14},{1,3,5,7,9,11,13,15},{16,18,20,22,24,26,28,30},{17..., dimensions={0} | all-to-all | bytes 3145728 | tf_op jit(solution)/shard_map/all_to_all | solution.py:40
  190.1 2.2 collective-permute-start.4
  192.3 3.0 collective-permute-done.4
  197.5 3.5 all-to-all-start.7
  202.7 8.6 %shard_map.273 = (bf16[2048,64]{1,0:T(8,128)(2,1)}, bf16[2048,64]{1,0:T(8,128)(2,1)}, bf16[2048,64]{1,0:T(8,128)(2,1)}, bf16[2048,64]{1,0:T(8,128)(2,1)}) custom-call(s32[32]{0:T(128)} %reshape.369.arrive_pos, s32[32]{0:T(128)} %reshape.370.ctx_pos, bf16[1024,768]{1,0:T(8,128)(2,1)} %bitcast.147, bf16[1024,768]{1,0:T(8,128)(2,1)} %bitcast.161, ...), custom_call_target="tpu_custom_call" | custom-call | flops 2000000000 | bytes 5000000 | tf_op jit(solution)/shard_map/pallas_call | solution.py:213
  214.5 12.4 %all_to_all.119 = bf16[16,128,64]{1,2,0:T(8,128)(2,1)S(1)} all-to-all(bf16[16,128,64]{1,2,0:T(8,128)(2,1)S(1)} %copy.70), channel_id=1, replica_groups=mesh['shard'=8,'ctx'=16] {'ctx'}, dimensions={0} | all-to-all | bytes 524288 | tf_op jit(solution)/shard_map/all_to_all | solution.py:40
  228.6 13.8 %all_to_all.120 = bf16[4,128,768]{2,1,0:T(8,128)(2,1)S(1)} all-to-all(bf16[4,128,768]{2,1,0:T(8,128)(2,1)S(1)} %broadcast_in_dim.57), channel_id=1, replica_groups={{0,2,4,6},{1,3,5,7},{8,10,12,14},{9,11,13,15},{16,18,20,22},{17,19,21,2..., dimensions={0} | all-to-all | bytes 1572864 | tf_op jit(solution)/shard_map/all_to_all | solution.py:40
  247.2 5.7 shard_map.274
  255.5 2.2 fusion.13
  257.7 3.5 all-to-all-start.10
  261.2 5.6 shard_map.275
  266.8 6.3 %all-to-all-done.10 = bf16[4,128,768]{2,1,0:T(8,128)(2,1)S(1)} async-done(((bf16[4,128,768]{2,1,0:T(8,128)(2,1)}), bf16[4,128,768]{2,1,0:T(8,128)(2,1)S(1)}, u32[]{:S(2)}, u32[]{:S(2)}) %all-to-all-start.10) | async-done | bytes 786464 | tf_op jit(solution)/shard_map/all_to_all | solution.py:40
  276.5 2.2 fusion.12
  278.7 3.5 all-to-all-start.11
  282.4 11.8 %all-to-all-done.11 = bf16[4,128,768]{2,1,0:T(8,128)(2,1)S(1)} async-done(((bf16[4,128,768]{2,1,0:T(8,128)(2,1)}), bf16[4,128,768]{2,1,0:T(8,128)(2,1)S(1)}, u32[]{:S(2)}, u32[]{:S(2)}) %all-to-all-start.11) | async-done | bytes 786464 | tf_op jit(solution)/shard_map/all_to_all | solution.py:40
  299.8 4.5 all-to-all-start.12
  305.1 5.8 shard_map.276
  314.1 4.0 all-to-all-start.13
  318.1 14.7 %shard_map.277 = (bf16[2048,256]{1,0:T(8,128)(2,1)}, bf16[1024,768]{1,0:T(8,128)(2,1)}, bf16[1024,768]{1,0:T(8,128)(2,1)}, f32[1,192]{1,0:T(1,128)}) custom-call(s32[32]{0:T(128)} %reshape.369.arrive_pos, s32[32]{0:T(128)} %reshape.370.ctx_pos, bf16[2048,64]{1,0:T(8,128)(2,1)} %get-tuple-element.127.q_ref, bf16[2048,64]{1,0:T(8,128)(2,1)} %get-tuple-element.128.k_ref, ...), custom_call_target="tpu_custom_call" | custom-call | flops 4000000000 | bytes 5000000 | tf_op jit(solution)/shard_map/pallas_call | solution.py:225
  333.7 3.2 collective-permute-done.10
  337.0 3.0 fusion.2
  340.0 7.1 %all-to-all-done.13 = bf16[8,192,768]{2,1,0:T(8,128)(2,1)S(1)} async-done(((bf16[8,192,768]{2,1,0:T(8,128)(2,1)}), bf16[8,192,768]{2,1,0:T(8,128)(2,1)S(1)}, u32[]{:S(2)}, u32[]{:S(2)}) %all-to-all-start.13) | async-done | bytes 2359328 | tf_op jit(solution)/shard_map/all_to_all | solution.py:40
  348.2 26.5 %all_to_all.121 = bf16[8,128,768]{2,1,0:T(8,128)(2,1)S(1)} all-to-all(bf16[8,128,768]{2,1,0:T(8,128)(2,1)} %fusion.2), channel_id=1, replica_groups={{0,2,4,6,8,10,12,14},{1,3,5,7,9,11,13,15},{16,18,20,22,24,26,28,30},{17..., dimensions={0} | all-to-all | bytes 3145728 | tf_op jit(solution)/shard_map/all_to_all | solution.py:40
  377.0 3.5 all-to-all-start.15
  384.1 4.3 shard_map.278.rest_6_
  390.3 3.5 collective-permute-start.11
  396.5 5.7 shard_map.279
  404.7 2.2 fusion.11
  407.0 3.6 all-to-all-start.16
  411.4 11.2 %all-to-all-done.16 = bf16[4,128,768]{2,1,0:T(8,128)(2,1)S(1)} async-done(((bf16[4,128,768]{2,1,0:T(8,128)(2,1)}), bf16[4,128,768]{2,1,0:T(8,128)(2,1)S(1)}, u32[]{:S(2)}, u32[]{:S(2)}) %all-to-all-start.16) | async-done | bytes 786464 | tf_op jit(solution)/shard_map/all_to_all | solution.py:40
  427.0 4.5 all-to-all-start.17
  432.3 5.8 shard_map.280
  438.1 2.2 all-to-all-done.17
  441.3 3.6 all-to-all-start.18
  445.1 14.7 %shard_map.281 = (bf16[2048,256]{1,0:T(8,128)(2,1)}, bf16[1024,768]{1,0:T(8,128)(2,1)}, bf16[1024,768]{1,0:T(8,128)(2,1)}, f32[1,192]{1,0:T(1,128)}) custom-call(s32[32]{0:T(128)} %reshape.369.arrive_pos, s32[32]{0:T(128)} %reshape.370.ctx_pos, bf16[2048,64]{1,0:T(8,128)(2,1)} %get-tuple-element.144.q_ref, bf16[2048,64]{1,0:T(8,128)(2,1)} %get-tuple-element.145.k_ref, ...), custom_call_target="tpu_custom_call" | custom-call | flops 4000000000 | bytes 5000000 | tf_op jit(solution)/shard_map/pallas_call | solution.py:225
  460.9 3.2 collective-permute-done.13
  464.2 3.0 fusion.1
  467.1 11.2 %all-to-all-done.18 = bf16[8,192,768]{2,1,0:T(8,128)(2,1)S(1)} async-done(((bf16[8,192,768]{2,1,0:T(8,128)(2,1)}), bf16[8,192,768]{2,1,0:T(8,128)(2,1)S(1)}, u32[]{:S(2)}, u32[]{:S(2)}) %all-to-all-start.18) | async-done | bytes 2359328 | tf_op jit(solution)/shard_map/all_to_all | solution.py:40
  479.6 6.2 %all-to-all-start.19 = ((bf16[8,128,768]{2,1,0:T(8,128)(2,1)}), bf16[8,128,768]{2,1,0:T(8,128)(2,1)S(1)}, u32[]{:S(2)}, u32[]{:S(2)}) async-start(bf16[8,128,768]{2,1,0:T(8,128)(2,1)} %fusion.1), calls=%async_computation.19 | async-start | bytes 3145728 | tf_op jit(solution)/shard_map/all_to_all | solution.py:40
  489.5 21.4 %all-to-all-done.19 = bf16[8,128,768]{2,1,0:T(8,128)(2,1)S(1)} async-done(((bf16[8,128,768]{2,1,0:T(8,128)(2,1)}), bf16[8,128,768]{2,1,0:T(8,128)(2,1)S(1)}, u32[]{:S(2)}, u32[]{:S(2)}) %all-to-all-start.19) | async-done | bytes 1572896 | tf_op jit(solution)/shard_map/all_to_all | solution.py:40
  510.9 4.2 all-to-all-start.21
  517.3 4.8 shard_map.282
  522.1 2.9 all-to-all-done.21
  525.1 3.6 all-to-all-start.20
  528.7 13.2 %all-to-all-done.20 = bf16[8,80,768]{2,1,0:T(8,128)(2,1)S(1)} async-done(((bf16[8,80,768]{2,1,0:T(8,128)(2,1)}), bf16[8,80,768]{2,1,0:T(8,128)(2,1)S(1)}, u32[]{:S(2)}, u32[]{:S(2)}) %all-to-all-start.20) | async-done | bytes 983072 | tf_op jit(solution)/shard_map/all_to_all | solution.py:40
  543.1 6.6 %all-to-all-start.22 = ((bf16[8,80,768]{2,1,0:T(8,128)(2,1)}), bf16[8,80,768]{2,1,0:T(8,128)(2,1)S(1)}, u32[]{:S(2)}, u32[]{:S(2)}) async-start(bf16[8,80,768]{2,1,0:T(8,128)(2,1)} %broadcast_in_dim.135), calls=%async_computation.22 | async-start | bytes 1966080 | tf_op jit(solution)/shard_map/all_to_all | solution.py:40
  549.7 6.5 %shard_map.283 = (f32[2,96,3072]{2,1,0:T(8,128)}, f32[2,384,768]{2,1,0:T(8,128)}) custom-call(bf16[16,96,768]{2,1,0:T(8,128)(2,1)} %bitcast.159, bf16[16,96,768]{2,1,0:T(8,128)(2,1)} %bitcast.158), custom_call_target="tpu_custom_call" | custom-call | flops 1000000 | bytes 10000000 | tf_op jit(solution)/shard_map/pallas_call | solution.py:448
  556.2 10.1 %all-to-all-done.22 = bf16[8,80,768]{2,1,0:T(8,128)(2,1)S(1)} async-done(((bf16[8,80,768]{2,1,0:T(8,128)(2,1)}), bf16[8,80,768]{2,1,0:T(8,128)(2,1)S(1)}, u32[]{:S(2)}, u32[]{:S(2)}) %all-to-all-start.22) | async-done | bytes 983072 | tf_op jit(solution)/shard_map/all_to_all | solution.py:40
  570.8 3.3 shard_map.284
  (369 shorter events, 92.6 us)
Async XLA Ops:
  7.2 39.1 %copy-start = (bf16[2,96,3072]{2,1,0:T(8,128)(2,1)S(1)}, bf16[2,96,3072]{2,1,0:T(8,128)(2,1)}, u32[]{:S(2)}) copy-start(bf16[2,96,3072]{2,1,0:T(8,128)(2,1)} %param.28) | copy-start | bytes 3538948
  9.6 9.7 %copy-start.27 = (bf16[2,96,2304]{2,1,0:T(8,128)(2,1)S(1)}, bf16[2,96,2304]{2,1,0:T(8,128)(2,1)}, u32[]{:S(2)}) copy-start(bf16[2,96,2304]{2,1,0:T(8,128)(2,1)} %param.21) | copy-start | bytes 2654212
  9.6 30.7 %all-to-all-start = ((bf16[8,128,768]{2,1,0:T(8,128)(2,1)}), bf16[8,128,768]{2,1,0:T(8,128)(2,1)}, u32[]{:S(2)}, u32[]{:S(2)}) async-start(bf16[8,128,768]{2,1,0:T(8,128)(2,1)} %broadcast_in_dim.48), calls=%async_computation | async-start | bytes 3145728 | tf_op jit(solution)/shard_map/all_to_all | solution.py:40
  41.2 16.7 %all-to-all-start.1 = ((bf16[8,64,768]{2,1,0:T(8,128)(2,1)}), bf16[8,64,768]{2,1,0:T(8,128)(2,1)S(1)}, u32[]{:S(2)}, u32[]{:S(2)}) async-start(bf16[8,64,768]{2,1,0:T(8,128)(2,1)} %broadcast_in_dim.51), calls=%async_computation.1 | async-start | bytes 1572864 | tf_op jit(solution)/shard_map/all_to_all | solution.py:40
  48.0 20.6 %collective-permute-start = (bf16[8,128,768]{2,1,0:T(8,128)(2,1)}, bf16[8,128,768]{2,1,0:T(8,128)(2,1)}, u32[]{:S(2)}, u32[]{:S(2)}) collective-permute-start(bf16[8,128,768]{2,1,0:T(8,128)(2,1)} %all-to-all-done), channel_id=1, source_target_pairs={{0,1},{1,0},{2,3},{3,2},{4,5},{5,4},{6,7},{7,6},{8,9},{9,8},{10,11... | collective-permute-start | bytes 4718600 | tf_op jit(solution)/shard_map/ppermute | solution.py:48
  59.3 24.9 %all-to-all-start.2 = ((bf16[8,144,768]{2,1,0:T(8,128)(2,1)}), bf16[8,144,768]{2,1,0:T(8,128)(2,1)S(1)}, u32[]{:S(2)}, u32[]{:S(2)}) async-start(bf16[8,144,768]{2,1,0:T(8,128)(2,1)} %broadcast_in_dim.53), calls=%async_computation.2 | async-start | bytes 3538944 | tf_op jit(solution)/shard_map/all_to_all | solution.py:40
  63.1 99.1 %all-gather.7.cloned.1.call-start = ((), (), s32[]{:S(2)}) async-start(), calls=%async_computation.23 | async-start | bytes 1990656 | tf_op jit(solution)/shard_map/all_gather | solution.py:635
  84.2 17.8 %copy-start.8 = (bf16[1,128,768]{2,1,0:T(8,128)(2,1)S(1)}, bf16[1,128,768]{2,1,0:T(8,128)(2,1)}, u32[]{:S(2)}) copy-start(bf16[1,128,768]{2,1,0:T(8,128)(2,1)} %param.16) | copy-start | bytes 589828
  84.3 19.6 %copy-start.34 = (bf16[8,96,384]{2,1,0:T(8,128)(2,1)}, bf16[8,96,384]{2,1,0:T(8,128)(2,1)S(1)}, u32[]{:S(2)}) copy-start(bf16[8,96,384]{2,1,0:T(8,128)(2,1)S(1)} %pad_maximum_fusion.1) | copy-start | bytes 1769476
  84.3 17.7 %collective-permute-start.1 = (bf16[768,384]{1,0:T(8,128)(2,1)S(1)}, bf16[768,384]{1,0:T(8,128)(2,1)}, u32[]{:S(2)}, u32[]{:S(2)}) collective-permute-start(bf16[768,384]{1,0:T(8,128)(2,1)S(1)} %bitcast.176), channel_id=1, source_target_pairs={{0,1},{1,0},{2,3},{3,2},{4,5},{5,4},{6,7},{7,6},{8,9},{9,8},{10,11... | collective-permute-start | bytes 1769480 | tf_op jit(solution)/shard_map/ppermute | solution.py:48
  104.1 16.5 %copy-start.39 = (bf16[48,768]{1,0:T(8,128)(2,1)S(1)}, bf16[48,768]{1,0:T(8,128)(2,1)}, u32[]{:S(2)}) copy-start(bf16[48,768]{1,0:T(8,128)(2,1)} %get-tuple-element.229) | copy-start | bytes 221188
  104.1 16.5 %copy-start.40 = (bf16[48,384]{1,0:T(8,128)(2,1)S(1)}, bf16[48,384]{1,0:T(8,128)(2,1)}, u32[]{:S(2)}) copy-start(bf16[48,384]{1,0:T(8,128)(2,1)} %get-tuple-element.238) | copy-start | bytes 110596
  104.1 16.5 %copy-start.41 = (bf16[48,384]{1,0:T(8,128)(2,1)S(1)}, bf16[48,384]{1,0:T(8,128)(2,1)}, u32[]{:S(2)}) copy-start(bf16[48,384]{1,0:T(8,128)(2,1)} %get-tuple-element.241) | copy-start | bytes 110596
  104.1 16.5 %copy-start.42 = (bf16[48,384]{1,0:T(8,128)(2,1)S(1)}, bf16[48,384]{1,0:T(8,128)(2,1)}, u32[]{:S(2)}) copy-start(bf16[48,384]{1,0:T(8,128)(2,1)} %get-tuple-element.243) | copy-start | bytes 110596
  104.2 16.5 %copy-start.43 = (bf16[48,384]{1,0:T(8,128)(2,1)S(1)}, bf16[48,384]{1,0:T(8,128)(2,1)}, u32[]{:S(2)}) copy-start(bf16[48,384]{1,0:T(8,128)(2,1)} %get-tuple-element.244) | copy-start | bytes 110596
  104.7 16.8 %copy-start.21 = (bf16[8,64,768]{2,1,0:T(8,128)(2,1)S(1)}, bf16[8,64,768]{2,1,0:T(8,128)(2,1)}, u32[]{:S(2)}) copy-start(bf16[8,64,768]{2,1,0:T(8,128)(2,1)} %copy-done.20) | copy-start | bytes 2359300
  118.6 4.3 collective-permute-start.2
  129.6 2.5 collective-permute-start.3
  133.4 14.8 %copy-start.48 = (f32[768]{0:T(1024)S(1)}, f32[768]{0:T(1024)}, u32[]{:S(2)}) copy-start(f32[768]{0:T(1024)} %get-tuple-element.204) | copy-start | bytes 9220
  148.3 41.8 %copy-start.55 = (f32[128]{0:T(128)}, f32[128]{0:T(128)S(1)}, u32[]{:S(2)}) copy-start(f32[128]{0:T(128)S(1)} %broadcast_multiply_fusion.2) | copy-start | bytes 1540
  148.5 41.6 %copy-start.75 = (f32[128]{0:T(128)}, f32[128]{0:T(128)S(1)}, u32[]{:S(2)}) copy-start(f32[128]{0:T(128)S(1)} %multiply_reduce_fusion.7) | copy-start | bytes 1540
  148.6 41.5 %copy-start.61 = (f32[128]{0:T(128)}, f32[128]{0:T(128)S(1)}, u32[]{:S(2)}) copy-start(f32[128]{0:T(128)S(1)} %fusion.39) | copy-start | bytes 1540
  162.3 34.2 %copy-start.22 = (bf16[1,128,768]{2,1,0:T(8,128)(2,1)S(1)}, bf16[1,128,768]{2,1,0:T(8,128)(2,1)}, u32[]{:S(2)}) copy-start(bf16[1,128,768]{2,1,0:T(8,128)(2,1)} %param.17) | copy-start | bytes 589828
  190.1 12.0 %copy-start.7 = (bf16[8,128,768]{2,1,0:T(8,128)(2,1)}, bf16[8,128,768]{2,1,0:T(8,128)(2,1)S(1)}, u32[]{:S(2)}) copy-start(bf16[8,128,768]{2,1,0:T(8,128)(2,1)S(1)} %all_to_all.118) | copy-start | bytes 4718596
  190.1 5.2 collective-permute-start.4
  197.5 15.5 %all-to-all-start.7 = ((bf16[4,128,768]{2,1,0:T(8,128)(2,1)}), bf16[4,128,768]{2,1,0:T(8,128)(2,1)S(1)}, u32[]{:S(2)}, u32[]{:S(2)}) async-start(bf16[4,128,768]{2,1,0:T(8,128)(2,1)} %broadcast_in_dim.56), calls=%async_computation.7 | async-start | bytes 1572864 | tf_op jit(solution)/shard_map/all_to_all | solution.py:40
  202.2 24.8 %copy-start.36 = (bf16[8,96,384]{2,1,0:T(8,128)(2,1)}, bf16[8,96,384]{2,1,0:T(8,128)(2,1)S(1)}, u32[]{:S(2)}) copy-start(bf16[8,96,384]{2,1,0:T(8,128)(2,1)S(1)} %pad_maximum_fusion.2) | copy-start | bytes 1769476
  202.2 24.7 %collective-permute-start.5 = (bf16[768,384]{1,0:T(8,128)(2,1)S(1)}, bf16[768,384]{1,0:T(8,128)(2,1)S(1)}, u32[]{:S(2)}, u32[]{:S(2)}) collective-permute-start(bf16[768,384]{1,0:T(8,128)(2,1)S(1)} %bitcast.179), channel_id=1, source_target_pairs={{0,1},{1,0},{2,3},{3,2},{4,5},{5,4},{6,7},{7,6},{8,9},{9,8},{10,11... | collective-permute-start | bytes 1769480 | tf_op jit(solution)/shard_map/ppermute | solution.py:48
  211.2 15.7 %copy-start.65 = (f32[768]{0:T(1024)S(1)}, f32[768]{0:T(1024)}, u32[]{:S(2)}) copy-start(f32[768]{0:T(1024)} %get-tuple-element.201) | copy-start | bytes 9220
  213.0 40.3 %copy-start.3 = (bf16[4,128,768]{2,1,0:T(8,128)(2,1)}, bf16[4,128,768]{2,1,0:T(8,128)(2,1)S(1)}, u32[]{:S(2)}) copy-start(bf16[4,128,768]{2,1,0:T(8,128)(2,1)S(1)} %all-to-all-done.7) | copy-start | bytes 2359300
  242.3 4.0 collective-permute-start.6
  253.0 2.5 collective-permute-start.7
  253.3 4.3 collective-permute-start.8
  257.7 15.5 %all-to-all-start.10 = ((bf16[4,128,768]{2,1,0:T(8,128)(2,1)}), bf16[4,128,768]{2,1,0:T(8,128)(2,1)S(1)}, u32[]{:S(2)}, u32[]{:S(2)}) async-start(bf16[4,128,768]{2,1,0:T(8,128)(2,1)} %fusion.13), calls=%async_computation.10 | async-start | bytes 1572864 | tf_op jit(solution)/shard_map/all_to_all | solution.py:40
  273.2 3.3 collective-permute-start.9
  278.7 15.5 %all-to-all-start.11 = ((bf16[4,128,768]{2,1,0:T(8,128)(2,1)}), bf16[4,128,768]{2,1,0:T(8,128)(2,1)S(1)}, u32[]{:S(2)}, u32[]{:S(2)}) async-start(bf16[4,128,768]{2,1,0:T(8,128)(2,1)} %fusion.12), calls=%async_computation.11 | async-start | bytes 1572864 | tf_op jit(solution)/shard_map/all_to_all | solution.py:40
  282.2 12.9 %copy-start.58 = (f32[128]{0:T(128)S(1)}, f32[128]{0:T(128)}, u32[]{:S(2)}) copy-start(f32[128]{0:T(128)} %copy-done.57) | copy-start | bytes 1540
  282.2 12.9 %copy-start.64 = (f32[128]{0:T(128)S(1)}, f32[128]{0:T(128)}, u32[]{:S(2)}) copy-start(f32[128]{0:T(128)} %copy-done.63) | copy-start | bytes 1540
  282.2 13.7 %copy-start.78 = (f32[128]{0:T(128)S(1)}, f32[128]{0:T(128)}, u32[]{:S(2)}) copy-start(f32[128]{0:T(128)} %copy-done.77) | copy-start | bytes 1540
  282.2 13.7 %copy-start.45 = (f32[768]{0:T(1024)S(1)}, f32[768]{0:T(1024)}, u32[]{:S(2)}) copy-start(f32[768]{0:T(1024)} %get-tuple-element.198) | copy-start | bytes 9220
  299.8 13.3 %all-to-all-start.12 = ((bf16[16,128,64]{1,2,0:T(8,128)(2,1)}), bf16[16,128,64]{1,2,0:T(8,128)(2,1)S(1)}, u32[]{:S(2)}, u32[]{:S(2)}) async-start(bf16[16,128,64]{1,2,0:T(8,128)(2,1)} %concatenate.70), calls=%async_computation.12 | async-start | bytes 524288 | tf_op jit(solution)/shard_map/all_to_all | solution.py:40
  314.1 33.0 %all-to-all-start.13 = ((bf16[8,192,768]{2,1,0:T(8,128)(2,1)}), bf16[8,192,768]{2,1,0:T(8,128)(2,1)S(1)}, u32[]{:S(2)}, u32[]{:S(2)}) async-start(bf16[8,192,768]{2,1,0:T(8,128)(2,1)} %shard_map.276), calls=%async_computation.13 | async-start | bytes 4718592 | tf_op jit(solution)/shard_map/all_to_all | solution.py:40
  332.8 4.2 collective-permute-start.10
  376.0 47.9 %copy-start.10 = (f32[128,768]{1,0:T(8,128)}, f32[128,768]{1,0:T(8,128)S(1)}, u32[]{:S(2)}) copy-start(f32[128,768]{1,0:T(8,128)S(1)} %get-tuple-element.212) | copy-start | bytes 1179652
  377.0 13.2 %all-to-all-start.15 = ((bf16[4,128,768]{2,1,0:T(8,128)(2,1)}), bf16[4,128,768]{2,1,0:T(8,128)(2,1)S(1)}, u32[]{:S(2)}, u32[]{:S(2)}) async-start(bf16[4,128,768]{2,1,0:T(8,128)(2,1)} %broadcast_in_dim.62), calls=%async_computation.15 | async-start | bytes 1572864 | tf_op jit(solution)/shard_map/all_to_all | solution.py:40
  390.3 5.4 collective-permute-start.11
  402.2 2.5 collective-permute-start.12
  407.0 16.0 %copy-start.54 = (f32[128]{0:T(128)S(1)}, f32[128]{0:T(128)}, u32[]{:S(2)}) copy-start(f32[128]{0:T(128)} %copy-done.53) | copy-start | bytes 1540
  407.0 16.0 %copy-start.60 = (f32[128]{0:T(128)S(1)}, f32[128]{0:T(128)}, u32[]{:S(2)}) copy-start(f32[128]{0:T(128)} %copy-done.59) | copy-start | bytes 1540
  407.0 15.6 %all-to-all-start.16 = ((bf16[4,128,768]{2,1,0:T(8,128)(2,1)}), bf16[4,128,768]{2,1,0:T(8,128)(2,1)S(1)}, u32[]{:S(2)}, u32[]{:S(2)}) async-start(bf16[4,128,768]{2,1,0:T(8,128)(2,1)} %fusion.11), calls=%async_computation.16 | async-start | bytes 1572864 | tf_op jit(solution)/shard_map/all_to_all | solution.py:40
  410.6 13.1 %copy-start.74 = (f32[128]{0:T(128)S(1)}, f32[128]{0:T(128)}, u32[]{:S(2)}) copy-start(f32[128]{0:T(128)} %copy-done.73) | copy-start | bytes 1540
  410.6 68.2 %all-gather.9.cloned.1.call-start = ((), (), s32[]{:S(2)}) async-start(), calls=%async_computation.24 | async-start | bytes 2506752 | tf_op jit(solution)/shard_map/all_gather | solution.py:680
  427.0 13.3 %all-to-all-start.17 = ((bf16[16,128,64]{1,2,0:T(8,128)(2,1)}), bf16[16,128,64]{1,2,0:T(8,128)(2,1)S(1)}, u32[]{:S(2)}, u32[]{:S(2)}) async-start(bf16[16,128,64]{1,2,0:T(8,128)(2,1)} %concatenate.71), calls=%async_computation.17 | async-start | bytes 524288 | tf_op jit(solution)/shard_map/all_to_all | solution.py:40
  441.3 37.1 %all-to-all-start.18 = ((bf16[8,192,768]{2,1,0:T(8,128)(2,1)}), bf16[8,192,768]{2,1,0:T(8,128)(2,1)S(1)}, u32[]{:S(2)}, u32[]{:S(2)}) async-start(bf16[8,192,768]{2,1,0:T(8,128)(2,1)} %shard_map.280), calls=%async_computation.18 | async-start | bytes 4718592 | tf_op jit(solution)/shard_map/all_to_all | solution.py:40
  444.9 104.8 %all-gather.11.cloned.1.call-start = ((), (), s32[]{:S(2)}) async-start(), calls=%async_computation.25 | async-start | bytes 2506752 | tf_op jit(solution)/shard_map/all_gather | solution.py:684
  459.9 4.3 collective-permute-start.13
  479.6 31.3 %all-to-all-start.19 = ((bf16[8,128,768]{2,1,0:T(8,128)(2,1)}), bf16[8,128,768]{2,1,0:T(8,128)(2,1)S(1)}, u32[]{:S(2)}, u32[]{:S(2)}) async-start(bf16[8,128,768]{2,1,0:T(8,128)(2,1)} %fusion.1), calls=%async_computation.19 | async-start | bytes 3145728 | tf_op jit(solution)/shard_map/all_to_all | solution.py:40
  510.9 14.2 %all-to-all-start.21 = ((bf16[16,16,768]{2,1,0:T(8,128)(2,1)}), bf16[16,16,768]{2,1,0:T(8,128)(2,1)S(1)}, u32[]{:S(2)}, u32[]{:S(2)}) async-start(bf16[16,16,768]{2,1,0:T(8,128)(2,1)} %pad.6.clone), calls=%async_computation.21 | async-start | bytes 786432 | tf_op jit(solution)/shard_map/all_to_all | solution.py:40
  525.1 16.8 %all-to-all-start.20 = ((bf16[8,80,768]{2,1,0:T(8,128)(2,1)}), bf16[8,80,768]{2,1,0:T(8,128)(2,1)S(1)}, u32[]{:S(2)}, u32[]{:S(2)}) async-start(bf16[8,80,768]{2,1,0:T(8,128)(2,1)} %shard_map.282), calls=%async_computation.20 | async-start | bytes 1966080 | tf_op jit(solution)/shard_map/all_to_all | solution.py:40
  543.1 23.2 %all-to-all-start.22 = ((bf16[8,80,768]{2,1,0:T(8,128)(2,1)}), bf16[8,80,768]{2,1,0:T(8,128)(2,1)S(1)}, u32[]{:S(2)}, u32[]{:S(2)}) async-start(bf16[8,80,768]{2,1,0:T(8,128)(2,1)} %broadcast_in_dim.135), calls=%async_computation.22 | async-start | bytes 1966080 | tf_op jit(solution)/shard_map/all_to_all | solution.py:40
  549.7 18.0 %copy-start.11 = (f32[128,768]{1,0:T(8,128)S(1)}, f32[128,768]{1,0:T(8,128)}, u32[]{:S(2)}) copy-start(f32[128,768]{1,0:T(8,128)} %copy-done.10) | copy-start | bytes 1179652
  549.7 18.0 %copy-start.13 = (f32[128,768]{1,0:T(8,128)S(1)}, f32[128,768]{1,0:T(8,128)}, u32[]{:S(2)}) copy-start(f32[128,768]{1,0:T(8,128)} %copy-done.12) | copy-start | bytes 1179652
  549.7 18.0 %copy-start.68 = (f32[128]{0:T(128)S(1)}, f32[128]{0:T(128)}, u32[]{:S(2)}) copy-start(f32[128]{0:T(128)} %copy-done.67) | copy-start | bytes 1540
  566.3 3.0 collective-permute-start.14
  (60 other events, 208.9 us)
Sparse Core Ops, SparseCore 0:
  121.5 40.6 all-gather.6
  413.9 53.9 all-gather.8
  479.7 59.7 all-gather.10

commit v8 on v7

--- a/solution.py
+++ b/solution.py
@@ -484,8 +484,10 @@
         mixed_head, layer_rows = lax.optimization_barrier((mixed_head, layer_rows))
     else:
         normed = layer_norm(flowing, gain_one, bias_one).astype(BF16)
-        normed, layer_rows = lax.optimization_barrier((normed, layer_rows))
-        own, other = (part.reshape(LEN // 2, D) for part in gather_ctx(normed))
+        own = spread_to(normed, 8, "ctx", CHIP_GROUPS)
+        own, layer_rows = lax.optimization_barrier((own, layer_rows))
+        other = swap_core(own).reshape(LEN // 2, D)
+        own = own.reshape(LEN // 2, D)
         own, other, carried = lax.optimization_barrier((own, other, carried))
         carried = spread_to(carried, 4, "ctx", X_GROUPS)
         mixed_head, queries, keys, values = attend(arrive_pos, ctx_pos, own, other, head_weight, head_shift)

time: 586 us -> 598 us (1.020)
  waiting for transfers between devices: 169 us -> 213 us
  blocking collectives: 122 us -> 81.6 us
  starting transfers between devices: 92 us -> 99.2 us
    all_to_all x7 -> x5, blocking collectives: 122 us -> 81.6 us  [exchange(): lax.all_to_all(parts, axis, 0, 0, tiled=True, axis_index_groups=groups)]
    all_gather x1, waiting for transfers between devices: 13.3 us -> 45.5 us  [shards(): lax.all_gather(layer_pieces[1], 'shard', axis=0)]
    all_to_all x16 -> x18, waiting for transfers between devices: 135 us -> 146 us  [exchange(): lax.all_to_all(parts, axis, 0, 0, tiled=True, axis_index_groups=groups)]
    all_to_all x16 -> x18, starting transfers between devices: 71.4 us -> 79.8 us  [exchange(): lax.all_to_all(parts, axis, 0, 0, tiled=True, axis_index_groups=groups)]
  transfers between devices with their start and end apart: 34 -> 36, of which waited for: 27 -> 29; matrix products, arithmetic and copies ran while one was open for 9% -> 9% of each run, Pallas kernels for 15% -> 14%
where the time goes in v8:
time: 598 us; the launch traced here: 593 us
  waiting for transfers between devices  213 us (36%)
  Pallas kernels  102 us (17%)
  starting transfers between devices  99.2 us (17%)
  blocking collectives  81.6 us (14%)
  local copies, waits for them, and re-layouts  46.8 us (8%)
  other arithmetic  30.1 us (5%)
  between operations  15.5 us (3%)
    all_to_all x18, waiting for transfers between devices, exchange(): lax.all_to_all(parts, axis, 0, 0, tiled=True, axis_index_groups=groups)  146 us
    all_to_all x5, blocking collectives, exchange(): lax.all_to_all(parts, axis, 0, 0, tiled=True, axis_index_groups=groups)  81.6 us
    all_to_all x18, starting transfers between devices, exchange(): lax.all_to_all(parts, axis, 0, 0, tiled=True, axis_index_groups=groups)  79.8 us
    all_gather x1, waiting for transfers between devices, shards(): lax.all_gather(layer_pieces[1], 'shard', axis=0)  45.5 us
    pallas_call x2, Pallas kernels, attend_back(): pl.pallas_call(attend_back_kernel, out_shape=(jax.ShapeDtypeStruct((LEN,...  29.4 us
    ppermute x15, waiting for transfers between devices, swap_core(): return lax.ppermute(part, 'ctx', SWAP)  21.6 us
    ppermute x15, starting transfers between devices, swap_core(): return lax.ppermute(part, 'ctx', SWAP)  19.1 us
    pallas_call x2, Pallas kernels, attend(): pl.pallas_call(functools.partial(attend_kernel, fresh), out_shape=outs, i...  18.9 us
  transfers between devices with their start and end apart: 36, of which 29 were waited for; matrix products, arithmetic and copies ran while one was open for 9% of the time, Pallas kernels for 14%

profile of v8, /device:TPU:1, one launch (start us, length us, event | category | flops | bytes accessed | tf_op | source)
XLA Modules:
  0.0 593.2 jit_solution(4817733255193691969)
XLA Ops:
  7.2 2.3 broadcast_in_dim.48
  9.6 7.6 %all-to-all-start = ((bf16[8,128,768]{2,1,0:T(8,128)(2,1)}), bf16[8,128,768]{2,1,0:T(8,128)(2,1)}, u32[]{:S(2)}, u32[]{:S(2)}) async-start(bf16[8,128,768]{2,1,0:T(8,128)(2,1)} %broadcast_in_dim.48), calls=%async_computation | async-start | bytes 3145728 | tf_op jit(solution)/shard_map/all_to_all | solution.py:40
  23.1 17.1 %all-to-all-done = bf16[8,128,768]{2,1,0:T(8,128)(2,1)} async-done(((bf16[8,128,768]{2,1,0:T(8,128)(2,1)}), bf16[8,128,768]{2,1,0:T(8,128)(2,1)}, u32[]{:S(2)}, u32[]{:S(2)}) %all-to-all-start) | async-done | bytes 1572896 | tf_op jit(solution)/shard_map/all_to_all | solution.py:40
  41.2 5.1 all-to-all-start.1
  49.1 8.7 %all-to-all-done.1 = bf16[8,64,768]{2,1,0:T(8,128)(2,1)S(1)} async-done(((bf16[8,64,768]{2,1,0:T(8,128)(2,1)}), bf16[8,64,768]{2,1,0:T(8,128)(2,1)S(1)}, u32[]{:S(2)}, u32[]{:S(2)}) %all-to-all-start.1) | async-done | bytes 786464 | tf_op jit(solution)/shard_map/all_to_all | solution.py:40
  59.3 4.4 all-to-all-start.2
  68.6 10.3 %shard_map.271 = (bf16[2048,64]{1,0:T(8,128)(2,1)}, bf16[2048,64]{1,0:T(8,128)(2,1)}, bf16[2048,64]{1,0:T(8,128)(2,1)}, bf16[2048,64]{1,0:T(8,128)(2,1)}, bf16[1...) custom-call(s32[32]{0:T(128)} %reshape.369.arrive_pos, s32[32]{0:T(128)} %reshape.370.ctx_pos, ...), custom_call_target="tpu_custom_call" | custom-call | flops 2000000000 | bytes 5000000 | tf_op jit(solution)/shard_map/pallas_call | solution.py:213
  78.9 5.8 all-to-all-done.2.rows_ref
  84.8 3.4 collective-permute-start.1
  89.5 13.0 %all_to_all.115 = bf16[16,128,64]{1,2,0:T(8,128)(2,1)S(1)} all-to-all(bf16[16,128,64]{1,2,0:T(8,128)(2,1)S(1)} %copy.69), channel_id=1, replica_groups=mesh['shard'=8,'ctx'=16] {'ctx'}, dimensions={0} | all-to-all | bytes 524288 | tf_op jit(solution)/shard_map/all_to_all | solution.py:40
  105.3 13.7 %all_to_all.116 = bf16[4,128,768]{2,1,0:T(8,128)(2,1)S(1)} all-to-all(bf16[4,128,768]{2,1,0:T(8,128)(2,1)S(1)} %broadcast_in_dim.54), channel_id=1, replica_groups={{0,2,4,6},{1,3,5,7},{8,10,12,14},{9,11,13,15},{16,18,20,22},{17,19,21,2..., dimensions={0} | all-to-all | bytes 1572864 | tf_op jit(solution)/shard_map/all_to_all | solution.py:40
  123.9 5.7 shard_map.272
  132.2 2.2 fusion.14
  134.4 3.6 all-to-all-start.5
  138.9 11.2 %all-to-all-done.5 = bf16[4,128,768]{2,1,0:T(8,128)(2,1)S(1)} async-done(((bf16[4,128,768]{2,1,0:T(8,128)(2,1)}), bf16[4,128,768]{2,1,0:T(8,128)(2,1)S(1)}, u32[]{:S(2)}, u32[]{:S(2)}) %all-to-all-start.5) | async-done | bytes 786464 | tf_op jit(solution)/shard_map/all_to_all | solution.py:40
  151.9 3.7 all-to-all-start.6
  155.7 45.5 %all-gather.7.cloned.1.call-done = bf16[1152,768]{1,0:T(8,128)(2,1)} async-done(((bf16[144,768]{1,0:T(8,128)(2,1)}), bf16[1152,768]{1,0:T(8,128)(2,1)}) %all-gather.7.cloned.1.call-update) | async-done | bytes 1769488 | tf_op jit(solution)/shard_map/all_gather | solution.py:637
  202.1 3.0 collective-permute-done.4
  207.2 4.0 all-to-all-start.7
  213.2 8.6 %shard_map.273 = (bf16[2048,64]{1,0:T(8,128)(2,1)}, bf16[2048,64]{1,0:T(8,128)(2,1)}, bf16[2048,64]{1,0:T(8,128)(2,1)}, bf16[2048,64]{1,0:T(8,128)(2,1)}) custom-call(s32[32]{0:T(128)} %reshape.369.arrive_pos, s32[32]{0:T(128)} %reshape.370.ctx_pos, bf16[1024,768]{1,0:T(8,128)(2,1)} %bitcast.147, bf16[1024,768]{1,0:T(8,128)(2,1)} %bitcast.161, ...), custom_call_target="tpu_custom_call" | custom-call | flops 2000000000 | bytes 5000000 | tf_op jit(solution)/shard_map/pallas_call | solution.py:213
  224.5 14.6 %all_to_all.117 = bf16[16,128,64]{1,2,0:T(8,128)(2,1)S(1)} all-to-all(bf16[16,128,64]{1,2,0:T(8,128)(2,1)S(1)} %copy.70), channel_id=1, replica_groups=mesh['shard'=8,'ctx'=16] {'ctx'}, dimensions={0} | all-to-all | bytes 524288 | tf_op jit(solution)/shard_map/all_to_all | solution.py:40
  240.8 13.7 %all_to_all.118 = bf16[4,128,768]{2,1,0:T(8,128)(2,1)S(1)} all-to-all(bf16[4,128,768]{2,1,0:T(8,128)(2,1)S(1)} %broadcast_in_dim.57), channel_id=1, replica_groups={{0,2,4,6},{1,3,5,7},{8,10,12,14},{9,11,13,15},{16,18,20,22},{17,19,21,2..., dimensions={0} | all-to-all | bytes 1572864 | tf_op jit(solution)/shard_map/all_to_all | solution.py:40
  259.4 5.7 shard_map.274
  267.7 2.2 fusion.13
  269.9 3.5 all-to-all-start.10
  273.4 5.7 shard_map.275
  279.0 6.3 %all-to-all-done.10 = bf16[4,128,768]{2,1,0:T(8,128)(2,1)S(1)} async-done(((bf16[4,128,768]{2,1,0:T(8,128)(2,1)}), bf16[4,128,768]{2,1,0:T(8,128)(2,1)S(1)}, u32[]{:S(2)}, u32[]{:S(2)}) %all-to-all-start.10) | async-done | bytes 786464 | tf_op jit(solution)/shard_map/all_to_all | solution.py:40
  288.7 2.2 fusion.12
  290.9 3.5 all-to-all-start.11
  294.6 11.8 %all-to-all-done.11 = bf16[4,128,768]{2,1,0:T(8,128)(2,1)S(1)} async-done(((bf16[4,128,768]{2,1,0:T(8,128)(2,1)}), bf16[4,128,768]{2,1,0:T(8,128)(2,1)S(1)}, u32[]{:S(2)}, u32[]{:S(2)}) %all-to-all-start.11) | async-done | bytes 786464 | tf_op jit(solution)/shard_map/all_to_all | solution.py:40
  312.0 4.5 all-to-all-start.12
  317.4 5.8 shard_map.276
  326.3 4.0 all-to-all-start.13
  330.3 14.7 %shard_map.277 = (bf16[2048,256]{1,0:T(8,128)(2,1)}, bf16[1024,768]{1,0:T(8,128)(2,1)}, bf16[1024,768]{1,0:T(8,128)(2,1)}, f32[1,192]{1,0:T(1,128)}) custom-call(s32[32]{0:T(128)} %reshape.369.arrive_pos, s32[32]{0:T(128)} %reshape.370.ctx_pos, bf16[2048,64]{1,0:T(8,128)(2,1)} %get-tuple-element.127.q_ref, bf16[2048,64]{1,0:T(8,128)(2,1)} %get-tuple-element.128.k_ref, ...), custom_call_target="tpu_custom_call" | custom-call | flops 4000000000 | bytes 5000000 | tf_op jit(solution)/shard_map/pallas_call | solution.py:225
  346.0 3.2 collective-permute-done.10
  349.2 3.0 fusion.2
  352.2 7.1 %all-to-all-done.13 = bf16[8,192,768]{2,1,0:T(8,128)(2,1)S(1)} async-done(((bf16[8,192,768]{2,1,0:T(8,128)(2,1)}), bf16[8,192,768]{2,1,0:T(8,128)(2,1)S(1)}, u32[]{:S(2)}, u32[]{:S(2)}) %all-to-all-start.13) | async-done | bytes 2359328 | tf_op jit(solution)/shard_map/all_to_all | solution.py:40
  360.4 26.5 %all_to_all.119 = bf16[8,128,768]{2,1,0:T(8,128)(2,1)S(1)} all-to-all(bf16[8,128,768]{2,1,0:T(8,128)(2,1)} %fusion.2), channel_id=1, replica_groups={{0,2,4,6,8,10,12,14},{1,3,5,7,9,11,13,15},{16,18,20,22,24,26,28,30},{17..., dimensions={0} | all-to-all | bytes 3145728 | tf_op jit(solution)/shard_map/all_to_all | solution.py:40
  389.3 3.5 all-to-all-start.15
  396.3 4.3 shard_map.278.rest_6_
  402.5 3.5 collective-permute-start.11
  408.8 5.7 shard_map.279
  416.9 2.2 fusion.11
  419.2 3.6 all-to-all-start.16
  423.6 11.2 %all-to-all-done.16 = bf16[4,128,768]{2,1,0:T(8,128)(2,1)S(1)} async-done(((bf16[4,128,768]{2,1,0:T(8,128)(2,1)}), bf16[4,128,768]{2,1,0:T(8,128)(2,1)S(1)}, u32[]{:S(2)}, u32[]{:S(2)}) %all-to-all-start.16) | async-done | bytes 786464 | tf_op jit(solution)/shard_map/all_to_all | solution.py:40
  439.2 4.5 all-to-all-start.17
  444.6 5.8 shard_map.280
  450.3 2.2 all-to-all-done.17
  453.5 3.6 all-to-all-start.18
  457.4 14.7 %shard_map.281 = (bf16[2048,256]{1,0:T(8,128)(2,1)}, bf16[1024,768]{1,0:T(8,128)(2,1)}, bf16[1024,768]{1,0:T(8,128)(2,1)}, f32[1,192]{1,0:T(1,128)}) custom-call(s32[32]{0:T(128)} %reshape.369.arrive_pos, s32[32]{0:T(128)} %reshape.370.ctx_pos, bf16[2048,64]{1,0:T(8,128)(2,1)} %get-tuple-element.144.q_ref, bf16[2048,64]{1,0:T(8,128)(2,1)} %get-tuple-element.145.k_ref, ...), custom_call_target="tpu_custom_call" | custom-call | flops 4000000000 | bytes 5000000 | tf_op jit(solution)/shard_map/pallas_call | solution.py:225
  473.1 3.2 collective-permute-done.13
  476.4 3.0 fusion.1
  479.3 11.3 %all-to-all-done.18 = bf16[8,192,768]{2,1,0:T(8,128)(2,1)S(1)} async-done(((bf16[8,192,768]{2,1,0:T(8,128)(2,1)}), bf16[8,192,768]{2,1,0:T(8,128)(2,1)S(1)}, u32[]{:S(2)}, u32[]{:S(2)}) %all-to-all-start.18) | async-done | bytes 2359328 | tf_op jit(solution)/shard_map/all_to_all | solution.py:40
  491.8 6.2 %all-to-all-start.19 = ((bf16[8,128,768]{2,1,0:T(8,128)(2,1)}), bf16[8,128,768]{2,1,0:T(8,128)(2,1)S(1)}, u32[]{:S(2)}, u32[]{:S(2)}) async-start(bf16[8,128,768]{2,1,0:T(8,128)(2,1)} %fusion.1), calls=%async_computation.19 | async-start | bytes 3145728 | tf_op jit(solution)/shard_map/all_to_all | solution.py:40
  501.7 21.4 %all-to-all-done.19 = bf16[8,128,768]{2,1,0:T(8,128)(2,1)S(1)} async-done(((bf16[8,128,768]{2,1,0:T(8,128)(2,1)}), bf16[8,128,768]{2,1,0:T(8,128)(2,1)S(1)}, u32[]{:S(2)}, u32[]{:S(2)}) %all-to-all-start.19) | async-done | bytes 1572896 | tf_op jit(solution)/shard_map/all_to_all | solution.py:40
  523.2 4.2 all-to-all-start.21
  529.6 4.8 shard_map.282
  534.4 2.9 all-to-all-done.21
  537.3 3.6 all-to-all-start.20
  540.9 13.2 %all-to-all-done.20 = bf16[8,80,768]{2,1,0:T(8,128)(2,1)S(1)} async-done(((bf16[8,80,768]{2,1,0:T(8,128)(2,1)}), bf16[8,80,768]{2,1,0:T(8,128)(2,1)S(1)}, u32[]{:S(2)}, u32[]{:S(2)}) %all-to-all-start.20) | async-done | bytes 983072 | tf_op jit(solution)/shard_map/all_to_all | solution.py:40
  555.3 6.5 %all-to-all-start.22 = ((bf16[8,80,768]{2,1,0:T(8,128)(2,1)}), bf16[8,80,768]{2,1,0:T(8,128)(2,1)S(1)}, u32[]{:S(2)}, u32[]{:S(2)}) async-start(bf16[8,80,768]{2,1,0:T(8,128)(2,1)} %broadcast_in_dim.135), calls=%async_computation.22 | async-start | bytes 1966080 | tf_op jit(solution)/shard_map/all_to_all | solution.py:40
  561.9 6.5 %shard_map.283 = (f32[2,96,3072]{2,1,0:T(8,128)}, f32[2,384,768]{2,1,0:T(8,128)}) custom-call(bf16[16,96,768]{2,1,0:T(8,128)(2,1)} %bitcast.159, bf16[16,96,768]{2,1,0:T(8,128)(2,1)} %bitcast.158), custom_call_target="tpu_custom_call" | custom-call | flops 1000000 | bytes 10000000 | tf_op jit(solution)/shard_map/pallas_call | solution.py:448
  568.4 10.1 %all-to-all-done.22 = bf16[8,80,768]{2,1,0:T(8,128)(2,1)S(1)} async-done(((bf16[8,80,768]{2,1,0:T(8,128)(2,1)}), bf16[8,80,768]{2,1,0:T(8,128)(2,1)S(1)}, u32[]{:S(2)}, u32[]{:S(2)}) %all-to-all-start.22) | async-done | bytes 983072 | tf_op jit(solution)/shard_map/all_to_all | solution.py:40
  583.0 3.3 shard_map.284
  (371 shorter events, 95.5 us)
Async XLA Ops:
  7.2 39.1 %copy-start = (bf16[2,96,3072]{2,1,0:T(8,128)(2,1)S(1)}, bf16[2,96,3072]{2,1,0:T(8,128)(2,1)}, u32[]{:S(2)}) copy-start(bf16[2,96,3072]{2,1,0:T(8,128)(2,1)} %param.28) | copy-start | bytes 3538948
  9.5 7.8 %copy-start.85 = (bf16[2,96]{1,0:T(2,128)(2,1)S(1)}, bf16[2,96]{1,0:T(2,128)(2,1)}, u32[]{:S(2)}) copy-start(bf16[2,96]{1,0:T(2,128)(2,1)} %param.25) | copy-start | bytes 1156
  9.5 7.8 %copy-start.86 = (bf16[2,96]{1,0:T(2,128)(2,1)S(1)}, bf16[2,96]{1,0:T(2,128)(2,1)}, u32[]{:S(2)}) copy-start(bf16[2,96]{1,0:T(2,128)(2,1)} %param.26) | copy-start | bytes 1156
  9.5 7.8 %copy-start.87 = (bf16[2,96]{1,0:T(2,128)(2,1)S(1)}, bf16[2,96]{1,0:T(2,128)(2,1)}, u32[]{:S(2)}) copy-start(bf16[2,96]{1,0:T(2,128)(2,1)} %param.27) | copy-start | bytes 1156
  9.5 7.8 %copy-start.88 = (bf16[2,96]{1,0:T(2,128)(2,1)S(1)}, bf16[2,96]{1,0:T(2,128)(2,1)}, u32[]{:S(2)}) copy-start(bf16[2,96]{1,0:T(2,128)(2,1)} %param.31) | copy-start | bytes 1156
  9.5 8.0 %copy-start.72 = (bf16[2,384]{1,0:T(2,128)(2,1)S(1)}, bf16[2,384]{1,0:T(2,128)(2,1)}, u32[]{:S(2)}) copy-start(bf16[2,384]{1,0:T(2,128)(2,1)} %param.29) | copy-start | bytes 4612
  9.6 9.7 %copy-start.27 = (bf16[2,96,2304]{2,1,0:T(8,128)(2,1)S(1)}, bf16[2,96,2304]{2,1,0:T(8,128)(2,1)}, u32[]{:S(2)}) copy-start(bf16[2,96,2304]{2,1,0:T(8,128)(2,1)} %param.21) | copy-start | bytes 2654212
  9.6 30.7 %all-to-all-start = ((bf16[8,128,768]{2,1,0:T(8,128)(2,1)}), bf16[8,128,768]{2,1,0:T(8,128)(2,1)}, u32[]{:S(2)}, u32[]{:S(2)}) async-start(bf16[8,128,768]{2,1,0:T(8,128)(2,1)} %broadcast_in_dim.48), calls=%async_computation | async-start | bytes 3145728 | tf_op jit(solution)/shard_map/all_to_all | solution.py:40
  41.2 16.7 %all-to-all-start.1 = ((bf16[8,64,768]{2,1,0:T(8,128)(2,1)}), bf16[8,64,768]{2,1,0:T(8,128)(2,1)S(1)}, u32[]{:S(2)}, u32[]{:S(2)}) async-start(bf16[8,64,768]{2,1,0:T(8,128)(2,1)} %broadcast_in_dim.51), calls=%async_computation.1 | async-start | bytes 1572864 | tf_op jit(solution)/shard_map/all_to_all | solution.py:40
  48.0 20.6 %collective-permute-start = (bf16[8,128,768]{2,1,0:T(8,128)(2,1)}, bf16[8,128,768]{2,1,0:T(8,128)(2,1)}, u32[]{:S(2)}, u32[]{:S(2)}) collective-permute-start(bf16[8,128,768]{2,1,0:T(8,128)(2,1)} %all-to-all-done), channel_id=1, source_target_pairs={{0,1},{1,0},{2,3},{3,2},{4,5},{5,4},{6,7},{7,6},{8,9},{9,8},{10,11... | collective-permute-start | bytes 4718600 | tf_op jit(solution)/shard_map/ppermute | solution.py:48
  59.3 25.4 %all-to-all-start.2 = ((bf16[8,144,768]{2,1,0:T(8,128)(2,1)}), bf16[8,144,768]{2,1,0:T(8,128)(2,1)S(1)}, u32[]{:S(2)}, u32[]{:S(2)}) async-start(bf16[8,144,768]{2,1,0:T(8,128)(2,1)} %broadcast_in_dim.53), calls=%async_computation.2 | async-start | bytes 3538944 | tf_op jit(solution)/shard_map/all_to_all | solution.py:40
  84.7 17.8 %copy-start.8 = (bf16[1,128,768]{2,1,0:T(8,128)(2,1)S(1)}, bf16[1,128,768]{2,1,0:T(8,128)(2,1)}, u32[]{:S(2)}) copy-start(bf16[1,128,768]{2,1,0:T(8,128)(2,1)} %param.16) | copy-start | bytes 589828
  84.8 19.6 %copy-start.34 = (bf16[8,96,384]{2,1,0:T(8,128)(2,1)}, bf16[8,96,384]{2,1,0:T(8,128)(2,1)S(1)}, u32[]{:S(2)}) copy-start(bf16[8,96,384]{2,1,0:T(8,128)(2,1)S(1)} %pad_maximum_fusion.1) | copy-start | bytes 1769476
  84.8 17.7 %collective-permute-start.1 = (bf16[768,384]{1,0:T(8,128)(2,1)S(1)}, bf16[768,384]{1,0:T(8,128)(2,1)}, u32[]{:S(2)}, u32[]{:S(2)}) collective-permute-start(bf16[768,384]{1,0:T(8,128)(2,1)S(1)} %bitcast.176), channel_id=1, source_target_pairs={{0,1},{1,0},{2,3},{3,2},{4,5},{5,4},{6,7},{7,6},{8,9},{9,8},{10,11... | collective-permute-start | bytes 1769480 | tf_op jit(solution)/shard_map/ppermute | solution.py:48
  104.6 16.4 %copy-start.21 = (bf16[8,64,768]{2,1,0:T(8,128)(2,1)S(1)}, bf16[8,64,768]{2,1,0:T(8,128)(2,1)}, u32[]{:S(2)}) copy-start(bf16[8,64,768]{2,1,0:T(8,128)(2,1)} %copy-done.20) | copy-start | bytes 2359300
  119.0 4.0 collective-permute-start.2
  129.6 2.5 collective-permute-start.3
  134.4 15.8 %copy-start.48 = (f32[768]{0:T(1024)S(1)}, f32[768]{0:T(1024)}, u32[]{:S(2)}) copy-start(f32[768]{0:T(1024)} %get-tuple-element.204) | copy-start | bytes 9220
  134.4 15.6 %all-to-all-start.5 = ((bf16[4,128,768]{2,1,0:T(8,128)(2,1)}), bf16[4,128,768]{2,1,0:T(8,128)(2,1)S(1)}, u32[]{:S(2)}, u32[]{:S(2)}) async-start(bf16[4,128,768]{2,1,0:T(8,128)(2,1)} %fusion.14), calls=%async_computation.5 | async-start | bytes 1572864 | tf_op jit(solution)/shard_map/all_to_all | solution.py:40
  138.0 63.1 %all-gather.7.cloned.1.call-start = ((), (), s32[]{:S(2)}) async-start(), calls=%async_computation.23 | async-start | bytes 1990656 | tf_op jit(solution)/shard_map/all_gather | solution.py:637
  138.8 11.7 %copy-start.47 = (f32[768]{0:T(1024)S(1)}, f32[768]{0:T(1024)}, u32[]{:S(2)}) copy-start(f32[768]{0:T(1024)} %get-tuple-element.202) | copy-start | bytes 9220
  151.9 54.4 %copy-start.22 = (bf16[1,128,768]{2,1,0:T(8,128)(2,1)S(1)}, bf16[1,128,768]{2,1,0:T(8,128)(2,1)}, u32[]{:S(2)}) copy-start(bf16[1,128,768]{2,1,0:T(8,128)(2,1)} %param.17) | copy-start | bytes 589828
  151.9 49.2 %all-to-all-start.6 = ((bf16[8,128,768]{2,1,0:T(8,128)(2,1)}), bf16[8,128,768]{2,1,0:T(8,128)(2,1)S(1)}, u32[]{:S(2)}, u32[]{:S(2)}) async-start(bf16[8,128,768]{2,1,0:T(8,128)(2,1)} %broadcast_in_dim.55), calls=%async_computation.6 | async-start | bytes 3145728 | tf_op jit(solution)/shard_map/all_to_all | solution.py:40
  201.2 11.2 %copy-start.7 = (bf16[8,128,768]{2,1,0:T(8,128)(2,1)}, bf16[8,128,768]{2,1,0:T(8,128)(2,1)S(1)}, u32[]{:S(2)}) copy-start(bf16[8,128,768]{2,1,0:T(8,128)(2,1)S(1)} %all-to-all-done.6) | copy-start | bytes 4718596
  201.2 3.9 collective-permute-start.4
  207.2 15.7 %all-to-all-start.7 = ((bf16[4,128,768]{2,1,0:T(8,128)(2,1)}), bf16[4,128,768]{2,1,0:T(8,128)(2,1)S(1)}, u32[]{:S(2)}, u32[]{:S(2)}) async-start(bf16[4,128,768]{2,1,0:T(8,128)(2,1)} %broadcast_in_dim.56), calls=%async_computation.7 | async-start | bytes 1572864 | tf_op jit(solution)/shard_map/all_to_all | solution.py:40
  212.4 26.7 %copy-start.36 = (bf16[8,96,384]{2,1,0:T(8,128)(2,1)}, bf16[8,96,384]{2,1,0:T(8,128)(2,1)S(1)}, u32[]{:S(2)}) copy-start(bf16[8,96,384]{2,1,0:T(8,128)(2,1)S(1)} %pad_maximum_fusion.2) | copy-start | bytes 1769476
  212.4 26.7 %collective-permute-start.5 = (bf16[768,384]{1,0:T(8,128)(2,1)S(1)}, bf16[768,384]{1,0:T(8,128)(2,1)S(1)}, u32[]{:S(2)}, u32[]{:S(2)}) collective-permute-start(bf16[768,384]{1,0:T(8,128)(2,1)S(1)} %bitcast.179), channel_id=1, source_target_pairs={{0,1},{1,0},{2,3},{3,2},{4,5},{5,4},{6,7},{7,6},{8,9},{9,8},{10,11... | collective-permute-start | bytes 1769480 | tf_op jit(solution)/shard_map/ppermute | solution.py:48
  221.7 17.4 %copy-start.65 = (f32[768]{0:T(1024)S(1)}, f32[768]{0:T(1024)}, u32[]{:S(2)}) copy-start(f32[768]{0:T(1024)} %get-tuple-element.201) | copy-start | bytes 9220
  222.9 42.6 %copy-start.3 = (bf16[4,128,768]{2,1,0:T(8,128)(2,1)}, bf16[4,128,768]{2,1,0:T(8,128)(2,1)S(1)}, u32[]{:S(2)}) copy-start(bf16[4,128,768]{2,1,0:T(8,128)(2,1)S(1)} %all-to-all-done.7) | copy-start | bytes 2359300
  254.5 4.0 collective-permute-start.6
  265.2 2.5 collective-permute-start.7
  265.5 4.3 collective-permute-start.8
  269.9 15.5 %all-to-all-start.10 = ((bf16[4,128,768]{2,1,0:T(8,128)(2,1)}), bf16[4,128,768]{2,1,0:T(8,128)(2,1)S(1)}, u32[]{:S(2)}, u32[]{:S(2)}) async-start(bf16[4,128,768]{2,1,0:T(8,128)(2,1)} %fusion.13), calls=%async_computation.10 | async-start | bytes 1572864 | tf_op jit(solution)/shard_map/all_to_all | solution.py:40
  285.4 3.3 collective-permute-start.9
  290.9 15.5 %all-to-all-start.11 = ((bf16[4,128,768]{2,1,0:T(8,128)(2,1)}), bf16[4,128,768]{2,1,0:T(8,128)(2,1)S(1)}, u32[]{:S(2)}, u32[]{:S(2)}) async-start(bf16[4,128,768]{2,1,0:T(8,128)(2,1)} %fusion.12), calls=%async_computation.11 | async-start | bytes 1572864 | tf_op jit(solution)/shard_map/all_to_all | solution.py:40
  294.4 12.9 %copy-start.58 = (f32[128]{0:T(128)S(1)}, f32[128]{0:T(128)}, u32[]{:S(2)}) copy-start(f32[128]{0:T(128)} %copy-done.57) | copy-start | bytes 1540
  294.4 12.9 %copy-start.64 = (f32[128]{0:T(128)S(1)}, f32[128]{0:T(128)}, u32[]{:S(2)}) copy-start(f32[128]{0:T(128)} %copy-done.63) | copy-start | bytes 1540
  294.4 13.7 %copy-start.78 = (f32[128]{0:T(128)S(1)}, f32[128]{0:T(128)}, u32[]{:S(2)}) copy-start(f32[128]{0:T(128)} %copy-done.77) | copy-start | bytes 1540
  294.4 13.7 %copy-start.45 = (f32[768]{0:T(1024)S(1)}, f32[768]{0:T(1024)}, u32[]{:S(2)}) copy-start(f32[768]{0:T(1024)} %get-tuple-element.198) | copy-start | bytes 9220
  312.0 13.3 %all-to-all-start.12 = ((bf16[16,128,64]{1,2,0:T(8,128)(2,1)}), bf16[16,128,64]{1,2,0:T(8,128)(2,1)S(1)}, u32[]{:S(2)}, u32[]{:S(2)}) async-start(bf16[16,128,64]{1,2,0:T(8,128)(2,1)} %concatenate.70), calls=%async_computation.12 | async-start | bytes 524288 | tf_op jit(solution)/shard_map/all_to_all | solution.py:40
  326.3 33.0 %all-to-all-start.13 = ((bf16[8,192,768]{2,1,0:T(8,128)(2,1)}), bf16[8,192,768]{2,1,0:T(8,128)(2,1)S(1)}, u32[]{:S(2)}, u32[]{:S(2)}) async-start(bf16[8,192,768]{2,1,0:T(8,128)(2,1)} %shard_map.276), calls=%async_computation.13 | async-start | bytes 4718592 | tf_op jit(solution)/shard_map/all_to_all | solution.py:40
  345.0 4.2 collective-permute-start.10
  388.2 47.9 %copy-start.10 = (f32[128,768]{1,0:T(8,128)}, f32[128,768]{1,0:T(8,128)S(1)}, u32[]{:S(2)}) copy-start(f32[128,768]{1,0:T(8,128)S(1)} %get-tuple-element.212) | copy-start | bytes 1179652
  389.3 13.2 %all-to-all-start.15 = ((bf16[4,128,768]{2,1,0:T(8,128)(2,1)}), bf16[4,128,768]{2,1,0:T(8,128)(2,1)S(1)}, u32[]{:S(2)}, u32[]{:S(2)}) async-start(bf16[4,128,768]{2,1,0:T(8,128)(2,1)} %broadcast_in_dim.62), calls=%async_computation.15 | async-start | bytes 1572864 | tf_op jit(solution)/shard_map/all_to_all | solution.py:40
  402.5 5.4 collective-permute-start.11
  414.4 2.5 collective-permute-start.12
  419.2 16.0 %copy-start.54 = (f32[128]{0:T(128)S(1)}, f32[128]{0:T(128)}, u32[]{:S(2)}) copy-start(f32[128]{0:T(128)} %copy-done.53) | copy-start | bytes 1540
  419.2 16.0 %copy-start.60 = (f32[128]{0:T(128)S(1)}, f32[128]{0:T(128)}, u32[]{:S(2)}) copy-start(f32[128]{0:T(128)} %copy-done.59) | copy-start | bytes 1540
  419.2 15.6 %all-to-all-start.16 = ((bf16[4,128,768]{2,1,0:T(8,128)(2,1)}), bf16[4,128,768]{2,1,0:T(8,128)(2,1)S(1)}, u32[]{:S(2)}, u32[]{:S(2)}) async-start(bf16[4,128,768]{2,1,0:T(8,128)(2,1)} %fusion.11), calls=%async_computation.16 | async-start | bytes 1572864 | tf_op jit(solution)/shard_map/all_to_all | solution.py:40
  422.8 13.1 %copy-start.74 = (f32[128]{0:T(128)S(1)}, f32[128]{0:T(128)}, u32[]{:S(2)}) copy-start(f32[128]{0:T(128)} %copy-done.73) | copy-start | bytes 1540
  422.8 68.2 %all-gather.9.cloned.1.call-start = ((), (), s32[]{:S(2)}) async-start(), calls=%async_computation.24 | async-start | bytes 2506752 | tf_op jit(solution)/shard_map/all_gather | solution.py:682
  439.2 13.3 %all-to-all-start.17 = ((bf16[16,128,64]{1,2,0:T(8,128)(2,1)}), bf16[16,128,64]{1,2,0:T(8,128)(2,1)S(1)}, u32[]{:S(2)}, u32[]{:S(2)}) async-start(bf16[16,128,64]{1,2,0:T(8,128)(2,1)} %concatenate.71), calls=%async_computation.17 | async-start | bytes 524288 | tf_op jit(solution)/shard_map/all_to_all | solution.py:40
  453.5 37.1 %all-to-all-start.18 = ((bf16[8,192,768]{2,1,0:T(8,128)(2,1)}), bf16[8,192,768]{2,1,0:T(8,128)(2,1)S(1)}, u32[]{:S(2)}, u32[]{:S(2)}) async-start(bf16[8,192,768]{2,1,0:T(8,128)(2,1)} %shard_map.280), calls=%async_computation.18 | async-start | bytes 4718592 | tf_op jit(solution)/shard_map/all_to_all | solution.py:40
  457.1 104.8 %all-gather.11.cloned.1.call-start = ((), (), s32[]{:S(2)}) async-start(), calls=%async_computation.25 | async-start | bytes 2506752 | tf_op jit(solution)/shard_map/all_gather | solution.py:686
  472.1 4.3 collective-permute-start.13
  491.8 31.3 %all-to-all-start.19 = ((bf16[8,128,768]{2,1,0:T(8,128)(2,1)}), bf16[8,128,768]{2,1,0:T(8,128)(2,1)S(1)}, u32[]{:S(2)}, u32[]{:S(2)}) async-start(bf16[8,128,768]{2,1,0:T(8,128)(2,1)} %fusion.1), calls=%async_computation.19 | async-start | bytes 3145728 | tf_op jit(solution)/shard_map/all_to_all | solution.py:40
  523.2 14.2 %all-to-all-start.21 = ((bf16[16,16,768]{2,1,0:T(8,128)(2,1)}), bf16[16,16,768]{2,1,0:T(8,128)(2,1)S(1)}, u32[]{:S(2)}, u32[]{:S(2)}) async-start(bf16[16,16,768]{2,1,0:T(8,128)(2,1)} %pad.6.clone), calls=%async_computation.21 | async-start | bytes 786432 | tf_op jit(solution)/shard_map/all_to_all | solution.py:40
  537.3 16.8 %all-to-all-start.20 = ((bf16[8,80,768]{2,1,0:T(8,128)(2,1)}), bf16[8,80,768]{2,1,0:T(8,128)(2,1)S(1)}, u32[]{:S(2)}, u32[]{:S(2)}) async-start(bf16[8,80,768]{2,1,0:T(8,128)(2,1)} %shard_map.282), calls=%async_computation.20 | async-start | bytes 1966080 | tf_op jit(solution)/shard_map/all_to_all | solution.py:40
  555.3 23.2 %all-to-all-start.22 = ((bf16[8,80,768]{2,1,0:T(8,128)(2,1)}), bf16[8,80,768]{2,1,0:T(8,128)(2,1)S(1)}, u32[]{:S(2)}, u32[]{:S(2)}) async-start(bf16[8,80,768]{2,1,0:T(8,128)(2,1)} %broadcast_in_dim.135), calls=%async_computation.22 | async-start | bytes 1966080 | tf_op jit(solution)/shard_map/all_to_all | solution.py:40
  561.9 18.0 %copy-start.11 = (f32[128,768]{1,0:T(8,128)S(1)}, f32[128,768]{1,0:T(8,128)}, u32[]{:S(2)}) copy-start(f32[128,768]{1,0:T(8,128)} %copy-done.10) | copy-start | bytes 1179652
  561.9 18.0 %copy-start.13 = (f32[128,768]{1,0:T(8,128)S(1)}, f32[128,768]{1,0:T(8,128)}, u32[]{:S(2)}) copy-start(f32[128,768]{1,0:T(8,128)} %copy-done.12) | copy-start | bytes 1179652
  561.9 18.0 %copy-start.68 = (f32[128]{0:T(128)S(1)}, f32[128]{0:T(128)}, u32[]{:S(2)}) copy-start(f32[128]{0:T(128)} %copy-done.67) | copy-start | bytes 1540
  578.5 3.0 collective-permute-start.14
  (62 other events, 202.1 us)
Sparse Core Ops, SparseCore 0:
  141.1 60.0 all-gather.6
  426.1 53.9 all-gather.8
  491.9 59.7 all-gather.10

commit v9 on v7

--- a/solution.py
+++ b/solution.py
@@ -631,8 +631,9 @@
         axis=0,
     )
     gathered = spread_to(packed, S, "shard")
-    gathered, first_piece = lax.optimization_barrier((gathered, layer_pieces[0]))
-    layer_rows = [spread_to(first_piece, S, "shard"), lax.all_gather(layer_pieces[1], "shard", axis=0)]
+    gathered, pieces = lax.optimization_barrier((gathered, jnp.concatenate(layer_pieces, axis=0)))
+    both_rows = spread_to(pieces, S, "shard")
+    layer_rows = [both_rows[:, :144], both_rows[:, 144:]]
     head_weights = gathered[:, :48].reshape(S, LAYERS, 96, 3 * HD)
     vectors = gathered[:, 48:50].reshape(S, 8, LAYERS, 96).transpose(2, 1, 0, 3).reshape(LAYERS, 8, D)
     vectors = vectors.astype(F32)

time: 586 us -> 603 us (1.029)
  waiting for transfers between devices: 169 us -> 182 us
  local copies, waits for them, and re-layouts: 45.7 us -> 54.4 us
    all_to_all x16, waiting for transfers between devices: 135 us -> 160 us  [exchange(): lax.all_to_all(parts, axis, 0, 0, tiled=True, axis_index_groups=groups)]
    all_gather x1 -> x0, waiting for transfers between devices: 13.3 us -> none  [shards(): lax.all_gather(layer_pieces[1], 'shard', axis=0)]
    unnamed x187 -> x140, local copies, waits for them, and re-layouts: 6.55 us -> 12.8 us
  transfers between devices with their start and end apart: 34 -> 33, of which waited for: 27 -> 26; matrix products, arithmetic and copies ran while one was open for 9% -> 7% of each run, Pallas kernels for 15% -> 14%
where the time goes in v9:
time: 603 us; the launch traced here: 598 us
  waiting for transfers between devices  182 us (30%)
  blocking collectives  117 us (19%)
  Pallas kernels  102 us (17%)
  starting transfers between devices  91.5 us (15%)
  local copies, waits for them, and re-layouts  54.4 us (9%)
  other arithmetic  27.9 us (5%)
  between operations  15.5 us (3%)
  matrix products  7.9 us (1%)
    all_to_all x16, waiting for transfers between devices, exchange(): lax.all_to_all(parts, axis, 0, 0, tiled=True, axis_index_groups=groups)  160 us
    all_to_all x7, blocking collectives, exchange(): lax.all_to_all(parts, axis, 0, 0, tiled=True, axis_index_groups=groups)  117 us
    all_to_all x16, starting transfers between devices, exchange(): lax.all_to_all(parts, axis, 0, 0, tiled=True, axis_index_groups=groups)  72.7 us
    pallas_call x2, Pallas kernels, attend_back(): pl.pallas_call(attend_back_kernel, out_shape=(jax.ShapeDtypeStruct((LEN,...  29.4 us
    ppermute x15, waiting for transfers between devices, swap_core(): return lax.ppermute(part, 'ctx', SWAP)  21.4 us
    pallas_call x2, Pallas kernels, attend(): pl.pallas_call(functools.partial(attend_kernel, fresh), out_shape=outs, i...  18.9 us
    ppermute x15, starting transfers between devices, swap_core(): return lax.ppermute(part, 'ctx', SWAP)  18.5 us
    unnamed x140, local copies, waits for them, and re-layouts  12.8 us
  transfers between devices with their start and end apart: 33, of which 26 were waited for; matrix products, arithmetic and copies ran while one was open for 7% of the time, Pallas kernels for 14%

profile of v9, /device:TPU:1, one launch (start us, length us, event | category | flops | bytes accessed | tf_op | source)
XLA Modules:
  0.0 597.7 jit_solution(17005738919932132732)
XLA Ops:
  17.0 6.9 %all-to-all-start.1 = ((bf16[8,64,768]{2,1,0:T(8,128)(2,1)}), bf16[8,64,768]{2,1,0:T(8,128)(2,1)S(1)}, u32[]{:S(2)}, u32[]{:S(2)}) async-start(bf16[8,64,768]{2,1,0:T(8,128)(2,1)} %broadcast_in_dim.51), calls=%async_computation.1 | async-start | bytes 1572864 | tf_op jit(solution)/shard_map/all_to_all | solution.py:40
  24.0 11.6 %all-to-all-done.1 = bf16[8,64,768]{2,1,0:T(8,128)(2,1)S(1)} async-done(((bf16[8,64,768]{2,1,0:T(8,128)(2,1)}), bf16[8,64,768]{2,1,0:T(8,128)(2,1)S(1)}, u32[]{:S(2)}, u32[]{:S(2)}) %all-to-all-start.1) | async-done | bytes 786464 | tf_op jit(solution)/shard_map/all_to_all | solution.py:40
  36.9 6.4 %all-to-all-start = ((bf16[8,128,768]{2,1,0:T(8,128)(2,1)}), bf16[8,128,768]{2,1,0:T(8,128)(2,1)}, u32[]{:S(2)}, u32[]{:S(2)}) async-start(bf16[8,128,768]{2,1,0:T(8,128)(2,1)} %broadcast_in_dim.48), calls=%async_computation | async-start | bytes 3145728 | tf_op jit(solution)/shard_map/all_to_all | solution.py:40
  46.2 20.1 %all-to-all-done = bf16[8,128,768]{2,1,0:T(8,128)(2,1)} async-done(((bf16[8,128,768]{2,1,0:T(8,128)(2,1)}), bf16[8,128,768]{2,1,0:T(8,128)(2,1)}, u32[]{:S(2)}, u32[]{:S(2)}) %all-to-all-start) | async-done | bytes 1572896 | tf_op jit(solution)/shard_map/all_to_all | solution.py:40
  68.4 4.6 all-to-all-start.2
  80.2 10.3 %shard_map.271 = (bf16[2048,64]{1,0:T(8,128)(2,1)}, bf16[2048,64]{1,0:T(8,128)(2,1)}, bf16[2048,64]{1,0:T(8,128)(2,1)}, bf16[2048,64]{1,0:T(8,128)(2,1)}, bf16[1...) custom-call(s32[32]{0:T(128)} %reshape.369.arrive_pos, s32[32]{0:T(128)} %reshape.370.ctx_pos, ...), custom_call_target="tpu_custom_call" | custom-call | flops 2000000000 | bytes 5000000 | tf_op jit(solution)/shard_map/pallas_call | solution.py:213
  90.5 24.1 %all-to-all-done.2 = bf16[8,288,768]{2,1,0:T(8,128)(2,1)} async-done(((bf16[8,288,768]{2,1,0:T(8,128)(2,1)}), bf16[8,288,768]{2,1,0:T(8,128)(2,1)}, u32[]{:S(2)}, u32[]{:S(2)}) %all-to-all-start.2) | async-done | bytes 3538976 | tf_op jit(solution)/shard_map/all_to_all | solution.py:40
  114.6 2.2 fusion.57
  121.7 12.3 %all_to_all.115 = bf16[16,128,64]{1,2,0:T(8,128)(2,1)S(1)} all-to-all(bf16[16,128,64]{1,2,0:T(8,128)(2,1)} %copy.69), channel_id=1, replica_groups=mesh['shard'=8,'ctx'=16] {'ctx'}, dimensions={0} | all-to-all | bytes 524288 | tf_op jit(solution)/shard_map/all_to_all | solution.py:40
  134.1 2.3 fusion.66
  137.4 13.8 %all_to_all.116 = bf16[4,128,768]{2,1,0:T(8,128)(2,1)S(1)} all-to-all(bf16[4,128,768]{2,1,0:T(8,128)(2,1)S(1)} %broadcast_in_dim.54), channel_id=1, replica_groups={{0,2,4,6},{1,3,5,7},{8,10,12,14},{9,11,13,15},{16,18,20,22},{17,19,21,2..., dimensions={0} | all-to-all | bytes 1572864 | tf_op jit(solution)/shard_map/all_to_all | solution.py:40
  155.5 5.8 shard_map.272
  161.4 2.4 collective-permute-done.3
  165.1 14.4 %all_to_all.117 = bf16[4,128,768]{2,1,0:T(8,128)(2,1)S(1)} all-to-all(bf16[4,128,768]{2,1,0:T(8,128)(2,1)S(1)} %fusion.14), channel_id=1, replica_groups={{0,2,4,6},{1,3,5,7},{8,10,12,14},{9,11,13,15},{16,18,20,22},{17,19,21,2..., dimensions={0} | all-to-all | bytes 1572864 | tf_op jit(solution)/shard_map/all_to_all | solution.py:40
  180.5 24.1 %all_to_all.118 = bf16[8,128,768]{2,1,0:T(8,128)(2,1)S(1)} all-to-all(bf16[8,128,768]{2,1,0:T(8,128)(2,1)S(1)} %broadcast_in_dim.55), channel_id=1, replica_groups={{0,2,4,6,8,10,12,14},{1,3,5,7,9,11,13,15},{16,18,20,22,24,26,28,30},{17..., dimensions={0} | all-to-all | bytes 3145728 | tf_op jit(solution)/shard_map/all_to_all | solution.py:40
  205.7 2.3 collective-permute-start.4
  208.0 3.0 collective-permute-done.4
  213.1 3.5 all-to-all-start.7
  217.2 8.6 %shard_map.273 = (bf16[2048,64]{1,0:T(8,128)(2,1)}, bf16[2048,64]{1,0:T(8,128)(2,1)}, bf16[2048,64]{1,0:T(8,128)(2,1)}, bf16[2048,64]{1,0:T(8,128)(2,1)}) custom-call(s32[32]{0:T(128)} %reshape.369.arrive_pos, s32[32]{0:T(128)} %reshape.370.ctx_pos, bf16[1024,768]{1,0:T(8,128)(2,1)} %bitcast.147, bf16[1024,768]{1,0:T(8,128)(2,1)} %bitcast.159, ...), custom_call_target="tpu_custom_call" | custom-call | flops 2000000000 | bytes 5000000 | tf_op jit(solution)/shard_map/pallas_call | solution.py:213
  225.8 2.8 all-to-all-done.7
  230.2 12.4 %all_to_all.119 = bf16[16,128,64]{1,2,0:T(8,128)(2,1)S(1)} all-to-all(bf16[16,128,64]{1,2,0:T(8,128)(2,1)S(1)} %copy.70), channel_id=1, replica_groups=mesh['shard'=8,'ctx'=16] {'ctx'}, dimensions={0} | all-to-all | bytes 524288 | tf_op jit(solution)/shard_map/all_to_all | solution.py:40
  246.0 13.7 %all_to_all.120 = bf16[4,128,768]{2,1,0:T(8,128)(2,1)S(1)} all-to-all(bf16[4,128,768]{2,1,0:T(8,128)(2,1)S(1)} %broadcast_in_dim.57), channel_id=1, replica_groups={{0,2,4,6},{1,3,5,7},{8,10,12,14},{9,11,13,15},{16,18,20,22},{17,19,21,2..., dimensions={0} | all-to-all | bytes 1572864 | tf_op jit(solution)/shard_map/all_to_all | solution.py:40
  264.6 5.7 shard_map.274
  272.9 2.2 fusion.13
  275.1 3.5 all-to-all-start.10
  278.6 5.7 shard_map.275
  284.3 6.3 %all-to-all-done.10 = bf16[4,128,768]{2,1,0:T(8,128)(2,1)S(1)} async-done(((bf16[4,128,768]{2,1,0:T(8,128)(2,1)}), bf16[4,128,768]{2,1,0:T(8,128)(2,1)S(1)}, u32[]{:S(2)}, u32[]{:S(2)}) %all-to-all-start.10) | async-done | bytes 786464 | tf_op jit(solution)/shard_map/all_to_all | solution.py:40
  293.9 2.2 fusion.12
  296.1 3.5 all-to-all-start.11
  299.8 11.8 %all-to-all-done.11 = bf16[4,128,768]{2,1,0:T(8,128)(2,1)S(1)} async-done(((bf16[4,128,768]{2,1,0:T(8,128)(2,1)}), bf16[4,128,768]{2,1,0:T(8,128)(2,1)S(1)}, u32[]{:S(2)}, u32[]{:S(2)}) %all-to-all-start.11) | async-done | bytes 786464 | tf_op jit(solution)/shard_map/all_to_all | solution.py:40
  316.5 4.5 all-to-all-start.12
  321.8 5.8 shard_map.276
  330.8 4.0 all-to-all-start.13
  334.8 14.7 %shard_map.277 = (bf16[2048,256]{1,0:T(8,128)(2,1)}, bf16[1024,768]{1,0:T(8,128)(2,1)}, bf16[1024,768]{1,0:T(8,128)(2,1)}, f32[1,192]{1,0:T(1,128)}) custom-call(s32[32]{0:T(128)} %reshape.369.arrive_pos, s32[32]{0:T(128)} %reshape.370.ctx_pos, bf16[2048,64]{1,0:T(8,128)(2,1)} %get-tuple-element.127.q_ref, bf16[2048,64]{1,0:T(8,128)(2,1)} %get-tuple-element.128.k_ref, ...), custom_call_target="tpu_custom_call" | custom-call | flops 4000000000 | bytes 5000000 | tf_op jit(solution)/shard_map/pallas_call | solution.py:225
  350.5 3.2 collective-permute-done.10
  353.8 3.0 fusion.2
  356.7 7.0 %all-to-all-done.13 = bf16[8,192,768]{2,1,0:T(8,128)(2,1)S(1)} async-done(((bf16[8,192,768]{2,1,0:T(8,128)(2,1)}), bf16[8,192,768]{2,1,0:T(8,128)(2,1)S(1)}, u32[]{:S(2)}, u32[]{:S(2)}) %all-to-all-start.13) | async-done | bytes 2359328 | tf_op jit(solution)/shard_map/all_to_all | solution.py:40
  364.9 26.5 %all_to_all.121 = bf16[8,128,768]{2,1,0:T(8,128)(2,1)S(1)} all-to-all(bf16[8,128,768]{2,1,0:T(8,128)(2,1)} %fusion.2), channel_id=1, replica_groups={{0,2,4,6,8,10,12,14},{1,3,5,7,9,11,13,15},{16,18,20,22,24,26,28,30},{17..., dimensions={0} | all-to-all | bytes 3145728 | tf_op jit(solution)/shard_map/all_to_all | solution.py:40
  393.7 3.5 all-to-all-start.15
  400.8 4.3 shard_map.278.rest_6_
  406.9 3.5 collective-permute-start.11
  413.3 5.6 shard_map.279
  421.4 2.2 fusion.11
  423.6 3.6 all-to-all-start.16
  428.0 11.2 %all-to-all-done.16 = bf16[4,128,768]{2,1,0:T(8,128)(2,1)S(1)} async-done(((bf16[4,128,768]{2,1,0:T(8,128)(2,1)}), bf16[4,128,768]{2,1,0:T(8,128)(2,1)S(1)}, u32[]{:S(2)}, u32[]{:S(2)}) %all-to-all-start.16) | async-done | bytes 786464 | tf_op jit(solution)/shard_map/all_to_all | solution.py:40
  440.2 2.3 convolution_convert_fusion
  443.4 4.5 all-to-all-start.17
  448.8 5.8 shard_map.280
  457.7 3.6 all-to-all-start.18
  461.6 14.7 %shard_map.281 = (bf16[2048,256]{1,0:T(8,128)(2,1)}, bf16[1024,768]{1,0:T(8,128)(2,1)}, bf16[1024,768]{1,0:T(8,128)(2,1)}, f32[1,192]{1,0:T(1,128)}) custom-call(s32[32]{0:T(128)} %reshape.369.arrive_pos, s32[32]{0:T(128)} %reshape.370.ctx_pos, bf16[2048,64]{1,0:T(8,128)(2,1)} %get-tuple-element.144.q_ref, bf16[2048,64]{1,0:T(8,128)(2,1)} %get-tuple-element.145.k_ref, ...), custom_call_target="tpu_custom_call" | custom-call | flops 4000000000 | bytes 5000000 | tf_op jit(solution)/shard_map/pallas_call | solution.py:225
  477.3 3.2 collective-permute-done.13
  480.6 3.0 fusion.1
  483.6 11.3 %all-to-all-done.18 = bf16[8,192,768]{2,1,0:T(8,128)(2,1)S(1)} async-done(((bf16[8,192,768]{2,1,0:T(8,128)(2,1)}), bf16[8,192,768]{2,1,0:T(8,128)(2,1)S(1)}, u32[]{:S(2)}, u32[]{:S(2)}) %all-to-all-start.18) | async-done | bytes 2359328 | tf_op jit(solution)/shard_map/all_to_all | solution.py:40
  496.1 6.2 %all-to-all-start.19 = ((bf16[8,128,768]{2,1,0:T(8,128)(2,1)}), bf16[8,128,768]{2,1,0:T(8,128)(2,1)S(1)}, u32[]{:S(2)}, u32[]{:S(2)}) async-start(bf16[8,128,768]{2,1,0:T(8,128)(2,1)} %fusion.1), calls=%async_computation.19 | async-start | bytes 3145728 | tf_op jit(solution)/shard_map/all_to_all | solution.py:40
  505.9 21.4 %all-to-all-done.19 = bf16[8,128,768]{2,1,0:T(8,128)(2,1)S(1)} async-done(((bf16[8,128,768]{2,1,0:T(8,128)(2,1)}), bf16[8,128,768]{2,1,0:T(8,128)(2,1)S(1)}, u32[]{:S(2)}, u32[]{:S(2)}) %all-to-all-start.19) | async-done | bytes 1572896 | tf_op jit(solution)/shard_map/all_to_all | solution.py:40
  527.4 4.2 all-to-all-start.21
  533.8 4.8 shard_map.282
  538.6 2.9 all-to-all-done.21
  541.5 3.6 all-to-all-start.20
  545.2 13.2 %all-to-all-done.20 = bf16[8,80,768]{2,1,0:T(8,128)(2,1)S(1)} async-done(((bf16[8,80,768]{2,1,0:T(8,128)(2,1)}), bf16[8,80,768]{2,1,0:T(8,128)(2,1)S(1)}, u32[]{:S(2)}, u32[]{:S(2)}) %all-to-all-start.20) | async-done | bytes 983072 | tf_op jit(solution)/shard_map/all_to_all | solution.py:40
  559.5 6.6 %all-to-all-start.22 = ((bf16[8,80,768]{2,1,0:T(8,128)(2,1)}), bf16[8,80,768]{2,1,0:T(8,128)(2,1)S(1)}, u32[]{:S(2)}, u32[]{:S(2)}) async-start(bf16[8,80,768]{2,1,0:T(8,128)(2,1)} %broadcast_in_dim.135), calls=%async_computation.22 | async-start | bytes 1966080 | tf_op jit(solution)/shard_map/all_to_all | solution.py:40
  566.2 6.5 %shard_map.283 = (f32[2,96,3072]{2,1,0:T(8,128)}, f32[2,384,768]{2,1,0:T(8,128)}) custom-call(bf16[16,96,768]{2,1,0:T(8,128)(2,1)} %bitcast.157, bf16[16,96,768]{2,1,0:T(8,128)(2,1)} %bitcast.156), custom_call_target="tpu_custom_call" | custom-call | flops 1000000 | bytes 10000000 | tf_op jit(solution)/shard_map/pallas_call | solution.py:448
  572.6 10.2 %all-to-all-done.22 = bf16[8,80,768]{2,1,0:T(8,128)(2,1)S(1)} async-done(((bf16[8,80,768]{2,1,0:T(8,128)(2,1)}), bf16[8,80,768]{2,1,0:T(8,128)(2,1)S(1)}, u32[]{:S(2)}, u32[]{:S(2)}) %all-to-all-start.22) | async-done | bytes 983072 | tf_op jit(solution)/shard_map/all_to_all | solution.py:40
  587.3 3.3 shard_map.284
  (321 shorter events, 99.6 us)
Async XLA Ops:
  7.2 36.2 %copy-start = (bf16[2,96,3072]{2,1,0:T(8,128)(2,1)S(1)}, bf16[2,96,3072]{2,1,0:T(8,128)(2,1)}, u32[]{:S(2)}) copy-start(bf16[2,96,3072]{2,1,0:T(8,128)(2,1)} %param.28) | copy-start | bytes 3538948
  15.7 8.2 %copy-start.32 = (bf16[2,96,768]{2,1,0:T(8,128)(2,1)S(1)}, bf16[2,96,768]{2,1,0:T(8,128)(2,1)}, u32[]{:S(2)}) copy-start(bf16[2,96,768]{2,1,0:T(8,128)(2,1)} %param.24) | copy-start | bytes 884740
  15.8 19.8 %copy-start.9 = (bf16[1,128,768]{2,1,0:T(8,128)(2,1)S(1)}, bf16[1,128,768]{2,1,0:T(8,128)(2,1)}, u32[]{:S(2)}) copy-start(bf16[1,128,768]{2,1,0:T(8,128)(2,1)} %param.16) | copy-start | bytes 589828
  17.0 18.6 %all-to-all-start.1 = ((bf16[8,64,768]{2,1,0:T(8,128)(2,1)}), bf16[8,64,768]{2,1,0:T(8,128)(2,1)S(1)}, u32[]{:S(2)}, u32[]{:S(2)}) async-start(bf16[8,64,768]{2,1,0:T(8,128)(2,1)} %broadcast_in_dim.51), calls=%async_computation.1 | async-start | bytes 1572864 | tf_op jit(solution)/shard_map/all_to_all | solution.py:40
  35.6 40.6 %copy-start.18 = (bf16[8,64,768]{2,1,0:T(8,128)(2,1)}, bf16[8,64,768]{2,1,0:T(8,128)(2,1)S(1)}, u32[]{:S(2)}) copy-start(bf16[8,64,768]{2,1,0:T(8,128)(2,1)S(1)} %all-to-all-done.1) | copy-start | bytes 2359300
  36.9 29.4 %all-to-all-start = ((bf16[8,128,768]{2,1,0:T(8,128)(2,1)}), bf16[8,128,768]{2,1,0:T(8,128)(2,1)}, u32[]{:S(2)}, u32[]{:S(2)}) async-start(bf16[8,128,768]{2,1,0:T(8,128)(2,1)} %broadcast_in_dim.48), calls=%async_computation | async-start | bytes 3145728 | tf_op jit(solution)/shard_map/all_to_all | solution.py:40
  68.4 4.6 copy-start.54
  68.4 46.3 %all-to-all-start.2 = ((bf16[8,288,768]{2,1,0:T(8,128)(2,1)}), bf16[8,288,768]{2,1,0:T(8,128)(2,1)}, u32[]{:S(2)}, u32[]{:S(2)}) async-start(bf16[8,288,768]{2,1,0:T(8,128)(2,1)} %broadcast_in_dim.53), calls=%async_computation.2 | async-start | bytes 7077888 | tf_op jit(solution)/shard_map/all_to_all | solution.py:40
  74.0 6.2 %collective-permute-start = (bf16[8,128,768]{2,1,0:T(8,128)(2,1)}, bf16[8,128,768]{2,1,0:T(8,128)(2,1)}, u32[]{:S(2)}, u32[]{:S(2)}) collective-permute-start(bf16[8,128,768]{2,1,0:T(8,128)(2,1)} %all-to-all-done), channel_id=1, source_target_pairs={{0,1},{1,0},{2,3},{3,2},{4,5},{5,4},{6,7},{7,6},{8,9},{9,8},{10,11... | collective-permute-start | bytes 4718600 | tf_op jit(solution)/shard_map/ppermute | solution.py:48
  116.9 4.8 copy-start.2
  116.9 99.8 %copy-start.3 = (bf16[8,144,768]{2,1,0:T(8,128)(2,1)}, bf16[8,144,768]{2,1,0:T(8,128)(2,1)S(1)}, u32[]{:S(2)}) copy-start(bf16[8,144,768]{2,1,0:T(8,128)(2,1)S(1)} %get-tuple-element.118.rows_ref) | copy-start | bytes 5308420
  118.0 16.1 %collective-permute-start.1 = (bf16[768,384]{1,0:T(8,128)(2,1)}, bf16[768,384]{1,0:T(8,128)(2,1)}, u32[]{:S(2)}, u32[]{:S(2)}) collective-permute-start(bf16[768,384]{1,0:T(8,128)(2,1)} %bitcast.31), channel_id=1, source_target_pairs={{0,1},{1,0},{2,3},{3,2},{4,5},{5,4},{6,7},{7,6},{8,9},{9,8},{10,11... | collective-permute-start | bytes 1769480 | tf_op jit(solution)/shard_map/ppermute | solution.py:48
  151.1 4.4 collective-permute-start.2
  161.3 2.5 collective-permute-start.3
  165.1 14.5 %copy-start.36 = (f32[768]{0:T(1024)S(1)}, f32[768]{0:T(1024)}, u32[]{:S(2)}) copy-start(f32[768]{0:T(1024)} %get-tuple-element.204) | copy-start | bytes 9220
  179.8 24.8 %copy-start.43 = (f32[128]{0:T(128)}, f32[128]{0:T(128)S(1)}, u32[]{:S(2)}) copy-start(f32[128]{0:T(128)S(1)} %broadcast_multiply_fusion.2) | copy-start | bytes 1540
  180.0 24.6 %copy-start.59 = (f32[128]{0:T(128)}, f32[128]{0:T(128)S(1)}, u32[]{:S(2)}) copy-start(f32[128]{0:T(128)S(1)} %multiply_reduce_fusion.7) | copy-start | bytes 1540
  180.0 24.5 %copy-start.49 = (f32[128]{0:T(128)}, f32[128]{0:T(128)S(1)}, u32[]{:S(2)}) copy-start(f32[128]{0:T(128)S(1)} %fusion.41) | copy-start | bytes 1540
  180.5 31.7 %copy-start.19 = (bf16[1,128,768]{2,1,0:T(8,128)(2,1)S(1)}, bf16[1,128,768]{2,1,0:T(8,128)(2,1)}, u32[]{:S(2)}) copy-start(bf16[1,128,768]{2,1,0:T(8,128)(2,1)} %param.17) | copy-start | bytes 589828
  205.7 5.3 collective-permute-start.4
  213.1 15.5 %all-to-all-start.7 = ((bf16[4,128,768]{2,1,0:T(8,128)(2,1)}), bf16[4,128,768]{2,1,0:T(8,128)(2,1)S(1)}, u32[]{:S(2)}, u32[]{:S(2)}) async-start(bf16[4,128,768]{2,1,0:T(8,128)(2,1)} %broadcast_in_dim.56), calls=%async_computation.7 | async-start | bytes 1572864 | tf_op jit(solution)/shard_map/all_to_all | solution.py:40
  216.8 26.7 %copy-start.30 = (bf16[8,96,384]{2,1,0:T(8,128)(2,1)}, bf16[8,96,384]{2,1,0:T(8,128)(2,1)S(1)}, u32[]{:S(2)}) copy-start(bf16[8,96,384]{2,1,0:T(8,128)(2,1)S(1)} %pad_maximum_fusion.2) | copy-start | bytes 1769476
  216.8 25.8 %collective-permute-start.5 = (bf16[768,384]{1,0:T(8,128)(2,1)S(1)}, bf16[768,384]{1,0:T(8,128)(2,1)S(1)}, u32[]{:S(2)}, u32[]{:S(2)}) collective-permute-start(bf16[768,384]{1,0:T(8,128)(2,1)S(1)} %bitcast.174), channel_id=1, source_target_pairs={{0,1},{1,0},{2,3},{3,2},{4,5},{5,4},{6,7},{7,6},{8,9},{9,8},{10,11... | collective-permute-start | bytes 1769480 | tf_op jit(solution)/shard_map/ppermute | solution.py:48
  225.8 17.6 %copy-start.53 = (f32[768]{0:T(1024)S(1)}, f32[768]{0:T(1024)}, u32[]{:S(2)}) copy-start(f32[768]{0:T(1024)} %get-tuple-element.201) | copy-start | bytes 9220
  228.6 42.1 %copy-start.4 = (bf16[4,128,768]{2,1,0:T(8,128)(2,1)}, bf16[4,128,768]{2,1,0:T(8,128)(2,1)S(1)}, u32[]{:S(2)}) copy-start(bf16[4,128,768]{2,1,0:T(8,128)(2,1)S(1)} %all-to-all-done.7) | copy-start | bytes 2359300
  259.8 4.0 collective-permute-start.6
  270.4 2.5 collective-permute-start.7
  270.8 4.3 collective-permute-start.8
  275.1 15.5 %all-to-all-start.10 = ((bf16[4,128,768]{2,1,0:T(8,128)(2,1)}), bf16[4,128,768]{2,1,0:T(8,128)(2,1)S(1)}, u32[]{:S(2)}, u32[]{:S(2)}) async-start(bf16[4,128,768]{2,1,0:T(8,128)(2,1)} %fusion.13), calls=%async_computation.10 | async-start | bytes 1572864 | tf_op jit(solution)/shard_map/all_to_all | solution.py:40
  290.6 3.3 collective-permute-start.9
  296.1 15.5 %all-to-all-start.11 = ((bf16[4,128,768]{2,1,0:T(8,128)(2,1)}), bf16[4,128,768]{2,1,0:T(8,128)(2,1)S(1)}, u32[]{:S(2)}, u32[]{:S(2)}) async-start(bf16[4,128,768]{2,1,0:T(8,128)(2,1)} %fusion.12), calls=%async_computation.11 | async-start | bytes 1572864 | tf_op jit(solution)/shard_map/all_to_all | solution.py:40
  299.6 12.9 %copy-start.46 = (f32[128]{0:T(128)S(1)}, f32[128]{0:T(128)}, u32[]{:S(2)}) copy-start(f32[128]{0:T(128)} %copy-done.45) | copy-start | bytes 1540
  299.7 12.9 %copy-start.52 = (f32[128]{0:T(128)S(1)}, f32[128]{0:T(128)}, u32[]{:S(2)}) copy-start(f32[128]{0:T(128)} %copy-done.51) | copy-start | bytes 1540
  299.7 13.7 %copy-start.62 = (f32[128]{0:T(128)S(1)}, f32[128]{0:T(128)}, u32[]{:S(2)}) copy-start(f32[128]{0:T(128)} %copy-done.61) | copy-start | bytes 1540
  299.7 13.7 %copy-start.33 = (f32[768]{0:T(1024)S(1)}, f32[768]{0:T(1024)}, u32[]{:S(2)}) copy-start(f32[768]{0:T(1024)} %get-tuple-element.198) | copy-start | bytes 9220
  314.9 6.1 %copy-start.27 = (bf16[12,128,64]{1,2,0:T(8,128)(2,1)S(1)}, bf16[12,128,64]{1,2,0:T(8,128)(2,1)}, u32[]{:S(2)}) copy-start(bf16[12,128,64]{1,2,0:T(8,128)(2,1)} %copy-done.26) | copy-start | bytes 589828
  316.5 13.3 %all-to-all-start.12 = ((bf16[16,128,64]{1,2,0:T(8,128)(2,1)}), bf16[16,128,64]{1,2,0:T(8,128)(2,1)S(1)}, u32[]{:S(2)}, u32[]{:S(2)}) async-start(bf16[16,128,64]{1,2,0:T(8,128)(2,1)} %concatenate.66), calls=%async_computation.12 | async-start | bytes 524288 | tf_op jit(solution)/shard_map/all_to_all | solution.py:40
  330.8 33.0 %all-to-all-start.13 = ((bf16[8,192,768]{2,1,0:T(8,128)(2,1)}), bf16[8,192,768]{2,1,0:T(8,128)(2,1)S(1)}, u32[]{:S(2)}, u32[]{:S(2)}) async-start(bf16[8,192,768]{2,1,0:T(8,128)(2,1)} %shard_map.276), calls=%async_computation.13 | async-start | bytes 4718592 | tf_op jit(solution)/shard_map/all_to_all | solution.py:40
  349.6 4.2 collective-permute-start.10
  392.8 5.1 copy-start.39
  392.8 5.7 copy-start.40
  393.7 13.2 %all-to-all-start.15 = ((bf16[4,128,768]{2,1,0:T(8,128)(2,1)}), bf16[4,128,768]{2,1,0:T(8,128)(2,1)S(1)}, u32[]{:S(2)}, u32[]{:S(2)}) async-start(bf16[4,128,768]{2,1,0:T(8,128)(2,1)} %broadcast_in_dim.62), calls=%async_computation.15 | async-start | bytes 1572864 | tf_op jit(solution)/shard_map/all_to_all | solution.py:40
  406.9 5.4 copy-start.5
  406.9 5.4 collective-permute-start.11
  418.9 2.5 collective-permute-start.12
  421.4 5.9 copy-start.23
  423.6 16.0 %copy-start.42 = (f32[128]{0:T(128)S(1)}, f32[128]{0:T(128)}, u32[]{:S(2)}) copy-start(f32[128]{0:T(128)} %copy-done.41) | copy-start | bytes 1540
  423.6 16.0 %copy-start.48 = (f32[128]{0:T(128)S(1)}, f32[128]{0:T(128)}, u32[]{:S(2)}) copy-start(f32[128]{0:T(128)} %copy-done.47) | copy-start | bytes 1540
  423.6 15.6 %all-to-all-start.16 = ((bf16[4,128,768]{2,1,0:T(8,128)(2,1)}), bf16[4,128,768]{2,1,0:T(8,128)(2,1)S(1)}, u32[]{:S(2)}, u32[]{:S(2)}) async-start(bf16[4,128,768]{2,1,0:T(8,128)(2,1)} %fusion.11), calls=%async_computation.16 | async-start | bytes 1572864 | tf_op jit(solution)/shard_map/all_to_all | solution.py:40
  427.3 12.6 %copy-start.58 = (f32[128]{0:T(128)S(1)}, f32[128]{0:T(128)}, u32[]{:S(2)}) copy-start(f32[128]{0:T(128)} %copy-done.57) | copy-start | bytes 1540
  427.3 68.1 %all-gather.5.cloned.1.call-start = ((), (), s32[]{:S(2)}) async-start(), calls=%async_computation.23 | async-start | bytes 2506752 | tf_op jit(solution)/shard_map/all_gather | solution.py:681
  440.2 7.7 %copy-start.25 = (bf16[12,128,64]{1,2,0:T(8,128)(2,1)S(1)}, bf16[12,128,64]{1,2,0:T(8,128)(2,1)}, u32[]{:S(2)}) copy-start(bf16[12,128,64]{1,2,0:T(8,128)(2,1)} %copy-done.24) | copy-start | bytes 589828
  443.4 13.3 %all-to-all-start.17 = ((bf16[16,128,64]{1,2,0:T(8,128)(2,1)}), bf16[16,128,64]{1,2,0:T(8,128)(2,1)S(1)}, u32[]{:S(2)}, u32[]{:S(2)}) async-start(bf16[16,128,64]{1,2,0:T(8,128)(2,1)} %concatenate.67), calls=%async_computation.17 | async-start | bytes 524288 | tf_op jit(solution)/shard_map/all_to_all | solution.py:40
  457.7 37.2 %all-to-all-start.18 = ((bf16[8,192,768]{2,1,0:T(8,128)(2,1)}), bf16[8,192,768]{2,1,0:T(8,128)(2,1)S(1)}, u32[]{:S(2)}, u32[]{:S(2)}) async-start(bf16[8,192,768]{2,1,0:T(8,128)(2,1)} %shard_map.280), calls=%async_computation.18 | async-start | bytes 4718592 | tf_op jit(solution)/shard_map/all_to_all | solution.py:40
  461.3 104.8 %all-gather.7.cloned.1.call-start = ((), (), s32[]{:S(2)}) async-start(), calls=%async_computation.24 | async-start | bytes 2506752 | tf_op jit(solution)/shard_map/all_gather | solution.py:685
  476.3 4.3 collective-permute-start.13
  496.1 6.2 %copy-start.10 = (bf16[1,128,768]{2,1,0:T(8,128)(2,1)S(1)}, bf16[1,128,768]{2,1,0:T(8,128)(2,1)}, u32[]{:S(2)}) copy-start(bf16[1,128,768]{2,1,0:T(8,128)(2,1)} %param.16) | copy-start | bytes 589828
  496.1 31.3 %all-to-all-start.19 = ((bf16[8,128,768]{2,1,0:T(8,128)(2,1)}), bf16[8,128,768]{2,1,0:T(8,128)(2,1)S(1)}, u32[]{:S(2)}, u32[]{:S(2)}) async-start(bf16[8,128,768]{2,1,0:T(8,128)(2,1)} %fusion.1), calls=%async_computation.19 | async-start | bytes 3145728 | tf_op jit(solution)/shard_map/all_to_all | solution.py:40
  527.4 14.2 %all-to-all-start.21 = ((bf16[16,16,768]{2,1,0:T(8,128)(2,1)}), bf16[16,16,768]{2,1,0:T(8,128)(2,1)S(1)}, u32[]{:S(2)}, u32[]{:S(2)}) async-start(bf16[16,16,768]{2,1,0:T(8,128)(2,1)} %pad.6.clone), calls=%async_computation.21 | async-start | bytes 786432 | tf_op jit(solution)/shard_map/all_to_all | solution.py:40
  541.5 16.8 %all-to-all-start.20 = ((bf16[8,80,768]{2,1,0:T(8,128)(2,1)}), bf16[8,80,768]{2,1,0:T(8,128)(2,1)S(1)}, u32[]{:S(2)}, u32[]{:S(2)}) async-start(bf16[8,80,768]{2,1,0:T(8,128)(2,1)} %shard_map.282), calls=%async_computation.20 | async-start | bytes 1966080 | tf_op jit(solution)/shard_map/all_to_all | solution.py:40
  559.5 23.3 %all-to-all-start.22 = ((bf16[8,80,768]{2,1,0:T(8,128)(2,1)}), bf16[8,80,768]{2,1,0:T(8,128)(2,1)S(1)}, u32[]{:S(2)}, u32[]{:S(2)}) async-start(bf16[8,80,768]{2,1,0:T(8,128)(2,1)} %broadcast_in_dim.135), calls=%async_computation.22 | async-start | bytes 1966080 | tf_op jit(solution)/shard_map/all_to_all | solution.py:40
  566.2 18.0 %copy-start.12 = (f32[128,768]{1,0:T(8,128)S(1)}, f32[128,768]{1,0:T(8,128)}, u32[]{:S(2)}) copy-start(f32[128,768]{1,0:T(8,128)} %copy-done.11) | copy-start | bytes 1179652
  582.8 3.0 collective-permute-start.14
  585.8 4.8 copy-start.1
  (34 other events, 55.7 us)
Sparse Core Ops, SparseCore 0:
  430.5 53.8 all-gather.4
  496.2 59.7 all-gather.6
